TPU v7x, 512 devices: a whole 4x8x8 slice. The times are simulated.
512 devices in a mesh: blk: 16 (over y, x_hi), rep: 32 (over x_lo, z, core).
Axes of the slice: x: 4 (x_hi: 2, x_lo: 2; x = x_hi * 2 + x_lo), y: 8, z: 8, core: 2. Of those that a mesh axis runs over, the one named last changes fastest.
Arguments:
- features: bfloat16 [131072, 2048], P(('rep', 'blk'))
- head_weight: bfloat16 [2048, 512], replicated, may hold values from -0.125 to 0.125
- partner: int32 [131072], P(('rep', 'blk')), may hold values from 0 to 4095, as said below
Outputs:
- update: float32 [2048, 512], P('blk')
Inputs may be any that keep to these rules, and one draw needn't show every extreme that they name: partner pairs the images of each replica group: partner[partner[i]] = i and partner[i] != i, indices counted from the group's first image.
All inputs are finite; a program needn't handle non-finite values.
Results may differ from a plain program's by a relative error of at most 0.004.
Values may be sent and summed in bfloat16 or wider, within the bound.
No kernel may reach another device: no remote copies, remote signals or barrier semaphores. Data moves between devices by JAX's collectives and lax.ppermute only.
A program may use at most 64 MiB of HBM per device.

v0:
```python
import jax
import jax.numpy as jnp
from jax import lax
from jax.sharding import PartitionSpec as P

softness_factor = 0.05


def on_device(features, head_weight, partner):
    rows_here = features.shape[0]
    row_start = lax.axis_index("blk") * rows_here
    hidden = jnp.dot(features, head_weight, preferred_element_type=jnp.float32)
    row_norm = jnp.sqrt(jnp.sum(hidden * hidden, axis=1, keepdims=True) + 1e-05)
    unit = hidden / row_norm
    unit_rows_halfprec = unit.astype(jnp.bfloat16)
    global_rows = row_start + jnp.arange(rows_here, dtype=jnp.int32)
    gathered = lax.all_gather(unit_rows_halfprec, "blk", axis=0, tiled=True)
    logit_scores = (
        lax.dot_general(
            unit_rows_halfprec,
            gathered,
            (((1,), (1,)), ((), ())),
            preferred_element_type=jnp.float32,
        )
        / softness_factor
    )
    columns = jnp.arange(gathered.shape[0], dtype=jnp.int32)
    self_mask = global_rows[:, None] == columns[None, :]
    logit_scores, self_mask, columns = (logit_scores, self_mask, columns)
    log_sum = jnp.log(jnp.sum(jnp.where(self_mask, 0.0, jnp.exp(logit_scores)), axis=1))
    log_all = lax.all_gather(log_sum, "blk", axis=0, tiled=True)
    target = (columns[None, :] == partner[:, None]).astype(jnp.float32)
    row_weight = (
        jnp.where(self_mask, 0.0, jnp.exp(logit_scores - log_sum[:, None])) - target
    ).astype(jnp.bfloat16)
    column_weight = (
        jnp.where(self_mask, 0.0, jnp.exp(logit_scores - log_all[None, :])) - target
    ).astype(jnp.bfloat16)
    unit_gradient_rows = (
        jnp.dot(row_weight, gathered, preferred_element_type=jnp.float32)
        + jnp.dot(column_weight, gathered, preferred_element_type=jnp.float32)
    ) / softness_factor
    along = jnp.sum(unit * unit_gradient_rows, axis=1, keepdims=True)
    grad_hidden = ((unit_gradient_rows - unit * along) / row_norm).astype(jnp.bfloat16)
    channel_total = head_weight.shape[0]
    entry_count = channel_total * head_weight.shape[1]
    partial_rows = lax.psum_scatter(
        lax.dot_general(
            features, grad_hidden, (((0,), (0,)), ((), ())), preferred_element_type=jnp.float32
        ),
        "blk",
        scatter_dimension=0,
        tiled=True,
    )
    summed = lax.psum(partial_rows, "rep")
    squares = lax.psum(jnp.sum(summed * summed), "blk")
    return summed / jnp.sqrt(squares / entry_count + 1e-06)


def solution(mesh):
    return jax.shard_map(
        on_device,
        mesh=mesh,
        in_specs=(P(("rep", "blk"), None), P(), P(("rep", "blk"))),
        out_specs=P("blk", None),
        check_vma=False,
    )
```

profile of v0, /device:TPU:2, one launch (start us, length us, event | category | flops | bytes accessed | tf_op | source)
XLA Modules:
  0.0 664.3 jit_solution(7478953457284558776)
XLA Ops:
  6.5 0.0 copy-start
  6.5 0.0 all-gather.3.cloned.1.call-start
  6.5 1.6 copy-done
  8.1 2.0 multiply_reduce_fusion.1
  10.1 0.8 fusion.24
  11.0 0.0 all-gather.3.cloned.1.call-update
  11.0 0.0 reduce-scatter.2.cloned.1.call-start
  11.1 0.0 copy-start.3
  11.1 109.1 %all-gather.3.cloned.1.call-done = bf16[4096,512]{1,0:T(8,128)(2,1)} async-done(((bf16[256,512]{1,0:T(8,128)(2,1)}), bf16[4096,512]{1,0:T(8,128)(2,1)}) %all-gather.3.cloned.1.call-update) | async-done | bytes 4194320 | tf_op jit(solution)/shard_map/all_gather | solution.py:17
  120.2 0.0 copy-start.2
  120.2 4.0 select_reduce_fusion
  124.2 38.4 %all-gather = f32[16,1,256]{2,1,0:T(1,128)S(1)} all-gather(f32[1,1,256]{2,1,0:T(1,128)S(1)} %bitcast.12), channel_id=1, replica_groups=mesh['blk'=16,'rep'=32] {'blk'}, dimensions={0}, use_global_device_ids=true | all-gather | bytes 17408 | tf_op jit(solution)/shard_map/all_gather | solution.py:31
  162.6 0.0 copy-done.3
  162.6 0.0 copy-done.2
  162.6 1.8 fusion.4
  164.4 0.0 copy-start.1
  164.4 1.8 multiply_reduce_fusion
  166.2 0.0 copy-done.1
  166.2 2.9 convolution_bitcast_fusion
  169.1 0.0 reduce-scatter.2.cloned.1.call-update
  169.1 0.0 all-reduce.2.cloned.1.call-start
  169.2 214.6 %reduce-scatter.2.cloned.1.call-done = f32[128,512]{0,1:T(8,128)} async-done(((f32[2048,512]{0,1:T(8,128)}), f32[128,512]{0,1:T(8,128)}) %reduce-scatter.2.cloned.1.call-update) | async-done | bytes 262160 | tf_op jit(solution)/shard_map/reduce_scatter | solution.py:47
  383.8 0.0 all-reduce.2.cloned.1.call-update
  383.8 227.9 %all-reduce.2.cloned.1.call-done = f32[128,512]{0,1:T(8,128)} async-done(((f32[128,512]{0,1:T(8,128)}), f32[128,512]{0,1:T(8,128)}) %all-reduce.2.cloned.1.call-update) | async-done | bytes 262160 | tf_op jit(solution)/shard_map/psum | solution.py:55
  611.7 1.6 multiply_reduce_fusion.2
  613.3 41.9 %psum.15 = f32[]{:T(128)} all-reduce(f32[]{:T(128)} %multiply_reduce_fusion.2), channel_id=1, replica_groups=mesh['blk'=16,'rep'=32] {'blk'}, use_global_device_ids=true, to_apply=%region_6.7 | all-reduce | flops 1 | bytes 8 | tf_op jit(solution)/shard_map/psum | solution.py:56
  655.9 1.0 broadcast_divide_fusion.1
  656.9 0.8 copy.5
  (3 shorter events, 0.0 us)
Async XLA Ops:
  6.5 1.6 copy-start
  6.5 113.6 %all-gather.3.cloned.1.call-start = ((), (), s32[]{:S(2)}) async-start(), calls=%async_computation.1 | async-start | bytes 4456448 | tf_op jit(solution)/shard_map/all_gather | solution.py:17
  11.0 372.8 %reduce-scatter.2.cloned.1.call-start = ((), (), s32[]{:S(2)}) async-start(), calls=%async_computation.2 | async-start | bytes 4456448 | tf_op jit(solution)/shard_map/reduce_scatter | solution.py:47
  11.1 151.6 %copy-start.3 = (s32[256]{0:T(256)S(1)}, s32[256]{0:T(256)}, u32[]{:S(2)}) copy-start(s32[256]{0:T(256)} %param.5) | copy-start | bytes 3076
  120.2 42.5 %copy-start.2 = (bf16[4096,512]{1,0:T(8,128)(2,1)S(1)}, bf16[4096,512]{1,0:T(8,128)(2,1)}, u32[]{:S(2)}) copy-start(bf16[4096,512]{1,0:T(8,128)(2,1)} %all-gather.3.cloned.1.call-done) | copy-start | bytes 12582916
  164.4 1.9 copy-start.1
  169.1 442.6 %all-reduce.2.cloned.1.call-start = ((), (), s32[]{:S(2)}) async-start(), calls=%async_computation.3 | async-start | bytes 524288 | tf_op jit(solution)/shard_map/psum | solution.py:55
Sparse Core Ops, SparseCore 0:
  11.1 109.0 all-gather.2
  169.3 214.4 reduce-scatter.1
  386.9 224.7 all-reduce.1
where the time goes:
time: 665 us; the launch traced here: 664 us
  waiting for transfers between devices  552 us (83%)
  blocking collectives  80.3 us (12%)
  between operations  13.9 us (2%)
  matrix products  12.5 us (2%)
    psum x1, waiting for transfers between devices, on_device(): summed = lax.psum(partial_rows, 'rep')  228 us
    reduce_scatter x1, waiting for transfers between devices, on_device(): lax.psum_scatter(lax.dot_general(features, grad_hidden, (((0,), (0,)), ((...  215 us
    all_gather x1, waiting for transfers between devices, on_device(): gathered = lax.all_gather(unit_rows_halfprec, 'blk', axis=0, tiled=True)  109 us
    psum x1, blocking collectives, on_device(): squares = lax.psum(jnp.sum(summed * summed), 'blk')  41.9 us
    all_gather x1, blocking collectives, on_device(): log_all = lax.all_gather(log_sum, 'blk', axis=0, tiled=True)  38.4 us
  transfers between devices with their start and end apart: 3, of which 3 were waited for; matrix products, arithmetic and copies ran while one was open for 0% of the time, Pallas kernels for 0%

commit v1 on v0

v1 whole, which is shorter than its diff:
```python
import jax
import jax.numpy as jnp
from jax import lax
from jax.experimental import pallas as pl
from jax.experimental.pallas import tpu as pltpu
from jax.sharding import PartitionSpec as P

softness_factor = 0.05
EXP2_SCALE = 1.4426950408889634 / softness_factor
BOTH = ("blk", "rep")
Y, XH, XL, Z, CORE = 8, 2, 2, 8, 2


def device_of(y, xh, xl, z, core):
    return (y * XH + xh) * (XL * Z * CORE) + (xl * Z + z) * CORE + core


PLACES = [
    (y, xh, xl, z, core)
    for y in range(Y)
    for xh in range(XH)
    for xl in range(XL)
    for z in range(Z)
    for core in range(CORE)
]
TO_HOST = [(device_of(y, h, l, z, c), device_of(y, c, l, z, h)) for y, h, l, z, c in PLACES]
TO_SIBLING = [(device_of(y, h, l, z, c), device_of(y, c, l, z, 1 - h)) for y, h, l, z, c in PLACES]
OTHER_CORE = [(r, r ^ 1) for r in range(XL * Z * CORE)]


def along_y(step):
    return [(b, ((b // XH + step) % Y) * XH + b % XH) for b in range(Y * XH)]


def contrast_kernel(*refs):
    core_ref, column_ref, side_ref = refs[:3]
    pieces = refs[3:-6]
    keep_ref, send_ref, units, per_lane, per_column, inverse = refs[-6:]
    wide = units.shape[1]
    blocks = units.shape[0]
    row = 0
    for piece in pieces:
        rows = piece.shape[0]
        block, start = divmod(row, wide)
        units[block, start : start + rows, :] = piece[...]
        row += rows
    per_lane[...] = jnp.zeros_like(per_lane)
    per_column[...] = jnp.zeros_like(per_column)

    def exponentials(left, right):
        scores = lax.dot_general(
            left, right, (((1,), (1,)), ((), ())), preferred_element_type=jnp.float32
        )
        return jnp.exp2(scores * EXP2_SCALE)

    def over_rows(values):
        return values.reshape(values.shape[0] // 8, 8, values.shape[1]).sum(0)

    def one_block(i, unused):
        left = units[i]
        values = exponentials(left, left)
        rows = lax.broadcasted_iota(jnp.int32, values.shape, 0)
        columns = lax.broadcasted_iota(jnp.int32, values.shape, 1)
        per_column[i] += over_rows(jnp.where(rows == columns, 0.0, values))

        def one_pair(j, unused):
            values = exponentials(left, units[j])
            per_column[j] += over_rows(values)
            per_lane[i] += sum(values[:, k : k + 128] for k in range(0, wide, 128))
            return unused

        return lax.fori_loop(i + 1, blocks, one_pair, unused)

    lax.fori_loop(0, blocks, one_block, 0)

    def invert(i, unused):
        total = per_column[i].sum(0, keepdims=True) + per_lane[i].T.sum(0, keepdims=True)
        inverse[i] = 1.0 / total
        return unused

    lax.fori_loop(0, blocks, invert, 0)

    own = units[0, :256, :]
    inverse_own = jnp.broadcast_to(inverse[0][:, :256], (128, 256)).T[:, :1]
    partner = side_ref[:, 0:1]
    row_ids = lax.broadcasted_iota(jnp.int32, (256, wide), 0)
    column_ids = lax.broadcasted_iota(jnp.int32, (256, wide), 1)

    def weigh(j, total):
        right = units[j]
        values = exponentials(own, right) * (inverse_own + inverse[j])
        values = jnp.where(row_ids == column_ids + j * wide, 0.0, values)
        values = jnp.where(column_ref[j] == partner, values - 2.0, values)
        return total + jnp.dot(
            values.astype(jnp.bfloat16), right, preferred_element_type=jnp.float32
        )

    grad_unit = lax.fori_loop(0, blocks, weigh, jnp.zeros(own.shape, jnp.float32))
    grad_unit = grad_unit * (1.0 / softness_factor)
    unit = own.astype(jnp.float32)
    along = jnp.sum(unit * grad_unit, axis=1, keepdims=True)
    grad_hidden = ((grad_unit - unit * along) * side_ref[:, 1:2]).astype(jnp.bfloat16)
    first, second = grad_hidden[:, :256], grad_hidden[:, 256:]
    low = core_ref[0] == 0
    keep_ref[...] = jnp.where(low, first, second)
    send_ref[...] = jnp.where(low, second, first)


def contrast(core, column_index, side, pieces):
    rows, width = pieces[0].shape
    half = jax.ShapeDtypeStruct((rows, width // 2), jnp.bfloat16)
    vmem = pl.BlockSpec(memory_space=pltpu.VMEM)
    return pl.pallas_call(
        contrast_kernel,
        out_shape=(half, half),
        in_specs=[pl.BlockSpec(memory_space=pltpu.SMEM)] + [vmem] * (2 + len(pieces)),
        out_specs=(vmem, vmem),
        scratch_shapes=[
            pltpu.VMEM((8, 512, width), jnp.bfloat16),
            pltpu.VMEM((8, 512, 128), jnp.float32),
            pltpu.VMEM((8, 8, 512), jnp.float32),
            pltpu.VMEM((8, 1, 512), jnp.float32),
        ],
        compiler_params=pltpu.CompilerParams(vmem_limit_bytes=40 * 1024 * 1024),
        cost_estimate=pl.CostEstimate(
            flops=14_000_000_000, bytes_accessed=5_000_000, transcendentals=10_000_000
        ),
        name="contrast",
    )(core, column_index, side, *pieces)


def on_device(features, head_weight, partner):
    rows = features.shape[0]
    channels, width = head_weight.shape
    y = lax.axis_index("blk") // XH
    core = lax.axis_index("rep") % CORE

    hidden = jnp.dot(features, head_weight, preferred_element_type=jnp.float32)
    row_norm = jnp.sqrt(jnp.sum(hidden * hidden, axis=1, keepdims=True) + 1e-05)
    unit = (hidden / row_norm).astype(jnp.bfloat16)
    side = jnp.stack([partner.astype(jnp.float32), 1.0 / row_norm[:, 0]])

    own = lax.ppermute(unit, BOTH, TO_HOST)
    up, down = along_y(1), along_y(-1)
    from_below, from_above = own, own
    near, places = [], []
    for distance in range(1, 4):
        from_below = lax.ppermute(from_below, "blk", up)
        from_above = lax.ppermute(from_above, "blk", down)
        near.append(jnp.concatenate([from_below, from_above]))
        places.append(((y - distance) % Y, (y + distance) % Y))
    half = rows // 2
    near.append(
        jnp.concatenate(
            [
                lax.ppermute(from_below[:half], "blk", up),
                lax.ppermute(from_above[half:], "blk", down),
            ]
        )
    )
    places.append(((y + Y // 2) % Y,))

    pieces = [own, lax.ppermute(own, "rep", OTHER_CORE)]
    starts = [(y * 2 + core) * rows, (y * 2 + 1 - core) * rows]
    for block, where in zip(near, places):
        pieces += [block, lax.ppermute(block, "rep", OTHER_CORE)]
        starts += [(w * 2 + core) * rows for w in where]
        starts += [(w * 2 + 1 - core) * rows for w in where]
    column_index = (
        jnp.stack(starts)[:, None] + jnp.arange(rows, dtype=jnp.int32)[None, :]
    ).astype(jnp.float32).reshape(8, 1, 512)

    later, own_again = lax.optimization_barrier((features, own))
    rows_here = lax.ppermute(later, BOTH, TO_HOST)
    rows_beside = lax.ppermute(later, BOTH, TO_SIBLING)
    side_here = lax.ppermute(side, BOTH, TO_HOST)

    kept, sent = contrast(core.reshape(1).astype(jnp.int32), column_index, side_here.T, pieces)
    beside = lax.ppermute(sent, "rep", OTHER_CORE)

    def contract(left, right):
        return lax.dot_general(
            left, right, (((0,), (0,)), ((), ())), preferred_element_type=jnp.float32
        )

    partial = (contract(rows_here, kept) + contract(rows_beside, beside)).astype(jnp.bfloat16)
    tiles = partial.reshape(channels // 8, 8, 2, 128).transpose(0, 2, 1, 3).reshape(512, 8, 128)
    received = lax.all_to_all(tiles, BOTH, 0, 0)
    fragment = received.reshape(256, 2, 8, 128).astype(jnp.float32).sum(0)
    spread = lax.all_to_all(jnp.broadcast_to(fragment[None], (32, 2, 8, 128)), "rep", 0, 0)
    gradient = spread.reshape(16, 2, 2, 8, 128).transpose(0, 3, 2, 1, 4).reshape(128, width)
    squares = jnp.sum(gradient * gradient)
    squares = lax.all_to_all(jnp.broadcast_to(squares, (16, 128)), "blk", 0, 0)
    total = jnp.sum(squares[:, 0])
    return gradient * lax.rsqrt(total / (channels * width) + 1e-06)


def solution(mesh):
    return jax.shard_map(
        on_device,
        mesh=mesh,
        in_specs=(P(("rep", "blk"), None), P(), P(("rep", "blk"))),
        out_specs=P("blk", None),
        check_vma=False,
    )
```

time: 665 us -> 197 us (0.30)
  the two profiles are of different devices: /device:TPU:2 before, /device:TPU:8 now
where the time goes in v1:
time: 197 us; the launch traced here: 196 us
  blocking collectives  81.4 us (41%)
  starting transfers between devices  59.9 us (30%)
  Pallas kernels  26.3 us (13%)
  waiting for transfers between devices  11.8 us (6%)
  local copies, waits for them, and re-layouts  10 us (5%)
  matrix products  3.01 us (2%)
  other arithmetic  2.43 us (1%)
    all_to_all x1, blocking collectives, on_device(): received = lax.all_to_all(tiles, BOTH, 0, 0)  50.4 us
    pallas_call x1, Pallas kernels, contrast(): pl.pallas_call(contrast_kernel, out_shape=(half, half), in_specs=[pl.Bloc...  26.3 us
    all_to_all x1, blocking collectives, on_device(): lax.all_to_all(jnp.broadcast_to(fragment[None], (32, 2, 8, 128)), 'rep',...  17.3 us
    ppermute x3, starting transfers between devices, on_device(): from_above = lax.ppermute(from_above, 'blk', down)  16.4 us
    ppermute x4, starting transfers between devices, on_device(): pieces += [block, lax.ppermute(block, 'rep', OTHER_CORE)]  16 us
    all_to_all x1, blocking collectives, on_device(): squares = lax.all_to_all(jnp.broadcast_to(squares, (16, 128)), 'blk', 0, 0)  13.7 us
    ppermute x1, waiting for transfers between devices, on_device(): lax.ppermute(from_below[:half], 'blk', up)  6.74 us
    ppermute x3, starting transfers between devices, on_device(): from_below = lax.ppermute(from_below, 'blk', up)  5.76 us
  transfers between devices with their start and end apart: 18, of which 4 were waited for; matrix products, arithmetic and copies ran while one was open for 4% of the time, Pallas kernels for 13%

profile of v1, /device:TPU:8, one launch (start us, length us, event | category | flops | bytes accessed | tf_op | source)
XLA Modules:
  0.0 196.1 jit_solution(10999929126299601524)
XLA Ops:
  0.0 1.6 copy-done
  1.6 2.0 %multiply_reduce_fusion = (f32[256]{0:T(256)S(1)}, f32[256,512]{1,0:T(8,128)S(1)}) fusion(bf16[256,2048]{1,0:T(8,128)(2,1)} %param.3, bf16[2048,512]{1,0:T(8,128)(2,1)S(1)} %copy-done), kind=kOutput, calls=%fused_computation.4 | convolution fusion | flops 537132800 | bytes 3671040 | tf_op jit(solution)/shard_map/dot_general | solution.py:138
  3.8 1.3 collective-permute-start
  5.1 7.7 %collective-permute-start.5 = (bf16[256,512]{1,0:T(8,128)(2,1)}, bf16[256,512]{1,0:T(8,128)(2,1)S(1)}, u32[]{:S(2)}, u32[]{:S(2)}) collective-permute-start(bf16[256,512]{1,0:T(8,128)(2,1)} %collective-permute-done.refs_3_), channel_id=1, source_target_pairs={{0,448},{32,480},{64,0},{96,32},{128,64},{160,96},{192,128},{224,1... | collective-permute-start | bytes 786440 | tf_op jit(solution)/shard_map/ppermute | solution.py:149
  12.8 1.9 collective-permute-start.4
  14.8 3.5 %collective-permute-done.5 = bf16[256,512]{1,0:T(8,128)(2,1)S(1)} collective-permute-done((bf16[256,512]{1,0:T(8,128)(2,1)}, bf16[256,512]{1,0:T(8,128)(2,1)S(1)}, u32[]{:S(2)}, u32[]{:S(2)}) %collective-permute-start.5) | collective-permute-done | bytes 262176 | tf_op jit(solution)/shard_map/ppermute | solution.py:149
  18.2 4.3 %collective-permute-start.8 = (bf16[256,512]{1,0:T(8,128)(2,1)S(1)}, bf16[256,512]{1,0:T(8,128)(2,1)S(1)}, u32[]{:S(2)}, u32[]{:S(2)}) collective-permute-start(bf16[256,512]{1,0:T(8,128)(2,1)S(1)} %collective-permute-done.5), channel_id=1, source_target_pairs={{0,448},{32,480},{64,0},{96,32},{128,64},{160,96},{192,128},{224,1... | collective-permute-start | bytes 786440 | tf_op jit(solution)/shard_map/ppermute | solution.py:149
  22.5 1.9 collective-permute-start.7
  24.5 0.8 copy.13
  25.3 1.6 collective-permute-start.2
  26.8 1.0 constant_dynamic-update-slice_fusion.1
  28.4 4.4 %collective-permute-start.11 = (bf16[256,512]{1,0:T(8,128)(2,1)S(1)}, bf16[256,512]{1,0:T(8,128)(2,1)S(1)}, u32[]{:S(2)}, u32[]{:S(2)}) collective-permute-start(bf16[256,512]{1,0:T(8,128)(2,1)S(1)} %collective-permute-done.8), channel_id=1, source_target_pairs={{0,448},{32,480},{64,0},{96,32},{128,64},{160,96},{192,128},{224,1... | collective-permute-start | bytes 786440 | tf_op jit(solution)/shard_map/ppermute | solution.py:149
  32.8 1.9 collective-permute-start.10
  34.7 1.0 constant_dynamic-update-slice_fusion.refs_5_
  35.7 10.3 %collective-permute-start.6 = (bf16[512,512]{1,0:T(8,128)(2,1)S(1)}, bf16[512,512]{1,0:T(8,128)(2,1)}, u32[]{:S(2)}, u32[]{:S(2)}) collective-permute-start(bf16[512,512]{1,0:T(8,128)(2,1)S(1)} %constant_dynamic-update-slice_fusion.refs_5_), channel_id=1, source_target_pairs={{0,1},{1,0},{2,3},{3,2},{4,5},{5,4},{6,7},{7,6},{8,9},{9,8},{10,11... | collective-permute-start | bytes 1572872 | tf_op jit(solution)/shard_map/ppermute | solution.py:166
  46.7 0.8 constant_dynamic-update-slice_fusion.2.refs_7_
  47.5 1.9 collective-permute-start.9
  49.4 5.1 %collective-permute-start.14 = (bf16[128,512]{1,0:T(8,128)(2,1)S(1)}, bf16[128,512]{1,0:T(8,128)(2,1)S(1)}, u32[]{:S(2)}, u32[]{:S(2)}) collective-permute-start(bf16[128,512]{1,0:T(8,128)(2,1)S(1)} %slice.13), channel_id=1, source_target_pairs={{0,448},{32,480},{64,0},{96,32},{128,64},{160,96},{192,128},{224,1... | collective-permute-start | bytes 393224 | tf_op jit(solution)/shard_map/ppermute | solution.py:157
  54.6 1.9 collective-permute-start.13
  56.6 6.7 %collective-permute-done.13 = bf16[128,512]{1,0:T(8,128)(2,1)S(1)} collective-permute-done((bf16[128,512]{1,0:T(8,128)(2,1)S(1)}, bf16[128,512]{1,0:T(8,128)(2,1)S(1)}, u32[]{:S(2)}, u32[]{:S(2)}) %collective-permute-start.13) | collective-permute-done | bytes 131104 | tf_op jit(solution)/shard_map/ppermute | solution.py:156
  63.3 1.9 collective-permute-start.12
  65.3 2.4 %collective-permute-start.3 = (bf16[256,512]{1,0:T(8,128)(2,1)}, bf16[256,512]{1,0:T(8,128)(2,1)}, u32[]{:S(2)}, u32[]{:S(2)}) collective-permute-start(bf16[256,512]{1,0:T(8,128)(2,1)} %collective-permute-done.refs_3_), channel_id=1, source_target_pairs={{0,1},{1,0},{2,3},{3,2},{4,5},{5,4},{6,7},{7,6},{8,9},{9,8},{10,11... | collective-permute-start | bytes 786440 | tf_op jit(solution)/shard_map/ppermute | solution.py:163
  67.7 1.9 collective-permute-start.15
  71.2 0.8 add.174
  73.3 2.4 %collective-permute-start.16 = (bf16[256,2048]{1,0:T(8,128)(2,1)}, bf16[256,2048]{1,0:T(8,128)(2,1)S(1)}, u32[]{:S(2)}, u32[]{:S(2)}) collective-permute-start(bf16[256,2048]{1,0:T(8,128)(2,1)} %param.3), channel_id=1, source_target_pairs={{0,1},{1,33},{2,3},{3,35},{4,5},{5,37},{6,7},{7,39},{8,9},{9,41},{... | collective-permute-start | bytes 3145736 | tf_op jit(solution)/shard_map/ppermute | solution.py:175
  75.7 1.9 collective-permute-start.1
  77.6 26.3 %contrast.1 = (bf16[256,256]{1,0:T(8,128)(2,1)S(1)}, bf16[256,256]{1,0:T(8,128)(2,1)S(1)}) custom-call(s32[1]{0:T(128)} %bitcast.refs_0_, f32[8,1,512]{2,1,0:T(1,128)S(1)} %add_convert_fusion.refs_1_, f32[256,2]{1,0:T(8,128)S(1)} %bitcast.41, bf16[256,512]{1,0:T(8,128)(2,1)} %collective-permute-done.refs_3_, ...), custom_call_target="tpu_custom_call" | custom-call | flops 14000000000 | bytes 5000000 | tf_op jit(solution)/shard_map/contrast/pallas_call | solution.py:113
  103.9 5.1 %collective-permute-start.17 = (bf16[256,256]{1,0:T(8,128)(2,1)S(1)}, bf16[256,256]{1,0:T(8,128)(2,1)S(1)}, u32[]{:S(2)}, u32[]{:S(2)}) collective-permute-start(bf16[256,256]{1,0:T(8,128)(2,1)S(1)} %get-tuple-element.10), channel_id=1, source_target_pairs={{0,1},{1,0},{2,3},{3,2},{4,5},{5,4},{6,7},{7,6},{8,9},{9,8},{10,11... | collective-permute-start | bytes 393224 | tf_op jit(solution)/shard_map/ppermute | solution.py:179
  109.1 1.0 collective-permute-done.17
  111.0 50.4 %all_to_all.19 = bf16[512,8,128]{2,1,0:T(8,128)(2,1)S(1)} all-to-all(bf16[512,8,128]{2,1,0:T(8,128)(2,1)S(1)} %bitcast.43), channel_id=1, replica_groups=mesh['blk'=16,'rep'=32] {'blk','rep'}, dimensions={0} | all-to-all | bytes 2097152 | tf_op jit(solution)/shard_map/all_to_all | solution.py:188
  161.8 17.3 %all_to_all.20 = f32[32,2,8,128]{3,2,1,0:T(8,128)S(1)} all-to-all(f32[32,2,8,128]{3,2,1,0:T(8,128)S(1)} %broadcast_in_dim.4), channel_id=1, replica_groups=mesh['blk'=16,'rep'=32] {'rep'}, dimensions={0} | all-to-all | bytes 524288 | tf_op jit(solution)/shard_map/all_to_all | solution.py:190
  180.4 13.7 %all_to_all.21 = f32[16,1,128]{2,1,0:T(1,128)S(1)} all-to-all(f32[16,1,128]{2,1,0:T(1,128)S(1)} %broadcast_in_dim.5), channel_id=1, replica_groups=mesh['blk'=16,'rep'=32] {'blk'}, dimensions={0} | all-to-all | bytes 16384 | tf_op jit(solution)/shard_map/all_to_all | solution.py:193
  (46 shorter events, 8.2 us)
Async XLA Ops:
  0.0 1.6 copy-start
  1.6 22.9 %copy-start.2 = (s32[256]{0:T(256)S(1)}, s32[256]{0:T(256)}, u32[]{:S(2)}) copy-start(s32[256]{0:T(256)} %param.5) | copy-start | bytes 3076
  3.8 1.3 collective-permute-start
  5.1 13.1 %collective-permute-start.5 = (bf16[256,512]{1,0:T(8,128)(2,1)}, bf16[256,512]{1,0:T(8,128)(2,1)S(1)}, u32[]{:S(2)}, u32[]{:S(2)}) collective-permute-start(bf16[256,512]{1,0:T(8,128)(2,1)} %collective-permute-done.refs_3_), channel_id=1, source_target_pairs={{0,448},{32,480},{64,0},{96,32},{128,64},{160,96},{192,128},{224,1... | collective-permute-start | bytes 786440 | tf_op jit(solution)/shard_map/ppermute | solution.py:149
  12.8 9.7 %collective-permute-start.4 = (bf16[256,512]{1,0:T(8,128)(2,1)}, bf16[256,512]{1,0:T(8,128)(2,1)}, u32[]{:S(2)}, u32[]{:S(2)}) collective-permute-start(bf16[256,512]{1,0:T(8,128)(2,1)} %collective-permute-done.refs_3_), channel_id=1, source_target_pairs={{0,64},{32,96},{64,128},{96,160},{128,192},{160,224},{192,256},{22... | collective-permute-start | bytes 786440 | tf_op jit(solution)/shard_map/ppermute | solution.py:148
  18.2 9.6 %copy-start.1 = (bf16[256,512]{1,0:T(8,128)(2,1)}, bf16[256,512]{1,0:T(8,128)(2,1)S(1)}, u32[]{:S(2)}) copy-start(bf16[256,512]{1,0:T(8,128)(2,1)S(1)} %collective-permute-done.5) | copy-start | bytes 786436
  18.2 10.2 %collective-permute-start.8 = (bf16[256,512]{1,0:T(8,128)(2,1)S(1)}, bf16[256,512]{1,0:T(8,128)(2,1)S(1)}, u32[]{:S(2)}, u32[]{:S(2)}) collective-permute-start(bf16[256,512]{1,0:T(8,128)(2,1)S(1)} %collective-permute-done.5), channel_id=1, source_target_pairs={{0,448},{32,480},{64,0},{96,32},{128,64},{160,96},{192,128},{224,1... | collective-permute-start | bytes 786440 | tf_op jit(solution)/shard_map/ppermute | solution.py:149
  22.5 10.2 %collective-permute-start.7 = (bf16[256,512]{1,0:T(8,128)(2,1)}, bf16[256,512]{1,0:T(8,128)(2,1)S(1)}, u32[]{:S(2)}, u32[]{:S(2)}) collective-permute-start(bf16[256,512]{1,0:T(8,128)(2,1)} %collective-permute-done.4), channel_id=1, source_target_pairs={{0,64},{32,96},{64,128},{96,160},{128,192},{160,224},{192,256},{22... | collective-permute-start | bytes 786440 | tf_op jit(solution)/shard_map/ppermute | solution.py:148
  25.3 42.4 %collective-permute-start.2 = (f32[2,256]{0,1:T(8,128)}, f32[2,256]{0,1:T(8,128)S(1)}, u32[]{:S(2)}, u32[]{:S(2)}) collective-permute-start(f32[2,256]{0,1:T(8,128)} %copy.13), channel_id=1, source_target_pairs={{0,0},{1,32},{2,2},{3,34},{4,4},{5,36},{6,6},{7,38},{8,8},{9,40},{... | collective-permute-start | bytes 6152 | tf_op jit(solution)/shard_map/ppermute | solution.py:176
  28.4 21.0 %collective-permute-start.11 = (bf16[256,512]{1,0:T(8,128)(2,1)S(1)}, bf16[256,512]{1,0:T(8,128)(2,1)S(1)}, u32[]{:S(2)}, u32[]{:S(2)}) collective-permute-start(bf16[256,512]{1,0:T(8,128)(2,1)S(1)} %collective-permute-done.8), channel_id=1, source_target_pairs={{0,448},{32,480},{64,0},{96,32},{128,64},{160,96},{192,128},{224,1... | collective-permute-start | bytes 786440 | tf_op jit(solution)/shard_map/ppermute | solution.py:149
  32.8 21.8 %collective-permute-start.10 = (bf16[256,512]{1,0:T(8,128)(2,1)S(1)}, bf16[256,512]{1,0:T(8,128)(2,1)S(1)}, u32[]{:S(2)}, u32[]{:S(2)}) collective-permute-start(bf16[256,512]{1,0:T(8,128)(2,1)S(1)} %collective-permute-done.7), channel_id=1, source_target_pairs={{0,64},{32,96},{64,128},{96,160},{128,192},{160,224},{192,256},{22... | collective-permute-start | bytes 786440 | tf_op jit(solution)/shard_map/ppermute | solution.py:148
  35.7 40.0 %collective-permute-start.6 = (bf16[512,512]{1,0:T(8,128)(2,1)S(1)}, bf16[512,512]{1,0:T(8,128)(2,1)}, u32[]{:S(2)}, u32[]{:S(2)}) collective-permute-start(bf16[512,512]{1,0:T(8,128)(2,1)S(1)} %constant_dynamic-update-slice_fusion.refs_5_), channel_id=1, source_target_pairs={{0,1},{1,0},{2,3},{3,2},{4,5},{5,4},{6,7},{7,6},{8,9},{9,8},{10,11... | collective-permute-start | bytes 1572872 | tf_op jit(solution)/shard_map/ppermute | solution.py:166
  47.5 30.1 %collective-permute-start.9 = (bf16[512,512]{1,0:T(8,128)(2,1)}, bf16[512,512]{1,0:T(8,128)(2,1)}, u32[]{:S(2)}, u32[]{:S(2)}) collective-permute-start(bf16[512,512]{1,0:T(8,128)(2,1)} %constant_dynamic-update-slice_fusion.2.refs_7_), channel_id=1, source_target_pairs={{0,1},{1,0},{2,3},{3,2},{4,5},{5,4},{6,7},{7,6},{8,9},{9,8},{10,11... | collective-permute-start | bytes 1572872 | tf_op jit(solution)/shard_map/ppermute | solution.py:166
  49.4 15.8 %collective-permute-start.14 = (bf16[128,512]{1,0:T(8,128)(2,1)S(1)}, bf16[128,512]{1,0:T(8,128)(2,1)S(1)}, u32[]{:S(2)}, u32[]{:S(2)}) collective-permute-start(bf16[128,512]{1,0:T(8,128)(2,1)S(1)} %slice.13), channel_id=1, source_target_pairs={{0,448},{32,480},{64,0},{96,32},{128,64},{160,96},{192,128},{224,1... | collective-permute-start | bytes 393224 | tf_op jit(solution)/shard_map/ppermute | solution.py:157
  54.6 8.7 %collective-permute-start.13 = (bf16[128,512]{1,0:T(8,128)(2,1)S(1)}, bf16[128,512]{1,0:T(8,128)(2,1)S(1)}, u32[]{:S(2)}, u32[]{:S(2)}) collective-permute-start(bf16[128,512]{1,0:T(8,128)(2,1)S(1)} %slice.12), channel_id=1, source_target_pairs={{0,64},{32,96},{64,128},{96,160},{128,192},{160,224},{192,256},{22... | collective-permute-start | bytes 393224 | tf_op jit(solution)/shard_map/ppermute | solution.py:156
  63.3 14.3 %collective-permute-start.12 = (bf16[512,512]{1,0:T(8,128)(2,1)S(1)}, bf16[512,512]{1,0:T(8,128)(2,1)}, u32[]{:S(2)}, u32[]{:S(2)}) collective-permute-start(bf16[512,512]{1,0:T(8,128)(2,1)S(1)} %constant_dynamic-update-slice_fusion.4.refs_9_), channel_id=1, source_target_pairs={{0,1},{1,0},{2,3},{3,2},{4,5},{5,4},{6,7},{7,6},{8,9},{9,8},{10,11... | collective-permute-start | bytes 1572872 | tf_op jit(solution)/shard_map/ppermute | solution.py:166
  65.3 8.0 %collective-permute-start.3 = (bf16[256,512]{1,0:T(8,128)(2,1)}, bf16[256,512]{1,0:T(8,128)(2,1)}, u32[]{:S(2)}, u32[]{:S(2)}) collective-permute-start(bf16[256,512]{1,0:T(8,128)(2,1)} %collective-permute-done.refs_3_), channel_id=1, source_target_pairs={{0,1},{1,0},{2,3},{3,2},{4,5},{5,4},{6,7},{7,6},{8,9},{9,8},{10,11... | collective-permute-start | bytes 786440 | tf_op jit(solution)/shard_map/ppermute | solution.py:163
  67.7 9.9 %collective-permute-start.15 = (bf16[256,512]{1,0:T(8,128)(2,1)S(1)}, bf16[256,512]{1,0:T(8,128)(2,1)}, u32[]{:S(2)}, u32[]{:S(2)}) collective-permute-start(bf16[256,512]{1,0:T(8,128)(2,1)S(1)} %constant_dynamic-update-slice_fusion.6.refs_11_), channel_id=1, source_target_pairs={{0,1},{1,0},{2,3},{3,2},{4,5},{5,4},{6,7},{7,6},{8,9},{9,8},{10,11... | collective-permute-start | bytes 786440 | tf_op jit(solution)/shard_map/ppermute | solution.py:166
  73.3 35.8 %collective-permute-start.16 = (bf16[256,2048]{1,0:T(8,128)(2,1)}, bf16[256,2048]{1,0:T(8,128)(2,1)S(1)}, u32[]{:S(2)}, u32[]{:S(2)}) collective-permute-start(bf16[256,2048]{1,0:T(8,128)(2,1)} %param.3), channel_id=1, source_target_pairs={{0,1},{1,33},{2,3},{3,35},{4,5},{5,37},{6,7},{7,39},{8,9},{9,41},{... | collective-permute-start | bytes 3145736 | tf_op jit(solution)/shard_map/ppermute | solution.py:175
  75.7 34.8 %collective-permute-start.1 = (bf16[256,2048]{1,0:T(8,128)(2,1)}, bf16[256,2048]{1,0:T(8,128)(2,1)S(1)}, u32[]{:S(2)}, u32[]{:S(2)}) collective-permute-start(bf16[256,2048]{1,0:T(8,128)(2,1)} %param.3), channel_id=1, source_target_pairs={{0,0},{1,32},{2,2},{3,34},{4,4},{5,36},{6,6},{7,38},{8,8},{9,40},{... | collective-permute-start | bytes 3145736 | tf_op jit(solution)/shard_map/ppermute | solution.py:174
  103.9 6.1 %collective-permute-start.17 = (bf16[256,256]{1,0:T(8,128)(2,1)S(1)}, bf16[256,256]{1,0:T(8,128)(2,1)S(1)}, u32[]{:S(2)}, u32[]{:S(2)}) collective-permute-start(bf16[256,256]{1,0:T(8,128)(2,1)S(1)} %get-tuple-element.10), channel_id=1, source_target_pairs={{0,1},{1,0},{2,3},{3,2},{4,5},{5,4},{6,7},{7,6},{8,9},{9,8},{10,11... | collective-permute-start | bytes 393224 | tf_op jit(solution)/shard_map/ppermute | solution.py:179

commit v2 on v0

v2 whole, which is shorter than its diff:
```python
import itertools

import jax
import jax.numpy as jnp
from jax import lax
from jax.experimental import pallas as pl
from jax.experimental.pallas import tpu as pltpu
from jax.sharding import Mesh
from jax.sharding import PartitionSpec as P

softness_factor = 0.05
EXP2_SCALE = 1.4426950408889634 / softness_factor
Y = 8
BITS = ("y2", "y1", "y0", "xh", "xl", "z2", "z1", "z0", "c")
YBITS = BITS[:3]
OTHER_CORE = [(0, 1), (1, 0)]


def moves(other_core):
    pairs = []
    for place in itertools.product((0, 1), repeat=len(BITS)):
        target = list(place)
        target[3], target[8] = place[8], place[3] ^ other_core
        index = [sum(bit << (8 - k) for k, bit in enumerate(bits)) for bits in (place, target)]
        pairs.append(tuple(index))
    return pairs


TO_HOST, TO_SIBLING = moves(0), moves(1)


def along_y(step):
    return [(k, (k + step) % Y) for k in range(Y)]


def exponentials(left, right):
    scores = lax.dot_general(
        left, right, (((1,), (1,)), ((), ())), preferred_element_type=jnp.float32
    )
    return jnp.exp2(scores * EXP2_SCALE)


def over_rows(values):
    return values.reshape(values.shape[0] // 8, 8, values.shape[1]).sum(0)


def over_lane_groups(values):
    return sum(values[:, k : k + 128] for k in range(0, values.shape[1], 128))


def same_block_kernel(mine_ref, sums_ref, per_lane, per_column):
    blocks, wide = per_lane.shape[0], per_lane.shape[1]
    per_lane[...] = jnp.zeros_like(per_lane)
    per_column[...] = jnp.zeros_like(per_column)
    for i in range(blocks):
        left = mine_ref[i * wide : (i + 1) * wide, :]
        values = exponentials(left, left)
        rows = lax.broadcasted_iota(jnp.int32, values.shape, 0)
        columns = lax.broadcasted_iota(jnp.int32, values.shape, 1)
        per_column[i] += over_rows(jnp.where(rows == columns, 0.0, values))
        for j in range(i + 1, blocks):
            values = exponentials(left, mine_ref[j * wide : (j + 1) * wide, :])
            per_column[j] += over_rows(values)
            per_lane[i] += over_lane_groups(values)
    for i in range(blocks):
        sums_ref[i] = per_column[i].sum(0, keepdims=True) + per_lane[i].T.sum(0, keepdims=True)


def cross_block_kernel(core_ref, mine_ref, sibling_ref, same_ref, sums_ref, units, per_lane, per_column):
    core = core_ref[0]
    blocks, wide = per_column.shape[0], per_column.shape[2]
    for k in range(blocks):
        units[blocks * core + k] = mine_ref[k * wide : (k + 1) * wide, :]
        units[blocks * (1 - core) + k] = sibling_ref[k * wide : (k + 1) * wide, :]
    per_lane[...] = jnp.zeros_like(per_lane)
    per_column[...] = jnp.zeros_like(per_column)
    for i in range(blocks // 2):
        left = units[blocks // 2 * core + i]
        for j in range(blocks):
            values = exponentials(left, units[blocks + j])
            per_column[j] += over_rows(values)
            per_lane[i] += over_lane_groups(values)
    for k in range(blocks):
        sums_ref[k] = jnp.zeros_like(sums_ref[k])
        sums_ref[blocks + k] = per_column[k].sum(0, keepdims=True)
    for i in range(blocks // 2):
        sums_ref[blocks // 2 * core + i] = per_lane[i].T.sum(0, keepdims=True)
    for k in range(blocks):
        sums_ref[blocks * core + k] += same_ref[k]


def weight_kernel(
    core_ref, start_ref, side_ref, sums_ref, mine_ref, sibling_ref, keep_ref, send_ref, total
):
    core = core_ref[0]
    wide = sums_ref.shape[2]
    blocks = sums_ref.shape[0] // 2
    rows = side_ref.shape[0]
    own = mine_ref[:rows, :]
    mine_sums = sums_ref[blocks * core][:, :rows]
    inverse_own = 1.0 / jnp.broadcast_to(mine_sums, (128, rows)).T[:, :1]
    partner = side_ref[:, 0:1].astype(jnp.int32)
    lanes = lax.broadcasted_iota(jnp.int32, (1, wide), 1)
    for part, ref in enumerate((mine_ref, sibling_ref)):
        for k in range(blocks):
            which = core if part == 0 else 1 - core
            right = ref[k * wide : (k + 1) * wide, :]
            inverse = 1.0 / sums_ref[blocks * which + k]
            values = exponentials(own, right) * (inverse_own + inverse)
            if part == 0 and k == 0:
                row_ids = lax.broadcasted_iota(jnp.int32, values.shape, 0)
                column_ids = lax.broadcasted_iota(jnp.int32, values.shape, 1)
                values = jnp.where(row_ids == column_ids, 0.0, values)
            first = start_ref[part * blocks * 2 + 2 * k]
            second = start_ref[part * blocks * 2 + 2 * k + 1]
            columns = lanes + jnp.where(lanes < rows, first, second - rows)
            values = jnp.where(columns == partner, values - 2.0, values)
            product = jnp.dot(
                values.astype(jnp.bfloat16), right, preferred_element_type=jnp.float32
            )
            if part == 0 and k == 0:
                total[...] = product
            else:
                total[...] += product
    grad_unit = total[...] * (1.0 / softness_factor)
    unit = own.astype(jnp.float32)
    along = jnp.sum(unit * grad_unit, axis=1, keepdims=True)
    grad_hidden = ((grad_unit - unit * along) * side_ref[:, 1:2]).astype(jnp.bfloat16)
    middle = grad_hidden.shape[1] // 2
    first, second = grad_hidden[:, :middle], grad_hidden[:, middle:]
    keep_ref[...] = jnp.where(core == 0, first, second)
    send_ref[...] = jnp.where(core == 0, second, first)


VMEM = pl.BlockSpec(memory_space=pltpu.VMEM)
SMEM = pl.BlockSpec(memory_space=pltpu.SMEM)


def kernel_call(body, outputs, in_specs, scratch, flops, name):
    return pl.pallas_call(
        body,
        out_shape=outputs,
        in_specs=in_specs,
        out_specs=jax.tree.map(lambda unused: VMEM, outputs),
        scratch_shapes=scratch,
        compiler_params=pltpu.CompilerParams(vmem_limit_bytes=40 * 1024 * 1024),
        cost_estimate=pl.CostEstimate(
            flops=flops, bytes_accessed=2_000_000, transcendentals=100_000
        ),
        name=name,
    )


def on_device(features, head_weight, partner):
    rows = features.shape[0]
    channels, width = head_weight.shape
    y = lax.axis_index("y2") * 4 + lax.axis_index("y1") * 2 + lax.axis_index("y0")
    core = lax.axis_index("c")
    core_scalar = core.reshape(1).astype(jnp.int32)

    hidden = jnp.dot(features, head_weight, preferred_element_type=jnp.float32)
    row_norm = jnp.sqrt(jnp.sum(hidden * hidden, axis=1, keepdims=True) + 1e-05)
    unit = (hidden / row_norm).astype(jnp.bfloat16)
    side = jnp.stack([partner.astype(jnp.float32), 1.0 / row_norm[:, 0]])

    own = lax.ppermute(unit, BITS, TO_HOST)
    side_here = lax.ppermute(side, BITS, TO_HOST)
    up, down = along_y(1), along_y(-1)
    from_below, from_above = own, own
    pieces, places = [own], [y]
    sends = []
    for distance in range(1, 4):
        from_below = lax.ppermute(from_below, YBITS, up)
        from_above = lax.ppermute(from_above, YBITS, down)
        pieces += [from_below, from_above]
        places += [(y - distance) % Y, (y + distance) % Y]
        if distance < 3:
            later, unused = lax.optimization_barrier((features, from_below))
            sends.append(lax.ppermute(later, BITS, (TO_HOST, TO_SIBLING)[distance - 1]))
    half = rows // 2
    pieces += [
        lax.ppermute(from_below[:half], YBITS, up),
        lax.ppermute(from_above[half:], YBITS, down),
    ]
    places.append((y + Y // 2) % Y)
    mine = jnp.concatenate(pieces)
    rows_here, rows_beside = sends
    places = jnp.stack(places)
    starts = jnp.concatenate([places * 2 + core, places * 2 + 1 - core]).astype(jnp.int32) * rows

    sibling = lax.ppermute(mine, "c", OTHER_CORE)
    lanes = pltpu.VMEM((4, 512, 128), jnp.float32)
    columns = pltpu.VMEM((4, 8, 512), jnp.float32)
    same = kernel_call(
        same_block_kernel,
        jax.ShapeDtypeStruct((4, 1, 512), jnp.float32),
        [VMEM],
        [lanes, columns],
        3_000_000_000,
        "same_parity_sums",
    )(mine)
    sums = kernel_call(
        cross_block_kernel,
        jax.ShapeDtypeStruct((8, 1, 512), jnp.float32),
        [SMEM, VMEM, VMEM, VMEM],
        [pltpu.VMEM((8, 512, width), jnp.bfloat16), lanes, columns],
        2_000_000_000,
        "cross_parity_sums",
    )(core_scalar, mine, sibling, same)
    sums = lax.psum(sums, "c")
    piece = jax.ShapeDtypeStruct((rows, width // 2), jnp.bfloat16)
    kept, sent = kernel_call(
        weight_kernel,
        (piece, piece),
        [SMEM, SMEM, VMEM, VMEM, VMEM, VMEM],
        [pltpu.VMEM((rows, width), jnp.float32)],
        2_000_000_000,
        "weights",
    )(core_scalar, starts, side_here.T, sums, mine, sibling)
    beside = lax.ppermute(sent, "c", OTHER_CORE)

    def contract(left, right):
        return lax.dot_general(
            left, right, (((0,), (0,)), ((), ())), preferred_element_type=jnp.float32
        )

    partial = (contract(rows_here, kept) + contract(rows_beside, beside)).astype(jnp.bfloat16)
    tiles = partial.reshape(4, 2, 2, 2, 4, 2, 8, 256)
    tiles = tiles.transpose(1, 3, 5, 0, 2, 4, 6, 7).reshape(8, 32 * 8, 256)
    received = lax.all_to_all(tiles, ("y0", "xl", "z0"), 0, 0)
    near_sum = received.astype(jnp.float32).sum(0).reshape(32, 8, 256)
    received = lax.all_to_all(near_sum, ("y2", "y1", "xh", "z2", "z1"), 0, 0)
    fragment = received.sum(0)
    spread = lax.all_to_all(
        jnp.broadcast_to(fragment[None], (32, 8, 256)), ("xl", "z2", "z1", "z0", "c"), 0, 0
    )
    gradient = spread.reshape(16, 2, 8, 256).transpose(0, 2, 1, 3).reshape(128, width)
    squares = jnp.sum(gradient * gradient)
    squares = lax.all_to_all(
        jnp.broadcast_to(squares, (16, 128)), ("y2", "y1", "y0", "xh"), 0, 0
    )
    total = jnp.sum(squares[:, 0])
    return gradient * lax.rsqrt(total / (channels * width) + 1e-06)


def solution(mesh):
    bits = Mesh(mesh.devices.reshape((2,) * len(BITS)), BITS)
    images = P(("xl", "z2", "z1", "z0", "c", "y2", "y1", "y0", "xh"))
    return jax.shard_map(
        on_device,
        mesh=bits,
        in_specs=(P(*images, None), P(), images),
        out_specs=P(("y2", "y1", "y0", "xh"), None),
        check_vma=False,
    )
```

time: 665 us -> 182 us (0.27)
  the two profiles are of different devices: /device:TPU:2 before, /device:TPU:8 now
where the time goes in v2:
time: 182 us; the launch traced here: 181 us
  blocking collectives  83.5 us (46%)
  starting transfers between devices  56.5 us (31%)
  Pallas kernels  15.1 us (8%)
  local copies, waits for them, and re-layouts  9.07 us (5%)
  waiting for transfers between devices  8.63 us (5%)
  matrix products  4.23 us (2%)
  other arithmetic  2.39 us (1%)
    all_to_all x1, blocking collectives, on_device(): received = lax.all_to_all(near_sum, ('y2', 'y1', 'xh', 'z2', 'z1'), 0, 0)  32.1 us
    all_to_all x1, blocking collectives, on_device(): received = lax.all_to_all(tiles, ('y0', 'xl', 'z0'), 0, 0)  19.7 us
    ppermute x2, starting transfers between devices, on_device(): sends.append(lax.ppermute(later, BITS, (TO_HOST, TO_SIBLING)[distance - 1]))  19 us
    ppermute x3, starting transfers between devices, on_device(): from_above = lax.ppermute(from_above, YBITS, down)  17 us
    all_to_all x1, blocking collectives, on_device(): lax.all_to_all(jnp.broadcast_to(fragment[None], (32, 8, 256)), ('xl', 'z2...  16.2 us
    all_to_all x1, blocking collectives, on_device(): lax.all_to_all(jnp.broadcast_to(squares, (16, 128)), ('y2', 'y1', 'y0', '...  12.2 us
    unnamed x12, local copies, waits for them, and re-layouts  7.37 us
    ppermute x3, starting transfers between devices, on_device(): from_below = lax.ppermute(from_below, YBITS, up)  7.3 us
  transfers between devices with their start and end apart: 14, of which 5 were waited for; matrix products, arithmetic and copies ran while one was open for 4% of the time, Pallas kernels for 8%

profile of v2, /device:TPU:8, one launch (start us, length us, event | category | flops | bytes accessed | tf_op | source)
XLA Modules:
  0.0 180.5 jit_solution(13908942026439099949)
XLA Ops:
  0.0 1.6 copy-done
  1.6 2.0 %multiply_reduce_fusion = (f32[256]{0:T(256)S(1)}, f32[256,512]{1,0:T(8,128)S(1)}) fusion(bf16[256,2048]{1,0:T(8,128)(2,1)} %param.3, bf16[2048,512]{1,0:T(8,128)(2,1)S(1)} %copy-done), kind=kOutput, calls=%fused_computation.4 | convolution fusion | flops 537132800 | bytes 3671040 | tf_op jit(solution)/shard_map/dot_general | solution.py:161
  4.4 3.5 %collective-permute-start.1 = (bf16[256,512]{1,0:T(8,128)(2,1)S(1)}, bf16[256,512]{1,0:T(8,128)(2,1)S(1)}, u32[]{:S(2)}, u32[]{:S(2)}) collective-permute-start(bf16[256,512]{1,0:T(8,128)(2,1)S(1)} %collective-permute-done), channel_id=1, source_target_pairs={{0,64},{64,128},{128,192},{192,256},{256,320},{320,384},{384,448},... | collective-permute-start | bytes 786440 | tf_op jit(solution)/shard_map/ppermute | solution.py:173
  7.9 6.2 %collective-permute-start.4 = (bf16[256,512]{1,0:T(8,128)(2,1)S(1)}, bf16[256,512]{1,0:T(8,128)(2,1)S(1)}, u32[]{:S(2)}, u32[]{:S(2)}) collective-permute-start(bf16[256,512]{1,0:T(8,128)(2,1)S(1)} %collective-permute-done), channel_id=1, source_target_pairs={{0,448},{64,0},{128,64},{192,128},{256,192},{320,256},{384,320},{4... | collective-permute-start | bytes 786440 | tf_op jit(solution)/shard_map/ppermute | solution.py:174
  14.1 2.4 %collective-permute-done.1 = bf16[256,512]{1,0:T(8,128)(2,1)S(1)} collective-permute-done((bf16[256,512]{1,0:T(8,128)(2,1)S(1)}, bf16[256,512]{1,0:T(8,128)(2,1)S(1)}, u32[]{:S(2)}, u32[]{:S(2)}) %collective-permute-start.1) | collective-permute-done | bytes 262176 | tf_op jit(solution)/shard_map/ppermute | solution.py:173
  16.5 1.9 %collective-permute-start.5 = (bf16[256,512]{1,0:T(8,128)(2,1)S(1)}, bf16[256,512]{1,0:T(8,128)(2,1)S(1)}, u32[]{:S(2)}, u32[]{:S(2)}) collective-permute-start(bf16[256,512]{1,0:T(8,128)(2,1)S(1)} %collective-permute-done.1), channel_id=1, source_target_pairs={{0,64},{64,128},{128,192},{192,256},{256,320},{320,384},{384,448},... | collective-permute-start | bytes 786440 | tf_op jit(solution)/shard_map/ppermute | solution.py:173
  18.4 5.3 %collective-permute-start.6 = (bf16[256,512]{1,0:T(8,128)(2,1)S(1)}, bf16[256,512]{1,0:T(8,128)(2,1)S(1)}, u32[]{:S(2)}, u32[]{:S(2)}) collective-permute-start(bf16[256,512]{1,0:T(8,128)(2,1)S(1)} %collective-permute-done.4), channel_id=1, source_target_pairs={{0,448},{64,0},{128,64},{192,128},{256,192},{320,256},{384,320},{4... | collective-permute-start | bytes 786440 | tf_op jit(solution)/shard_map/ppermute | solution.py:174
  23.8 0.7 constant_dynamic-update-slice_fusion.8
  25.2 1.9 %collective-permute-done.5 = bf16[256,512]{1,0:T(8,128)(2,1)S(1)} collective-permute-done((bf16[256,512]{1,0:T(8,128)(2,1)S(1)}, bf16[256,512]{1,0:T(8,128)(2,1)S(1)}, u32[]{:S(2)}, u32[]{:S(2)}) %collective-permute-start.5) | collective-permute-done | bytes 262176 | tf_op jit(solution)/shard_map/ppermute | solution.py:173
  27.1 1.9 %collective-permute-start.7 = (bf16[256,512]{1,0:T(8,128)(2,1)S(1)}, bf16[256,512]{1,0:T(8,128)(2,1)S(1)}, u32[]{:S(2)}, u32[]{:S(2)}) collective-permute-start(bf16[256,512]{1,0:T(8,128)(2,1)S(1)} %collective-permute-done.5), channel_id=1, source_target_pairs={{0,64},{64,128},{128,192},{192,256},{256,320},{320,384},{384,448},... | collective-permute-start | bytes 786440 | tf_op jit(solution)/shard_map/ppermute | solution.py:173
  29.0 5.5 %collective-permute-start.8 = (bf16[256,512]{1,0:T(8,128)(2,1)S(1)}, bf16[256,512]{1,0:T(8,128)(2,1)S(1)}, u32[]{:S(2)}, u32[]{:S(2)}) collective-permute-start(bf16[256,512]{1,0:T(8,128)(2,1)S(1)} %collective-permute-done.6), channel_id=1, source_target_pairs={{0,448},{64,0},{128,64},{192,128},{256,192},{320,256},{384,320},{4... | collective-permute-start | bytes 786440 | tf_op jit(solution)/shard_map/ppermute | solution.py:174
  34.6 0.7 constant_dynamic-update-slice_fusion.6
  35.3 0.7 constant_dynamic-update-slice_fusion.5
  36.8 2.3 %collective-permute-done.7 = bf16[256,512]{1,0:T(8,128)(2,1)S(1)} collective-permute-done((bf16[256,512]{1,0:T(8,128)(2,1)S(1)}, bf16[256,512]{1,0:T(8,128)(2,1)S(1)}, u32[]{:S(2)}, u32[]{:S(2)}) %collective-permute-start.7) | collective-permute-done | bytes 262176 | tf_op jit(solution)/shard_map/ppermute | solution.py:173
  39.0 1.9 %collective-permute-start.9 = (bf16[128,512]{1,0:T(8,128)(2,1)S(1)}, bf16[128,512]{1,0:T(8,128)(2,1)S(1)}, u32[]{:S(2)}, u32[]{:S(2)}) collective-permute-start(bf16[128,512]{1,0:T(8,128)(2,1)S(1)} %slice.12), channel_id=1, source_target_pairs={{0,64},{64,128},{128,192},{192,256},{256,320},{320,384},{384,448},... | collective-permute-start | bytes 393224 | tf_op jit(solution)/shard_map/ppermute | solution.py:182
  41.0 5.8 %collective-permute-start.10 = (bf16[128,512]{1,0:T(8,128)(2,1)S(1)}, bf16[128,512]{1,0:T(8,128)(2,1)S(1)}, u32[]{:S(2)}, u32[]{:S(2)}) collective-permute-start(bf16[128,512]{1,0:T(8,128)(2,1)S(1)} %slice.13), channel_id=1, source_target_pairs={{0,448},{64,0},{128,64},{192,128},{256,192},{320,256},{384,320},{4... | collective-permute-start | bytes 393224 | tf_op jit(solution)/shard_map/ppermute | solution.py:183
  46.8 0.7 constant_dynamic-update-slice_fusion.3
  49.0 1.0 collective-permute-done.10
  50.7 1.9 %collective-permute-start.11 = (bf16[2048,512]{1,0:T(8,128)(2,1)}, bf16[2048,512]{1,0:T(8,128)(2,1)}, u32[]{:S(2)}, u32[]{:S(2)}) collective-permute-start(bf16[2048,512]{1,0:T(8,128)(2,1)} %constant_dynamic-update-slice_fusion.mine_ref), channel_id=1, source_target_pairs={{0,1},{1,0},{2,3},{3,2},{4,5},{5,4},{6,7},{7,6},{8,9},{9,8},{10,11... | collective-permute-start | bytes 6291464 | tf_op jit(solution)/shard_map/ppermute | solution.py:191
  53.6 9.5 %collective-permute-start.12 = (bf16[256,2048]{1,0:T(8,128)(2,1)}, bf16[256,2048]{1,0:T(8,128)(2,1)S(1)}, u32[]{:S(2)}, u32[]{:S(2)}) collective-permute-start(bf16[256,2048]{1,0:T(8,128)(2,1)} %param.3), channel_id=1, source_target_pairs={{0,1},{1,33},{2,3},{3,35},{4,5},{5,37},{6,7},{7,39},{8,9},{9,41},{... | collective-permute-start | bytes 3145736 | tf_op jit(solution)/shard_map/ppermute | solution.py:179
  63.2 9.5 %collective-permute-start.2 = (bf16[256,2048]{1,0:T(8,128)(2,1)}, bf16[256,2048]{1,0:T(8,128)(2,1)}, u32[]{:S(2)}, u32[]{:S(2)}) collective-permute-start(bf16[256,2048]{1,0:T(8,128)(2,1)} %param.3), channel_id=1, source_target_pairs={{0,0},{1,32},{2,2},{3,34},{4,4},{5,36},{6,6},{7,38},{8,8},{9,40},{... | collective-permute-start | bytes 3145736 | tf_op jit(solution)/shard_map/ppermute | solution.py:179
  72.7 4.5 %same_parity_sums.1.same_ref = f32[4,1,512]{2,1,0:T(1,128)S(1)} custom-call(bf16[2048,512]{1,0:T(8,128)(2,1)} %constant_dynamic-update-slice_fusion.mine_ref), custom_call_target="tpu_custom_call" | custom-call | flops 3000000000 | bytes 2000000 | tf_op jit(solution)/shard_map/same_parity_sums/pallas_call | solution.py:194
  77.3 5.0 %cross_parity_sums.1 = f32[8,1,512]{2,1,0:T(1,128)S(1)} custom-call(s32[1]{0:T(128)} %bitcast.core_ref, bf16[2048,512]{1,0:T(8,128)(2,1)} %constant_dynamic-update-slice_fusion.mine_ref, bf16[2048,512]{1,0:T(8,128)(2,1)} %collective-permute-done.11.sibling_ref, f32[4,1,512]{2,1,0:T(1,128)S(1)} %same_parity_sums.1.same_ref), custom_call_target="tpu_custom_call" | custom-call | flops 2000000000 | bytes 2000000 | tf_op jit(solution)/shard_map/cross_parity_sums/pallas_call | solution.py:202
  82.3 3.4 %psum.7.sums_ref = f32[8,1,512]{2,1,0:T(1,128)S(1)} all-reduce(f32[8,1,512]{2,1,0:T(1,128)S(1)} %cross_parity_sums.1), channel_id=1, replica_groups=mesh['y2'=2,'y1'=2,'y0'=2,'xh'=2,'xl'=2,'z2'=2,'z1'=2,'z0'=2,'c'=2] {'c'}, use_global_device_ids=true, to_apply=%region_1.2 | all-reduce | flops 4096 | bytes 32768 | tf_op jit(solution)/shard_map/psum | solution.py:210
  85.6 5.6 %weights.1 = (bf16[256,256]{1,0:T(8,128)(2,1)S(1)}, bf16[256,256]{1,0:T(8,128)(2,1)S(1)}) custom-call(s32[1]{0:T(128)} %bitcast.core_ref, s32[16]{0:T(128)S(1)} %add_multiply_fusion.start_ref, f32[256,2]{1,0:T(8,128)S(1)} %bitcast.29, f32[8,1,512]{2,1,0:T(1,128)S(1)} %psum.7.sums_ref, bf16[2048,512]{1,0:T(8,128)(2,1)} %constant_dynamic-update-slice_fusion.mine_ref, ...), custom_call_target="tpu_custom_call" | custom-call | flops 2000000000 | bytes 2000000 | tf_op jit(solution)/shard_map/weights/pallas_call | solution.py:212
  91.2 2.2 %collective-permute-start.13 = (bf16[256,256]{1,0:T(8,128)(2,1)S(1)}, bf16[256,256]{1,0:T(8,128)(2,1)S(1)}, u32[]{:S(2)}, u32[]{:S(2)}) collective-permute-start(bf16[256,256]{1,0:T(8,128)(2,1)S(1)} %get-tuple-element.12), channel_id=1, source_target_pairs={{0,1},{1,0},{2,3},{3,2},{4,5},{5,4},{6,7},{7,6},{8,9},{9,8},{10,11... | collective-permute-start | bytes 393224 | tf_op jit(solution)/shard_map/ppermute | solution.py:220
  93.4 1.0 collective-permute-done.13
  94.9 1.7 fusion
  96.8 19.7 %all_to_all.24 = bf16[8,256,256]{2,1,0:T(8,128)(2,1)S(1)} all-to-all(bf16[8,256,256]{2,1,0:T(8,128)(2,1)S(1)} %bitcast.30), channel_id=1, replica_groups=mesh['y2'=2,'y1'=2,'y0'=2,'xh'=2,'xl'=2,'z2'=2,'z1'=2,'z0'=2,'c'=2] {'y0..., dimensions={0} | all-to-all | bytes 2097152 | tf_op jit(solution)/shard_map/all_to_all | solution.py:230
  116.6 32.1 %all_to_all.25 = f32[32,8,256]{2,1,0:T(8,128)S(1)} all-to-all(f32[32,8,256]{2,1,0:T(8,128)S(1)} %bitcast.32), channel_id=1, replica_groups=mesh['y2'=2,'y1'=2,'y0'=2,'xh'=2,'xl'=2,'z2'=2,'z1'=2,'z0'=2,'c'=2] {'y2..., dimensions={0} | all-to-all | bytes 524288 | tf_op jit(solution)/shard_map/all_to_all | solution.py:232
  148.8 16.2 %all_to_all.26 = f32[32,8,256]{2,1,0:T(8,128)S(1)} all-to-all(f32[32,8,256]{2,1,0:T(8,128)S(1)} %broadcast_in_dim.4), channel_id=1, replica_groups=mesh['y2'=2,'y1'=2,'y0'=2,'xh'=2,'xl'=2,'z2'=2,'z1'=2,'z0'=2,'c'=2] {'xl..., dimensions={0} | all-to-all | bytes 524288 | tf_op jit(solution)/shard_map/all_to_all | solution.py:234
  166.3 12.2 %all_to_all.27 = f32[16,1,128]{2,1,0:T(1,128)S(1)} all-to-all(f32[16,1,128]{2,1,0:T(1,128)S(1)} %broadcast_in_dim.5), channel_id=1, replica_groups=mesh['y2'=2,'y1'=2,'y0'=2,'xh'=2,'xl'=2,'z2'=2,'z1'=2,'z0'=2,'c'=2] {'y2..., dimensions={0} | all-to-all | bytes 16384 | tf_op jit(solution)/shard_map/all_to_all | solution.py:239
  (38 shorter events, 8.8 us)
Async XLA Ops:
  0.0 1.6 copy-start
  3.7 0.7 collective-permute-start
  4.4 12.1 %collective-permute-start.1 = (bf16[256,512]{1,0:T(8,128)(2,1)S(1)}, bf16[256,512]{1,0:T(8,128)(2,1)S(1)}, u32[]{:S(2)}, u32[]{:S(2)}) collective-permute-start(bf16[256,512]{1,0:T(8,128)(2,1)S(1)} %collective-permute-done), channel_id=1, source_target_pairs={{0,64},{64,128},{128,192},{192,256},{256,320},{320,384},{384,448},... | collective-permute-start | bytes 786440 | tf_op jit(solution)/shard_map/ppermute | solution.py:173
  7.9 10.5 %collective-permute-start.4 = (bf16[256,512]{1,0:T(8,128)(2,1)S(1)}, bf16[256,512]{1,0:T(8,128)(2,1)S(1)}, u32[]{:S(2)}, u32[]{:S(2)}) collective-permute-start(bf16[256,512]{1,0:T(8,128)(2,1)S(1)} %collective-permute-done), channel_id=1, source_target_pairs={{0,448},{64,0},{128,64},{192,128},{256,192},{320,256},{384,320},{4... | collective-permute-start | bytes 786440 | tf_op jit(solution)/shard_map/ppermute | solution.py:174
  16.5 10.6 %collective-permute-start.5 = (bf16[256,512]{1,0:T(8,128)(2,1)S(1)}, bf16[256,512]{1,0:T(8,128)(2,1)S(1)}, u32[]{:S(2)}, u32[]{:S(2)}) collective-permute-start(bf16[256,512]{1,0:T(8,128)(2,1)S(1)} %collective-permute-done.1), channel_id=1, source_target_pairs={{0,64},{64,128},{128,192},{192,256},{256,320},{320,384},{384,448},... | collective-permute-start | bytes 786440 | tf_op jit(solution)/shard_map/ppermute | solution.py:173
  18.4 10.6 %collective-permute-start.6 = (bf16[256,512]{1,0:T(8,128)(2,1)S(1)}, bf16[256,512]{1,0:T(8,128)(2,1)S(1)}, u32[]{:S(2)}, u32[]{:S(2)}) collective-permute-start(bf16[256,512]{1,0:T(8,128)(2,1)S(1)} %collective-permute-done.4), channel_id=1, source_target_pairs={{0,448},{64,0},{128,64},{192,128},{256,192},{320,256},{384,320},{4... | collective-permute-start | bytes 786440 | tf_op jit(solution)/shard_map/ppermute | solution.py:174
  24.5 28.1 %copy-start.1 = (s32[256]{0:T(256)S(1)}, s32[256]{0:T(256)}, u32[]{:S(2)}) copy-start(s32[256]{0:T(256)} %param.5) | copy-start | bytes 3076
  27.1 11.9 %collective-permute-start.7 = (bf16[256,512]{1,0:T(8,128)(2,1)S(1)}, bf16[256,512]{1,0:T(8,128)(2,1)S(1)}, u32[]{:S(2)}, u32[]{:S(2)}) collective-permute-start(bf16[256,512]{1,0:T(8,128)(2,1)S(1)} %collective-permute-done.5), channel_id=1, source_target_pairs={{0,64},{64,128},{128,192},{192,256},{256,320},{320,384},{384,448},... | collective-permute-start | bytes 786440 | tf_op jit(solution)/shard_map/ppermute | solution.py:173
  29.0 11.9 %collective-permute-start.8 = (bf16[256,512]{1,0:T(8,128)(2,1)S(1)}, bf16[256,512]{1,0:T(8,128)(2,1)S(1)}, u32[]{:S(2)}, u32[]{:S(2)}) collective-permute-start(bf16[256,512]{1,0:T(8,128)(2,1)S(1)} %collective-permute-done.6), channel_id=1, source_target_pairs={{0,448},{64,0},{128,64},{192,128},{256,192},{320,256},{384,320},{4... | collective-permute-start | bytes 786440 | tf_op jit(solution)/shard_map/ppermute | solution.py:174
  39.0 9.3 %collective-permute-start.9 = (bf16[128,512]{1,0:T(8,128)(2,1)S(1)}, bf16[128,512]{1,0:T(8,128)(2,1)S(1)}, u32[]{:S(2)}, u32[]{:S(2)}) collective-permute-start(bf16[128,512]{1,0:T(8,128)(2,1)S(1)} %slice.12), channel_id=1, source_target_pairs={{0,64},{64,128},{128,192},{192,256},{256,320},{320,384},{384,448},... | collective-permute-start | bytes 393224 | tf_op jit(solution)/shard_map/ppermute | solution.py:182
  41.0 9.0 %collective-permute-start.10 = (bf16[128,512]{1,0:T(8,128)(2,1)S(1)}, bf16[128,512]{1,0:T(8,128)(2,1)S(1)}, u32[]{:S(2)}, u32[]{:S(2)}) collective-permute-start(bf16[128,512]{1,0:T(8,128)(2,1)S(1)} %slice.13), channel_id=1, source_target_pairs={{0,448},{64,0},{128,64},{192,128},{256,192},{320,256},{384,320},{4... | collective-permute-start | bytes 393224 | tf_op jit(solution)/shard_map/ppermute | solution.py:183
  50.7 26.6 %collective-permute-start.11 = (bf16[2048,512]{1,0:T(8,128)(2,1)}, bf16[2048,512]{1,0:T(8,128)(2,1)}, u32[]{:S(2)}, u32[]{:S(2)}) collective-permute-start(bf16[2048,512]{1,0:T(8,128)(2,1)} %constant_dynamic-update-slice_fusion.mine_ref), channel_id=1, source_target_pairs={{0,1},{1,0},{2,3},{3,2},{4,5},{5,4},{6,7},{7,6},{8,9},{9,8},{10,11... | collective-permute-start | bytes 6291464 | tf_op jit(solution)/shard_map/ppermute | solution.py:191
  52.8 32.9 %collective-permute-start.3 = (f32[2,256]{0,1:T(8,128)S(1)}, f32[2,256]{0,1:T(8,128)S(1)}, u32[]{:S(2)}, u32[]{:S(2)}) collective-permute-start(f32[2,256]{0,1:T(8,128)S(1)} %copy.11), channel_id=1, source_target_pairs={{0,0},{1,32},{2,2},{3,34},{4,4},{5,36},{6,6},{7,38},{8,8},{9,40},{... | collective-permute-start | bytes 6152 | tf_op jit(solution)/shard_map/ppermute | solution.py:167
  53.6 39.8 %collective-permute-start.12 = (bf16[256,2048]{1,0:T(8,128)(2,1)}, bf16[256,2048]{1,0:T(8,128)(2,1)S(1)}, u32[]{:S(2)}, u32[]{:S(2)}) collective-permute-start(bf16[256,2048]{1,0:T(8,128)(2,1)} %param.3), channel_id=1, source_target_pairs={{0,1},{1,33},{2,3},{3,35},{4,5},{5,37},{6,7},{7,39},{8,9},{9,41},{... | collective-permute-start | bytes 3145736 | tf_op jit(solution)/shard_map/ppermute | solution.py:179
  63.2 31.7 %collective-permute-start.2 = (bf16[256,2048]{1,0:T(8,128)(2,1)}, bf16[256,2048]{1,0:T(8,128)(2,1)}, u32[]{:S(2)}, u32[]{:S(2)}) collective-permute-start(bf16[256,2048]{1,0:T(8,128)(2,1)} %param.3), channel_id=1, source_target_pairs={{0,0},{1,32},{2,2},{3,34},{4,4},{5,36},{6,6},{7,38},{8,8},{9,40},{... | collective-permute-start | bytes 3145736 | tf_op jit(solution)/shard_map/ppermute | solution.py:179
  91.2 3.2 %collective-permute-start.13 = (bf16[256,256]{1,0:T(8,128)(2,1)S(1)}, bf16[256,256]{1,0:T(8,128)(2,1)S(1)}, u32[]{:S(2)}, u32[]{:S(2)}) collective-permute-start(bf16[256,256]{1,0:T(8,128)(2,1)S(1)} %get-tuple-element.12), channel_id=1, source_target_pairs={{0,1},{1,0},{2,3},{3,2},{4,5},{5,4},{6,7},{7,6},{8,9},{9,8},{10,11... | collective-permute-start | bytes 393224 | tf_op jit(solution)/shard_map/ppermute | solution.py:220

commit v3 on v2

--- a/solution.py
+++ b/solution.py
@@ -20,7 +20,8 @@
     pairs = []
     for place in itertools.product((0, 1), repeat=len(BITS)):
         target = list(place)
-        target[3], target[8] = place[8], place[3] ^ other_core
+        xh, xl, core = place[3], place[4], place[8]
+        target[3], target[4], target[8] = core ^ xl, 1 - xl, xh ^ other_core
         index = [sum(bit << (8 - k) for k, bit in enumerate(bits)) for bits in (place, target)]
         pairs.append(tuple(index))
     return pairs
@@ -29,8 +30,7 @@
 TO_HOST, TO_SIBLING = moves(0), moves(1)
 
 
-def along_y(step):
-    return [(k, (k + step) % Y) for k in range(Y)]
+ROUND = [(2 * y + c, 2 * ((y + (1, -1)[c]) % Y) + c) for y in range(Y) for c in range(2)]
 
 
 def exponentials(left, right):
@@ -66,25 +66,34 @@
         sums_ref[i] = per_column[i].sum(0, keepdims=True) + per_lane[i].T.sum(0, keepdims=True)
 
 
-def cross_block_kernel(core_ref, mine_ref, sibling_ref, same_ref, sums_ref, units, per_lane, per_column):
+def cross_block_kernel(core_ref, mine_ref, sibling_ref, same_ref, sums_ref, per_lane, per_column):
     core = core_ref[0]
     blocks, wide = per_column.shape[0], per_column.shape[2]
-    for k in range(blocks):
-        units[blocks * core + k] = mine_ref[k * wide : (k + 1) * wide, :]
-        units[blocks * (1 - core) + k] = sibling_ref[k * wide : (k + 1) * wide, :]
+    half = blocks // 2
     per_lane[...] = jnp.zeros_like(per_lane)
     per_column[...] = jnp.zeros_like(per_column)
-    for i in range(blocks // 2):
-        left = units[blocks // 2 * core + i]
-        for j in range(blocks):
-            values = exponentials(left, units[blocks + j])
-            per_column[j] += over_rows(values)
-            per_lane[i] += over_lane_groups(values)
-    for k in range(blocks):
-        sums_ref[k] = jnp.zeros_like(sums_ref[k])
-        sums_ref[blocks + k] = per_column[k].sum(0, keepdims=True)
-    for i in range(blocks // 2):
-        sums_ref[blocks // 2 * core + i] = per_lane[i].T.sum(0, keepdims=True)
+
+    def pairs(left_ref, first, right_ref):
+        for i in range(half):
+            left = left_ref[(first + i) * wide : (first + i + 1) * wide, :]
+            for j in range(blocks):
+                values = exponentials(left, right_ref[j * wide : (j + 1) * wide, :])
+                per_column[j] += over_rows(values)
+                per_lane[i] += over_lane_groups(values)
+        for k in range(blocks):
+            sums_ref[k] = jnp.zeros_like(sums_ref[k])
+            sums_ref[blocks + k] = per_column[k].sum(0, keepdims=True)
+        for i in range(half):
+            sums_ref[first + i] = per_lane[i].T.sum(0, keepdims=True)
+
+    @pl.when(core == 0)
+    def _():
+        pairs(mine_ref, 0, sibling_ref)
+
+    @pl.when(core == 1)
+    def _():
+        pairs(sibling_ref, half, mine_ref)
+
     for k in range(blocks):
         sums_ref[blocks * core + k] += same_ref[k]
 
@@ -165,28 +174,32 @@
 
     own = lax.ppermute(unit, BITS, TO_HOST)
     side_here = lax.ppermute(side, BITS, TO_HOST)
-    up, down = along_y(1), along_y(-1)
-    from_below, from_above = own, own
-    pieces, places = [own], [y]
+    sign = jnp.where(core == 0, -1, 1)
+    same_core = own
+    other_core = lax.ppermute(own, "c", OTHER_CORE)
+    pieces, places = [own], [y * 2 + core]
     sends = []
-    for distance in range(1, 4):
-        from_below = lax.ppermute(from_below, YBITS, up)
-        from_above = lax.ppermute(from_above, YBITS, down)
-        pieces += [from_below, from_above]
-        places += [(y - distance) % Y, (y + distance) % Y]
+    for distance in range(1, 5):
+        place = (y + sign * distance) % Y * 2
+        same_core = lax.ppermute(same_core, (*YBITS, "c"), ROUND)
+        pieces.append(same_core)
+        places.append(place + core)
+        if distance == 4:
+            break
+        other_core = lax.ppermute(other_core, (*YBITS, "c"), ROUND)
+        pieces.append(other_core)
+        places.append(place + 1 - core)
         if distance < 3:
-            later, unused = lax.optimization_barrier((features, from_below))
+            later, unused = lax.optimization_barrier((features, same_core))
             sends.append(lax.ppermute(later, BITS, (TO_HOST, TO_SIBLING)[distance - 1]))
-    half = rows // 2
-    pieces += [
-        lax.ppermute(from_below[:half], YBITS, up),
-        lax.ppermute(from_above[half:], YBITS, down),
-    ]
-    places.append((y + Y // 2) % Y)
+    sign, core_there = -sign, 1 - core
+    places.append(y * 2 + core_there)
+    for distance in range(1, 5):
+        place = (y + sign * distance) % Y * 2
+        places += [place + core_there, place + 1 - core_there][: 1 if distance == 4 else 2]
     mine = jnp.concatenate(pieces)
+    starts = jnp.stack(places).astype(jnp.int32) * rows
     rows_here, rows_beside = sends
-    places = jnp.stack(places)
-    starts = jnp.concatenate([places * 2 + core, places * 2 + 1 - core]).astype(jnp.int32) * rows
 
     sibling = lax.ppermute(mine, "c", OTHER_CORE)
     lanes = pltpu.VMEM((4, 512, 128), jnp.float32)
@@ -203,7 +216,7 @@
         cross_block_kernel,
         jax.ShapeDtypeStruct((8, 1, 512), jnp.float32),
         [SMEM, VMEM, VMEM, VMEM],
-        [pltpu.VMEM((8, 512, width), jnp.bfloat16), lanes, columns],
+        [lanes, columns],
         2_000_000_000,
         "cross_parity_sums",
     )(core_scalar, mine, sibling, same)
@@ -226,15 +239,16 @@
 
     partial = (contract(rows_here, kept) + contract(rows_beside, beside)).astype(jnp.bfloat16)
     tiles = partial.reshape(4, 2, 2, 2, 4, 2, 8, 256)
-    tiles = tiles.transpose(1, 3, 5, 0, 2, 4, 6, 7).reshape(8, 32 * 8, 256)
-    received = lax.all_to_all(tiles, ("y0", "xl", "z0"), 0, 0)
-    near_sum = received.astype(jnp.float32).sum(0).reshape(32, 8, 256)
-    received = lax.all_to_all(near_sum, ("y2", "y1", "xh", "z2", "z1"), 0, 0)
-    fragment = received.sum(0)
+    tiles = tiles.transpose(1, 2, 3, 5, 0, 4, 6, 7).reshape(16, 16 * 8, 256)
+    received = lax.all_to_all(tiles, ("y0", "xh", "xl", "z0"), 0, 0)
+    near_sum = received.astype(jnp.float32).sum(0).reshape(4, 4 * 8, 256)
+    along_y_sum = lax.all_to_all(near_sum, ("y2", "y1"), 0, 0).sum(0).reshape(4, 8, 256)
+    fragment = lax.all_to_all(along_y_sum, ("z2", "z1"), 0, 0).sum(0).astype(jnp.bfloat16)
     spread = lax.all_to_all(
         jnp.broadcast_to(fragment[None], (32, 8, 256)), ("xl", "z2", "z1", "z0", "c"), 0, 0
     )
     gradient = spread.reshape(16, 2, 8, 256).transpose(0, 2, 1, 3).reshape(128, width)
+    gradient = gradient.astype(jnp.float32)
     squares = jnp.sum(gradient * gradient)
     squares = lax.all_to_all(
         jnp.broadcast_to(squares, (16, 128)), ("y2", "y1", "y0", "xh"), 0, 0

time: 182 us -> 175 us (0.962)
  starting transfers between devices: 56.5 us -> 35.4 us
  waiting for transfers between devices: 8.63 us -> 23 us
    ppermute x8, starting transfers between devices: 32 us -> 19.3 us  [the longest x4 9.53 us: on_device(): same_core = lax.ppermute(same_core, (*YBITS, 'c'), ROUND)]
    ppermute x2, starting transfers between devices: 19 us -> 6.42 us  [on_device(): sends.append(lax.ppermute(later, BITS, (TO_HOST, TO_SIBLING)[distance - 1]))]
    ppermute x8, waiting for transfers between devices: 7.64 us -> 17.9 us  [the longest x4 17 us: on_device(): same_core = lax.ppermute(same_core, (*YBITS, 'c'), ROUND)]
    ppermute x1, waiting for transfers between devices: 0.01 us -> 4.28 us  [on_device(): own = lax.ppermute(unit, BITS, TO_HOST)]
    all_to_all x1, blocking collectives: 16.2 us -> 13.4 us  [on_device(): lax.all_to_all(jnp.broadcast_to(fragment[None], (32, 8, 256)), ('xl', 'z2...]
    ppermute x1, starting transfers between devices: 0.68 us -> 3.4 us  [on_device(): own = lax.ppermute(unit, BITS, TO_HOST)]
    all_to_all x2 -> x3, blocking collectives: 51.8 us -> 54.2 us  [the longest x1 21.4 us: on_device(): received = lax.all_to_all(tiles, ('y0', 'xh', 'xl', 'z0'), 0, 0)]
    unnamed x12 -> x11, local copies, waits for them, and re-layouts: 7.37 us -> 6.7 us
  transfers between devices with their start and end apart: 14 -> 14, of which waited for: 5 -> 7; matrix products, arithmetic and copies ran while one was open for 4% -> 3% of each run, Pallas kernels for 8% -> 9%
where the time goes in v3:
time: 175 us; the launch traced here: 174 us
  blocking collectives  84.4 us (48%)
  starting transfers between devices  35.4 us (20%)
  waiting for transfers between devices  23 us (13%)
  Pallas kernels  14.8 us (8%)
  local copies, waits for them, and re-layouts  8.44 us (5%)
  matrix products  4.23 us (2%)
  other arithmetic  2.29 us (1%)
    all_to_all x1, blocking collectives, on_device(): received = lax.all_to_all(tiles, ('y0', 'xh', 'xl', 'z0'), 0, 0)  21.4 us
    all_to_all x1, blocking collectives, on_device(): lax.all_to_all(along_y_sum, ('z2', 'z1'), 0, 0).sum(0).astype(jnp.bfloat16)  17.1 us
    ppermute x4, waiting for transfers between devices, on_device(): same_core = lax.ppermute(same_core, (*YBITS, 'c'), ROUND)  17 us
    all_to_all x1, blocking collectives, on_device(): lax.all_to_all(near_sum, ('y2', 'y1'), 0, 0).sum(0).reshape(4, 8, 256)  15.7 us
    all_to_all x1, blocking collectives, on_device(): lax.all_to_all(jnp.broadcast_to(squares, (16, 128)), ('y2', 'y1', 'y0', '...  13.4 us
    all_to_all x1, blocking collectives, on_device(): lax.all_to_all(jnp.broadcast_to(fragment[None], (32, 8, 256)), ('xl', 'z2...  13.4 us
    ppermute x4, starting transfers between devices, on_device(): same_core = lax.ppermute(same_core, (*YBITS, 'c'), ROUND)  9.53 us
    ppermute x3, starting transfers between devices, on_device(): other_core = lax.ppermute(other_core, (*YBITS, 'c'), ROUND)  7.39 us
  transfers between devices with their start and end apart: 14, of which 7 were waited for; matrix products, arithmetic and copies ran while one was open for 3% of the time, Pallas kernels for 9%

profile of v3, /device:TPU:8, one launch (start us, length us, event | category | flops | bytes accessed | tf_op | source)
XLA Modules:
  0.0 173.7 jit_solution(3129954470957808290)
XLA Ops:
  0.0 1.6 copy-done
  1.6 2.0 %multiply_reduce_fusion = (f32[256]{0:T(256)S(1)}, f32[256,512]{1,0:T(8,128)S(1)}) fusion(bf16[256,2048]{1,0:T(8,128)(2,1)} %param.3, bf16[2048,512]{1,0:T(8,128)(2,1)S(1)} %copy-done), kind=kOutput, calls=%fused_computation.4 | convolution fusion | flops 537132800 | bytes 3671040 | tf_op jit(solution)/shard_map/dot_general | solution.py:170
  3.8 3.4 %collective-permute-start = (bf16[256,512]{1,0:T(8,128)(2,1)S(1)}, bf16[256,512]{1,0:T(8,128)(2,1)S(1)}, u32[]{:S(2)}, u32[]{:S(2)}) collective-permute-start(bf16[256,512]{1,0:T(8,128)(2,1)S(1)} %divide_convert_fusion), channel_id=1, source_target_pairs={{0,16},{1,48},{2,18},{3,50},{4,20},{5,52},{6,22},{7,54},{8,24},{9,... | collective-permute-start | bytes 786440 | tf_op jit(solution)/shard_map/ppermute | solution.py:175
  7.2 4.3 %collective-permute-done = bf16[256,512]{1,0:T(8,128)(2,1)S(1)} collective-permute-done((bf16[256,512]{1,0:T(8,128)(2,1)S(1)}, bf16[256,512]{1,0:T(8,128)(2,1)S(1)}, u32[]{:S(2)}, u32[]{:S(2)}) %collective-permute-start) | collective-permute-done | bytes 262176 | tf_op jit(solution)/shard_map/ppermute | solution.py:175
  11.4 2.4 %collective-permute-start.4 = (bf16[256,512]{1,0:T(8,128)(2,1)S(1)}, bf16[256,512]{1,0:T(8,128)(2,1)S(1)}, u32[]{:S(2)}, u32[]{:S(2)}) collective-permute-start(bf16[256,512]{1,0:T(8,128)(2,1)S(1)} %collective-permute-done), channel_id=1, source_target_pairs={{0,1},{1,0},{2,3},{3,2},{4,5},{5,4},{6,7},{7,6},{8,9},{9,8},{10,11... | collective-permute-start | bytes 786440 | tf_op jit(solution)/shard_map/ppermute | solution.py:179
  13.8 3.5 %collective-permute-start.1 = (bf16[256,512]{1,0:T(8,128)(2,1)S(1)}, bf16[256,512]{1,0:T(8,128)(2,1)S(1)}, u32[]{:S(2)}, u32[]{:S(2)}) collective-permute-start(bf16[256,512]{1,0:T(8,128)(2,1)S(1)} %collective-permute-done), channel_id=1, source_target_pairs={{0,64},{1,449},{64,128},{65,1},{128,192},{129,65},{192,256},{193,1... | collective-permute-start | bytes 786440 | tf_op jit(solution)/shard_map/ppermute | solution.py:184
  17.3 3.5 %collective-permute-start.5 = (bf16[256,512]{1,0:T(8,128)(2,1)S(1)}, bf16[256,512]{1,0:T(8,128)(2,1)S(1)}, u32[]{:S(2)}, u32[]{:S(2)}) collective-permute-start(bf16[256,512]{1,0:T(8,128)(2,1)S(1)} %collective-permute-done.4), channel_id=1, source_target_pairs={{0,64},{1,449},{64,128},{65,1},{128,192},{129,65},{192,256},{193,1... | collective-permute-start | bytes 786440 | tf_op jit(solution)/shard_map/ppermute | solution.py:189
  20.8 4.6 %collective-permute-done.1 = bf16[256,512]{1,0:T(8,128)(2,1)S(1)} collective-permute-done((bf16[256,512]{1,0:T(8,128)(2,1)S(1)}, bf16[256,512]{1,0:T(8,128)(2,1)S(1)}, u32[]{:S(2)}, u32[]{:S(2)}) %collective-permute-start.1) | collective-permute-done | bytes 262176 | tf_op jit(solution)/shard_map/ppermute | solution.py:184
  25.4 1.9 %collective-permute-start.6 = (bf16[256,512]{1,0:T(8,128)(2,1)S(1)}, bf16[256,512]{1,0:T(8,128)(2,1)S(1)}, u32[]{:S(2)}, u32[]{:S(2)}) collective-permute-start(bf16[256,512]{1,0:T(8,128)(2,1)S(1)} %collective-permute-done.1), channel_id=1, source_target_pairs={{0,64},{1,449},{64,128},{65,1},{128,192},{129,65},{192,256},{193,1... | collective-permute-start | bytes 786440 | tf_op jit(solution)/shard_map/ppermute | solution.py:184
  27.4 0.9 collective-permute-done.5
  28.2 1.9 %collective-permute-start.7 = (bf16[256,512]{1,0:T(8,128)(2,1)S(1)}, bf16[256,512]{1,0:T(8,128)(2,1)S(1)}, u32[]{:S(2)}, u32[]{:S(2)}) collective-permute-start(bf16[256,512]{1,0:T(8,128)(2,1)S(1)} %collective-permute-done.5), channel_id=1, source_target_pairs={{0,64},{1,449},{64,128},{65,1},{128,192},{129,65},{192,256},{193,1... | collective-permute-start | bytes 786440 | tf_op jit(solution)/shard_map/ppermute | solution.py:189
  30.9 4.0 %collective-permute-done.6 = bf16[256,512]{1,0:T(8,128)(2,1)S(1)} collective-permute-done((bf16[256,512]{1,0:T(8,128)(2,1)S(1)}, bf16[256,512]{1,0:T(8,128)(2,1)S(1)}, u32[]{:S(2)}, u32[]{:S(2)}) %collective-permute-start.6) | collective-permute-done | bytes 262176 | tf_op jit(solution)/shard_map/ppermute | solution.py:184
  34.9 1.9 %collective-permute-start.8 = (bf16[256,512]{1,0:T(8,128)(2,1)S(1)}, bf16[256,512]{1,0:T(8,128)(2,1)S(1)}, u32[]{:S(2)}, u32[]{:S(2)}) collective-permute-start(bf16[256,512]{1,0:T(8,128)(2,1)S(1)} %collective-permute-done.6), channel_id=1, source_target_pairs={{0,64},{1,449},{64,128},{65,1},{128,192},{129,65},{192,256},{193,1... | collective-permute-start | bytes 786440 | tf_op jit(solution)/shard_map/ppermute | solution.py:184
  38.3 2.0 %collective-permute-start.9 = (bf16[256,512]{1,0:T(8,128)(2,1)S(1)}, bf16[256,512]{1,0:T(8,128)(2,1)S(1)}, u32[]{:S(2)}, u32[]{:S(2)}) collective-permute-start(bf16[256,512]{1,0:T(8,128)(2,1)S(1)} %collective-permute-done.7), channel_id=1, source_target_pairs={{0,64},{1,449},{64,128},{65,1},{128,192},{129,65},{192,256},{193,1... | collective-permute-start | bytes 786440 | tf_op jit(solution)/shard_map/ppermute | solution.py:189
  41.0 3.4 %collective-permute-done.8 = bf16[256,512]{1,0:T(8,128)(2,1)S(1)} collective-permute-done((bf16[256,512]{1,0:T(8,128)(2,1)S(1)}, bf16[256,512]{1,0:T(8,128)(2,1)S(1)}, u32[]{:S(2)}, u32[]{:S(2)}) %collective-permute-start.8) | collective-permute-done | bytes 262176 | tf_op jit(solution)/shard_map/ppermute | solution.py:184
  44.4 2.2 %collective-permute-start.10 = (bf16[256,512]{1,0:T(8,128)(2,1)S(1)}, bf16[256,512]{1,0:T(8,128)(2,1)S(1)}, u32[]{:S(2)}, u32[]{:S(2)}) collective-permute-start(bf16[256,512]{1,0:T(8,128)(2,1)S(1)} %collective-permute-done.8), channel_id=1, source_target_pairs={{0,64},{1,449},{64,128},{65,1},{128,192},{129,65},{192,256},{193,1... | collective-permute-start | bytes 786440 | tf_op jit(solution)/shard_map/ppermute | solution.py:184
  48.8 5.0 %collective-permute-done.10 = bf16[256,512]{1,0:T(8,128)(2,1)S(1)} collective-permute-done((bf16[256,512]{1,0:T(8,128)(2,1)S(1)}, bf16[256,512]{1,0:T(8,128)(2,1)S(1)}, u32[]{:S(2)}, u32[]{:S(2)}) %collective-permute-start.10) | collective-permute-done | bytes 262176 | tf_op jit(solution)/shard_map/ppermute | solution.py:184
  54.6 1.9 %collective-permute-start.11 = (bf16[2048,512]{1,0:T(8,128)(2,1)}, bf16[2048,512]{1,0:T(8,128)(2,1)}, u32[]{:S(2)}, u32[]{:S(2)}) collective-permute-start(bf16[2048,512]{1,0:T(8,128)(2,1)} %constant_dynamic-update-slice_fusion.mine_ref), channel_id=1, source_target_pairs={{0,1},{1,0},{2,3},{3,2},{4,5},{5,4},{6,7},{7,6},{8,9},{9,8},{10,11... | collective-permute-start | bytes 6291464 | tf_op jit(solution)/shard_map/ppermute | solution.py:204
  56.5 2.6 %collective-permute-start.12 = (bf16[256,2048]{1,0:T(8,128)(2,1)}, bf16[256,2048]{1,0:T(8,128)(2,1)S(1)}, u32[]{:S(2)}, u32[]{:S(2)}) collective-permute-start(bf16[256,2048]{1,0:T(8,128)(2,1)} %param.3), channel_id=1, source_target_pairs={{0,17},{1,49},{2,19},{3,51},{4,21},{5,53},{6,23},{7,55},{8,25},{9,... | collective-permute-start | bytes 3145736 | tf_op jit(solution)/shard_map/ppermute | solution.py:194
  59.3 1.9 %collective-permute-start.3 = (f32[2,256]{0,1:T(8,128)S(1)}, f32[2,256]{0,1:T(8,128)S(1)}, u32[]{:S(2)}, u32[]{:S(2)}) collective-permute-start(f32[2,256]{0,1:T(8,128)S(1)} %copy.11), channel_id=1, source_target_pairs={{0,16},{1,48},{2,18},{3,50},{4,20},{5,52},{6,22},{7,54},{8,24},{9,... | collective-permute-start | bytes 6152 | tf_op jit(solution)/shard_map/ppermute | solution.py:176
  61.5 3.8 %collective-permute-start.2 = (bf16[256,2048]{1,0:T(8,128)(2,1)}, bf16[256,2048]{1,0:T(8,128)(2,1)}, u32[]{:S(2)}, u32[]{:S(2)}) collective-permute-start(bf16[256,2048]{1,0:T(8,128)(2,1)} %param.3), channel_id=1, source_target_pairs={{0,16},{1,48},{2,18},{3,50},{4,20},{5,52},{6,22},{7,54},{8,24},{9,... | collective-permute-start | bytes 3145736 | tf_op jit(solution)/shard_map/ppermute | solution.py:194
  65.3 4.5 %same_parity_sums.1.same_ref = f32[4,1,512]{2,1,0:T(1,128)S(1)} custom-call(bf16[2048,512]{1,0:T(8,128)(2,1)} %constant_dynamic-update-slice_fusion.mine_ref), custom_call_target="tpu_custom_call" | custom-call | flops 3000000000 | bytes 2000000 | tf_op jit(solution)/shard_map/same_parity_sums/pallas_call | solution.py:207
  69.8 4.7 %cross_parity_sums.1 = f32[8,1,512]{2,1,0:T(1,128)S(1)} custom-call(s32[1]{0:T(128)} %bitcast.core_ref, bf16[2048,512]{1,0:T(8,128)(2,1)} %constant_dynamic-update-slice_fusion.mine_ref, bf16[2048,512]{1,0:T(8,128)(2,1)} %collective-permute-done.11.sibling_ref, f32[4,1,512]{2,1,0:T(1,128)S(1)} %same_parity_sums.1.same_ref), custom_call_target="tpu_custom_call" | custom-call | flops 2000000000 | bytes 2000000 | tf_op jit(solution)/shard_map/cross_parity_sums/pallas_call | solution.py:215
  74.6 3.4 %psum.7.sums_ref = f32[8,1,512]{2,1,0:T(1,128)S(1)} all-reduce(f32[8,1,512]{2,1,0:T(1,128)S(1)} %cross_parity_sums.1), channel_id=1, replica_groups=mesh['y2'=2,'y1'=2,'y0'=2,'xh'=2,'xl'=2,'z2'=2,'z1'=2,'z0'=2,'c'=2] {'c'}, use_global_device_ids=true, to_apply=%region_1.2 | all-reduce | flops 4096 | bytes 32768 | tf_op jit(solution)/shard_map/psum | solution.py:223
  77.9 5.6 %weights.1 = (bf16[256,256]{1,0:T(8,128)(2,1)S(1)}, bf16[256,256]{1,0:T(8,128)(2,1)S(1)}) custom-call(s32[1]{0:T(128)} %bitcast.core_ref, s32[16]{0:T(128)S(1)} %broadcast_multiply_fusion.start_ref, f32[256,2]{1,0:T(8,128)S(1)} %bitcast.38, f32[8,1,512]{2,1,0:T(1,128)S(1)} %psum.7.sums_ref, bf16[2048,512]{1,0:T(8,128)(2,1)} %constant_dynamic-update-slice_fusion.mine_ref, ...), custom_call_target="tpu_custom_call" | custom-call | flops 2000000000 | bytes 2000000 | tf_op jit(solution)/shard_map/weights/pallas_call | solution.py:225
  83.5 2.4 %collective-permute-start.13 = (bf16[256,256]{1,0:T(8,128)(2,1)S(1)}, bf16[256,256]{1,0:T(8,128)(2,1)S(1)}, u32[]{:S(2)}, u32[]{:S(2)}) collective-permute-start(bf16[256,256]{1,0:T(8,128)(2,1)S(1)} %get-tuple-element.12), channel_id=1, source_target_pairs={{0,1},{1,0},{2,3},{3,2},{4,5},{5,4},{6,7},{7,6},{8,9},{9,8},{10,11... | collective-permute-start | bytes 393224 | tf_op jit(solution)/shard_map/ppermute | solution.py:233
  87.2 1.7 %fusion = bf16[2048,256]{1,0:T(8,128)(2,1)S(1)} fusion(f32[2048,256]{1,0:T(8,128)S(1)} %fusion.2, bf16[256,2048]{1,0:T(8,128)(2,1)} %collective-permute-done.2, bf16[256,256]{1,0:T(8,128)(2,1)S(1)} %get-tuple-element.10), kind=kOutput, calls=%fused_computation.1 | convolution fusion | flops 269484032 | bytes 4325376 | tf_op jit(solution)/shard_map/dot_general | solution.py:236
  89.1 21.4 %all_to_all.29 = bf16[16,128,256]{2,1,0:T(8,128)(2,1)S(1)} all-to-all(bf16[16,128,256]{2,1,0:T(8,128)(2,1)S(1)} %bitcast.39), channel_id=1, replica_groups=mesh['y2'=2,'y1'=2,'y0'=2,'xh'=2,'xl'=2,'z2'=2,'z1'=2,'z0'=2,'c'=2] {'y0..., dimensions={0} | all-to-all | bytes 2097152 | tf_op jit(solution)/shard_map/all_to_all | solution.py:243
  110.7 15.7 %all_to_all.30 = f32[4,32,256]{2,1,0:T(8,128)S(1)} all-to-all(f32[4,32,256]{2,1,0:T(8,128)S(1)} %bitcast.41), channel_id=1, replica_groups=mesh['y2'=2,'y1'=2,'y0'=2,'xh'=2,'xl'=2,'z2'=2,'z1'=2,'z0'=2,'c'=2] {'y2..., dimensions={0} | all-to-all | bytes 262144 | tf_op jit(solution)/shard_map/all_to_all | solution.py:245
  126.4 17.1 %all_to_all.31 = f32[4,8,256]{2,1,0:T(8,128)S(1)} all-to-all(f32[4,8,256]{2,1,0:T(8,128)S(1)} %bitcast.42), channel_id=1, replica_groups=mesh['y2'=2,'y1'=2,'y0'=2,'xh'=2,'xl'=2,'z2'=2,'z1'=2,'z0'=2,'c'=2] {'z2..., dimensions={0} | all-to-all | bytes 65536 | tf_op jit(solution)/shard_map/all_to_all | solution.py:246
  143.5 13.4 %all_to_all.32 = bf16[32,8,256]{2,1,0:T(8,128)(2,1)S(1)} all-to-all(bf16[32,8,256]{2,1,0:T(8,128)(2,1)S(1)} %broadcast_in_dim.4), channel_id=1, replica_groups=mesh['y2'=2,'y1'=2,'y0'=2,'xh'=2,'xl'=2,'z2'=2,'z1'=2,'z0'=2,'c'=2] {'xl..., dimensions={0} | all-to-all | bytes 262144 | tf_op jit(solution)/shard_map/all_to_all | solution.py:247
  158.2 13.4 %all_to_all.33 = f32[16,1,128]{2,1,0:T(1,128)S(1)} all-to-all(f32[16,1,128]{2,1,0:T(1,128)S(1)} %broadcast_in_dim.5), channel_id=1, replica_groups=mesh['y2'=2,'y1'=2,'y0'=2,'xh'=2,'xl'=2,'z2'=2,'z1'=2,'z0'=2,'c'=2] {'y2..., dimensions={0} | all-to-all | bytes 16384 | tf_op jit(solution)/shard_map/all_to_all | solution.py:253
  (36 shorter events, 10.4 us)
Async XLA Ops:
  0.0 1.6 copy-start
  3.7 52.7 %copy-start.1 = (s32[256]{0:T(256)S(1)}, s32[256]{0:T(256)}, u32[]{:S(2)}) copy-start(s32[256]{0:T(256)} %param.5) | copy-start | bytes 3076
  3.8 7.7 %collective-permute-start = (bf16[256,512]{1,0:T(8,128)(2,1)S(1)}, bf16[256,512]{1,0:T(8,128)(2,1)S(1)}, u32[]{:S(2)}, u32[]{:S(2)}) collective-permute-start(bf16[256,512]{1,0:T(8,128)(2,1)S(1)} %divide_convert_fusion), channel_id=1, source_target_pairs={{0,16},{1,48},{2,18},{3,50},{4,20},{5,52},{6,22},{7,54},{8,24},{9,... | collective-permute-start | bytes 786440 | tf_op jit(solution)/shard_map/ppermute | solution.py:175
  11.4 5.9 %collective-permute-start.4 = (bf16[256,512]{1,0:T(8,128)(2,1)S(1)}, bf16[256,512]{1,0:T(8,128)(2,1)S(1)}, u32[]{:S(2)}, u32[]{:S(2)}) collective-permute-start(bf16[256,512]{1,0:T(8,128)(2,1)S(1)} %collective-permute-done), channel_id=1, source_target_pairs={{0,1},{1,0},{2,3},{3,2},{4,5},{5,4},{6,7},{7,6},{8,9},{9,8},{10,11... | collective-permute-start | bytes 786440 | tf_op jit(solution)/shard_map/ppermute | solution.py:179
  13.8 11.6 %collective-permute-start.1 = (bf16[256,512]{1,0:T(8,128)(2,1)S(1)}, bf16[256,512]{1,0:T(8,128)(2,1)S(1)}, u32[]{:S(2)}, u32[]{:S(2)}) collective-permute-start(bf16[256,512]{1,0:T(8,128)(2,1)S(1)} %collective-permute-done), channel_id=1, source_target_pairs={{0,64},{1,449},{64,128},{65,1},{128,192},{129,65},{192,256},{193,1... | collective-permute-start | bytes 786440 | tf_op jit(solution)/shard_map/ppermute | solution.py:184
  17.3 10.9 %collective-permute-start.5 = (bf16[256,512]{1,0:T(8,128)(2,1)S(1)}, bf16[256,512]{1,0:T(8,128)(2,1)S(1)}, u32[]{:S(2)}, u32[]{:S(2)}) collective-permute-start(bf16[256,512]{1,0:T(8,128)(2,1)S(1)} %collective-permute-done.4), channel_id=1, source_target_pairs={{0,64},{1,449},{64,128},{65,1},{128,192},{129,65},{192,256},{193,1... | collective-permute-start | bytes 786440 | tf_op jit(solution)/shard_map/ppermute | solution.py:189
  25.4 9.5 %collective-permute-start.6 = (bf16[256,512]{1,0:T(8,128)(2,1)S(1)}, bf16[256,512]{1,0:T(8,128)(2,1)S(1)}, u32[]{:S(2)}, u32[]{:S(2)}) collective-permute-start(bf16[256,512]{1,0:T(8,128)(2,1)S(1)} %collective-permute-done.1), channel_id=1, source_target_pairs={{0,64},{1,449},{64,128},{65,1},{128,192},{129,65},{192,256},{193,1... | collective-permute-start | bytes 786440 | tf_op jit(solution)/shard_map/ppermute | solution.py:184
  28.2 10.0 %collective-permute-start.7 = (bf16[256,512]{1,0:T(8,128)(2,1)S(1)}, bf16[256,512]{1,0:T(8,128)(2,1)S(1)}, u32[]{:S(2)}, u32[]{:S(2)}) collective-permute-start(bf16[256,512]{1,0:T(8,128)(2,1)S(1)} %collective-permute-done.5), channel_id=1, source_target_pairs={{0,64},{1,449},{64,128},{65,1},{128,192},{129,65},{192,256},{193,1... | collective-permute-start | bytes 786440 | tf_op jit(solution)/shard_map/ppermute | solution.py:189
  34.9 9.5 %collective-permute-start.8 = (bf16[256,512]{1,0:T(8,128)(2,1)S(1)}, bf16[256,512]{1,0:T(8,128)(2,1)S(1)}, u32[]{:S(2)}, u32[]{:S(2)}) collective-permute-start(bf16[256,512]{1,0:T(8,128)(2,1)S(1)} %collective-permute-done.6), channel_id=1, source_target_pairs={{0,64},{1,449},{64,128},{65,1},{128,192},{129,65},{192,256},{193,1... | collective-permute-start | bytes 786440 | tf_op jit(solution)/shard_map/ppermute | solution.py:184
  38.3 9.8 %collective-permute-start.9 = (bf16[256,512]{1,0:T(8,128)(2,1)S(1)}, bf16[256,512]{1,0:T(8,128)(2,1)S(1)}, u32[]{:S(2)}, u32[]{:S(2)}) collective-permute-start(bf16[256,512]{1,0:T(8,128)(2,1)S(1)} %collective-permute-done.7), channel_id=1, source_target_pairs={{0,64},{1,449},{64,128},{65,1},{128,192},{129,65},{192,256},{193,1... | collective-permute-start | bytes 786440 | tf_op jit(solution)/shard_map/ppermute | solution.py:189
  44.4 9.5 %collective-permute-start.10 = (bf16[256,512]{1,0:T(8,128)(2,1)S(1)}, bf16[256,512]{1,0:T(8,128)(2,1)S(1)}, u32[]{:S(2)}, u32[]{:S(2)}) collective-permute-start(bf16[256,512]{1,0:T(8,128)(2,1)S(1)} %collective-permute-done.8), channel_id=1, source_target_pairs={{0,64},{1,449},{64,128},{65,1},{128,192},{129,65},{192,256},{193,1... | collective-permute-start | bytes 786440 | tf_op jit(solution)/shard_map/ppermute | solution.py:184
  54.6 15.3 %collective-permute-start.11 = (bf16[2048,512]{1,0:T(8,128)(2,1)}, bf16[2048,512]{1,0:T(8,128)(2,1)}, u32[]{:S(2)}, u32[]{:S(2)}) collective-permute-start(bf16[2048,512]{1,0:T(8,128)(2,1)} %constant_dynamic-update-slice_fusion.mine_ref), channel_id=1, source_target_pairs={{0,1},{1,0},{2,3},{3,2},{4,5},{5,4},{6,7},{7,6},{8,9},{9,8},{10,11... | collective-permute-start | bytes 6291464 | tf_op jit(solution)/shard_map/ppermute | solution.py:204
  56.5 29.4 %collective-permute-start.12 = (bf16[256,2048]{1,0:T(8,128)(2,1)}, bf16[256,2048]{1,0:T(8,128)(2,1)S(1)}, u32[]{:S(2)}, u32[]{:S(2)}) collective-permute-start(bf16[256,2048]{1,0:T(8,128)(2,1)} %param.3), channel_id=1, source_target_pairs={{0,17},{1,49},{2,19},{3,51},{4,21},{5,53},{6,23},{7,55},{8,25},{9,... | collective-permute-start | bytes 3145736 | tf_op jit(solution)/shard_map/ppermute | solution.py:194
  59.3 18.7 %collective-permute-start.3 = (f32[2,256]{0,1:T(8,128)S(1)}, f32[2,256]{0,1:T(8,128)S(1)}, u32[]{:S(2)}, u32[]{:S(2)}) collective-permute-start(f32[2,256]{0,1:T(8,128)S(1)} %copy.11), channel_id=1, source_target_pairs={{0,16},{1,48},{2,18},{3,50},{4,20},{5,52},{6,22},{7,54},{8,24},{9,... | collective-permute-start | bytes 6152 | tf_op jit(solution)/shard_map/ppermute | solution.py:176
  61.5 25.8 %collective-permute-start.2 = (bf16[256,2048]{1,0:T(8,128)(2,1)}, bf16[256,2048]{1,0:T(8,128)(2,1)}, u32[]{:S(2)}, u32[]{:S(2)}) collective-permute-start(bf16[256,2048]{1,0:T(8,128)(2,1)} %param.3), channel_id=1, source_target_pairs={{0,16},{1,48},{2,18},{3,50},{4,20},{5,52},{6,22},{7,54},{8,24},{9,... | collective-permute-start | bytes 3145736 | tf_op jit(solution)/shard_map/ppermute | solution.py:194
  83.5 3.2 %collective-permute-start.13 = (bf16[256,256]{1,0:T(8,128)(2,1)S(1)}, bf16[256,256]{1,0:T(8,128)(2,1)S(1)}, u32[]{:S(2)}, u32[]{:S(2)}) collective-permute-start(bf16[256,256]{1,0:T(8,128)(2,1)S(1)} %get-tuple-element.12), channel_id=1, source_target_pairs={{0,1},{1,0},{2,3},{3,2},{4,5},{5,4},{6,7},{7,6},{8,9},{9,8},{10,11... | collective-permute-start | bytes 393224 | tf_op jit(solution)/shard_map/ppermute | solution.py:233

commit v4 on v3

--- a/solution.py
+++ b/solution.py
@@ -16,20 +16,21 @@
 OTHER_CORE = [(0, 1), (1, 0)]
 
 
-def moves(other_core):
+def moves(other_core, step):
     pairs = []
-    for place in itertools.product((0, 1), repeat=len(BITS)):
-        target = list(place)
-        xh, xl, core = place[3], place[4], place[8]
-        target[3], target[4], target[8] = core ^ xl, 1 - xl, xh ^ other_core
-        index = [sum(bit << (8 - k) for k, bit in enumerate(bits)) for bits in (place, target)]
-        pairs.append(tuple(index))
+    for y, xh, xl, z, core in itertools.product(range(Y), range(2), range(2), range(8), range(2)):
+        there = xh ^ other_core
+        y_there = (y + step * (1, -1)[there]) % Y
+        pairs.append((place(y, xh, xl, z, core), place(y_there, core ^ xl, 1 - xl, z, there)))
     return pairs
 
 
-TO_HOST, TO_SIBLING = moves(0), moves(1)
-
-
+def place(y, xh, xl, z, core):
+    return (((y * 2 + xh) * 2 + xl) * 8 + z) * 2 + core
+
+
+TO_HOST, TO_SIBLING = moves(0, 0), moves(1, 0)
+TO_NEXT_SAME, TO_NEXT_OTHER = moves(0, 1), moves(1, 1)
 ROUND = [(2 * y + c, 2 * ((y + (1, -1)[c]) % Y) + c) for y in range(Y) for c in range(2)]
 
 
@@ -172,34 +173,42 @@
     unit = (hidden / row_norm).astype(jnp.bfloat16)
     side = jnp.stack([partner.astype(jnp.float32), 1.0 / row_norm[:, 0]])
 
+    sign = jnp.where(core == 0, -1, 1)
+    same_core = lax.ppermute(unit, BITS, TO_NEXT_SAME)
+    other_core = lax.ppermute(unit, BITS, TO_NEXT_OTHER)
     own = lax.ppermute(unit, BITS, TO_HOST)
     side_here = lax.ppermute(side, BITS, TO_HOST)
-    sign = jnp.where(core == 0, -1, 1)
-    same_core = own
-    other_core = lax.ppermute(own, "c", OTHER_CORE)
+    later, unused = lax.optimization_barrier((features, same_core))
+    rows_here = lax.ppermute(later, BITS, TO_HOST)
+    later, unused = lax.optimization_barrier((features, other_core))
+    rows_beside = lax.ppermute(later, BITS, TO_SIBLING)
     pieces, places = [own], [y * 2 + core]
-    sends = []
     for distance in range(1, 5):
-        place = (y + sign * distance) % Y * 2
-        same_core = lax.ppermute(same_core, (*YBITS, "c"), ROUND)
+        place_there = (y + sign * distance) % Y * 2
+        if distance == 3:
+            same_core, side_here = lax.optimization_barrier((same_core, side_here))
+        if distance == 4:
+            same_core, rows_here = lax.optimization_barrier((same_core, rows_here))
+        if distance > 1:
+            same_core = lax.ppermute(same_core, (*YBITS, "c"), ROUND)
+        if distance == 4:
+            same_core, rows_beside = lax.optimization_barrier((same_core, rows_beside))
         pieces.append(same_core)
-        places.append(place + core)
+        places.append(place_there + core)
         if distance == 4:
             break
-        other_core = lax.ppermute(other_core, (*YBITS, "c"), ROUND)
+        if distance > 1:
+            other_core = lax.ppermute(other_core, (*YBITS, "c"), ROUND)
         pieces.append(other_core)
-        places.append(place + 1 - core)
-        if distance < 3:
-            later, unused = lax.optimization_barrier((features, same_core))
-            sends.append(lax.ppermute(later, BITS, (TO_HOST, TO_SIBLING)[distance - 1]))
+        places.append(place_there + 1 - core)
     sign, core_there = -sign, 1 - core
     places.append(y * 2 + core_there)
     for distance in range(1, 5):
-        place = (y + sign * distance) % Y * 2
-        places += [place + core_there, place + 1 - core_there][: 1 if distance == 4 else 2]
+        place_there = (y + sign * distance) % Y * 2
+        there = [place_there + core_there, place_there + 1 - core_there]
+        places += there[: 1 if distance == 4 else 2]
     mine = jnp.concatenate(pieces)
     starts = jnp.stack(places).astype(jnp.int32) * rows
-    rows_here, rows_beside = sends
 
     sibling = lax.ppermute(mine, "c", OTHER_CORE)
     lanes = pltpu.VMEM((4, 512, 128), jnp.float32)
@@ -238,17 +247,16 @@
         )
 
     partial = (contract(rows_here, kept) + contract(rows_beside, beside)).astype(jnp.bfloat16)
-    tiles = partial.reshape(4, 2, 2, 2, 4, 2, 8, 256)
-    tiles = tiles.transpose(1, 2, 3, 5, 0, 4, 6, 7).reshape(16, 16 * 8, 256)
+    tiles = partial.reshape(4, 2, 2, 2, 2, 2, 2, 8, 256)
+    tiles = tiles.transpose(1, 2, 3, 6, 0, 5, 4, 7, 8).reshape(16, 16 * 8, 256)
     received = lax.all_to_all(tiles, ("y0", "xh", "xl", "z0"), 0, 0)
-    near_sum = received.astype(jnp.float32).sum(0).reshape(4, 4 * 8, 256)
-    along_y_sum = lax.all_to_all(near_sum, ("y2", "y1"), 0, 0).sum(0).reshape(4, 8, 256)
-    fragment = lax.all_to_all(along_y_sum, ("z2", "z1"), 0, 0).sum(0).astype(jnp.bfloat16)
+    near_sum = received.astype(jnp.float32).sum(0).reshape(8, 2 * 8, 256)
+    part = lax.all_to_all(near_sum, ("y2", "y1", "z1"), 0, 0).sum(0).astype(jnp.bfloat16)
     spread = lax.all_to_all(
-        jnp.broadcast_to(fragment[None], (32, 8, 256)), ("xl", "z2", "z1", "z0", "c"), 0, 0
-    )
-    gradient = spread.reshape(16, 2, 8, 256).transpose(0, 2, 1, 3).reshape(128, width)
-    gradient = gradient.astype(jnp.float32)
+        jnp.broadcast_to(part[None], (32, 2 * 8, 256)), ("xl", "z2", "z1", "z0", "c"), 0, 0
+    )
+    spread = spread.reshape(2, 2, 4, 2, 2, 8, 256).astype(jnp.float32)
+    gradient = (spread[:, 0] + spread[:, 1]).transpose(0, 3, 1, 4, 2, 5).reshape(128, width)
     squares = jnp.sum(gradient * gradient)
     squares = lax.all_to_all(
         jnp.broadcast_to(squares, (16, 128)), ("y2", "y1", "y0", "xh"), 0, 0

time: 175 us -> 182 us (1.040)
  starting transfers between devices: 35.4 us -> 45.3 us
  waiting for transfers between devices: 23 us -> 18.2 us
  local copies, waits for them, and re-layouts: 8.44 us -> 13.2 us
  blocking collectives: 84.4 us -> 82 us
    ppermute x4 -> x3, waiting for transfers between devices: 17 us -> 1.7 us  [on_device(): same_core = lax.ppermute(same_core, (*YBITS, 'c'), ROUND)]
    ppermute x3 -> x4, waiting for transfers between devices: 0.01 us -> 11.5 us  [the longest x1 6.34 us: on_device(): same_core = lax.ppermute(unit, BITS, TO_NEXT_SAME)]
    ppermute x3 -> x4, starting transfers between devices: 8.79 us -> 16.5 us  [the longest x1 5.61 us: on_device(): rows_here = lax.ppermute(later, BITS, TO_HOST)]
    all_to_all x3 -> x2, blocking collectives: 46.2 us -> 39.1 us  [the longest x1 21 us: on_device(): lax.all_to_all(jnp.broadcast_to(part[None], (32, 2 * 8, 256)), ('xl', 'z2...]
    unnamed x11 -> x12, local copies, waits for them, and re-layouts: 6.7 us -> 11.3 us
    ppermute x1, waiting for transfers between devices: 4.28 us -> 0.01 us  [on_device(): own = lax.ppermute(unit, BITS, TO_HOST)]
    ppermute x1, waiting for transfers between devices: 0.01 us -> 4.06 us  [on_device(): side_here = lax.ppermute(side, BITS, TO_HOST)]
    ppermute x3 -> x2, starting transfers between devices: 7.39 us -> 10.4 us  [on_device(): other_core = lax.ppermute(other_core, (*YBITS, 'c'), ROUND)]
  transfers between devices with their start and end apart: 14 -> 13, of which waited for: 7 -> 5; matrix products, arithmetic and copies ran while one was open for 3% -> 5% of each run, Pallas kernels for 9% -> 3%
where the time goes in v4:
time: 182 us; the launch traced here: 181 us
  blocking collectives  82 us (45%)
  starting transfers between devices  45.3 us (25%)
  waiting for transfers between devices  18.2 us (10%)
  Pallas kernels  14.8 us (8%)
  local copies, waits for them, and re-layouts  13.2 us (7%)
  matrix products  4.24 us (2%)
  other arithmetic  2.36 us (1%)
    all_to_all x1, blocking collectives, on_device(): received = lax.all_to_all(tiles, ('y0', 'xh', 'xl', 'z0'), 0, 0)  24.2 us
    all_to_all x1, blocking collectives, on_device(): lax.all_to_all(jnp.broadcast_to(part[None], (32, 2 * 8, 256)), ('xl', 'z2...  21 us
    all_to_all x1, blocking collectives, on_device(): lax.all_to_all(near_sum, ('y2', 'y1', 'z1'), 0, 0).sum(0)  18.1 us
    all_to_all x1, blocking collectives, on_device(): lax.all_to_all(jnp.broadcast_to(squares, (16, 128)), ('y2', 'y1', 'y0', '...  15 us
    unnamed x12, local copies, waits for them, and re-layouts  11.3 us
    ppermute x2, starting transfers between devices, on_device(): other_core = lax.ppermute(other_core, (*YBITS, 'c'), ROUND)  10.4 us
    ppermute x3, starting transfers between devices, on_device(): same_core = lax.ppermute(same_core, (*YBITS, 'c'), ROUND)  10.3 us
    ppermute x1, waiting for transfers between devices, on_device(): same_core = lax.ppermute(unit, BITS, TO_NEXT_SAME)  6.34 us
  transfers between devices with their start and end apart: 13, of which 5 were waited for; matrix products, arithmetic and copies ran while one was open for 5% of the time, Pallas kernels for 3%

profile of v4, /device:TPU:8, one launch (start us, length us, event | category | flops | bytes accessed | tf_op | source)
XLA Modules:
  0.0 181.2 jit_solution(4762844494728319999)
XLA Ops:
  0.0 1.6 copy-done
  1.6 2.0 %multiply_reduce_fusion = (f32[256]{0:T(256)S(1)}, f32[256,512]{1,0:T(8,128)S(1)}) fusion(bf16[256,2048]{1,0:T(8,128)(2,1)} %param.3, bf16[2048,512]{1,0:T(8,128)(2,1)S(1)} %copy-done), kind=kOutput, calls=%fused_computation.4 | convolution fusion | flops 537132800 | bytes 3671040 | tf_op jit(solution)/shard_map/dot_general | solution.py:171
  4.5 4.4 %collective-permute-start = (bf16[256,512]{1,0:T(8,128)(2,1)}, bf16[256,512]{1,0:T(8,128)(2,1)}, u32[]{:S(2)}, u32[]{:S(2)}) collective-permute-start(bf16[256,512]{1,0:T(8,128)(2,1)} %divide_convert_fusion), channel_id=1, source_target_pairs={{0,80},{1,112},{2,82},{3,114},{4,84},{5,116},{6,86},{7,118},{8,88}... | collective-permute-start | bytes 786440 | tf_op jit(solution)/shard_map/ppermute | solution.py:177
  8.9 6.3 %collective-permute-done = bf16[256,512]{1,0:T(8,128)(2,1)} collective-permute-done((bf16[256,512]{1,0:T(8,128)(2,1)}, bf16[256,512]{1,0:T(8,128)(2,1)}, u32[]{:S(2)}, u32[]{:S(2)}) %collective-permute-start) | collective-permute-done | bytes 262176 | tf_op jit(solution)/shard_map/ppermute | solution.py:177
  15.2 5.6 %collective-permute-start.4 = (bf16[256,2048]{1,0:T(8,128)(2,1)}, bf16[256,2048]{1,0:T(8,128)(2,1)}, u32[]{:S(2)}, u32[]{:S(2)}) collective-permute-start(bf16[256,2048]{1,0:T(8,128)(2,1)} %param.3), channel_id=1, source_target_pairs={{0,16},{1,48},{2,18},{3,50},{4,20},{5,52},{6,22},{7,54},{8,24},{9,... | collective-permute-start | bytes 3145736 | tf_op jit(solution)/shard_map/ppermute | solution.py:182
  20.8 4.6 %collective-permute-start.6 = (bf16[256,512]{1,0:T(8,128)(2,1)}, bf16[256,512]{1,0:T(8,128)(2,1)}, u32[]{:S(2)}, u32[]{:S(2)}) collective-permute-start(bf16[256,512]{1,0:T(8,128)(2,1)} %divide_convert_fusion), channel_id=1, source_target_pairs={{0,465},{1,497},{2,467},{3,499},{4,469},{5,501},{6,471},{7,503},{8... | collective-permute-start | bytes 786440 | tf_op jit(solution)/shard_map/ppermute | solution.py:178
  25.4 1.9 %collective-permute-start.5 = (bf16[256,512]{1,0:T(8,128)(2,1)}, bf16[256,512]{1,0:T(8,128)(2,1)}, u32[]{:S(2)}, u32[]{:S(2)}) collective-permute-start(bf16[256,512]{1,0:T(8,128)(2,1)} %divide_convert_fusion), channel_id=1, source_target_pairs={{0,16},{1,48},{2,18},{3,50},{4,20},{5,52},{6,22},{7,54},{8,24},{9,... | collective-permute-start | bytes 786440 | tf_op jit(solution)/shard_map/ppermute | solution.py:179
  27.3 5.1 %collective-permute-done.6 = bf16[256,512]{1,0:T(8,128)(2,1)} collective-permute-done((bf16[256,512]{1,0:T(8,128)(2,1)}, bf16[256,512]{1,0:T(8,128)(2,1)}, u32[]{:S(2)}, u32[]{:S(2)}) %collective-permute-start.6) | collective-permute-done | bytes 262176 | tf_op jit(solution)/shard_map/ppermute | solution.py:178
  32.4 1.9 %collective-permute-start.10 = (bf16[256,2048]{1,0:T(8,128)(2,1)}, bf16[256,2048]{1,0:T(8,128)(2,1)S(1)}, u32[]{:S(2)}, u32[]{:S(2)}) collective-permute-start(bf16[256,2048]{1,0:T(8,128)(2,1)} %param.3), channel_id=1, source_target_pairs={{0,17},{1,49},{2,19},{3,51},{4,21},{5,53},{6,23},{7,55},{8,25},{9,... | collective-permute-start | bytes 3145736 | tf_op jit(solution)/shard_map/ppermute | solution.py:184
  34.3 3.3 %collective-permute-start.1 = (bf16[256,512]{1,0:T(8,128)(2,1)}, bf16[256,512]{1,0:T(8,128)(2,1)}, u32[]{:S(2)}, u32[]{:S(2)}) collective-permute-start(bf16[256,512]{1,0:T(8,128)(2,1)} %collective-permute-done), channel_id=1, source_target_pairs={{0,64},{1,449},{64,128},{65,1},{128,192},{129,65},{192,256},{193,1... | collective-permute-start | bytes 786440 | tf_op jit(solution)/shard_map/ppermute | solution.py:193
  37.8 2.0 %collective-permute-start.2 = (f32[2,256]{0,1:T(8,128)S(1)}, f32[2,256]{0,1:T(8,128)S(1)}, u32[]{:S(2)}, u32[]{:S(2)}) collective-permute-start(f32[2,256]{0,1:T(8,128)S(1)} %copy.17), channel_id=1, source_target_pairs={{0,16},{1,48},{2,18},{3,50},{4,20},{5,52},{6,22},{7,54},{8,24},{9,... | collective-permute-start | bytes 6152 | tf_op jit(solution)/shard_map/ppermute | solution.py:180
  39.8 6.0 %collective-permute-start.7 = (bf16[256,512]{1,0:T(8,128)(2,1)}, bf16[256,512]{1,0:T(8,128)(2,1)S(1)}, u32[]{:S(2)}, u32[]{:S(2)}) collective-permute-start(bf16[256,512]{1,0:T(8,128)(2,1)} %collective-permute-done.6), channel_id=1, source_target_pairs={{0,64},{1,449},{64,128},{65,1},{128,192},{129,65},{192,256},{193,1... | collective-permute-start | bytes 786440 | tf_op jit(solution)/shard_map/ppermute | solution.py:201
  45.8 1.7 constant_dynamic-update-slice_fusion.7
  47.5 4.1 %collective-permute-done.2 = f32[2,256]{0,1:T(8,128)S(1)} collective-permute-done((f32[2,256]{0,1:T(8,128)S(1)}, f32[2,256]{0,1:T(8,128)S(1)}, u32[]{:S(2)}, u32[]{:S(2)}) %collective-permute-start.2) | collective-permute-done | bytes 2080 | tf_op jit(solution)/shard_map/ppermute | solution.py:180
  51.6 2.1 %collective-permute-start.3 = (bf16[256,512]{1,0:T(8,128)(2,1)}, bf16[256,512]{1,0:T(8,128)(2,1)S(1)}, u32[]{:S(2)}, u32[]{:S(2)}) collective-permute-start(bf16[256,512]{1,0:T(8,128)(2,1)} %collective-permute-done.1), channel_id=1, source_target_pairs={{0,64},{1,449},{64,128},{65,1},{128,192},{129,65},{192,256},{193,1... | collective-permute-start | bytes 786440 | tf_op jit(solution)/shard_map/ppermute | solution.py:193
  53.7 1.7 constant_dynamic-update-slice_fusion.6
  55.4 1.7 constant_dynamic-update-slice_fusion.5
  57.1 4.5 %collective-permute-start.8 = (bf16[256,512]{1,0:T(8,128)(2,1)S(1)}, bf16[256,512]{1,0:T(8,128)(2,1)S(1)}, u32[]{:S(2)}, u32[]{:S(2)}) collective-permute-start(bf16[256,512]{1,0:T(8,128)(2,1)S(1)} %collective-permute-done.7), channel_id=1, source_target_pairs={{0,64},{1,449},{64,128},{65,1},{128,192},{129,65},{192,256},{193,1... | collective-permute-start | bytes 786440 | tf_op jit(solution)/shard_map/ppermute | solution.py:201
  61.6 1.7 constant_dynamic-update-slice_fusion.4
  63.3 4.9 %collective-permute-start.9 = (bf16[256,512]{1,0:T(8,128)(2,1)S(1)}, bf16[256,512]{1,0:T(8,128)(2,1)S(1)}, u32[]{:S(2)}, u32[]{:S(2)}) collective-permute-start(bf16[256,512]{1,0:T(8,128)(2,1)S(1)} %collective-permute-done.3), channel_id=1, source_target_pairs={{0,64},{1,449},{64,128},{65,1},{128,192},{129,65},{192,256},{193,1... | collective-permute-start | bytes 786440 | tf_op jit(solution)/shard_map/ppermute | solution.py:193
  70.4 1.7 collective-permute-done.9
  72.8 1.9 %collective-permute-start.11 = (bf16[2048,512]{1,0:T(8,128)(2,1)}, bf16[2048,512]{1,0:T(8,128)(2,1)}, u32[]{:S(2)}, u32[]{:S(2)}) collective-permute-start(bf16[2048,512]{1,0:T(8,128)(2,1)} %constant_dynamic-update-slice_fusion.mine_ref), channel_id=1, source_target_pairs={{0,1},{1,0},{2,3},{3,2},{4,5},{5,4},{6,7},{7,6},{8,9},{9,8},{10,11... | collective-permute-start | bytes 6291464 | tf_op jit(solution)/shard_map/ppermute | solution.py:213
  75.0 4.5 %same_parity_sums.1.same_ref = f32[4,1,512]{2,1,0:T(1,128)S(1)} custom-call(bf16[2048,512]{1,0:T(8,128)(2,1)} %constant_dynamic-update-slice_fusion.mine_ref), custom_call_target="tpu_custom_call" | custom-call | flops 3000000000 | bytes 2000000 | tf_op jit(solution)/shard_map/same_parity_sums/pallas_call | solution.py:216
  79.5 4.7 %cross_parity_sums.1 = f32[8,1,512]{2,1,0:T(1,128)S(1)} custom-call(s32[1]{0:T(128)} %bitcast.2.core_ref, bf16[2048,512]{1,0:T(8,128)(2,1)} %constant_dynamic-update-slice_fusion.mine_ref, bf16[2048,512]{1,0:T(8,128)(2,1)} %collective-permute-done.11.sibling_ref, f32[4,1,512]{2,1,0:T(1,128)S(1)} %same_parity_sums.1.same_ref), custom_call_target="tpu_custom_call" | custom-call | flops 2000000000 | bytes 2000000 | tf_op jit(solution)/shard_map/cross_parity_sums/pallas_call | solution.py:224
  84.2 3.7 %psum.7.sums_ref = f32[8,1,512]{2,1,0:T(1,128)S(1)} all-reduce(f32[8,1,512]{2,1,0:T(1,128)S(1)} %cross_parity_sums.1), channel_id=1, replica_groups=mesh['y2'=2,'y1'=2,'y0'=2,'xh'=2,'xl'=2,'z2'=2,'z1'=2,'z0'=2,'c'=2] {'c'}, use_global_device_ids=true, to_apply=%region_1.2 | all-reduce | flops 4096 | bytes 32768 | tf_op jit(solution)/shard_map/psum | solution.py:232
  88.0 5.5 %weights.1 = (bf16[256,256]{1,0:T(8,128)(2,1)S(1)}, bf16[256,256]{1,0:T(8,128)(2,1)S(1)}) custom-call(s32[1]{0:T(128)} %bitcast.2.core_ref, s32[16]{0:T(128)S(1)} %broadcast_multiply_fusion.start_ref, f32[256,2]{1,0:T(8,128)S(1)} %bitcast.41, f32[8,1,512]{2,1,0:T(1,128)S(1)} %psum.7.sums_ref, bf16[2048,512]{1,0:T(8,128)(2,1)} %constant_dynamic-update-slice_fusion.mine_ref, ...), custom_call_target="tpu_custom_call" | custom-call | flops 2000000000 | bytes 2000000 | tf_op jit(solution)/shard_map/weights/pallas_call | solution.py:234
  93.5 2.3 %collective-permute-start.12 = (bf16[256,256]{1,0:T(8,128)(2,1)S(1)}, bf16[256,256]{1,0:T(8,128)(2,1)S(1)}, u32[]{:S(2)}, u32[]{:S(2)}) collective-permute-start(bf16[256,256]{1,0:T(8,128)(2,1)S(1)} %get-tuple-element.24), channel_id=1, source_target_pairs={{0,1},{1,0},{2,3},{3,2},{4,5},{5,4},{6,7},{7,6},{8,9},{9,8},{10,11... | collective-permute-start | bytes 393224 | tf_op jit(solution)/shard_map/ppermute | solution.py:242
  97.2 1.7 fusion
  99.1 24.2 %all_to_all.24 = bf16[16,128,256]{2,1,0:T(8,128)(2,1)S(1)} all-to-all(bf16[16,128,256]{2,1,0:T(8,128)(2,1)S(1)} %bitcast.42), channel_id=1, replica_groups=mesh['y2'=2,'y1'=2,'y0'=2,'xh'=2,'xl'=2,'z2'=2,'z1'=2,'z0'=2,'c'=2] {'y0..., dimensions={0} | all-to-all | bytes 2097152 | tf_op jit(solution)/shard_map/all_to_all | solution.py:252
  123.5 18.1 %all_to_all.25 = f32[8,16,256]{2,1,0:T(8,128)S(1)} all-to-all(f32[8,16,256]{2,1,0:T(8,128)S(1)} %bitcast.46), channel_id=1, replica_groups=mesh['y2'=2,'y1'=2,'y0'=2,'xh'=2,'xl'=2,'z2'=2,'z1'=2,'z0'=2,'c'=2] {'y2..., dimensions={0} | all-to-all | bytes 262144 | tf_op jit(solution)/shard_map/all_to_all | solution.py:254
  141.6 21.0 %all_to_all.26 = bf16[32,16,256]{2,1,0:T(8,128)(2,1)S(1)} all-to-all(bf16[32,16,256]{2,1,0:T(8,128)(2,1)S(1)} %broadcast_in_dim.4), channel_id=1, replica_groups=mesh['y2'=2,'y1'=2,'y0'=2,'xh'=2,'xl'=2,'z2'=2,'z1'=2,'z0'=2,'c'=2] {'xl..., dimensions={0} | all-to-all | bytes 524288 | tf_op jit(solution)/shard_map/all_to_all | solution.py:255
  164.0 15.0 %all_to_all.27 = f32[16,1,128]{2,1,0:T(1,128)S(1)} all-to-all(f32[16,1,128]{2,1,0:T(1,128)S(1)} %broadcast_in_dim.5), channel_id=1, replica_groups=mesh['y2'=2,'y1'=2,'y0'=2,'xh'=2,'xl'=2,'z2'=2,'z1'=2,'z0'=2,'c'=2] {'y2..., dimensions={0} | all-to-all | bytes 16384 | tf_op jit(solution)/shard_map/all_to_all | solution.py:261
  (35 shorter events, 8.7 us)
Async XLA Ops:
  0.0 1.6 copy-start
  1.6 36.0 %copy-start.1 = (s32[256]{0:T(256)S(1)}, s32[256]{0:T(256)}, u32[]{:S(2)}) copy-start(s32[256]{0:T(256)} %param.5) | copy-start | bytes 3076
  4.5 10.8 %collective-permute-start = (bf16[256,512]{1,0:T(8,128)(2,1)}, bf16[256,512]{1,0:T(8,128)(2,1)}, u32[]{:S(2)}, u32[]{:S(2)}) collective-permute-start(bf16[256,512]{1,0:T(8,128)(2,1)} %divide_convert_fusion), channel_id=1, source_target_pairs={{0,80},{1,112},{2,82},{3,114},{4,84},{5,116},{6,86},{7,118},{8,88}... | collective-permute-start | bytes 786440 | tf_op jit(solution)/shard_map/ppermute | solution.py:177
  15.2 48.1 %collective-permute-start.4 = (bf16[256,2048]{1,0:T(8,128)(2,1)}, bf16[256,2048]{1,0:T(8,128)(2,1)}, u32[]{:S(2)}, u32[]{:S(2)}) collective-permute-start(bf16[256,2048]{1,0:T(8,128)(2,1)} %param.3), channel_id=1, source_target_pairs={{0,16},{1,48},{2,18},{3,50},{4,20},{5,52},{6,22},{7,54},{8,24},{9,... | collective-permute-start | bytes 3145736 | tf_op jit(solution)/shard_map/ppermute | solution.py:182
  20.8 11.6 %collective-permute-start.6 = (bf16[256,512]{1,0:T(8,128)(2,1)}, bf16[256,512]{1,0:T(8,128)(2,1)}, u32[]{:S(2)}, u32[]{:S(2)}) collective-permute-start(bf16[256,512]{1,0:T(8,128)(2,1)} %divide_convert_fusion), channel_id=1, source_target_pairs={{0,465},{1,497},{2,467},{3,499},{4,469},{5,501},{6,471},{7,503},{8... | collective-permute-start | bytes 786440 | tf_op jit(solution)/shard_map/ppermute | solution.py:178
  25.4 14.4 %collective-permute-start.5 = (bf16[256,512]{1,0:T(8,128)(2,1)}, bf16[256,512]{1,0:T(8,128)(2,1)}, u32[]{:S(2)}, u32[]{:S(2)}) collective-permute-start(bf16[256,512]{1,0:T(8,128)(2,1)} %divide_convert_fusion), channel_id=1, source_target_pairs={{0,16},{1,48},{2,18},{3,50},{4,20},{5,52},{6,22},{7,54},{8,24},{9,... | collective-permute-start | bytes 786440 | tf_op jit(solution)/shard_map/ppermute | solution.py:179
  32.4 37.9 %collective-permute-start.10 = (bf16[256,2048]{1,0:T(8,128)(2,1)}, bf16[256,2048]{1,0:T(8,128)(2,1)S(1)}, u32[]{:S(2)}, u32[]{:S(2)}) collective-permute-start(bf16[256,2048]{1,0:T(8,128)(2,1)} %param.3), channel_id=1, source_target_pairs={{0,17},{1,49},{2,19},{3,51},{4,21},{5,53},{6,23},{7,55},{8,25},{9,... | collective-permute-start | bytes 3145736 | tf_op jit(solution)/shard_map/ppermute | solution.py:184
  34.3 17.2 %collective-permute-start.1 = (bf16[256,512]{1,0:T(8,128)(2,1)}, bf16[256,512]{1,0:T(8,128)(2,1)}, u32[]{:S(2)}, u32[]{:S(2)}) collective-permute-start(bf16[256,512]{1,0:T(8,128)(2,1)} %collective-permute-done), channel_id=1, source_target_pairs={{0,64},{1,449},{64,128},{65,1},{128,192},{129,65},{192,256},{193,1... | collective-permute-start | bytes 786440 | tf_op jit(solution)/shard_map/ppermute | solution.py:193
  37.8 13.8 %collective-permute-start.2 = (f32[2,256]{0,1:T(8,128)S(1)}, f32[2,256]{0,1:T(8,128)S(1)}, u32[]{:S(2)}, u32[]{:S(2)}) collective-permute-start(f32[2,256]{0,1:T(8,128)S(1)} %copy.17), channel_id=1, source_target_pairs={{0,16},{1,48},{2,18},{3,50},{4,20},{5,52},{6,22},{7,54},{8,24},{9,... | collective-permute-start | bytes 6152 | tf_op jit(solution)/shard_map/ppermute | solution.py:180
  39.8 17.3 %collective-permute-start.7 = (bf16[256,512]{1,0:T(8,128)(2,1)}, bf16[256,512]{1,0:T(8,128)(2,1)S(1)}, u32[]{:S(2)}, u32[]{:S(2)}) collective-permute-start(bf16[256,512]{1,0:T(8,128)(2,1)} %collective-permute-done.6), channel_id=1, source_target_pairs={{0,64},{1,449},{64,128},{65,1},{128,192},{129,65},{192,256},{193,1... | collective-permute-start | bytes 786440 | tf_op jit(solution)/shard_map/ppermute | solution.py:201
  51.6 11.7 %collective-permute-start.3 = (bf16[256,512]{1,0:T(8,128)(2,1)}, bf16[256,512]{1,0:T(8,128)(2,1)S(1)}, u32[]{:S(2)}, u32[]{:S(2)}) collective-permute-start(bf16[256,512]{1,0:T(8,128)(2,1)} %collective-permute-done.1), channel_id=1, source_target_pairs={{0,64},{1,449},{64,128},{65,1},{128,192},{129,65},{192,256},{193,1... | collective-permute-start | bytes 786440 | tf_op jit(solution)/shard_map/ppermute | solution.py:193
  57.1 12.6 %collective-permute-start.8 = (bf16[256,512]{1,0:T(8,128)(2,1)S(1)}, bf16[256,512]{1,0:T(8,128)(2,1)S(1)}, u32[]{:S(2)}, u32[]{:S(2)}) collective-permute-start(bf16[256,512]{1,0:T(8,128)(2,1)S(1)} %collective-permute-done.7), channel_id=1, source_target_pairs={{0,64},{1,449},{64,128},{65,1},{128,192},{129,65},{192,256},{193,1... | collective-permute-start | bytes 786440 | tf_op jit(solution)/shard_map/ppermute | solution.py:201
  63.3 8.8 %collective-permute-start.9 = (bf16[256,512]{1,0:T(8,128)(2,1)S(1)}, bf16[256,512]{1,0:T(8,128)(2,1)S(1)}, u32[]{:S(2)}, u32[]{:S(2)}) collective-permute-start(bf16[256,512]{1,0:T(8,128)(2,1)S(1)} %collective-permute-done.3), channel_id=1, source_target_pairs={{0,64},{1,449},{64,128},{65,1},{128,192},{129,65},{192,256},{193,1... | collective-permute-start | bytes 786440 | tf_op jit(solution)/shard_map/ppermute | solution.py:193
  72.8 6.7 %collective-permute-start.11 = (bf16[2048,512]{1,0:T(8,128)(2,1)}, bf16[2048,512]{1,0:T(8,128)(2,1)}, u32[]{:S(2)}, u32[]{:S(2)}) collective-permute-start(bf16[2048,512]{1,0:T(8,128)(2,1)} %constant_dynamic-update-slice_fusion.mine_ref), channel_id=1, source_target_pairs={{0,1},{1,0},{2,3},{3,2},{4,5},{5,4},{6,7},{7,6},{8,9},{9,8},{10,11... | collective-permute-start | bytes 6291464 | tf_op jit(solution)/shard_map/ppermute | solution.py:213
  93.5 3.2 %collective-permute-start.12 = (bf16[256,256]{1,0:T(8,128)(2,1)S(1)}, bf16[256,256]{1,0:T(8,128)(2,1)S(1)}, u32[]{:S(2)}, u32[]{:S(2)}) collective-permute-start(bf16[256,256]{1,0:T(8,128)(2,1)S(1)} %get-tuple-element.24), channel_id=1, source_target_pairs={{0,1},{1,0},{2,3},{3,2},{4,5},{5,4},{6,7},{7,6},{8,9},{9,8},{10,11... | collective-permute-start | bytes 393224 | tf_op jit(solution)/shard_map/ppermute | solution.py:242

commit v5 on v4

--- a/solution.py
+++ b/solution.py
@@ -178,25 +178,21 @@
     other_core = lax.ppermute(unit, BITS, TO_NEXT_OTHER)
     own = lax.ppermute(unit, BITS, TO_HOST)
     side_here = lax.ppermute(side, BITS, TO_HOST)
-    later, unused = lax.optimization_barrier((features, same_core))
-    rows_here = lax.ppermute(later, BITS, TO_HOST)
-    later, unused = lax.optimization_barrier((features, other_core))
-    rows_beside = lax.ppermute(later, BITS, TO_SIBLING)
     pieces, places = [own], [y * 2 + core]
     for distance in range(1, 5):
         place_there = (y + sign * distance) % Y * 2
-        if distance == 3:
-            same_core, side_here = lax.optimization_barrier((same_core, side_here))
-        if distance == 4:
-            same_core, rows_here = lax.optimization_barrier((same_core, rows_here))
         if distance > 1:
             same_core = lax.ppermute(same_core, (*YBITS, "c"), ROUND)
         if distance == 4:
-            same_core, rows_beside = lax.optimization_barrier((same_core, rows_beside))
+            same_core, side_here = lax.optimization_barrier((same_core, side_here))
         pieces.append(same_core)
         places.append(place_there + core)
         if distance == 4:
             break
+        if distance == 3:
+            later, unused = lax.optimization_barrier((features, same_core))
+            rows_here = lax.ppermute(later, BITS, TO_HOST)
+            rows_beside = lax.ppermute(later, BITS, TO_SIBLING)
         if distance > 1:
             other_core = lax.ppermute(other_core, (*YBITS, "c"), ROUND)
         pieces.append(other_core)
@@ -247,16 +243,12 @@
         )
 
     partial = (contract(rows_here, kept) + contract(rows_beside, beside)).astype(jnp.bfloat16)
-    tiles = partial.reshape(4, 2, 2, 2, 2, 2, 2, 8, 256)
-    tiles = tiles.transpose(1, 2, 3, 6, 0, 5, 4, 7, 8).reshape(16, 16 * 8, 256)
-    received = lax.all_to_all(tiles, ("y0", "xh", "xl", "z0"), 0, 0)
-    near_sum = received.astype(jnp.float32).sum(0).reshape(8, 2 * 8, 256)
-    part = lax.all_to_all(near_sum, ("y2", "y1", "z1"), 0, 0).sum(0).astype(jnp.bfloat16)
-    spread = lax.all_to_all(
-        jnp.broadcast_to(part[None], (32, 2 * 8, 256)), ("xl", "z2", "z1", "z0", "c"), 0, 0
-    )
-    spread = spread.reshape(2, 2, 4, 2, 2, 8, 256).astype(jnp.float32)
-    gradient = (spread[:, 0] + spread[:, 1]).transpose(0, 3, 1, 4, 2, 5).reshape(128, width)
+    tiles = partial.reshape(channels // 8, 8, 2, 128).transpose(0, 2, 1, 3).reshape(512, 8, 128)
+    received = lax.all_to_all(tiles, BITS, 0, 0).reshape(256, 2, 8, 128)
+    fragment = received.astype(jnp.float32).sum(0).astype(jnp.bfloat16)
+    spread = lax.all_to_all(jnp.broadcast_to(fragment[None], (32, 2, 8, 128)), BITS[4:], 0, 0)
+    gradient = spread.reshape(16, 2, 2, 8, 128).transpose(0, 3, 2, 1, 4).reshape(128, width)
+    gradient = gradient.astype(jnp.float32)
     squares = jnp.sum(gradient * gradient)
     squares = lax.all_to_all(
         jnp.broadcast_to(squares, (16, 128)), ("y2", "y1", "y0", "xh"), 0, 0

time: 182 us -> 165 us (0.907)
  waiting for transfers between devices: 18.2 us -> 3.44 us
  blocking collectives: 82 us -> 85.4 us
  local copies, waits for them, and re-layouts: 13.2 us -> 9.94 us
    ppermute x2, starting transfers between devices: 10.4 us -> 3.96 us  [on_device(): other_core = lax.ppermute(other_core, (*YBITS, 'c'), ROUND)]
    ppermute x1, waiting for transfers between devices: 6.34 us -> 0.01 us  [on_device(): same_core = lax.ppermute(unit, BITS, TO_NEXT_SAME)]
    ppermute x1, waiting for transfers between devices: 5.11 us -> 0.01 us  [on_device(): other_core = lax.ppermute(unit, BITS, TO_NEXT_OTHER)]
    all_to_all x3 -> x2, blocking collectives: 63.3 us -> 67.9 us  [the longest x1 53.3 us: on_device(): received = lax.all_to_all(tiles, BITS, 0, 0).reshape(256, 2, 8, 128)]
    ppermute x1, waiting for transfers between devices: 4.06 us -> 0.01 us  [on_device(): side_here = lax.ppermute(side, BITS, TO_HOST)]
    ppermute x1, starting transfers between devices: 2.01 us -> 6.01 us  [on_device(): side_here = lax.ppermute(side, BITS, TO_HOST)]
    unnamed x12 -> x11, local copies, waits for them, and re-layouts: 11.3 us -> 7.6 us
    ppermute x1, starting transfers between devices: 1.92 us -> 5.4 us  [on_device(): own = lax.ppermute(unit, BITS, TO_HOST)]
  transfers between devices with their start and end apart: 13 -> 13, of which waited for: 5 -> 2; matrix products, arithmetic and copies ran while one was open for 5% -> 4% of each run, Pallas kernels for 3% -> 9%
where the time goes in v5:
time: 165 us; the launch traced here: 164 us
  blocking collectives  85.4 us (52%)
  starting transfers between devices  43.6 us (26%)
  Pallas kernels  14.8 us (9%)
  local copies, waits for them, and re-layouts  9.94 us (6%)
  matrix products  4.24 us (3%)
  waiting for transfers between devices  3.44 us (2%)
  other arithmetic  1.71 us (1%)
    all_to_all x1, blocking collectives, on_device(): received = lax.all_to_all(tiles, BITS, 0, 0).reshape(256, 2, 8, 128)  53.3 us
    all_to_all x1, blocking collectives, on_device(): lax.all_to_all(jnp.broadcast_to(fragment[None], (32, 2, 8, 128)), BITS[4:...  14.6 us
    all_to_all x1, blocking collectives, on_device(): lax.all_to_all(jnp.broadcast_to(squares, (16, 128)), ('y2', 'y1', 'y0', '...  13.7 us
    ppermute x3, starting transfers between devices, on_device(): same_core = lax.ppermute(same_core, (*YBITS, 'c'), ROUND)  11.9 us
    unnamed x11, local copies, waits for them, and re-layouts  7.6 us
    ppermute x1, starting transfers between devices, on_device(): side_here = lax.ppermute(side, BITS, TO_HOST)  6.01 us
    pallas_call x1, Pallas kernels, on_device(): kernel_call(weight_kernel, (piece, piece), [SMEM, SMEM, VMEM, VMEM, VMEM,...  5.56 us
    ppermute x1, starting transfers between devices, on_device(): own = lax.ppermute(unit, BITS, TO_HOST)  5.4 us
  transfers between devices with their start and end apart: 13, of which 2 were waited for; matrix products, arithmetic and copies ran while one was open for 4% of the time, Pallas kernels for 9%

profile of v5, /device:TPU:8, one launch (start us, length us, event | category | flops | bytes accessed | tf_op | source)
XLA Modules:
  0.0 164.3 jit_solution(15738493034649811078)
XLA Ops:
  0.0 1.6 copy-done
  1.6 2.0 %multiply_reduce_fusion = (f32[256]{0:T(256)S(1)}, f32[256,512]{1,0:T(8,128)S(1)}) fusion(bf16[256,2048]{1,0:T(8,128)(2,1)} %param.3, bf16[2048,512]{1,0:T(8,128)(2,1)S(1)} %copy-done), kind=kOutput, calls=%fused_computation.3 | convolution fusion | flops 537132800 | bytes 3671040 | tf_op jit(solution)/shard_map/dot_general | solution.py:171
  3.8 4.4 %collective-permute-start = (bf16[256,512]{1,0:T(8,128)(2,1)S(1)}, bf16[256,512]{1,0:T(8,128)(2,1)S(1)}, u32[]{:S(2)}, u32[]{:S(2)}) collective-permute-start(bf16[256,512]{1,0:T(8,128)(2,1)S(1)} %divide_convert_fusion), channel_id=1, source_target_pairs={{0,80},{1,112},{2,82},{3,114},{4,84},{5,116},{6,86},{7,118},{8,88}... | collective-permute-start | bytes 786440 | tf_op jit(solution)/shard_map/ppermute | solution.py:177
  8.2 2.0 %collective-permute-start.7 = (bf16[256,512]{1,0:T(8,128)(2,1)S(1)}, bf16[256,512]{1,0:T(8,128)(2,1)S(1)}, u32[]{:S(2)}, u32[]{:S(2)}) collective-permute-start(bf16[256,512]{1,0:T(8,128)(2,1)S(1)} %divide_convert_fusion), channel_id=1, source_target_pairs={{0,465},{1,497},{2,467},{3,499},{4,469},{5,501},{6,471},{7,503},{8... | collective-permute-start | bytes 786440 | tf_op jit(solution)/shard_map/ppermute | solution.py:178
  10.2 5.4 %collective-permute-start.6 = (bf16[256,512]{1,0:T(8,128)(2,1)S(1)}, bf16[256,512]{1,0:T(8,128)(2,1)}, u32[]{:S(2)}, u32[]{:S(2)}) collective-permute-start(bf16[256,512]{1,0:T(8,128)(2,1)S(1)} %divide_convert_fusion), channel_id=1, source_target_pairs={{0,16},{1,48},{2,18},{3,50},{4,20},{5,52},{6,22},{7,54},{8,24},{9,... | collective-permute-start | bytes 786440 | tf_op jit(solution)/shard_map/ppermute | solution.py:179
  15.6 2.0 %collective-permute-start.1 = (bf16[256,512]{1,0:T(8,128)(2,1)S(1)}, bf16[256,512]{1,0:T(8,128)(2,1)S(1)}, u32[]{:S(2)}, u32[]{:S(2)}) collective-permute-start(bf16[256,512]{1,0:T(8,128)(2,1)S(1)} %collective-permute-done), channel_id=1, source_target_pairs={{0,64},{1,449},{64,128},{65,1},{128,192},{129,65},{192,256},{193,1... | collective-permute-start | bytes 786440 | tf_op jit(solution)/shard_map/ppermute | solution.py:185
  17.9 6.0 %collective-permute-start.5 = (f32[2,256]{0,1:T(8,128)S(1)}, f32[2,256]{0,1:T(8,128)S(1)}, u32[]{:S(2)}, u32[]{:S(2)}) collective-permute-start(f32[2,256]{0,1:T(8,128)S(1)} %copy.13), channel_id=1, source_target_pairs={{0,16},{1,48},{2,18},{3,50},{4,20},{5,52},{6,22},{7,54},{8,24},{9,... | collective-permute-start | bytes 6152 | tf_op jit(solution)/shard_map/ppermute | solution.py:180
  23.9 2.1 %collective-permute-start.8 = (bf16[256,512]{1,0:T(8,128)(2,1)S(1)}, bf16[256,512]{1,0:T(8,128)(2,1)S(1)}, u32[]{:S(2)}, u32[]{:S(2)}) collective-permute-start(bf16[256,512]{1,0:T(8,128)(2,1)S(1)} %collective-permute-done.7), channel_id=1, source_target_pairs={{0,64},{1,449},{64,128},{65,1},{128,192},{129,65},{192,256},{193,1... | collective-permute-start | bytes 786440 | tf_op jit(solution)/shard_map/ppermute | solution.py:197
  26.0 1.7 %constant_dynamic-update-slice_fusion.7 = bf16[2048,512]{1,0:T(8,128)(2,1)} fusion(bf16[256,512]{1,0:T(8,128)(2,1)} %collective-permute-done.6), kind=kLoop, calls=%fused_computation.14 | loop fusion | bytes 524288
  27.7 5.7 %collective-permute-start.2 = (bf16[256,512]{1,0:T(8,128)(2,1)S(1)}, bf16[256,512]{1,0:T(8,128)(2,1)S(1)}, u32[]{:S(2)}, u32[]{:S(2)}) collective-permute-start(bf16[256,512]{1,0:T(8,128)(2,1)S(1)} %collective-permute-done.1), channel_id=1, source_target_pairs={{0,64},{1,449},{64,128},{65,1},{128,192},{129,65},{192,256},{193,1... | collective-permute-start | bytes 786440 | tf_op jit(solution)/shard_map/ppermute | solution.py:185
  33.3 0.7 constant_dynamic-update-slice_fusion.6
  34.1 0.7 constant_dynamic-update-slice_fusion.5
  34.8 1.9 %collective-permute-start.9 = (bf16[256,512]{1,0:T(8,128)(2,1)S(1)}, bf16[256,512]{1,0:T(8,128)(2,1)S(1)}, u32[]{:S(2)}, u32[]{:S(2)}) collective-permute-start(bf16[256,512]{1,0:T(8,128)(2,1)S(1)} %collective-permute-done.8), channel_id=1, source_target_pairs={{0,64},{1,449},{64,128},{65,1},{128,192},{129,65},{192,256},{193,1... | collective-permute-start | bytes 786440 | tf_op jit(solution)/shard_map/ppermute | solution.py:197
  36.7 0.7 constant_dynamic-update-slice_fusion.4
  37.4 4.1 %collective-permute-start.4 = (bf16[256,512]{1,0:T(8,128)(2,1)S(1)}, bf16[256,512]{1,0:T(8,128)(2,1)S(1)}, u32[]{:S(2)}, u32[]{:S(2)}) collective-permute-start(bf16[256,512]{1,0:T(8,128)(2,1)S(1)} %collective-permute-done.2), channel_id=1, source_target_pairs={{0,64},{1,449},{64,128},{65,1},{128,192},{129,65},{192,256},{193,1... | collective-permute-start | bytes 786440 | tf_op jit(solution)/shard_map/ppermute | solution.py:185
  42.3 0.7 constant_dynamic-update-slice_fusion.2
  43.7 2.4 %collective-permute-done.4 = bf16[256,512]{1,0:T(8,128)(2,1)S(1)} collective-permute-done((bf16[256,512]{1,0:T(8,128)(2,1)S(1)}, bf16[256,512]{1,0:T(8,128)(2,1)S(1)}, u32[]{:S(2)}, u32[]{:S(2)}) %collective-permute-start.4) | collective-permute-done | bytes 262176 | tf_op jit(solution)/shard_map/ppermute | solution.py:185
  46.2 0.7 constant_dynamic-update-slice_fusion.mine_ref
  46.9 1.9 %collective-permute-start.10 = (bf16[2048,512]{1,0:T(8,128)(2,1)}, bf16[2048,512]{1,0:T(8,128)(2,1)}, u32[]{:S(2)}, u32[]{:S(2)}) collective-permute-start(bf16[2048,512]{1,0:T(8,128)(2,1)} %constant_dynamic-update-slice_fusion.mine_ref), channel_id=1, source_target_pairs={{0,1},{1,0},{2,3},{3,2},{4,5},{5,4},{6,7},{7,6},{8,9},{9,8},{10,11... | collective-permute-start | bytes 6291464 | tf_op jit(solution)/shard_map/ppermute | solution.py:209
  48.8 3.5 %collective-permute-start.11 = (bf16[256,2048]{1,0:T(8,128)(2,1)}, bf16[256,2048]{1,0:T(8,128)(2,1)S(1)}, u32[]{:S(2)}, u32[]{:S(2)}) collective-permute-start(bf16[256,2048]{1,0:T(8,128)(2,1)} %param.3), channel_id=1, source_target_pairs={{0,17},{1,49},{2,19},{3,51},{4,21},{5,53},{6,23},{7,55},{8,25},{9,... | collective-permute-start | bytes 3145736 | tf_op jit(solution)/shard_map/ppermute | solution.py:195
  52.6 2.3 %collective-permute-start.3 = (bf16[256,2048]{1,0:T(8,128)(2,1)}, bf16[256,2048]{1,0:T(8,128)(2,1)}, u32[]{:S(2)}, u32[]{:S(2)}) collective-permute-start(bf16[256,2048]{1,0:T(8,128)(2,1)} %param.3), channel_id=1, source_target_pairs={{0,16},{1,48},{2,18},{3,50},{4,20},{5,52},{6,22},{7,54},{8,24},{9,... | collective-permute-start | bytes 3145736 | tf_op jit(solution)/shard_map/ppermute | solution.py:194
  54.9 4.5 %same_parity_sums.1.same_ref = f32[4,1,512]{2,1,0:T(1,128)S(1)} custom-call(bf16[2048,512]{1,0:T(8,128)(2,1)} %constant_dynamic-update-slice_fusion.mine_ref), custom_call_target="tpu_custom_call" | custom-call | flops 3000000000 | bytes 2000000 | tf_op jit(solution)/shard_map/same_parity_sums/pallas_call | solution.py:212
  59.5 4.7 %cross_parity_sums.1 = f32[8,1,512]{2,1,0:T(1,128)S(1)} custom-call(s32[1]{0:T(128)} %bitcast.core_ref, bf16[2048,512]{1,0:T(8,128)(2,1)} %constant_dynamic-update-slice_fusion.mine_ref, bf16[2048,512]{1,0:T(8,128)(2,1)} %collective-permute-done.10.sibling_ref, f32[4,1,512]{2,1,0:T(1,128)S(1)} %same_parity_sums.1.same_ref), custom_call_target="tpu_custom_call" | custom-call | flops 2000000000 | bytes 2000000 | tf_op jit(solution)/shard_map/cross_parity_sums/pallas_call | solution.py:220
  64.2 3.8 %psum.7.sums_ref = f32[8,1,512]{2,1,0:T(1,128)S(1)} all-reduce(f32[8,1,512]{2,1,0:T(1,128)S(1)} %cross_parity_sums.1), channel_id=1, replica_groups=mesh['y2'=2,'y1'=2,'y0'=2,'xh'=2,'xl'=2,'z2'=2,'z1'=2,'z0'=2,'c'=2] {'c'}, use_global_device_ids=true, to_apply=%region_1.2 | all-reduce | flops 4096 | bytes 32768 | tf_op jit(solution)/shard_map/psum | solution.py:228
  68.0 5.6 %weights.1 = (bf16[256,256]{1,0:T(8,128)(2,1)S(1)}, bf16[256,256]{1,0:T(8,128)(2,1)S(1)}) custom-call(s32[1]{0:T(128)} %bitcast.core_ref, s32[16]{0:T(128)S(1)} %broadcast_multiply_fusion.start_ref, f32[256,2]{1,0:T(8,128)S(1)} %bitcast.37, f32[8,1,512]{2,1,0:T(1,128)S(1)} %psum.7.sums_ref, bf16[2048,512]{1,0:T(8,128)(2,1)} %constant_dynamic-update-slice_fusion.mine_ref, ...), custom_call_target="tpu_custom_call" | custom-call | flops 2000000000 | bytes 2000000 | tf_op jit(solution)/shard_map/weights/pallas_call | solution.py:230
  73.6 2.2 %collective-permute-start.12 = (bf16[256,256]{1,0:T(8,128)(2,1)S(1)}, bf16[256,256]{1,0:T(8,128)(2,1)S(1)}, u32[]{:S(2)}, u32[]{:S(2)}) collective-permute-start(bf16[256,256]{1,0:T(8,128)(2,1)S(1)} %get-tuple-element.14), channel_id=1, source_target_pairs={{0,1},{1,0},{2,3},{3,2},{4,5},{5,4},{6,7},{7,6},{8,9},{9,8},{10,11... | collective-permute-start | bytes 393224 | tf_op jit(solution)/shard_map/ppermute | solution.py:238
  75.8 1.0 collective-permute-done.12
  77.3 1.7 %fusion = bf16[2048,256]{1,0:T(8,128)(2,1)S(1)} fusion(f32[2048,256]{1,0:T(8,128)S(1)} %fusion.2, bf16[256,2048]{1,0:T(8,128)(2,1)} %collective-permute-done.3, bf16[256,256]{1,0:T(8,128)(2,1)S(1)} %get-tuple-element.13), kind=kOutput, calls=%fused_computation.1 | convolution fusion | flops 269484032 | bytes 4325376 | tf_op jit(solution)/shard_map/dot_general | solution.py:241
  79.1 53.3 %all_to_all.19 = bf16[512,8,128]{2,1,0:T(8,128)(2,1)S(1)} all-to-all(bf16[512,8,128]{2,1,0:T(8,128)(2,1)S(1)} %bitcast.39), channel_id=1, replica_groups=mesh['y2'=2,'y1'=2,'y0'=2,'xh'=2,'xl'=2,'z2'=2,'z1'=2,'z0'=2,'c'=2] {'y2..., dimensions={0} | all-to-all | bytes 2097152 | tf_op jit(solution)/shard_map/all_to_all | solution.py:247
  132.6 14.6 %all_to_all.20 = bf16[32,2,8,128]{3,2,1,0:T(8,128)(2,1)S(1)} all-to-all(bf16[32,2,8,128]{3,2,1,0:T(8,128)(2,1)S(1)} %broadcast_in_dim.4), channel_id=1, replica_groups=mesh['y2'=2,'y1'=2,'y0'=2,'xh'=2,'xl'=2,'z2'=2,'z1'=2,'z0'=2,'c'=2] {'xl..., dimensions={0} | all-to-all | bytes 262144 | tf_op jit(solution)/shard_map/all_to_all | solution.py:249
  148.6 13.7 %all_to_all.21 = f32[16,1,128]{2,1,0:T(1,128)S(1)} all-to-all(f32[16,1,128]{2,1,0:T(1,128)S(1)} %broadcast_in_dim.5), channel_id=1, replica_groups=mesh['y2'=2,'y1'=2,'y0'=2,'xh'=2,'xl'=2,'z2'=2,'z1'=2,'z0'=2,'c'=2] {'y2..., dimensions={0} | all-to-all | bytes 16384 | tf_op jit(solution)/shard_map/all_to_all | solution.py:253
  163.6 0.7 copy.15
  (30 shorter events, 4.5 us)
Async XLA Ops:
  0.0 1.6 copy-start
  1.6 16.1 %copy-start.1 = (s32[256]{0:T(256)S(1)}, s32[256]{0:T(256)}, u32[]{:S(2)}) copy-start(s32[256]{0:T(256)} %param.5) | copy-start | bytes 3076
  3.8 11.9 %collective-permute-start = (bf16[256,512]{1,0:T(8,128)(2,1)S(1)}, bf16[256,512]{1,0:T(8,128)(2,1)S(1)}, u32[]{:S(2)}, u32[]{:S(2)}) collective-permute-start(bf16[256,512]{1,0:T(8,128)(2,1)S(1)} %divide_convert_fusion), channel_id=1, source_target_pairs={{0,80},{1,112},{2,82},{3,114},{4,84},{5,116},{6,86},{7,118},{8,88}... | collective-permute-start | bytes 786440 | tf_op jit(solution)/shard_map/ppermute | solution.py:177
  8.2 15.7 %collective-permute-start.7 = (bf16[256,512]{1,0:T(8,128)(2,1)S(1)}, bf16[256,512]{1,0:T(8,128)(2,1)S(1)}, u32[]{:S(2)}, u32[]{:S(2)}) collective-permute-start(bf16[256,512]{1,0:T(8,128)(2,1)S(1)} %divide_convert_fusion), channel_id=1, source_target_pairs={{0,465},{1,497},{2,467},{3,499},{4,469},{5,501},{6,471},{7,503},{8... | collective-permute-start | bytes 786440 | tf_op jit(solution)/shard_map/ppermute | solution.py:178
  10.2 15.7 %collective-permute-start.6 = (bf16[256,512]{1,0:T(8,128)(2,1)S(1)}, bf16[256,512]{1,0:T(8,128)(2,1)}, u32[]{:S(2)}, u32[]{:S(2)}) collective-permute-start(bf16[256,512]{1,0:T(8,128)(2,1)S(1)} %divide_convert_fusion), channel_id=1, source_target_pairs={{0,16},{1,48},{2,18},{3,50},{4,20},{5,52},{6,22},{7,54},{8,24},{9,... | collective-permute-start | bytes 786440 | tf_op jit(solution)/shard_map/ppermute | solution.py:179
  15.6 12.0 %collective-permute-start.1 = (bf16[256,512]{1,0:T(8,128)(2,1)S(1)}, bf16[256,512]{1,0:T(8,128)(2,1)S(1)}, u32[]{:S(2)}, u32[]{:S(2)}) collective-permute-start(bf16[256,512]{1,0:T(8,128)(2,1)S(1)} %collective-permute-done), channel_id=1, source_target_pairs={{0,64},{1,449},{64,128},{65,1},{128,192},{129,65},{192,256},{193,1... | collective-permute-start | bytes 786440 | tf_op jit(solution)/shard_map/ppermute | solution.py:185
  17.9 25.9 %collective-permute-start.5 = (f32[2,256]{0,1:T(8,128)S(1)}, f32[2,256]{0,1:T(8,128)S(1)}, u32[]{:S(2)}, u32[]{:S(2)}) collective-permute-start(f32[2,256]{0,1:T(8,128)S(1)} %copy.13), channel_id=1, source_target_pairs={{0,16},{1,48},{2,18},{3,50},{4,20},{5,52},{6,22},{7,54},{8,24},{9,... | collective-permute-start | bytes 6152 | tf_op jit(solution)/shard_map/ppermute | solution.py:180
  23.9 10.9 %collective-permute-start.8 = (bf16[256,512]{1,0:T(8,128)(2,1)S(1)}, bf16[256,512]{1,0:T(8,128)(2,1)S(1)}, u32[]{:S(2)}, u32[]{:S(2)}) collective-permute-start(bf16[256,512]{1,0:T(8,128)(2,1)S(1)} %collective-permute-done.7), channel_id=1, source_target_pairs={{0,64},{1,449},{64,128},{65,1},{128,192},{129,65},{192,256},{193,1... | collective-permute-start | bytes 786440 | tf_op jit(solution)/shard_map/ppermute | solution.py:197
  27.7 9.8 %collective-permute-start.2 = (bf16[256,512]{1,0:T(8,128)(2,1)S(1)}, bf16[256,512]{1,0:T(8,128)(2,1)S(1)}, u32[]{:S(2)}, u32[]{:S(2)}) collective-permute-start(bf16[256,512]{1,0:T(8,128)(2,1)S(1)} %collective-permute-done.1), channel_id=1, source_target_pairs={{0,64},{1,449},{64,128},{65,1},{128,192},{129,65},{192,256},{193,1... | collective-permute-start | bytes 786440 | tf_op jit(solution)/shard_map/ppermute | solution.py:185
  34.8 8.3 %collective-permute-start.9 = (bf16[256,512]{1,0:T(8,128)(2,1)S(1)}, bf16[256,512]{1,0:T(8,128)(2,1)S(1)}, u32[]{:S(2)}, u32[]{:S(2)}) collective-permute-start(bf16[256,512]{1,0:T(8,128)(2,1)S(1)} %collective-permute-done.8), channel_id=1, source_target_pairs={{0,64},{1,449},{64,128},{65,1},{128,192},{129,65},{192,256},{193,1... | collective-permute-start | bytes 786440 | tf_op jit(solution)/shard_map/ppermute | solution.py:197
  37.4 8.7 %collective-permute-start.4 = (bf16[256,512]{1,0:T(8,128)(2,1)S(1)}, bf16[256,512]{1,0:T(8,128)(2,1)S(1)}, u32[]{:S(2)}, u32[]{:S(2)}) collective-permute-start(bf16[256,512]{1,0:T(8,128)(2,1)S(1)} %collective-permute-done.2), channel_id=1, source_target_pairs={{0,64},{1,449},{64,128},{65,1},{128,192},{129,65},{192,256},{193,1... | collective-permute-start | bytes 786440 | tf_op jit(solution)/shard_map/ppermute | solution.py:185
  46.9 12.5 %collective-permute-start.10 = (bf16[2048,512]{1,0:T(8,128)(2,1)}, bf16[2048,512]{1,0:T(8,128)(2,1)}, u32[]{:S(2)}, u32[]{:S(2)}) collective-permute-start(bf16[2048,512]{1,0:T(8,128)(2,1)} %constant_dynamic-update-slice_fusion.mine_ref), channel_id=1, source_target_pairs={{0,1},{1,0},{2,3},{3,2},{4,5},{5,4},{6,7},{7,6},{8,9},{9,8},{10,11... | collective-permute-start | bytes 6291464 | tf_op jit(solution)/shard_map/ppermute | solution.py:209
  48.8 27.0 %collective-permute-start.11 = (bf16[256,2048]{1,0:T(8,128)(2,1)}, bf16[256,2048]{1,0:T(8,128)(2,1)S(1)}, u32[]{:S(2)}, u32[]{:S(2)}) collective-permute-start(bf16[256,2048]{1,0:T(8,128)(2,1)} %param.3), channel_id=1, source_target_pairs={{0,17},{1,49},{2,19},{3,51},{4,21},{5,53},{6,23},{7,55},{8,25},{9,... | collective-permute-start | bytes 3145736 | tf_op jit(solution)/shard_map/ppermute | solution.py:195
  52.6 24.7 %collective-permute-start.3 = (bf16[256,2048]{1,0:T(8,128)(2,1)}, bf16[256,2048]{1,0:T(8,128)(2,1)}, u32[]{:S(2)}, u32[]{:S(2)}) collective-permute-start(bf16[256,2048]{1,0:T(8,128)(2,1)} %param.3), channel_id=1, source_target_pairs={{0,16},{1,48},{2,18},{3,50},{4,20},{5,52},{6,22},{7,54},{8,24},{9,... | collective-permute-start | bytes 3145736 | tf_op jit(solution)/shard_map/ppermute | solution.py:194
  73.6 3.2 %collective-permute-start.12 = (bf16[256,256]{1,0:T(8,128)(2,1)S(1)}, bf16[256,256]{1,0:T(8,128)(2,1)S(1)}, u32[]{:S(2)}, u32[]{:S(2)}) collective-permute-start(bf16[256,256]{1,0:T(8,128)(2,1)S(1)} %get-tuple-element.14), channel_id=1, source_target_pairs={{0,1},{1,0},{2,3},{3,2},{4,5},{5,4},{6,7},{7,6},{8,9},{9,8},{10,11... | collective-permute-start | bytes 393224 | tf_op jit(solution)/shard_map/ppermute | solution.py:238

commit v6 on v5

--- a/solution.py
+++ b/solution.py
@@ -243,11 +243,14 @@
         )
 
     partial = (contract(rows_here, kept) + contract(rows_beside, beside)).astype(jnp.bfloat16)
-    tiles = partial.reshape(channels // 8, 8, 2, 128).transpose(0, 2, 1, 3).reshape(512, 8, 128)
-    received = lax.all_to_all(tiles, BITS, 0, 0).reshape(256, 2, 8, 128)
+    tiles = partial.reshape(4, 2, 2, 2, 4, 2, 8, 256)
+    tiles = tiles.transpose(1, 3, 5, 0, 2, 4, 6, 7).reshape(8, 32 * 8, 256)
+    received = lax.all_to_all(tiles, ("y0", "xl", "z0"), 0, 0)
+    near_sum = received.astype(jnp.float32).sum(0).astype(jnp.bfloat16).reshape(32, 8, 256)
+    received = lax.all_to_all(near_sum, ("y2", "y1", "xh", "z2", "z1"), 0, 0)
     fragment = received.astype(jnp.float32).sum(0).astype(jnp.bfloat16)
-    spread = lax.all_to_all(jnp.broadcast_to(fragment[None], (32, 2, 8, 128)), BITS[4:], 0, 0)
-    gradient = spread.reshape(16, 2, 2, 8, 128).transpose(0, 3, 2, 1, 4).reshape(128, width)
+    spread = lax.all_to_all(jnp.broadcast_to(fragment[None], (32, 8, 256)), BITS[4:], 0, 0)
+    gradient = spread.reshape(16, 2, 8, 256).transpose(0, 2, 1, 3).reshape(128, width)
     gradient = gradient.astype(jnp.float32)
     squares = jnp.sum(gradient * gradient)
     squares = lax.all_to_all(

time: 165 us -> 161 us (0.976)
  blocking collectives: 85.4 us -> 81 us
    all_to_all x2 -> x3, blocking collectives: 67.9 us -> 65.1 us  [the longest x1 30.2 us: on_device(): received = lax.all_to_all(near_sum, ('y2', 'y1', 'xh', 'z2', 'z1'), 0, 0)]
where the time goes in v6:
time: 161 us; the launch traced here: 160 us
  blocking collectives  81 us (50%)
  starting transfers between devices  43.6 us (27%)
  Pallas kernels  14.8 us (9%)
  local copies, waits for them, and re-layouts  9.42 us (6%)
  matrix products  4.24 us (3%)
  waiting for transfers between devices  3.38 us (2%)
  other arithmetic  2.32 us (1%)
    all_to_all x1, blocking collectives, on_device(): received = lax.all_to_all(near_sum, ('y2', 'y1', 'xh', 'z2', 'z1'), 0, 0)  30.2 us
    all_to_all x1, blocking collectives, on_device(): received = lax.all_to_all(tiles, ('y0', 'xl', 'z0'), 0, 0)  21.5 us
    all_to_all x1, blocking collectives, on_device(): lax.all_to_all(jnp.broadcast_to(fragment[None], (32, 8, 256)), BITS[4:],...  13.4 us
    all_to_all x1, blocking collectives, on_device(): lax.all_to_all(jnp.broadcast_to(squares, (16, 128)), ('y2', 'y1', 'y0', '...  12.1 us
    ppermute x3, starting transfers between devices, on_device(): same_core = lax.ppermute(same_core, (*YBITS, 'c'), ROUND)  11.8 us
    unnamed x11, local copies, waits for them, and re-layouts  7.68 us
    ppermute x1, starting transfers between devices, on_device(): side_here = lax.ppermute(side, BITS, TO_HOST)  6.01 us
    pallas_call x1, Pallas kernels, on_device(): kernel_call(weight_kernel, (piece, piece), [SMEM, SMEM, VMEM, VMEM, VMEM,...  5.55 us
  transfers between devices with their start and end apart: 13, of which 2 were waited for; matrix products, arithmetic and copies ran while one was open for 4% of the time, Pallas kernels for 9%

profile of v6, /device:TPU:8, one launch (start us, length us, event | category | flops | bytes accessed | tf_op | source)
XLA Modules:
  0.0 159.9 jit_solution(16006497244991703951)
XLA Ops:
  0.0 1.6 copy-done
  1.6 2.0 %multiply_reduce_fusion = (f32[256]{0:T(256)S(1)}, f32[256,512]{1,0:T(8,128)S(1)}) fusion(bf16[256,2048]{1,0:T(8,128)(2,1)} %param.3, bf16[2048,512]{1,0:T(8,128)(2,1)S(1)} %copy-done), kind=kOutput, calls=%fused_computation.3 | convolution fusion | flops 537132800 | bytes 3671040 | tf_op jit(solution)/shard_map/dot_general | solution.py:171
  3.8 4.4 %collective-permute-start = (bf16[256,512]{1,0:T(8,128)(2,1)S(1)}, bf16[256,512]{1,0:T(8,128)(2,1)S(1)}, u32[]{:S(2)}, u32[]{:S(2)}) collective-permute-start(bf16[256,512]{1,0:T(8,128)(2,1)S(1)} %divide_convert_fusion), channel_id=1, source_target_pairs={{0,80},{1,112},{2,82},{3,114},{4,84},{5,116},{6,86},{7,118},{8,88}... | collective-permute-start | bytes 786440 | tf_op jit(solution)/shard_map/ppermute | solution.py:177
  8.2 2.0 %collective-permute-start.7 = (bf16[256,512]{1,0:T(8,128)(2,1)S(1)}, bf16[256,512]{1,0:T(8,128)(2,1)S(1)}, u32[]{:S(2)}, u32[]{:S(2)}) collective-permute-start(bf16[256,512]{1,0:T(8,128)(2,1)S(1)} %divide_convert_fusion), channel_id=1, source_target_pairs={{0,465},{1,497},{2,467},{3,499},{4,469},{5,501},{6,471},{7,503},{8... | collective-permute-start | bytes 786440 | tf_op jit(solution)/shard_map/ppermute | solution.py:178
  10.2 5.4 %collective-permute-start.6 = (bf16[256,512]{1,0:T(8,128)(2,1)S(1)}, bf16[256,512]{1,0:T(8,128)(2,1)}, u32[]{:S(2)}, u32[]{:S(2)}) collective-permute-start(bf16[256,512]{1,0:T(8,128)(2,1)S(1)} %divide_convert_fusion), channel_id=1, source_target_pairs={{0,16},{1,48},{2,18},{3,50},{4,20},{5,52},{6,22},{7,54},{8,24},{9,... | collective-permute-start | bytes 786440 | tf_op jit(solution)/shard_map/ppermute | solution.py:179
  15.6 2.0 %collective-permute-start.1 = (bf16[256,512]{1,0:T(8,128)(2,1)S(1)}, bf16[256,512]{1,0:T(8,128)(2,1)S(1)}, u32[]{:S(2)}, u32[]{:S(2)}) collective-permute-start(bf16[256,512]{1,0:T(8,128)(2,1)S(1)} %collective-permute-done), channel_id=1, source_target_pairs={{0,64},{1,449},{64,128},{65,1},{128,192},{129,65},{192,256},{193,1... | collective-permute-start | bytes 786440 | tf_op jit(solution)/shard_map/ppermute | solution.py:185
  17.9 6.0 %collective-permute-start.5 = (f32[2,256]{0,1:T(8,128)S(1)}, f32[2,256]{0,1:T(8,128)S(1)}, u32[]{:S(2)}, u32[]{:S(2)}) collective-permute-start(f32[2,256]{0,1:T(8,128)S(1)} %copy.11), channel_id=1, source_target_pairs={{0,16},{1,48},{2,18},{3,50},{4,20},{5,52},{6,22},{7,54},{8,24},{9,... | collective-permute-start | bytes 6152 | tf_op jit(solution)/shard_map/ppermute | solution.py:180
  23.9 2.1 %collective-permute-start.8 = (bf16[256,512]{1,0:T(8,128)(2,1)S(1)}, bf16[256,512]{1,0:T(8,128)(2,1)S(1)}, u32[]{:S(2)}, u32[]{:S(2)}) collective-permute-start(bf16[256,512]{1,0:T(8,128)(2,1)S(1)} %collective-permute-done.7), channel_id=1, source_target_pairs={{0,64},{1,449},{64,128},{65,1},{128,192},{129,65},{192,256},{193,1... | collective-permute-start | bytes 786440 | tf_op jit(solution)/shard_map/ppermute | solution.py:197
  26.0 1.7 %constant_dynamic-update-slice_fusion.7 = bf16[2048,512]{1,0:T(8,128)(2,1)} fusion(bf16[256,512]{1,0:T(8,128)(2,1)} %collective-permute-done.6), kind=kLoop, calls=%fused_computation.14 | loop fusion | bytes 524288
  27.7 5.7 %collective-permute-start.2 = (bf16[256,512]{1,0:T(8,128)(2,1)S(1)}, bf16[256,512]{1,0:T(8,128)(2,1)S(1)}, u32[]{:S(2)}, u32[]{:S(2)}) collective-permute-start(bf16[256,512]{1,0:T(8,128)(2,1)S(1)} %collective-permute-done.1), channel_id=1, source_target_pairs={{0,64},{1,449},{64,128},{65,1},{128,192},{129,65},{192,256},{193,1... | collective-permute-start | bytes 786440 | tf_op jit(solution)/shard_map/ppermute | solution.py:185
  33.4 0.7 constant_dynamic-update-slice_fusion.6
  34.1 0.7 constant_dynamic-update-slice_fusion.5
  34.8 1.9 %collective-permute-start.9 = (bf16[256,512]{1,0:T(8,128)(2,1)S(1)}, bf16[256,512]{1,0:T(8,128)(2,1)S(1)}, u32[]{:S(2)}, u32[]{:S(2)}) collective-permute-start(bf16[256,512]{1,0:T(8,128)(2,1)S(1)} %collective-permute-done.8), channel_id=1, source_target_pairs={{0,64},{1,449},{64,128},{65,1},{128,192},{129,65},{192,256},{193,1... | collective-permute-start | bytes 786440 | tf_op jit(solution)/shard_map/ppermute | solution.py:197
  36.7 0.7 constant_dynamic-update-slice_fusion.4
  37.5 4.1 %collective-permute-start.4 = (bf16[256,512]{1,0:T(8,128)(2,1)S(1)}, bf16[256,512]{1,0:T(8,128)(2,1)S(1)}, u32[]{:S(2)}, u32[]{:S(2)}) collective-permute-start(bf16[256,512]{1,0:T(8,128)(2,1)S(1)} %collective-permute-done.2), channel_id=1, source_target_pairs={{0,64},{1,449},{64,128},{65,1},{128,192},{129,65},{192,256},{193,1... | collective-permute-start | bytes 786440 | tf_op jit(solution)/shard_map/ppermute | solution.py:185
  41.6 0.7 constant_dynamic-update-slice_fusion.3
  43.8 2.4 %collective-permute-done.4 = bf16[256,512]{1,0:T(8,128)(2,1)S(1)} collective-permute-done((bf16[256,512]{1,0:T(8,128)(2,1)S(1)}, bf16[256,512]{1,0:T(8,128)(2,1)S(1)}, u32[]{:S(2)}, u32[]{:S(2)}) %collective-permute-start.4) | collective-permute-done | bytes 262176 | tf_op jit(solution)/shard_map/ppermute | solution.py:185
  46.9 1.9 %collective-permute-start.10 = (bf16[2048,512]{1,0:T(8,128)(2,1)}, bf16[2048,512]{1,0:T(8,128)(2,1)}, u32[]{:S(2)}, u32[]{:S(2)}) collective-permute-start(bf16[2048,512]{1,0:T(8,128)(2,1)} %constant_dynamic-update-slice_fusion.mine_ref), channel_id=1, source_target_pairs={{0,1},{1,0},{2,3},{3,2},{4,5},{5,4},{6,7},{7,6},{8,9},{9,8},{10,11... | collective-permute-start | bytes 6291464 | tf_op jit(solution)/shard_map/ppermute | solution.py:209
  48.8 3.5 %collective-permute-start.11 = (bf16[256,2048]{1,0:T(8,128)(2,1)}, bf16[256,2048]{1,0:T(8,128)(2,1)S(1)}, u32[]{:S(2)}, u32[]{:S(2)}) collective-permute-start(bf16[256,2048]{1,0:T(8,128)(2,1)} %param.3), channel_id=1, source_target_pairs={{0,17},{1,49},{2,19},{3,51},{4,21},{5,53},{6,23},{7,55},{8,25},{9,... | collective-permute-start | bytes 3145736 | tf_op jit(solution)/shard_map/ppermute | solution.py:195
  52.6 2.3 %collective-permute-start.3 = (bf16[256,2048]{1,0:T(8,128)(2,1)}, bf16[256,2048]{1,0:T(8,128)(2,1)}, u32[]{:S(2)}, u32[]{:S(2)}) collective-permute-start(bf16[256,2048]{1,0:T(8,128)(2,1)} %param.3), channel_id=1, source_target_pairs={{0,16},{1,48},{2,18},{3,50},{4,20},{5,52},{6,22},{7,54},{8,24},{9,... | collective-permute-start | bytes 3145736 | tf_op jit(solution)/shard_map/ppermute | solution.py:194
  54.9 4.5 %same_parity_sums.1.same_ref = f32[4,1,512]{2,1,0:T(1,128)S(1)} custom-call(bf16[2048,512]{1,0:T(8,128)(2,1)} %constant_dynamic-update-slice_fusion.mine_ref), custom_call_target="tpu_custom_call" | custom-call | flops 3000000000 | bytes 2000000 | tf_op jit(solution)/shard_map/same_parity_sums/pallas_call | solution.py:212
  59.5 4.7 %cross_parity_sums.1 = f32[8,1,512]{2,1,0:T(1,128)S(1)} custom-call(s32[1]{0:T(128)} %bitcast.core_ref, bf16[2048,512]{1,0:T(8,128)(2,1)} %constant_dynamic-update-slice_fusion.mine_ref, bf16[2048,512]{1,0:T(8,128)(2,1)} %collective-permute-done.10.sibling_ref, f32[4,1,512]{2,1,0:T(1,128)S(1)} %same_parity_sums.1.same_ref), custom_call_target="tpu_custom_call" | custom-call | flops 2000000000 | bytes 2000000 | tf_op jit(solution)/shard_map/cross_parity_sums/pallas_call | solution.py:220
  64.2 3.8 %psum.7.sums_ref = f32[8,1,512]{2,1,0:T(1,128)S(1)} all-reduce(f32[8,1,512]{2,1,0:T(1,128)S(1)} %cross_parity_sums.1), channel_id=1, replica_groups=mesh['y2'=2,'y1'=2,'y0'=2,'xh'=2,'xl'=2,'z2'=2,'z1'=2,'z0'=2,'c'=2] {'c'}, use_global_device_ids=true, to_apply=%region_1.2 | all-reduce | flops 4096 | bytes 32768 | tf_op jit(solution)/shard_map/psum | solution.py:228
  68.0 5.5 %weights.1 = (bf16[256,256]{1,0:T(8,128)(2,1)S(1)}, bf16[256,256]{1,0:T(8,128)(2,1)S(1)}) custom-call(s32[1]{0:T(128)} %bitcast.core_ref, s32[16]{0:T(128)S(1)} %broadcast_multiply_fusion.start_ref, f32[256,2]{1,0:T(8,128)S(1)} %bitcast.37, f32[8,1,512]{2,1,0:T(1,128)S(1)} %psum.7.sums_ref, bf16[2048,512]{1,0:T(8,128)(2,1)} %constant_dynamic-update-slice_fusion.mine_ref, ...), custom_call_target="tpu_custom_call" | custom-call | flops 2000000000 | bytes 2000000 | tf_op jit(solution)/shard_map/weights/pallas_call | solution.py:230
  73.6 2.3 %collective-permute-start.12 = (bf16[256,256]{1,0:T(8,128)(2,1)S(1)}, bf16[256,256]{1,0:T(8,128)(2,1)S(1)}, u32[]{:S(2)}, u32[]{:S(2)}) collective-permute-start(bf16[256,256]{1,0:T(8,128)(2,1)S(1)} %get-tuple-element.14), channel_id=1, source_target_pairs={{0,1},{1,0},{2,3},{3,2},{4,5},{5,4},{6,7},{7,6},{8,9},{9,8},{10,11... | collective-permute-start | bytes 393224 | tf_op jit(solution)/shard_map/ppermute | solution.py:238
  75.9 1.0 collective-permute-done.12
  77.3 1.7 %fusion = bf16[2048,256]{1,0:T(8,128)(2,1)S(1)} fusion(f32[2048,256]{1,0:T(8,128)S(1)} %fusion.2, bf16[256,2048]{1,0:T(8,128)(2,1)} %collective-permute-done.3, bf16[256,256]{1,0:T(8,128)(2,1)S(1)} %get-tuple-element.13), kind=kOutput, calls=%fused_computation.1 | convolution fusion | flops 269484032 | bytes 4325376 | tf_op jit(solution)/shard_map/dot_general | solution.py:241
  79.2 21.5 %all_to_all.24 = bf16[8,256,256]{2,1,0:T(8,128)(2,1)S(1)} all-to-all(bf16[8,256,256]{2,1,0:T(8,128)(2,1)S(1)} %bitcast.38), channel_id=1, replica_groups=mesh['y2'=2,'y1'=2,'y0'=2,'xh'=2,'xl'=2,'z2'=2,'z1'=2,'z0'=2,'c'=2] {'y0..., dimensions={0} | all-to-all | bytes 2097152 | tf_op jit(solution)/shard_map/all_to_all | solution.py:248
  100.8 30.2 %all_to_all.25 = bf16[32,8,256]{2,1,0:T(8,128)(2,1)S(1)} all-to-all(bf16[32,8,256]{2,1,0:T(8,128)(2,1)S(1)} %bitcast.40), channel_id=1, replica_groups=mesh['y2'=2,'y1'=2,'y0'=2,'xh'=2,'xl'=2,'z2'=2,'z1'=2,'z0'=2,'c'=2] {'y2..., dimensions={0} | all-to-all | bytes 262144 | tf_op jit(solution)/shard_map/all_to_all | solution.py:250
  131.0 13.4 %all_to_all.26 = bf16[32,8,256]{2,1,0:T(8,128)(2,1)S(1)} all-to-all(bf16[32,8,256]{2,1,0:T(8,128)(2,1)S(1)} %broadcast_in_dim.4), channel_id=1, replica_groups=mesh['y2'=2,'y1'=2,'y0'=2,'xh'=2,'xl'=2,'z2'=2,'z1'=2,'z0'=2,'c'=2] {'xl..., dimensions={0} | all-to-all | bytes 262144 | tf_op jit(solution)/shard_map/all_to_all | solution.py:252
  145.8 12.1 %all_to_all.27 = f32[16,1,128]{2,1,0:T(1,128)S(1)} all-to-all(f32[16,1,128]{2,1,0:T(1,128)S(1)} %broadcast_in_dim.5), channel_id=1, replica_groups=mesh['y2'=2,'y1'=2,'y0'=2,'xh'=2,'xl'=2,'z2'=2,'z1'=2,'z0'=2,'c'=2] {'y2..., dimensions={0} | all-to-all | bytes 16384 | tf_op jit(solution)/shard_map/all_to_all | solution.py:256
  159.2 0.7 convert_multiply_fusion
  (32 shorter events, 5.3 us)
Async XLA Ops:
  0.0 1.6 copy-start
  1.6 16.1 %copy-start.1 = (s32[256]{0:T(256)S(1)}, s32[256]{0:T(256)}, u32[]{:S(2)}) copy-start(s32[256]{0:T(256)} %param.5) | copy-start | bytes 3076
  3.8 11.9 %collective-permute-start = (bf16[256,512]{1,0:T(8,128)(2,1)S(1)}, bf16[256,512]{1,0:T(8,128)(2,1)S(1)}, u32[]{:S(2)}, u32[]{:S(2)}) collective-permute-start(bf16[256,512]{1,0:T(8,128)(2,1)S(1)} %divide_convert_fusion), channel_id=1, source_target_pairs={{0,80},{1,112},{2,82},{3,114},{4,84},{5,116},{6,86},{7,118},{8,88}... | collective-permute-start | bytes 786440 | tf_op jit(solution)/shard_map/ppermute | solution.py:177
  8.2 15.7 %collective-permute-start.7 = (bf16[256,512]{1,0:T(8,128)(2,1)S(1)}, bf16[256,512]{1,0:T(8,128)(2,1)S(1)}, u32[]{:S(2)}, u32[]{:S(2)}) collective-permute-start(bf16[256,512]{1,0:T(8,128)(2,1)S(1)} %divide_convert_fusion), channel_id=1, source_target_pairs={{0,465},{1,497},{2,467},{3,499},{4,469},{5,501},{6,471},{7,503},{8... | collective-permute-start | bytes 786440 | tf_op jit(solution)/shard_map/ppermute | solution.py:178
  10.2 15.7 %collective-permute-start.6 = (bf16[256,512]{1,0:T(8,128)(2,1)S(1)}, bf16[256,512]{1,0:T(8,128)(2,1)}, u32[]{:S(2)}, u32[]{:S(2)}) collective-permute-start(bf16[256,512]{1,0:T(8,128)(2,1)S(1)} %divide_convert_fusion), channel_id=1, source_target_pairs={{0,16},{1,48},{2,18},{3,50},{4,20},{5,52},{6,22},{7,54},{8,24},{9,... | collective-permute-start | bytes 786440 | tf_op jit(solution)/shard_map/ppermute | solution.py:179
  15.6 12.0 %collective-permute-start.1 = (bf16[256,512]{1,0:T(8,128)(2,1)S(1)}, bf16[256,512]{1,0:T(8,128)(2,1)S(1)}, u32[]{:S(2)}, u32[]{:S(2)}) collective-permute-start(bf16[256,512]{1,0:T(8,128)(2,1)S(1)} %collective-permute-done), channel_id=1, source_target_pairs={{0,64},{1,449},{64,128},{65,1},{128,192},{129,65},{192,256},{193,1... | collective-permute-start | bytes 786440 | tf_op jit(solution)/shard_map/ppermute | solution.py:185
  17.9 25.9 %collective-permute-start.5 = (f32[2,256]{0,1:T(8,128)S(1)}, f32[2,256]{0,1:T(8,128)S(1)}, u32[]{:S(2)}, u32[]{:S(2)}) collective-permute-start(f32[2,256]{0,1:T(8,128)S(1)} %copy.11), channel_id=1, source_target_pairs={{0,16},{1,48},{2,18},{3,50},{4,20},{5,52},{6,22},{7,54},{8,24},{9,... | collective-permute-start | bytes 6152 | tf_op jit(solution)/shard_map/ppermute | solution.py:180
  23.9 10.9 %collective-permute-start.8 = (bf16[256,512]{1,0:T(8,128)(2,1)S(1)}, bf16[256,512]{1,0:T(8,128)(2,1)S(1)}, u32[]{:S(2)}, u32[]{:S(2)}) collective-permute-start(bf16[256,512]{1,0:T(8,128)(2,1)S(1)} %collective-permute-done.7), channel_id=1, source_target_pairs={{0,64},{1,449},{64,128},{65,1},{128,192},{129,65},{192,256},{193,1... | collective-permute-start | bytes 786440 | tf_op jit(solution)/shard_map/ppermute | solution.py:197
  27.7 9.8 %collective-permute-start.2 = (bf16[256,512]{1,0:T(8,128)(2,1)S(1)}, bf16[256,512]{1,0:T(8,128)(2,1)S(1)}, u32[]{:S(2)}, u32[]{:S(2)}) collective-permute-start(bf16[256,512]{1,0:T(8,128)(2,1)S(1)} %collective-permute-done.1), channel_id=1, source_target_pairs={{0,64},{1,449},{64,128},{65,1},{128,192},{129,65},{192,256},{193,1... | collective-permute-start | bytes 786440 | tf_op jit(solution)/shard_map/ppermute | solution.py:185
  34.8 8.3 %collective-permute-start.9 = (bf16[256,512]{1,0:T(8,128)(2,1)S(1)}, bf16[256,512]{1,0:T(8,128)(2,1)S(1)}, u32[]{:S(2)}, u32[]{:S(2)}) collective-permute-start(bf16[256,512]{1,0:T(8,128)(2,1)S(1)} %collective-permute-done.8), channel_id=1, source_target_pairs={{0,64},{1,449},{64,128},{65,1},{128,192},{129,65},{192,256},{193,1... | collective-permute-start | bytes 786440 | tf_op jit(solution)/shard_map/ppermute | solution.py:197
  37.5 8.7 %collective-permute-start.4 = (bf16[256,512]{1,0:T(8,128)(2,1)S(1)}, bf16[256,512]{1,0:T(8,128)(2,1)S(1)}, u32[]{:S(2)}, u32[]{:S(2)}) collective-permute-start(bf16[256,512]{1,0:T(8,128)(2,1)S(1)} %collective-permute-done.2), channel_id=1, source_target_pairs={{0,64},{1,449},{64,128},{65,1},{128,192},{129,65},{192,256},{193,1... | collective-permute-start | bytes 786440 | tf_op jit(solution)/shard_map/ppermute | solution.py:185
  46.9 12.6 %collective-permute-start.10 = (bf16[2048,512]{1,0:T(8,128)(2,1)}, bf16[2048,512]{1,0:T(8,128)(2,1)}, u32[]{:S(2)}, u32[]{:S(2)}) collective-permute-start(bf16[2048,512]{1,0:T(8,128)(2,1)} %constant_dynamic-update-slice_fusion.mine_ref), channel_id=1, source_target_pairs={{0,1},{1,0},{2,3},{3,2},{4,5},{5,4},{6,7},{7,6},{8,9},{9,8},{10,11... | collective-permute-start | bytes 6291464 | tf_op jit(solution)/shard_map/ppermute | solution.py:209
  48.8 27.0 %collective-permute-start.11 = (bf16[256,2048]{1,0:T(8,128)(2,1)}, bf16[256,2048]{1,0:T(8,128)(2,1)S(1)}, u32[]{:S(2)}, u32[]{:S(2)}) collective-permute-start(bf16[256,2048]{1,0:T(8,128)(2,1)} %param.3), channel_id=1, source_target_pairs={{0,17},{1,49},{2,19},{3,51},{4,21},{5,53},{6,23},{7,55},{8,25},{9,... | collective-permute-start | bytes 3145736 | tf_op jit(solution)/shard_map/ppermute | solution.py:195
  52.6 24.7 %collective-permute-start.3 = (bf16[256,2048]{1,0:T(8,128)(2,1)}, bf16[256,2048]{1,0:T(8,128)(2,1)}, u32[]{:S(2)}, u32[]{:S(2)}) collective-permute-start(bf16[256,2048]{1,0:T(8,128)(2,1)} %param.3), channel_id=1, source_target_pairs={{0,16},{1,48},{2,18},{3,50},{4,20},{5,52},{6,22},{7,54},{8,24},{9,... | collective-permute-start | bytes 3145736 | tf_op jit(solution)/shard_map/ppermute | solution.py:194
  73.6 3.2 %collective-permute-start.12 = (bf16[256,256]{1,0:T(8,128)(2,1)S(1)}, bf16[256,256]{1,0:T(8,128)(2,1)S(1)}, u32[]{:S(2)}, u32[]{:S(2)}) collective-permute-start(bf16[256,256]{1,0:T(8,128)(2,1)S(1)} %get-tuple-element.14), channel_id=1, source_target_pairs={{0,1},{1,0},{2,3},{3,2},{4,5},{5,4},{6,7},{7,6},{8,9},{9,8},{10,11... | collective-permute-start | bytes 393224 | tf_op jit(solution)/shard_map/ppermute | solution.py:238

commit v7 on v5

--- a/solution.py
+++ b/solution.py
@@ -49,22 +49,51 @@
     return sum(values[:, k : k + 128] for k in range(0, values.shape[1], 128))
 
 
-def same_block_kernel(mine_ref, sums_ref, per_lane, per_column):
-    blocks, wide = per_lane.shape[0], per_lane.shape[1]
+def row_totals(per_lane):
+    ones = jnp.ones((8, per_lane.shape[1]), jnp.float32)
+    totals = lax.dot_general(
+        ones,
+        per_lane,
+        (((1,), (1,)), ((), ())),
+        precision=lax.Precision.HIGHEST,
+        preferred_element_type=jnp.float32,
+    )
+    return totals[0:1, :]
+
+
+def without_self(values):
+    rows = lax.broadcasted_iota(jnp.int32, values.shape, 0)
+    columns = lax.broadcasted_iota(jnp.int32, values.shape, 1)
+    return jnp.where(rows == columns, 0.0, values)
+
+
+def early_sums_kernel(*refs):
+    pieces, (sums_ref, per_lane, per_column) = refs[:-3], refs[-3:]
+    rows = per_lane.shape[1]
     per_lane[...] = jnp.zeros_like(per_lane)
-    per_column[...] = jnp.zeros_like(per_column)
-    for i in range(blocks):
-        left = mine_ref[i * wide : (i + 1) * wide, :]
-        values = exponentials(left, left)
-        rows = lax.broadcasted_iota(jnp.int32, values.shape, 0)
-        columns = lax.broadcasted_iota(jnp.int32, values.shape, 1)
-        per_column[i] += over_rows(jnp.where(rows == columns, 0.0, values))
-        for j in range(i + 1, blocks):
-            values = exponentials(left, mine_ref[j * wide : (j + 1) * wide, :])
-            per_column[j] += over_rows(values)
+    for i, piece in enumerate(pieces):
+        left = piece[...]
+        own = over_rows(without_self(exponentials(left, left)))
+        per_column[i] = own if i == 0 else per_column[i] + own
+        for j in range(i + 1, len(pieces)):
+            values = exponentials(left, pieces[j][...])
+            column = over_rows(values)
+            per_column[j] = column if i == 0 else per_column[j] + column
             per_lane[i] += over_lane_groups(values)
-    for i in range(blocks):
-        sums_ref[i] = per_column[i].sum(0, keepdims=True) + per_lane[i].T.sum(0, keepdims=True)
+    for i in range(len(pieces)):
+        total = per_column[i].sum(0, keepdims=True) + row_totals(per_lane[i])
+        sums_ref[i // 2, :, i % 2 * rows : (i % 2 + 1) * rows] = total
+
+
+def late_sums_kernel(mine_ref, early_ref, sums_ref):
+    blocks, wide = sums_ref.shape[0], sums_ref.shape[2]
+    last = mine_ref[(blocks - 1) * wide :, :]
+    column = over_rows(without_self(exponentials(last, last)))
+    for i in range(blocks - 1):
+        values = exponentials(mine_ref[i * wide : (i + 1) * wide, :], last)
+        column += over_rows(values)
+        sums_ref[i] = early_ref[i] + row_totals(over_lane_groups(values))
+    sums_ref[blocks - 1] = column.sum(0, keepdims=True)
 
 
 def cross_block_kernel(core_ref, mine_ref, sibling_ref, same_ref, sums_ref, per_lane, per_column):
@@ -85,7 +114,7 @@
             sums_ref[k] = jnp.zeros_like(sums_ref[k])
             sums_ref[blocks + k] = per_column[k].sum(0, keepdims=True)
         for i in range(half):
-            sums_ref[first + i] = per_lane[i].T.sum(0, keepdims=True)
+            sums_ref[first + i] = row_totals(per_lane[i])
 
     @pl.when(core == 0)
     def _():
@@ -100,7 +129,7 @@
 
 
 def weight_kernel(
-    core_ref, start_ref, side_ref, sums_ref, mine_ref, sibling_ref, keep_ref, send_ref, total
+    core_ref, start_ref, side_ref, sums_ref, mine_ref, sibling_ref, keep_ref, send_ref, weights
 ):
     core = core_ref[0]
     wide = sums_ref.shape[2]
@@ -116,23 +145,19 @@
             which = core if part == 0 else 1 - core
             right = ref[k * wide : (k + 1) * wide, :]
             inverse = 1.0 / sums_ref[blocks * which + k]
-            values = exponentials(own, right) * (inverse_own + inverse)
+            values = exponentials(own, right)
             if part == 0 and k == 0:
-                row_ids = lax.broadcasted_iota(jnp.int32, values.shape, 0)
-                column_ids = lax.broadcasted_iota(jnp.int32, values.shape, 1)
-                values = jnp.where(row_ids == column_ids, 0.0, values)
+                values = without_self(values)
             first = start_ref[part * blocks * 2 + 2 * k]
             second = start_ref[part * blocks * 2 + 2 * k + 1]
             columns = lanes + jnp.where(lanes < rows, first, second - rows)
-            values = jnp.where(columns == partner, values - 2.0, values)
-            product = jnp.dot(
-                values.astype(jnp.bfloat16), right, preferred_element_type=jnp.float32
-            )
-            if part == 0 and k == 0:
-                total[...] = product
-            else:
-                total[...] += product
-    grad_unit = total[...] * (1.0 / softness_factor)
+            target = jnp.where(columns == partner, 1.0, 0.0)
+            place_here = slice(k * wide, (k + 1) * wide)
+            weights[part, :rows, place_here] = (values * inverse_own - target).astype(jnp.bfloat16)
+            weights[part, rows:, place_here] = (values * inverse - target).astype(jnp.bfloat16)
+    total = jnp.dot(weights[0], mine_ref[...], preferred_element_type=jnp.float32)
+    total += jnp.dot(weights[1], sibling_ref[...], preferred_element_type=jnp.float32)
+    grad_unit = (total[:rows] + total[rows:]) * (1.0 / softness_factor)
     unit = own.astype(jnp.float32)
     along = jnp.sum(unit * grad_unit, axis=1, keepdims=True)
     grad_hidden = ((grad_unit - unit * along) * side_ref[:, 1:2]).astype(jnp.bfloat16)
@@ -184,7 +209,15 @@
         if distance > 1:
             same_core = lax.ppermute(same_core, (*YBITS, "c"), ROUND)
         if distance == 4:
-            same_core, side_here = lax.optimization_barrier((same_core, side_here))
+            early = kernel_call(
+                early_sums_kernel,
+                jax.ShapeDtypeStruct((3, 1, 512), jnp.float32),
+                [VMEM] * 6,
+                [pltpu.VMEM((6, rows, 128), jnp.float32), pltpu.VMEM((6, 8, rows), jnp.float32)],
+                2_000_000_000,
+                "early_sums",
+            )(*pieces[:6])
+            same_core, side_here, early = lax.optimization_barrier((same_core, side_here, early))
         pieces.append(same_core)
         places.append(place_there + core)
         if distance == 4:
@@ -210,13 +243,13 @@
     lanes = pltpu.VMEM((4, 512, 128), jnp.float32)
     columns = pltpu.VMEM((4, 8, 512), jnp.float32)
     same = kernel_call(
-        same_block_kernel,
+        late_sums_kernel,
         jax.ShapeDtypeStruct((4, 1, 512), jnp.float32),
-        [VMEM],
-        [lanes, columns],
-        3_000_000_000,
-        "same_parity_sums",
-    )(mine)
+        [VMEM, VMEM],
+        [],
+        1_000_000_000,
+        "late_sums",
+    )(mine, early)
     sums = kernel_call(
         cross_block_kernel,
         jax.ShapeDtypeStruct((8, 1, 512), jnp.float32),
@@ -231,7 +264,7 @@
         weight_kernel,
         (piece, piece),
         [SMEM, SMEM, VMEM, VMEM, VMEM, VMEM],
-        [pltpu.VMEM((rows, width), jnp.float32)],
+        [pltpu.VMEM((2, 2 * rows, 8 * rows), jnp.bfloat16)],
         2_000_000_000,
         "weights",
     )(core_scalar, starts, side_here.T, sums, mine, sibling)
@@ -243,11 +276,16 @@
         )
 
     partial = (contract(rows_here, kept) + contract(rows_beside, beside)).astype(jnp.bfloat16)
-    tiles = partial.reshape(channels // 8, 8, 2, 128).transpose(0, 2, 1, 3).reshape(512, 8, 128)
-    received = lax.all_to_all(tiles, BITS, 0, 0).reshape(256, 2, 8, 128)
+    tiles = partial.reshape(4, 2, 2, 2, 4, 2, 8, 256)
+    tiles = tiles.transpose(5, 3, 1, 2, 4, 0, 6, 7).reshape(16, 16 * 8, 256)
+    received = lax.all_to_all(tiles, ("z0", "xl", "y0", "xh"), 0, 0)
+    near_sum = received.astype(jnp.float32).sum(0).astype(jnp.bfloat16).reshape(16, 8, 256)
+    received = lax.all_to_all(near_sum, ("z2", "z1", "y2", "y1"), 0, 0)
     fragment = received.astype(jnp.float32).sum(0).astype(jnp.bfloat16)
-    spread = lax.all_to_all(jnp.broadcast_to(fragment[None], (32, 2, 8, 128)), BITS[4:], 0, 0)
-    gradient = spread.reshape(16, 2, 2, 8, 128).transpose(0, 3, 2, 1, 4).reshape(128, width)
+    spread = lax.all_to_all(
+        jnp.broadcast_to(fragment[None], (32, 8, 256)), ("c", "xl", "z2", "z1", "z0"), 0, 0
+    )
+    gradient = spread.reshape(2, 16, 8, 256).transpose(1, 2, 0, 3).reshape(128, width)
     gradient = gradient.astype(jnp.float32)
     squares = jnp.sum(gradient * gradient)
     squares = lax.all_to_all(

time: 165 us -> 161 us (0.976)
  blocking collectives: 85.4 us -> 79.1 us
  Pallas kernels: 14.8 us -> 17 us
  waiting for transfers between devices: 3.44 us -> 1.72 us
    all_to_all x2 -> x3, blocking collectives: 67.9 us -> 61.9 us  [the longest x1 24.5 us: on_device(): received = lax.all_to_all(tiles, ('z0', 'xl', 'y0', 'xh'), 0, 0)]
    ppermute x3, waiting for transfers between devices: 2.44 us -> 0.56 us  [on_device(): same_core = lax.ppermute(same_core, (*YBITS, 'c'), ROUND)]
    pallas_call x1 -> x2, Pallas kernels: 4.54 us -> 6.07 us  [the longest x1 3.92 us: on_device(): kernel_call(late_sums_kernel, jax.ShapeDtypeStruct((4, 1, 512), jnp.float...]
    unnamed x11 -> x12, local copies, waits for them, and re-layouts: 7.6 us -> 7.45 us
  transfers between devices with their start and end apart: 13 -> 13, of which waited for: 2 -> 2; matrix products, arithmetic and copies ran while one was open for 4% -> 5% of each run, Pallas kernels for 9% -> 11%
where the time goes in v7:
time: 161 us; the launch traced here: 160 us
  blocking collectives  79.1 us (49%)
  starting transfers between devices  43.9 us (27%)
  Pallas kernels  17 us (11%)
  local copies, waits for them, and re-layouts  10.1 us (6%)
  matrix products  5.46 us (3%)
  waiting for transfers between devices  1.72 us (1%)
    all_to_all x1, blocking collectives, on_device(): received = lax.all_to_all(tiles, ('z0', 'xl', 'y0', 'xh'), 0, 0)  24.5 us
    all_to_all x1, blocking collectives, on_device(): received = lax.all_to_all(near_sum, ('z2', 'z1', 'y2', 'y1'), 0, 0)  24.3 us
    all_to_all x1, blocking collectives, on_device(): lax.all_to_all(jnp.broadcast_to(squares, (16, 128)), ('y2', 'y1', 'y0', '...  13.4 us
    all_to_all x1, blocking collectives, on_device(): lax.all_to_all(jnp.broadcast_to(fragment[None], (32, 8, 256)), ('c', 'xl'...  13.1 us
    ppermute x3, starting transfers between devices, on_device(): same_core = lax.ppermute(same_core, (*YBITS, 'c'), ROUND)  11.8 us
    unnamed x12, local copies, waits for them, and re-layouts  7.45 us
    ppermute x1, starting transfers between devices, on_device(): side_here = lax.ppermute(side, BITS, TO_HOST)  6 us
    pallas_call x1, Pallas kernels, on_device(): kernel_call(weight_kernel, (piece, piece), [SMEM, SMEM, VMEM, VMEM, VMEM,...  5.86 us
  transfers between devices with their start and end apart: 13, of which 2 were waited for; matrix products, arithmetic and copies ran while one was open for 5% of the time, Pallas kernels for 11%

profile of v7, /device:TPU:8, one launch (start us, length us, event | category | flops | bytes accessed | tf_op | source)
XLA Modules:
  0.0 159.9 jit_solution(5659528484436811716)
XLA Ops:
  0.0 1.6 copy-done
  1.6 2.0 %multiply_reduce_fusion = (f32[256]{0:T(256)S(1)}, f32[256,512]{1,0:T(8,128)S(1)}) fusion(bf16[256,2048]{1,0:T(8,128)(2,1)} %param.3, bf16[2048,512]{1,0:T(8,128)(2,1)S(1)} %copy-done), kind=kOutput, calls=%fused_computation.3 | convolution fusion | flops 537132800 | bytes 3671040 | tf_op jit(solution)/shard_map/dot_general | solution.py:196
  3.8 4.4 %collective-permute-start = (bf16[256,512]{1,0:T(8,128)(2,1)S(1)}, bf16[256,512]{1,0:T(8,128)(2,1)S(1)}, u32[]{:S(2)}, u32[]{:S(2)}) collective-permute-start(bf16[256,512]{1,0:T(8,128)(2,1)S(1)} %divide_convert_fusion), channel_id=1, source_target_pairs={{0,80},{1,112},{2,82},{3,114},{4,84},{5,116},{6,86},{7,118},{8,88}... | collective-permute-start | bytes 786440 | tf_op jit(solution)/shard_map/ppermute | solution.py:202
  8.2 2.0 %collective-permute-start.7 = (bf16[256,512]{1,0:T(8,128)(2,1)S(1)}, bf16[256,512]{1,0:T(8,128)(2,1)S(1)}, u32[]{:S(2)}, u32[]{:S(2)}) collective-permute-start(bf16[256,512]{1,0:T(8,128)(2,1)S(1)} %divide_convert_fusion), channel_id=1, source_target_pairs={{0,465},{1,497},{2,467},{3,499},{4,469},{5,501},{6,471},{7,503},{8... | collective-permute-start | bytes 786440 | tf_op jit(solution)/shard_map/ppermute | solution.py:203
  10.2 5.4 %collective-permute-start.6 = (bf16[256,512]{1,0:T(8,128)(2,1)S(1)}, bf16[256,512]{1,0:T(8,128)(2,1)S(1)}, u32[]{:S(2)}, u32[]{:S(2)}) collective-permute-start(bf16[256,512]{1,0:T(8,128)(2,1)S(1)} %divide_convert_fusion), channel_id=1, source_target_pairs={{0,16},{1,48},{2,18},{3,50},{4,20},{5,52},{6,22},{7,54},{8,24},{9,... | collective-permute-start | bytes 786440 | tf_op jit(solution)/shard_map/ppermute | solution.py:204
  15.7 2.0 %collective-permute-start.1 = (bf16[256,512]{1,0:T(8,128)(2,1)S(1)}, bf16[256,512]{1,0:T(8,128)(2,1)S(1)}, u32[]{:S(2)}, u32[]{:S(2)}) collective-permute-start(bf16[256,512]{1,0:T(8,128)(2,1)S(1)} %collective-permute-done.refs_1_), channel_id=1, source_target_pairs={{0,64},{1,449},{64,128},{65,1},{128,192},{129,65},{192,256},{193,1... | collective-permute-start | bytes 786440 | tf_op jit(solution)/shard_map/ppermute | solution.py:210
  17.7 0.8 copy.17
  18.5 6.0 %collective-permute-start.5 = (f32[2,256]{0,1:T(8,128)}, f32[2,256]{0,1:T(8,128)S(1)}, u32[]{:S(2)}, u32[]{:S(2)}) collective-permute-start(f32[2,256]{0,1:T(8,128)} %copy.17), channel_id=1, source_target_pairs={{0,16},{1,48},{2,18},{3,50},{4,20},{5,52},{6,22},{7,54},{8,24},{9,... | collective-permute-start | bytes 6152 | tf_op jit(solution)/shard_map/ppermute | solution.py:205
  24.5 2.1 %collective-permute-start.8 = (bf16[256,512]{1,0:T(8,128)(2,1)S(1)}, bf16[256,512]{1,0:T(8,128)(2,1)S(1)}, u32[]{:S(2)}, u32[]{:S(2)}) collective-permute-start(bf16[256,512]{1,0:T(8,128)(2,1)S(1)} %collective-permute-done.7.refs_2_), channel_id=1, source_target_pairs={{0,64},{1,449},{64,128},{65,1},{128,192},{129,65},{192,256},{193,1... | collective-permute-start | bytes 786440 | tf_op jit(solution)/shard_map/ppermute | solution.py:230
  26.6 0.8 constant_dynamic-update-slice_fusion.7
  27.4 0.7 constant_dynamic-update-slice_fusion.6
  28.1 5.7 %collective-permute-start.2 = (bf16[256,512]{1,0:T(8,128)(2,1)S(1)}, bf16[256,512]{1,0:T(8,128)(2,1)S(1)}, u32[]{:S(2)}, u32[]{:S(2)}) collective-permute-start(bf16[256,512]{1,0:T(8,128)(2,1)S(1)} %collective-permute-done.1.refs_3_), channel_id=1, source_target_pairs={{0,64},{1,449},{64,128},{65,1},{128,192},{129,65},{192,256},{193,1... | collective-permute-start | bytes 786440 | tf_op jit(solution)/shard_map/ppermute | solution.py:210
  34.5 1.9 %collective-permute-start.9 = (bf16[256,512]{1,0:T(8,128)(2,1)S(1)}, bf16[256,512]{1,0:T(8,128)(2,1)S(1)}, u32[]{:S(2)}, u32[]{:S(2)}) collective-permute-start(bf16[256,512]{1,0:T(8,128)(2,1)S(1)} %collective-permute-done.8.refs_4_), channel_id=1, source_target_pairs={{0,64},{1,449},{64,128},{65,1},{128,192},{129,65},{192,256},{193,1... | collective-permute-start | bytes 786440 | tf_op jit(solution)/shard_map/ppermute | solution.py:230
  36.4 0.7 constant_dynamic-update-slice_fusion.4
  37.2 0.7 constant_dynamic-update-slice_fusion.3
  37.9 4.1 %collective-permute-start.4 = (bf16[256,512]{1,0:T(8,128)(2,1)S(1)}, bf16[256,512]{1,0:T(8,128)(2,1)S(1)}, u32[]{:S(2)}, u32[]{:S(2)}) collective-permute-start(bf16[256,512]{1,0:T(8,128)(2,1)S(1)} %collective-permute-done.2.refs_5_), channel_id=1, source_target_pairs={{0,64},{1,449},{64,128},{65,1},{128,192},{129,65},{192,256},{193,1... | collective-permute-start | bytes 786440 | tf_op jit(solution)/shard_map/ppermute | solution.py:210
  42.0 2.2 %early_sums.1.early_ref = f32[3,1,512]{2,1,0:T(1,128)S(1)} custom-call(bf16[256,512]{1,0:T(8,128)(2,1)S(1)} %collective-permute-done.6.refs_0_, bf16[256,512]{1,0:T(8,128)(2,1)S(1)} %collective-permute-done.refs_1_, bf16[256,512]{1,0:T(8,128)(2,1)S(1)} %collective-permute-done.7.refs_2_, bf16[256,512]{1,0:T(8,128)(2,1)S(1)} %collective-permute-done.1.refs_3_, ...), custom_call_target="tpu_custom_call" | custom-call | flops 2000000000 | bytes 2000000 | tf_op jit(solution)/shard_map/early_sums/pallas_call | solution.py:212
  46.9 1.9 %collective-permute-start.10 = (bf16[2048,512]{1,0:T(8,128)(2,1)}, bf16[2048,512]{1,0:T(8,128)(2,1)}, u32[]{:S(2)}, u32[]{:S(2)}) collective-permute-start(bf16[2048,512]{1,0:T(8,128)(2,1)} %constant_dynamic-update-slice_fusion.mine_ref), channel_id=1, source_target_pairs={{0,1},{1,0},{2,3},{3,2},{4,5},{5,4},{6,7},{7,6},{8,9},{9,8},{10,11... | collective-permute-start | bytes 6291464 | tf_op jit(solution)/shard_map/ppermute | solution.py:242
  48.8 3.8 %collective-permute-start.11 = (bf16[256,2048]{1,0:T(8,128)(2,1)}, bf16[256,2048]{1,0:T(8,128)(2,1)}, u32[]{:S(2)}, u32[]{:S(2)}) collective-permute-start(bf16[256,2048]{1,0:T(8,128)(2,1)} %param.3), channel_id=1, source_target_pairs={{0,17},{1,49},{2,19},{3,51},{4,21},{5,53},{6,23},{7,55},{8,25},{9,... | collective-permute-start | bytes 3145736 | tf_op jit(solution)/shard_map/ppermute | solution.py:228
  52.9 2.4 %collective-permute-start.3 = (bf16[256,2048]{1,0:T(8,128)(2,1)}, bf16[256,2048]{1,0:T(8,128)(2,1)}, u32[]{:S(2)}, u32[]{:S(2)}) collective-permute-start(bf16[256,2048]{1,0:T(8,128)(2,1)} %param.3), channel_id=1, source_target_pairs={{0,16},{1,48},{2,18},{3,50},{4,20},{5,52},{6,22},{7,54},{8,24},{9,... | collective-permute-start | bytes 3145736 | tf_op jit(solution)/shard_map/ppermute | solution.py:227
  55.4 3.9 %late_sums.1.same_ref = f32[4,1,512]{2,1,0:T(1,128)S(1)} custom-call(bf16[2048,512]{1,0:T(8,128)(2,1)} %constant_dynamic-update-slice_fusion.mine_ref, f32[3,1,512]{2,1,0:T(1,128)S(1)} %early_sums.1.early_ref), custom_call_target="tpu_custom_call" | custom-call | flops 1000000000 | bytes 2000000 | tf_op jit(solution)/shard_map/late_sums/pallas_call | solution.py:245
  59.3 5.1 %cross_parity_sums.1 = f32[8,1,512]{2,1,0:T(1,128)S(1)} custom-call(s32[1]{0:T(128)} %bitcast.core_ref, bf16[2048,512]{1,0:T(8,128)(2,1)} %constant_dynamic-update-slice_fusion.mine_ref, bf16[2048,512]{1,0:T(8,128)(2,1)} %collective-permute-done.10.sibling_ref, f32[4,1,512]{2,1,0:T(1,128)S(1)} %late_sums.1.same_ref), custom_call_target="tpu_custom_call" | custom-call | flops 2000000000 | bytes 2000000 | tf_op jit(solution)/shard_map/cross_parity_sums/pallas_call | solution.py:253
  64.3 3.8 %psum.7.sums_ref = f32[8,1,512]{2,1,0:T(1,128)S(1)} all-reduce(f32[8,1,512]{2,1,0:T(1,128)S(1)} %cross_parity_sums.1), channel_id=1, replica_groups=mesh['y2'=2,'y1'=2,'y0'=2,'xh'=2,'xl'=2,'z2'=2,'z1'=2,'z0'=2,'c'=2] {'c'}, use_global_device_ids=true, to_apply=%region_1.2 | all-reduce | flops 4096 | bytes 32768 | tf_op jit(solution)/shard_map/psum | solution.py:261
  68.2 5.9 %weights.1 = (bf16[256,256]{1,0:T(8,128)(2,1)S(1)}, bf16[256,256]{1,0:T(8,128)(2,1)S(1)}) custom-call(s32[1]{0:T(128)} %bitcast.core_ref, s32[16]{0:T(128)S(1)} %broadcast_multiply_fusion.start_ref, f32[256,2]{1,0:T(8,128)S(1)} %bitcast.40, f32[8,1,512]{2,1,0:T(1,128)S(1)} %psum.7.sums_ref, bf16[2048,512]{1,0:T(8,128)(2,1)} %constant_dynamic-update-slice_fusion.mine_ref, ...), custom_call_target="tpu_custom_call" | custom-call | flops 2000000000 | bytes 2000000 | tf_op jit(solution)/shard_map/weights/pallas_call | solution.py:263
  74.0 2.1 %collective-permute-start.12 = (bf16[256,256]{1,0:T(8,128)(2,1)S(1)}, bf16[256,256]{1,0:T(8,128)(2,1)S(1)}, u32[]{:S(2)}, u32[]{:S(2)}) collective-permute-start(bf16[256,256]{1,0:T(8,128)(2,1)S(1)} %get-tuple-element.16), channel_id=1, source_target_pairs={{0,1},{1,0},{2,3},{3,2},{4,5},{5,4},{6,7},{7,6},{8,9},{9,8},{10,11... | collective-permute-start | bytes 393224 | tf_op jit(solution)/shard_map/ppermute | solution.py:271
  76.1 1.1 collective-permute-done.12
  77.3 1.7 %fusion.2 = f32[2048,256]{1,0:T(8,128)S(1)} fusion(bf16[256,2048]{1,0:T(8,128)(2,1)} %collective-permute-done.11, bf16[256,256]{1,0:T(8,128)(2,1)S(1)} %collective-permute-done.12), kind=kOutput, calls=%fused_computation.21 | convolution fusion | flops 268435456 | bytes 3276800 | tf_op jit(solution)/shard_map/dot_general | solution.py:274
  79.0 1.7 %fusion = bf16[2048,256]{1,0:T(8,128)(2,1)S(1)} fusion(f32[2048,256]{1,0:T(8,128)S(1)} %fusion.2, bf16[256,2048]{1,0:T(8,128)(2,1)} %collective-permute-done.3, bf16[256,256]{1,0:T(8,128)(2,1)S(1)} %get-tuple-element.15), kind=kOutput, calls=%fused_computation.1 | convolution fusion | flops 269484032 | bytes 4325376 | tf_op jit(solution)/shard_map/dot_general | solution.py:274
  80.9 24.5 %all_to_all.24 = bf16[16,128,256]{2,1,0:T(8,128)(2,1)S(1)} all-to-all(bf16[16,128,256]{2,1,0:T(8,128)(2,1)S(1)} %bitcast.41), channel_id=1, replica_groups=mesh['y2'=2,'y1'=2,'y0'=2,'xh'=2,'xl'=2,'z2'=2,'z1'=2,'z0'=2,'c'=2] {'z0..., dimensions={0} | all-to-all | bytes 2097152 | tf_op jit(solution)/shard_map/all_to_all | solution.py:281
  105.5 24.3 %all_to_all.25 = bf16[16,8,256]{2,1,0:T(8,128)(2,1)S(1)} all-to-all(bf16[16,8,256]{2,1,0:T(8,128)(2,1)S(1)} %bitcast.44), channel_id=1, replica_groups=mesh['y2'=2,'y1'=2,'y0'=2,'xh'=2,'xl'=2,'z2'=2,'z1'=2,'z0'=2,'c'=2] {'z2..., dimensions={0} | all-to-all | bytes 131072 | tf_op jit(solution)/shard_map/all_to_all | solution.py:283
  129.9 13.1 %all_to_all.26 = bf16[32,8,256]{2,1,0:T(8,128)(2,1)S(1)} all-to-all(bf16[32,8,256]{2,1,0:T(8,128)(2,1)S(1)} %broadcast_in_dim.4), channel_id=1, replica_groups=mesh['y2'=2,'y1'=2,'y0'=2,'xh'=2,'xl'=2,'z2'=2,'z1'=2,'z0'=2,'c'=2] {'c'..., dimensions={0} | all-to-all | bytes 262144 | tf_op jit(solution)/shard_map/all_to_all | solution.py:285
  144.3 13.4 %all_to_all.27 = f32[16,1,128]{2,1,0:T(1,128)S(1)} all-to-all(f32[16,1,128]{2,1,0:T(1,128)S(1)} %broadcast_in_dim.5), channel_id=1, replica_groups=mesh['y2'=2,'y1'=2,'y0'=2,'xh'=2,'xl'=2,'z2'=2,'z1'=2,'z0'=2,'c'=2] {'y2..., dimensions={0} | all-to-all | bytes 16384 | tf_op jit(solution)/shard_map/all_to_all | solution.py:291
  (35 shorter events, 6.9 us)
Async XLA Ops:
  0.0 1.6 copy-start
  1.6 14.0 %copy-start.1 = (s32[256]{0:T(256)S(1)}, s32[256]{0:T(256)}, u32[]{:S(2)}) copy-start(s32[256]{0:T(256)} %param.5) | copy-start | bytes 3076
  3.8 11.9 %collective-permute-start = (bf16[256,512]{1,0:T(8,128)(2,1)S(1)}, bf16[256,512]{1,0:T(8,128)(2,1)S(1)}, u32[]{:S(2)}, u32[]{:S(2)}) collective-permute-start(bf16[256,512]{1,0:T(8,128)(2,1)S(1)} %divide_convert_fusion), channel_id=1, source_target_pairs={{0,80},{1,112},{2,82},{3,114},{4,84},{5,116},{6,86},{7,118},{8,88}... | collective-permute-start | bytes 786440 | tf_op jit(solution)/shard_map/ppermute | solution.py:202
  8.2 16.3 %collective-permute-start.7 = (bf16[256,512]{1,0:T(8,128)(2,1)S(1)}, bf16[256,512]{1,0:T(8,128)(2,1)S(1)}, u32[]{:S(2)}, u32[]{:S(2)}) collective-permute-start(bf16[256,512]{1,0:T(8,128)(2,1)S(1)} %divide_convert_fusion), channel_id=1, source_target_pairs={{0,465},{1,497},{2,467},{3,499},{4,469},{5,501},{6,471},{7,503},{8... | collective-permute-start | bytes 786440 | tf_op jit(solution)/shard_map/ppermute | solution.py:203
  10.2 16.4 %collective-permute-start.6 = (bf16[256,512]{1,0:T(8,128)(2,1)S(1)}, bf16[256,512]{1,0:T(8,128)(2,1)S(1)}, u32[]{:S(2)}, u32[]{:S(2)}) collective-permute-start(bf16[256,512]{1,0:T(8,128)(2,1)S(1)} %divide_convert_fusion), channel_id=1, source_target_pairs={{0,16},{1,48},{2,18},{3,50},{4,20},{5,52},{6,22},{7,54},{8,24},{9,... | collective-permute-start | bytes 786440 | tf_op jit(solution)/shard_map/ppermute | solution.py:204
  15.7 12.4 %collective-permute-start.1 = (bf16[256,512]{1,0:T(8,128)(2,1)S(1)}, bf16[256,512]{1,0:T(8,128)(2,1)S(1)}, u32[]{:S(2)}, u32[]{:S(2)}) collective-permute-start(bf16[256,512]{1,0:T(8,128)(2,1)S(1)} %collective-permute-done.refs_1_), channel_id=1, source_target_pairs={{0,64},{1,449},{64,128},{65,1},{128,192},{129,65},{192,256},{193,1... | collective-permute-start | bytes 786440 | tf_op jit(solution)/shard_map/ppermute | solution.py:210
  18.5 27.1 %collective-permute-start.5 = (f32[2,256]{0,1:T(8,128)}, f32[2,256]{0,1:T(8,128)S(1)}, u32[]{:S(2)}, u32[]{:S(2)}) collective-permute-start(f32[2,256]{0,1:T(8,128)} %copy.17), channel_id=1, source_target_pairs={{0,16},{1,48},{2,18},{3,50},{4,20},{5,52},{6,22},{7,54},{8,24},{9,... | collective-permute-start | bytes 6152 | tf_op jit(solution)/shard_map/ppermute | solution.py:205
  24.5 10.0 %collective-permute-start.8 = (bf16[256,512]{1,0:T(8,128)(2,1)S(1)}, bf16[256,512]{1,0:T(8,128)(2,1)S(1)}, u32[]{:S(2)}, u32[]{:S(2)}) collective-permute-start(bf16[256,512]{1,0:T(8,128)(2,1)S(1)} %collective-permute-done.7.refs_2_), channel_id=1, source_target_pairs={{0,64},{1,449},{64,128},{65,1},{128,192},{129,65},{192,256},{193,1... | collective-permute-start | bytes 786440 | tf_op jit(solution)/shard_map/ppermute | solution.py:230
  28.1 9.8 %collective-permute-start.2 = (bf16[256,512]{1,0:T(8,128)(2,1)S(1)}, bf16[256,512]{1,0:T(8,128)(2,1)S(1)}, u32[]{:S(2)}, u32[]{:S(2)}) collective-permute-start(bf16[256,512]{1,0:T(8,128)(2,1)S(1)} %collective-permute-done.1.refs_3_), channel_id=1, source_target_pairs={{0,64},{1,449},{64,128},{65,1},{128,192},{129,65},{192,256},{193,1... | collective-permute-start | bytes 786440 | tf_op jit(solution)/shard_map/ppermute | solution.py:210
  34.5 10.4 %collective-permute-start.9 = (bf16[256,512]{1,0:T(8,128)(2,1)S(1)}, bf16[256,512]{1,0:T(8,128)(2,1)S(1)}, u32[]{:S(2)}, u32[]{:S(2)}) collective-permute-start(bf16[256,512]{1,0:T(8,128)(2,1)S(1)} %collective-permute-done.8.refs_4_), channel_id=1, source_target_pairs={{0,64},{1,449},{64,128},{65,1},{128,192},{129,65},{192,256},{193,1... | collective-permute-start | bytes 786440 | tf_op jit(solution)/shard_map/ppermute | solution.py:230
  37.9 8.3 %collective-permute-start.4 = (bf16[256,512]{1,0:T(8,128)(2,1)S(1)}, bf16[256,512]{1,0:T(8,128)(2,1)S(1)}, u32[]{:S(2)}, u32[]{:S(2)}) collective-permute-start(bf16[256,512]{1,0:T(8,128)(2,1)S(1)} %collective-permute-done.2.refs_5_), channel_id=1, source_target_pairs={{0,64},{1,449},{64,128},{65,1},{128,192},{129,65},{192,256},{193,1... | collective-permute-start | bytes 786440 | tf_op jit(solution)/shard_map/ppermute | solution.py:210
  46.9 12.4 %collective-permute-start.10 = (bf16[2048,512]{1,0:T(8,128)(2,1)}, bf16[2048,512]{1,0:T(8,128)(2,1)}, u32[]{:S(2)}, u32[]{:S(2)}) collective-permute-start(bf16[2048,512]{1,0:T(8,128)(2,1)} %constant_dynamic-update-slice_fusion.mine_ref), channel_id=1, source_target_pairs={{0,1},{1,0},{2,3},{3,2},{4,5},{5,4},{6,7},{7,6},{8,9},{9,8},{10,11... | collective-permute-start | bytes 6291464 | tf_op jit(solution)/shard_map/ppermute | solution.py:242
  48.8 27.3 %collective-permute-start.11 = (bf16[256,2048]{1,0:T(8,128)(2,1)}, bf16[256,2048]{1,0:T(8,128)(2,1)}, u32[]{:S(2)}, u32[]{:S(2)}) collective-permute-start(bf16[256,2048]{1,0:T(8,128)(2,1)} %param.3), channel_id=1, source_target_pairs={{0,17},{1,49},{2,19},{3,51},{4,21},{5,53},{6,23},{7,55},{8,25},{9,... | collective-permute-start | bytes 3145736 | tf_op jit(solution)/shard_map/ppermute | solution.py:228
  52.9 26.1 %collective-permute-start.3 = (bf16[256,2048]{1,0:T(8,128)(2,1)}, bf16[256,2048]{1,0:T(8,128)(2,1)}, u32[]{:S(2)}, u32[]{:S(2)}) collective-permute-start(bf16[256,2048]{1,0:T(8,128)(2,1)} %param.3), channel_id=1, source_target_pairs={{0,16},{1,48},{2,18},{3,50},{4,20},{5,52},{6,22},{7,54},{8,24},{9,... | collective-permute-start | bytes 3145736 | tf_op jit(solution)/shard_map/ppermute | solution.py:227
  74.0 3.2 %collective-permute-start.12 = (bf16[256,256]{1,0:T(8,128)(2,1)S(1)}, bf16[256,256]{1,0:T(8,128)(2,1)S(1)}, u32[]{:S(2)}, u32[]{:S(2)}) collective-permute-start(bf16[256,256]{1,0:T(8,128)(2,1)S(1)} %get-tuple-element.16), channel_id=1, source_target_pairs={{0,1},{1,0},{2,3},{3,2},{4,5},{5,4},{6,7},{7,6},{8,9},{9,8},{10,11... | collective-permute-start | bytes 393224 | tf_op jit(solution)/shard_map/ppermute | solution.py:271

commit v8 on v7

--- a/solution.py
+++ b/solution.py
@@ -85,56 +85,105 @@
         sums_ref[i // 2, :, i % 2 * rows : (i % 2 + 1) * rows] = total
 
 
-def late_sums_kernel(mine_ref, early_ref, sums_ref):
-    blocks, wide = sums_ref.shape[0], sums_ref.shape[2]
-    last = mine_ref[(blocks - 1) * wide :, :]
-    column = over_rows(without_self(exponentials(last, last)))
-    for i in range(blocks - 1):
-        values = exponentials(mine_ref[i * wide : (i + 1) * wide, :], last)
-        column += over_rows(values)
-        sums_ref[i] = early_ref[i] + row_totals(over_lane_groups(values))
-    sums_ref[blocks - 1] = column.sum(0, keepdims=True)
-
-
-def cross_block_kernel(core_ref, mine_ref, sibling_ref, same_ref, sums_ref, per_lane, per_column):
+def block_copies(source, target, semaphores, order, first):
+    rows = target.shape[0] // len(order)
+    copies = {}
+    for position, k in enumerate(order):
+        part = pl.ds(k * rows, rows)
+        copies[k] = pltpu.make_async_copy(
+            source.at[part], target.at[part], semaphores.at[first + position]
+        )
+        copies[k].start()
+    return copies
+
+
+def pair_sums_kernel(
+    core_ref, mine_hbm, sibling_hbm, early_ref, sums_ref, mine, sibling, per_lane, per_column, semaphores
+):
     core = core_ref[0]
     blocks, wide = per_column.shape[0], per_column.shape[2]
     half = blocks // 2
+    mine_copies = block_copies(mine_hbm, mine, semaphores, (3, 0, 1, 2), 0)
+    sibling_copies = block_copies(sibling_hbm, sibling, semaphores, (2, 3, 0, 1), blocks)
     per_lane[...] = jnp.zeros_like(per_lane)
     per_column[...] = jnp.zeros_like(per_column)
 
-    def pairs(left_ref, first, right_ref):
+    def block(ref, k):
+        return ref[k * wide : (k + 1) * wide, :]
+
+    mine_copies[blocks - 1].wait()
+    last = block(mine, blocks - 1)
+    column = over_rows(without_self(exponentials(last, last)))
+    same = []
+    for i in range(blocks - 1):
+        mine_copies[i].wait()
+        values = exponentials(block(mine, i), last)
+        column += over_rows(values)
+        same.append(early_ref[i] + row_totals(over_lane_groups(values)))
+    same.append(column.sum(0, keepdims=True))
+
+    def pairs(left_ref, first, right_ref, columns):
         for i in range(half):
-            left = left_ref[(first + i) * wide : (first + i + 1) * wide, :]
-            for j in range(blocks):
-                values = exponentials(left, right_ref[j * wide : (j + 1) * wide, :])
+            left = block(left_ref, first + i)
+            for j in columns:
+                values = exponentials(left, block(right_ref, j))
                 per_column[j] += over_rows(values)
                 per_lane[i] += over_lane_groups(values)
-        for k in range(blocks):
-            sums_ref[k] = jnp.zeros_like(sums_ref[k])
-            sums_ref[blocks + k] = per_column[k].sum(0, keepdims=True)
-        for i in range(half):
-            sums_ref[first + i] = row_totals(per_lane[i])
+
+    sibling_copies[2].wait()
+    sibling_copies[3].wait()
 
     @pl.when(core == 0)
     def _():
-        pairs(mine_ref, 0, sibling_ref)
+        pairs(mine, 0, sibling, (2, 3))
 
     @pl.when(core == 1)
     def _():
-        pairs(sibling_ref, half, mine_ref)
+        pairs(sibling, half, mine, (0, 1))
+
+    sibling_copies[0].wait()
+    sibling_copies[1].wait()
+
+    @pl.when(core == 0)
+    def _():
+        pairs(mine, 0, sibling, (0, 1))
+
+    @pl.when(core == 1)
+    def _():
+        pairs(sibling, half, mine, (2, 3))
 
     for k in range(blocks):
-        sums_ref[blocks * core + k] += same_ref[k]
+        sums_ref[k] = jnp.zeros_like(sums_ref[k])
+        sums_ref[blocks + k] = per_column[k].sum(0, keepdims=True)
+    for i in range(half):
+        sums_ref[half * core + i] = row_totals(per_lane[i])
+    for k in range(blocks):
+        sums_ref[blocks * core + k] += same[k]
 
 
 def weight_kernel(
-    core_ref, start_ref, side_ref, sums_ref, mine_ref, sibling_ref, keep_ref, send_ref, weights
+    core_ref,
+    start_ref,
+    side_ref,
+    sums_ref,
+    mine_hbm,
+    sibling_hbm,
+    keep_ref,
+    send_ref,
+    mine_ref,
+    sibling_ref,
+    weights,
+    semaphores,
 ):
     core = core_ref[0]
     wide = sums_ref.shape[2]
     blocks = sums_ref.shape[0] // 2
     rows = side_ref.shape[0]
+    copies = (
+        block_copies(mine_hbm, mine_ref, semaphores, range(blocks), 0),
+        block_copies(sibling_hbm, sibling_ref, semaphores, range(blocks), blocks),
+    )
+    copies[0][0].wait()
     own = mine_ref[:rows, :]
     mine_sums = sums_ref[blocks * core][:, :rows]
     inverse_own = 1.0 / jnp.broadcast_to(mine_sums, (128, rows)).T[:, :1]
@@ -143,6 +192,8 @@
     for part, ref in enumerate((mine_ref, sibling_ref)):
         for k in range(blocks):
             which = core if part == 0 else 1 - core
+            if part > 0 or k > 0:
+                copies[part][k].wait()
             right = ref[k * wide : (k + 1) * wide, :]
             inverse = 1.0 / sums_ref[blocks * which + k]
             values = exponentials(own, right)
@@ -169,6 +220,7 @@
 
 VMEM = pl.BlockSpec(memory_space=pltpu.VMEM)
 SMEM = pl.BlockSpec(memory_space=pltpu.SMEM)
+ANYWHERE = pl.BlockSpec(memory_space=pl.ANY)
 
 
 def kernel_call(body, outputs, in_specs, scratch, flops, name):
@@ -178,7 +230,7 @@
         in_specs=in_specs,
         out_specs=jax.tree.map(lambda unused: VMEM, outputs),
         scratch_shapes=scratch,
-        compiler_params=pltpu.CompilerParams(vmem_limit_bytes=40 * 1024 * 1024),
+        compiler_params=pltpu.CompilerParams(vmem_limit_bytes=24 * 1024 * 1024),
         cost_estimate=pl.CostEstimate(
             flops=flops, bytes_accessed=2_000_000, transcendentals=100_000
         ),
@@ -240,31 +292,28 @@
     starts = jnp.stack(places).astype(jnp.int32) * rows
 
     sibling = lax.ppermute(mine, "c", OTHER_CORE)
-    lanes = pltpu.VMEM((4, 512, 128), jnp.float32)
-    columns = pltpu.VMEM((4, 8, 512), jnp.float32)
-    same = kernel_call(
-        late_sums_kernel,
-        jax.ShapeDtypeStruct((4, 1, 512), jnp.float32),
-        [VMEM, VMEM],
-        [],
-        1_000_000_000,
-        "late_sums",
-    )(mine, early)
+    held = [pltpu.VMEM(mine.shape, jnp.bfloat16)] * 2
+    semaphores = pltpu.SemaphoreType.DMA((8,))
     sums = kernel_call(
-        cross_block_kernel,
+        pair_sums_kernel,
         jax.ShapeDtypeStruct((8, 1, 512), jnp.float32),
-        [SMEM, VMEM, VMEM, VMEM],
-        [lanes, columns],
-        2_000_000_000,
-        "cross_parity_sums",
-    )(core_scalar, mine, sibling, same)
+        [SMEM, ANYWHERE, ANYWHERE, VMEM],
+        held
+        + [
+            pltpu.VMEM((2, 512, 128), jnp.float32),
+            pltpu.VMEM((4, 8, 512), jnp.float32),
+            semaphores,
+        ],
+        3_000_000_000,
+        "pair_sums",
+    )(core_scalar, mine, sibling, early)
     sums = lax.psum(sums, "c")
     piece = jax.ShapeDtypeStruct((rows, width // 2), jnp.bfloat16)
     kept, sent = kernel_call(
         weight_kernel,
         (piece, piece),
-        [SMEM, SMEM, VMEM, VMEM, VMEM, VMEM],
-        [pltpu.VMEM((2, 2 * rows, 8 * rows), jnp.bfloat16)],
+        [SMEM, SMEM, VMEM, VMEM, ANYWHERE, ANYWHERE],
+        held + [pltpu.VMEM((2, 2 * rows, 8 * rows), jnp.bfloat16), semaphores],
         2_000_000_000,
         "weights",
     )(core_scalar, starts, side_here.T, sums, mine, sibling)

time: 161 us -> 160 us (level)
    pallas_call x3 -> x2, Pallas kernels: 14.8 us -> 14.2 us  [the longest x1 7.13 us: on_device(): kernel_call(pair_sums_kernel, jax.ShapeDtypeStruct((8, 1, 512), jnp.float...]
  transfers between devices with their start and end apart: 13 -> 13, of which waited for: 2 -> 2; matrix products, arithmetic and copies ran while one was open for 5% -> 5% of each run, Pallas kernels for 11% -> 10%
where the time goes in v8:
time: 160 us; the launch traced here: 159 us
  blocking collectives  79.1 us (49%)
  starting transfers between devices  43.9 us (27%)
  Pallas kernels  16.4 us (10%)
  local copies, waits for them, and re-layouts  10.1 us (6%)
  matrix products  5.46 us (3%)
  waiting for transfers between devices  1.72 us (1%)
  other arithmetic  1.6 us (1%)
    all_to_all x1, blocking collectives, on_device(): received = lax.all_to_all(tiles, ('z0', 'xl', 'y0', 'xh'), 0, 0)  24.5 us
    all_to_all x1, blocking collectives, on_device(): received = lax.all_to_all(near_sum, ('z2', 'z1', 'y2', 'y1'), 0, 0)  24.4 us
    all_to_all x1, blocking collectives, on_device(): lax.all_to_all(jnp.broadcast_to(squares, (16, 128)), ('y2', 'y1', 'y0', '...  13.4 us
    all_to_all x1, blocking collectives, on_device(): lax.all_to_all(jnp.broadcast_to(fragment[None], (32, 8, 256)), ('c', 'xl'...  13.1 us
    ppermute x3, starting transfers between devices, on_device(): same_core = lax.ppermute(same_core, (*YBITS, 'c'), ROUND)  11.8 us
    unnamed x12, local copies, waits for them, and re-layouts  7.45 us
    pallas_call x1, Pallas kernels, on_device(): kernel_call(pair_sums_kernel, jax.ShapeDtypeStruct((8, 1, 512), jnp.float...  7.13 us
    pallas_call x1, Pallas kernels, on_device(): kernel_call(weight_kernel, (piece, piece), [SMEM, SMEM, VMEM, VMEM, ANYWH...  7.11 us
  transfers between devices with their start and end apart: 13, of which 2 were waited for; matrix products, arithmetic and copies ran while one was open for 5% of the time, Pallas kernels for 10%

profile of v8, /device:TPU:8, one launch (start us, length us, event | category | flops | bytes accessed | tf_op | source)
XLA Modules:
  0.0 159.4 jit_solution(16088151106088454623)
XLA Ops:
  0.0 1.6 copy-done
  1.6 2.0 %multiply_reduce_fusion = (f32[256]{0:T(256)S(1)}, f32[256,512]{1,0:T(8,128)S(1)}) fusion(bf16[256,2048]{1,0:T(8,128)(2,1)} %param.3, bf16[2048,512]{1,0:T(8,128)(2,1)S(1)} %copy-done), kind=kOutput, calls=%fused_computation.3 | convolution fusion | flops 537132800 | bytes 3671040 | tf_op jit(solution)/shard_map/dot_general | solution.py:248
  3.8 4.4 %collective-permute-start = (bf16[256,512]{1,0:T(8,128)(2,1)S(1)}, bf16[256,512]{1,0:T(8,128)(2,1)S(1)}, u32[]{:S(2)}, u32[]{:S(2)}) collective-permute-start(bf16[256,512]{1,0:T(8,128)(2,1)S(1)} %divide_convert_fusion), channel_id=1, source_target_pairs={{0,80},{1,112},{2,82},{3,114},{4,84},{5,116},{6,86},{7,118},{8,88}... | collective-permute-start | bytes 786440 | tf_op jit(solution)/shard_map/ppermute | solution.py:254
  8.2 2.0 %collective-permute-start.7 = (bf16[256,512]{1,0:T(8,128)(2,1)S(1)}, bf16[256,512]{1,0:T(8,128)(2,1)S(1)}, u32[]{:S(2)}, u32[]{:S(2)}) collective-permute-start(bf16[256,512]{1,0:T(8,128)(2,1)S(1)} %divide_convert_fusion), channel_id=1, source_target_pairs={{0,465},{1,497},{2,467},{3,499},{4,469},{5,501},{6,471},{7,503},{8... | collective-permute-start | bytes 786440 | tf_op jit(solution)/shard_map/ppermute | solution.py:255
  10.2 5.4 %collective-permute-start.6 = (bf16[256,512]{1,0:T(8,128)(2,1)S(1)}, bf16[256,512]{1,0:T(8,128)(2,1)S(1)}, u32[]{:S(2)}, u32[]{:S(2)}) collective-permute-start(bf16[256,512]{1,0:T(8,128)(2,1)S(1)} %divide_convert_fusion), channel_id=1, source_target_pairs={{0,16},{1,48},{2,18},{3,50},{4,20},{5,52},{6,22},{7,54},{8,24},{9,... | collective-permute-start | bytes 786440 | tf_op jit(solution)/shard_map/ppermute | solution.py:256
  15.7 2.0 %collective-permute-start.1 = (bf16[256,512]{1,0:T(8,128)(2,1)S(1)}, bf16[256,512]{1,0:T(8,128)(2,1)S(1)}, u32[]{:S(2)}, u32[]{:S(2)}) collective-permute-start(bf16[256,512]{1,0:T(8,128)(2,1)S(1)} %collective-permute-done.refs_1_), channel_id=1, source_target_pairs={{0,64},{1,449},{64,128},{65,1},{128,192},{129,65},{192,256},{193,1... | collective-permute-start | bytes 786440 | tf_op jit(solution)/shard_map/ppermute | solution.py:262
  17.7 0.8 copy.17
  18.5 6.0 %collective-permute-start.5 = (f32[2,256]{0,1:T(8,128)}, f32[2,256]{0,1:T(8,128)S(1)}, u32[]{:S(2)}, u32[]{:S(2)}) collective-permute-start(f32[2,256]{0,1:T(8,128)} %copy.17), channel_id=1, source_target_pairs={{0,16},{1,48},{2,18},{3,50},{4,20},{5,52},{6,22},{7,54},{8,24},{9,... | collective-permute-start | bytes 6152 | tf_op jit(solution)/shard_map/ppermute | solution.py:257
  24.5 2.1 %collective-permute-start.8 = (bf16[256,512]{1,0:T(8,128)(2,1)S(1)}, bf16[256,512]{1,0:T(8,128)(2,1)S(1)}, u32[]{:S(2)}, u32[]{:S(2)}) collective-permute-start(bf16[256,512]{1,0:T(8,128)(2,1)S(1)} %collective-permute-done.7.refs_2_), channel_id=1, source_target_pairs={{0,64},{1,449},{64,128},{65,1},{128,192},{129,65},{192,256},{193,1... | collective-permute-start | bytes 786440 | tf_op jit(solution)/shard_map/ppermute | solution.py:282
  26.6 0.8 constant_dynamic-update-slice_fusion.7
  27.4 0.7 constant_dynamic-update-slice_fusion.6
  28.1 5.7 %collective-permute-start.2 = (bf16[256,512]{1,0:T(8,128)(2,1)S(1)}, bf16[256,512]{1,0:T(8,128)(2,1)S(1)}, u32[]{:S(2)}, u32[]{:S(2)}) collective-permute-start(bf16[256,512]{1,0:T(8,128)(2,1)S(1)} %collective-permute-done.1.refs_3_), channel_id=1, source_target_pairs={{0,64},{1,449},{64,128},{65,1},{128,192},{129,65},{192,256},{193,1... | collective-permute-start | bytes 786440 | tf_op jit(solution)/shard_map/ppermute | solution.py:262
  33.8 0.7 constant_dynamic-update-slice_fusion.5
  34.5 1.9 %collective-permute-start.9 = (bf16[256,512]{1,0:T(8,128)(2,1)S(1)}, bf16[256,512]{1,0:T(8,128)(2,1)S(1)}, u32[]{:S(2)}, u32[]{:S(2)}) collective-permute-start(bf16[256,512]{1,0:T(8,128)(2,1)S(1)} %collective-permute-done.8.refs_4_), channel_id=1, source_target_pairs={{0,64},{1,449},{64,128},{65,1},{128,192},{129,65},{192,256},{193,1... | collective-permute-start | bytes 786440 | tf_op jit(solution)/shard_map/ppermute | solution.py:282
  36.4 0.7 constant_dynamic-update-slice_fusion.4
  37.2 0.7 constant_dynamic-update-slice_fusion.3
  37.9 4.1 %collective-permute-start.4 = (bf16[256,512]{1,0:T(8,128)(2,1)S(1)}, bf16[256,512]{1,0:T(8,128)(2,1)S(1)}, u32[]{:S(2)}, u32[]{:S(2)}) collective-permute-start(bf16[256,512]{1,0:T(8,128)(2,1)S(1)} %collective-permute-done.2.refs_5_), channel_id=1, source_target_pairs={{0,64},{1,449},{64,128},{65,1},{128,192},{129,65},{192,256},{193,1... | collective-permute-start | bytes 786440 | tf_op jit(solution)/shard_map/ppermute | solution.py:262
  42.0 2.2 %early_sums.1.early_ref = f32[3,1,512]{2,1,0:T(1,128)S(1)} custom-call(bf16[256,512]{1,0:T(8,128)(2,1)S(1)} %collective-permute-done.6.refs_0_, bf16[256,512]{1,0:T(8,128)(2,1)S(1)} %collective-permute-done.refs_1_, bf16[256,512]{1,0:T(8,128)(2,1)S(1)} %collective-permute-done.7.refs_2_, bf16[256,512]{1,0:T(8,128)(2,1)S(1)} %collective-permute-done.1.refs_3_, ...), custom_call_target="tpu_custom_call" | custom-call | flops 2000000000 | bytes 2000000 | tf_op jit(solution)/shard_map/early_sums/pallas_call | solution.py:264
  46.9 1.9 %collective-permute-start.10 = (bf16[2048,512]{1,0:T(8,128)(2,1)}, bf16[2048,512]{1,0:T(8,128)(2,1)}, u32[]{:S(2)}, u32[]{:S(2)}) collective-permute-start(bf16[2048,512]{1,0:T(8,128)(2,1)} %constant_dynamic-update-slice_fusion.mine_hbm), channel_id=1, source_target_pairs={{0,1},{1,0},{2,3},{3,2},{4,5},{5,4},{6,7},{7,6},{8,9},{9,8},{10,11... | collective-permute-start | bytes 6291464 | tf_op jit(solution)/shard_map/ppermute | solution.py:294
  48.8 3.8 %collective-permute-start.11 = (bf16[256,2048]{1,0:T(8,128)(2,1)}, bf16[256,2048]{1,0:T(8,128)(2,1)}, u32[]{:S(2)}, u32[]{:S(2)}) collective-permute-start(bf16[256,2048]{1,0:T(8,128)(2,1)} %param.3), channel_id=1, source_target_pairs={{0,17},{1,49},{2,19},{3,51},{4,21},{5,53},{6,23},{7,55},{8,25},{9,... | collective-permute-start | bytes 3145736 | tf_op jit(solution)/shard_map/ppermute | solution.py:280
  52.9 2.4 %collective-permute-start.3 = (bf16[256,2048]{1,0:T(8,128)(2,1)}, bf16[256,2048]{1,0:T(8,128)(2,1)}, u32[]{:S(2)}, u32[]{:S(2)}) collective-permute-start(bf16[256,2048]{1,0:T(8,128)(2,1)} %param.3), channel_id=1, source_target_pairs={{0,16},{1,48},{2,18},{3,50},{4,20},{5,52},{6,22},{7,54},{8,24},{9,... | collective-permute-start | bytes 3145736 | tf_op jit(solution)/shard_map/ppermute | solution.py:279
  55.4 7.1 %pair_sums.1 = f32[8,1,512]{2,1,0:T(1,128)S(1)} custom-call(s32[1]{0:T(128)} %bitcast.core_ref, bf16[2048,512]{1,0:T(8,128)(2,1)} %constant_dynamic-update-slice_fusion.mine_hbm, bf16[2048,512]{1,0:T(8,128)(2,1)} %collective-permute-done.10.sibling_hbm, f32[3,1,512]{2,1,0:T(1,128)S(1)} %early_sums.1.early_ref), custom_call_target="tpu_custom_call" | custom-call | flops 3000000000 | bytes 2000000 | tf_op jit(solution)/shard_map/pair_sums/pallas_call | solution.py:297
  62.5 3.8 %psum.7.sums_ref = f32[8,1,512]{2,1,0:T(1,128)S(1)} all-reduce(f32[8,1,512]{2,1,0:T(1,128)S(1)} %pair_sums.1), channel_id=1, replica_groups=mesh['y2'=2,'y1'=2,'y0'=2,'xh'=2,'xl'=2,'z2'=2,'z1'=2,'z0'=2,'c'=2] {'c'}, use_global_device_ids=true, to_apply=%region_1.2 | all-reduce | flops 4096 | bytes 32768 | tf_op jit(solution)/shard_map/psum | solution.py:310
  66.3 7.1 %weights.1 = (bf16[256,256]{1,0:T(8,128)(2,1)S(1)}, bf16[256,256]{1,0:T(8,128)(2,1)S(1)}) custom-call(s32[1]{0:T(128)} %bitcast.core_ref, s32[16]{0:T(128)S(1)} %broadcast_multiply_fusion.start_ref, f32[256,2]{1,0:T(8,128)S(1)} %bitcast.40, f32[8,1,512]{2,1,0:T(1,128)S(1)} %psum.7.sums_ref, bf16[2048,512]{1,0:T(8,128)(2,1)} %constant_dynamic-update-slice_fusion.mine_hbm, ...), custom_call_target="tpu_custom_call" | custom-call | flops 2000000000 | bytes 2000000 | tf_op jit(solution)/shard_map/weights/pallas_call | solution.py:312
  73.4 2.1 %collective-permute-start.12 = (bf16[256,256]{1,0:T(8,128)(2,1)S(1)}, bf16[256,256]{1,0:T(8,128)(2,1)S(1)}, u32[]{:S(2)}, u32[]{:S(2)}) collective-permute-start(bf16[256,256]{1,0:T(8,128)(2,1)S(1)} %get-tuple-element.16), channel_id=1, source_target_pairs={{0,1},{1,0},{2,3},{3,2},{4,5},{5,4},{6,7},{7,6},{8,9},{9,8},{10,11... | collective-permute-start | bytes 393224 | tf_op jit(solution)/shard_map/ppermute | solution.py:320
  75.5 1.1 collective-permute-done.12
  76.7 1.7 %fusion.2 = f32[2048,256]{1,0:T(8,128)S(1)} fusion(bf16[256,2048]{1,0:T(8,128)(2,1)} %collective-permute-done.11, bf16[256,256]{1,0:T(8,128)(2,1)S(1)} %collective-permute-done.12), kind=kOutput, calls=%fused_computation.21 | convolution fusion | flops 268435456 | bytes 3276800 | tf_op jit(solution)/shard_map/dot_general | solution.py:323
  78.4 1.7 %fusion = bf16[2048,256]{1,0:T(8,128)(2,1)S(1)} fusion(f32[2048,256]{1,0:T(8,128)S(1)} %fusion.2, bf16[256,2048]{1,0:T(8,128)(2,1)} %collective-permute-done.3, bf16[256,256]{1,0:T(8,128)(2,1)S(1)} %get-tuple-element.15), kind=kOutput, calls=%fused_computation.1 | convolution fusion | flops 269484032 | bytes 4325376 | tf_op jit(solution)/shard_map/dot_general | solution.py:323
  80.3 24.5 %all_to_all.24 = bf16[16,128,256]{2,1,0:T(8,128)(2,1)S(1)} all-to-all(bf16[16,128,256]{2,1,0:T(8,128)(2,1)S(1)} %bitcast.41), channel_id=1, replica_groups=mesh['y2'=2,'y1'=2,'y0'=2,'xh'=2,'xl'=2,'z2'=2,'z1'=2,'z0'=2,'c'=2] {'z0..., dimensions={0} | all-to-all | bytes 2097152 | tf_op jit(solution)/shard_map/all_to_all | solution.py:330
  104.9 24.4 %all_to_all.25 = bf16[16,8,256]{2,1,0:T(8,128)(2,1)S(1)} all-to-all(bf16[16,8,256]{2,1,0:T(8,128)(2,1)S(1)} %bitcast.44), channel_id=1, replica_groups=mesh['y2'=2,'y1'=2,'y0'=2,'xh'=2,'xl'=2,'z2'=2,'z1'=2,'z0'=2,'c'=2] {'z2..., dimensions={0} | all-to-all | bytes 131072 | tf_op jit(solution)/shard_map/all_to_all | solution.py:332
  129.3 13.1 %all_to_all.26 = bf16[32,8,256]{2,1,0:T(8,128)(2,1)S(1)} all-to-all(bf16[32,8,256]{2,1,0:T(8,128)(2,1)S(1)} %broadcast_in_dim.4), channel_id=1, replica_groups=mesh['y2'=2,'y1'=2,'y0'=2,'xh'=2,'xl'=2,'z2'=2,'z1'=2,'z0'=2,'c'=2] {'c'..., dimensions={0} | all-to-all | bytes 262144 | tf_op jit(solution)/shard_map/all_to_all | solution.py:334
  143.7 13.4 %all_to_all.27 = f32[16,1,128]{2,1,0:T(1,128)S(1)} all-to-all(f32[16,1,128]{2,1,0:T(1,128)S(1)} %broadcast_in_dim.5), channel_id=1, replica_groups=mesh['y2'=2,'y1'=2,'y0'=2,'xh'=2,'xl'=2,'z2'=2,'z1'=2,'z0'=2,'c'=2] {'y2..., dimensions={0} | all-to-all | bytes 16384 | tf_op jit(solution)/shard_map/all_to_all | solution.py:340
  (34 shorter events, 6.1 us)
Async XLA Ops:
  0.0 1.6 copy-start
  1.6 14.0 %copy-start.1 = (s32[256]{0:T(256)S(1)}, s32[256]{0:T(256)}, u32[]{:S(2)}) copy-start(s32[256]{0:T(256)} %param.5) | copy-start | bytes 3076
  3.8 11.9 %collective-permute-start = (bf16[256,512]{1,0:T(8,128)(2,1)S(1)}, bf16[256,512]{1,0:T(8,128)(2,1)S(1)}, u32[]{:S(2)}, u32[]{:S(2)}) collective-permute-start(bf16[256,512]{1,0:T(8,128)(2,1)S(1)} %divide_convert_fusion), channel_id=1, source_target_pairs={{0,80},{1,112},{2,82},{3,114},{4,84},{5,116},{6,86},{7,118},{8,88}... | collective-permute-start | bytes 786440 | tf_op jit(solution)/shard_map/ppermute | solution.py:254
  8.2 16.3 %collective-permute-start.7 = (bf16[256,512]{1,0:T(8,128)(2,1)S(1)}, bf16[256,512]{1,0:T(8,128)(2,1)S(1)}, u32[]{:S(2)}, u32[]{:S(2)}) collective-permute-start(bf16[256,512]{1,0:T(8,128)(2,1)S(1)} %divide_convert_fusion), channel_id=1, source_target_pairs={{0,465},{1,497},{2,467},{3,499},{4,469},{5,501},{6,471},{7,503},{8... | collective-permute-start | bytes 786440 | tf_op jit(solution)/shard_map/ppermute | solution.py:255
  10.2 16.4 %collective-permute-start.6 = (bf16[256,512]{1,0:T(8,128)(2,1)S(1)}, bf16[256,512]{1,0:T(8,128)(2,1)S(1)}, u32[]{:S(2)}, u32[]{:S(2)}) collective-permute-start(bf16[256,512]{1,0:T(8,128)(2,1)S(1)} %divide_convert_fusion), channel_id=1, source_target_pairs={{0,16},{1,48},{2,18},{3,50},{4,20},{5,52},{6,22},{7,54},{8,24},{9,... | collective-permute-start | bytes 786440 | tf_op jit(solution)/shard_map/ppermute | solution.py:256
  15.7 12.4 %collective-permute-start.1 = (bf16[256,512]{1,0:T(8,128)(2,1)S(1)}, bf16[256,512]{1,0:T(8,128)(2,1)S(1)}, u32[]{:S(2)}, u32[]{:S(2)}) collective-permute-start(bf16[256,512]{1,0:T(8,128)(2,1)S(1)} %collective-permute-done.refs_1_), channel_id=1, source_target_pairs={{0,64},{1,449},{64,128},{65,1},{128,192},{129,65},{192,256},{193,1... | collective-permute-start | bytes 786440 | tf_op jit(solution)/shard_map/ppermute | solution.py:262
  18.5 27.1 %collective-permute-start.5 = (f32[2,256]{0,1:T(8,128)}, f32[2,256]{0,1:T(8,128)S(1)}, u32[]{:S(2)}, u32[]{:S(2)}) collective-permute-start(f32[2,256]{0,1:T(8,128)} %copy.17), channel_id=1, source_target_pairs={{0,16},{1,48},{2,18},{3,50},{4,20},{5,52},{6,22},{7,54},{8,24},{9,... | collective-permute-start | bytes 6152 | tf_op jit(solution)/shard_map/ppermute | solution.py:257
  24.5 10.0 %collective-permute-start.8 = (bf16[256,512]{1,0:T(8,128)(2,1)S(1)}, bf16[256,512]{1,0:T(8,128)(2,1)S(1)}, u32[]{:S(2)}, u32[]{:S(2)}) collective-permute-start(bf16[256,512]{1,0:T(8,128)(2,1)S(1)} %collective-permute-done.7.refs_2_), channel_id=1, source_target_pairs={{0,64},{1,449},{64,128},{65,1},{128,192},{129,65},{192,256},{193,1... | collective-permute-start | bytes 786440 | tf_op jit(solution)/shard_map/ppermute | solution.py:282
  28.1 9.8 %collective-permute-start.2 = (bf16[256,512]{1,0:T(8,128)(2,1)S(1)}, bf16[256,512]{1,0:T(8,128)(2,1)S(1)}, u32[]{:S(2)}, u32[]{:S(2)}) collective-permute-start(bf16[256,512]{1,0:T(8,128)(2,1)S(1)} %collective-permute-done.1.refs_3_), channel_id=1, source_target_pairs={{0,64},{1,449},{64,128},{65,1},{128,192},{129,65},{192,256},{193,1... | collective-permute-start | bytes 786440 | tf_op jit(solution)/shard_map/ppermute | solution.py:262
  34.5 10.4 %collective-permute-start.9 = (bf16[256,512]{1,0:T(8,128)(2,1)S(1)}, bf16[256,512]{1,0:T(8,128)(2,1)S(1)}, u32[]{:S(2)}, u32[]{:S(2)}) collective-permute-start(bf16[256,512]{1,0:T(8,128)(2,1)S(1)} %collective-permute-done.8.refs_4_), channel_id=1, source_target_pairs={{0,64},{1,449},{64,128},{65,1},{128,192},{129,65},{192,256},{193,1... | collective-permute-start | bytes 786440 | tf_op jit(solution)/shard_map/ppermute | solution.py:282
  37.9 8.3 %collective-permute-start.4 = (bf16[256,512]{1,0:T(8,128)(2,1)S(1)}, bf16[256,512]{1,0:T(8,128)(2,1)S(1)}, u32[]{:S(2)}, u32[]{:S(2)}) collective-permute-start(bf16[256,512]{1,0:T(8,128)(2,1)S(1)} %collective-permute-done.2.refs_5_), channel_id=1, source_target_pairs={{0,64},{1,449},{64,128},{65,1},{128,192},{129,65},{192,256},{193,1... | collective-permute-start | bytes 786440 | tf_op jit(solution)/shard_map/ppermute | solution.py:262
  46.9 8.4 %collective-permute-start.10 = (bf16[2048,512]{1,0:T(8,128)(2,1)}, bf16[2048,512]{1,0:T(8,128)(2,1)}, u32[]{:S(2)}, u32[]{:S(2)}) collective-permute-start(bf16[2048,512]{1,0:T(8,128)(2,1)} %constant_dynamic-update-slice_fusion.mine_hbm), channel_id=1, source_target_pairs={{0,1},{1,0},{2,3},{3,2},{4,5},{5,4},{6,7},{7,6},{8,9},{9,8},{10,11... | collective-permute-start | bytes 6291464 | tf_op jit(solution)/shard_map/ppermute | solution.py:294
  48.8 26.7 %collective-permute-start.11 = (bf16[256,2048]{1,0:T(8,128)(2,1)}, bf16[256,2048]{1,0:T(8,128)(2,1)}, u32[]{:S(2)}, u32[]{:S(2)}) collective-permute-start(bf16[256,2048]{1,0:T(8,128)(2,1)} %param.3), channel_id=1, source_target_pairs={{0,17},{1,49},{2,19},{3,51},{4,21},{5,53},{6,23},{7,55},{8,25},{9,... | collective-permute-start | bytes 3145736 | tf_op jit(solution)/shard_map/ppermute | solution.py:280
  52.9 25.5 %collective-permute-start.3 = (bf16[256,2048]{1,0:T(8,128)(2,1)}, bf16[256,2048]{1,0:T(8,128)(2,1)}, u32[]{:S(2)}, u32[]{:S(2)}) collective-permute-start(bf16[256,2048]{1,0:T(8,128)(2,1)} %param.3), channel_id=1, source_target_pairs={{0,16},{1,48},{2,18},{3,50},{4,20},{5,52},{6,22},{7,54},{8,24},{9,... | collective-permute-start | bytes 3145736 | tf_op jit(solution)/shard_map/ppermute | solution.py:279
  73.4 3.2 %collective-permute-start.12 = (bf16[256,256]{1,0:T(8,128)(2,1)S(1)}, bf16[256,256]{1,0:T(8,128)(2,1)S(1)}, u32[]{:S(2)}, u32[]{:S(2)}) collective-permute-start(bf16[256,256]{1,0:T(8,128)(2,1)S(1)} %get-tuple-element.16), channel_id=1, source_target_pairs={{0,1},{1,0},{2,3},{3,2},{4,5},{5,4},{6,7},{7,6},{8,9},{9,8},{10,11... | collective-permute-start | bytes 393224 | tf_op jit(solution)/shard_map/ppermute | solution.py:320

commit v9 on v8

--- a/solution.py
+++ b/solution.py
@@ -166,24 +166,16 @@
     start_ref,
     side_ref,
     sums_ref,
-    mine_hbm,
-    sibling_hbm,
+    mine_ref,
+    sibling_ref,
     keep_ref,
     send_ref,
-    mine_ref,
-    sibling_ref,
     weights,
-    semaphores,
 ):
     core = core_ref[0]
     wide = sums_ref.shape[2]
     blocks = sums_ref.shape[0] // 2
     rows = side_ref.shape[0]
-    copies = (
-        block_copies(mine_hbm, mine_ref, semaphores, range(blocks), 0),
-        block_copies(sibling_hbm, sibling_ref, semaphores, range(blocks), blocks),
-    )
-    copies[0][0].wait()
     own = mine_ref[:rows, :]
     mine_sums = sums_ref[blocks * core][:, :rows]
     inverse_own = 1.0 / jnp.broadcast_to(mine_sums, (128, rows)).T[:, :1]
@@ -192,8 +184,6 @@
     for part, ref in enumerate((mine_ref, sibling_ref)):
         for k in range(blocks):
             which = core if part == 0 else 1 - core
-            if part > 0 or k > 0:
-                copies[part][k].wait()
             right = ref[k * wide : (k + 1) * wide, :]
             inverse = 1.0 / sums_ref[blocks * which + k]
             values = exponentials(own, right)
@@ -218,6 +208,71 @@
     send_ref[...] = jnp.where(core == 0, second, first)
 
 
+def unit_kernel(features_ref, weight_ref, unit_ref, inverse_ref, hidden):
+    step = pl.program_id(0)
+    product = jnp.dot(features_ref[...], weight_ref[...], preferred_element_type=jnp.float32)
+
+    @pl.when(step == 0)
+    def _():
+        hidden[...] = product
+
+    @pl.when(step > 0)
+    def _():
+        hidden[...] += product
+
+    @pl.when(step == pl.num_programs(0) - 1)
+    def _():
+        squares = hidden[...] * hidden[...]
+        inverse = 1.0 / jnp.sqrt(jnp.sum(squares, axis=1, keepdims=True) + 1e-05)
+        unit_ref[...] = (hidden[...] * inverse).astype(jnp.bfloat16)
+        inverse_ref[...] = 1.0 / jnp.sqrt(row_totals(over_lane_groups(squares)) + 1e-05)
+
+
+def units(features, head_weight):
+    rows, channels = features.shape
+    width = head_weight.shape[1]
+    deep = channels // 4
+    return pl.pallas_call(
+        unit_kernel,
+        grid=(4,),
+        out_shape=(
+            jax.ShapeDtypeStruct((rows, width), jnp.bfloat16),
+            jax.ShapeDtypeStruct((1, rows), jnp.float32),
+        ),
+        in_specs=[
+            pl.BlockSpec((rows, deep), lambda k: (0, k)),
+            pl.BlockSpec((deep, width), lambda k: (k, 0)),
+        ],
+        out_specs=(
+            pl.BlockSpec((rows, width), lambda k: (0, 0)),
+            pl.BlockSpec((1, rows), lambda k: (0, 0)),
+        ),
+        scratch_shapes=[pltpu.VMEM((rows, width), jnp.float32)],
+        compiler_params=pltpu.CompilerParams(vmem_limit_bytes=60 * 1024 * 1024),
+        cost_estimate=pl.CostEstimate(
+            flops=2 * rows * channels * width, bytes_accessed=3_000_000, transcendentals=0
+        ),
+        name="units",
+    )(features, head_weight)
+
+
+def squares_kernel(spread_ref, squares_ref):
+    values = spread_ref[...].astype(jnp.float32)
+    squares_ref[...] = jnp.full(squares_ref.shape, jnp.sum(values * values), jnp.float32)
+
+
+def scale_kernel(spread_ref, squares_ref, update_ref):
+    total = jnp.sum(squares_ref[...], axis=0, keepdims=True)
+    entries = 16 * update_ref.shape[0] * update_ref.shape[1]
+    scale = 1.0 / jnp.sqrt(total * (1.0 / entries) + 1e-06)
+    for core in range(2):
+        for row in range(16):
+            for half in range(2):
+                column = 256 * half + 128 * core
+                tile = spread_ref[16 * core + row, half].astype(jnp.float32)
+                update_ref[8 * row : 8 * row + 8, column : column + 128] = tile * scale
+
+
 VMEM = pl.BlockSpec(memory_space=pltpu.VMEM)
 SMEM = pl.BlockSpec(memory_space=pltpu.SMEM)
 ANYWHERE = pl.BlockSpec(memory_space=pl.ANY)
@@ -245,10 +300,8 @@
     core = lax.axis_index("c")
     core_scalar = core.reshape(1).astype(jnp.int32)
 
-    hidden = jnp.dot(features, head_weight, preferred_element_type=jnp.float32)
-    row_norm = jnp.sqrt(jnp.sum(hidden * hidden, axis=1, keepdims=True) + 1e-05)
-    unit = (hidden / row_norm).astype(jnp.bfloat16)
-    side = jnp.stack([partner.astype(jnp.float32), 1.0 / row_norm[:, 0]])
+    unit, inverse_norm = units(features, head_weight)
+    side = jnp.concatenate([partner.astype(jnp.float32)[None], inverse_norm])
 
     sign = jnp.where(core == 0, -1, 1)
     same_core = lax.ppermute(unit, BITS, TO_NEXT_SAME)
@@ -312,8 +365,8 @@
     kept, sent = kernel_call(
         weight_kernel,
         (piece, piece),
-        [SMEM, SMEM, VMEM, VMEM, ANYWHERE, ANYWHERE],
-        held + [pltpu.VMEM((2, 2 * rows, 8 * rows), jnp.bfloat16), semaphores],
+        [SMEM, SMEM, VMEM, VMEM, VMEM, VMEM],
+        [pltpu.VMEM((2, 2 * rows, 8 * rows), jnp.bfloat16)],
         2_000_000_000,
         "weights",
     )(core_scalar, starts, side_here.T, sums, mine, sibling)
@@ -325,23 +378,25 @@
         )
 
     partial = (contract(rows_here, kept) + contract(rows_beside, beside)).astype(jnp.bfloat16)
-    tiles = partial.reshape(4, 2, 2, 2, 4, 2, 8, 256)
-    tiles = tiles.transpose(5, 3, 1, 2, 4, 0, 6, 7).reshape(16, 16 * 8, 256)
-    received = lax.all_to_all(tiles, ("z0", "xl", "y0", "xh"), 0, 0)
-    near_sum = received.astype(jnp.float32).sum(0).astype(jnp.bfloat16).reshape(16, 8, 256)
-    received = lax.all_to_all(near_sum, ("z2", "z1", "y2", "y1"), 0, 0)
-    fragment = received.astype(jnp.float32).sum(0).astype(jnp.bfloat16)
+    tiles = partial.reshape(*(2,) * 8, 8, 2, 128)
+    tiles = tiles.transpose(9, 7, 6, 5, 4, 3, 2, 1, 0, 8, 10).reshape(512, 8, 128)
+    received = lax.all_to_all(tiles, BITS[::-1], 0, 0).reshape(2, 256, 8, 128)
+    fragment = received.astype(jnp.float32).sum(1).astype(jnp.bfloat16)
     spread = lax.all_to_all(
-        jnp.broadcast_to(fragment[None], (32, 8, 256)), ("c", "xl", "z2", "z1", "z0"), 0, 0
+        jnp.broadcast_to(fragment[None], (32, 2, 8, 128)), ("c", "xl", "z2", "z1", "z0"), 0, 0
     )
-    gradient = spread.reshape(2, 16, 8, 256).transpose(1, 2, 0, 3).reshape(128, width)
-    gradient = gradient.astype(jnp.float32)
-    squares = jnp.sum(gradient * gradient)
-    squares = lax.all_to_all(
-        jnp.broadcast_to(squares, (16, 128)), ("y2", "y1", "y0", "xh"), 0, 0
-    )
-    total = jnp.sum(squares[:, 0])
-    return gradient * lax.rsqrt(total / (channels * width) + 1e-06)
+    squares = kernel_call(
+        squares_kernel, jax.ShapeDtypeStruct((16, 128), jnp.float32), [VMEM], [], 100_000, "squares"
+    )(spread)
+    squares = lax.all_to_all(squares, ("y2", "y1", "y0", "xh"), 0, 0)
+    return kernel_call(
+        scale_kernel,
+        jax.ShapeDtypeStruct((channels // 16, width), jnp.float32),
+        [VMEM, VMEM],
+        [],
+        100_000,
+        "scale",
+    )(spread, squares)
 
 
 def solution(mesh):

time: 160 us -> 163 us (1.019)
  local copies, waits for them, and re-layouts: 10.1 us -> 0.69 us
  waiting for transfers between devices: 1.72 us -> 8.8 us
  blocking collectives: 79.1 us -> 85.6 us
  Pallas kernels: 16.4 us -> 18.9 us
  matrix products: 5.46 us -> 3.45 us
    unnamed x12 -> x9, local copies, waits for them, and re-layouts: 7.45 us -> 0.14 us
    all_to_all x4 -> x3, blocking collectives: 75.3 us -> 81.8 us  [the longest x1 53.8 us: on_device(): received = lax.all_to_all(tiles, BITS[::-1], 0, 0).reshape(2, 256, 8, 128)]
    ppermute x3, waiting for transfers between devices: 0.56 us -> 4.65 us  [on_device(): same_core = lax.ppermute(same_core, (*YBITS, 'c'), ROUND)]
    pallas_call x1 -> x4, Pallas kernels: 7.11 us -> 10.5 us  [the longest x1 5.23 us: on_device(): kernel_call(weight_kernel, (piece, piece), [SMEM, SMEM, VMEM, VMEM, VMEM,...]
    ppermute x1, waiting for transfers between devices: 0.01 us -> 2.59 us  [on_device(): rows_here = lax.ppermute(later, BITS, TO_HOST)]
    dot_general x1 -> x0, matrix products: 2.02 us -> none  [on_device(): hidden = jnp.dot(features, head_weight, preferred_element_type=jnp.float32)]
    ppermute x1, starting transfers between devices: 3.81 us -> 2.11 us  [on_device(): rows_beside = lax.ppermute(later, BITS, TO_SIBLING)]
  transfers between devices with their start and end apart: 13 -> 13, of which waited for: 2 -> 6; matrix products, arithmetic and copies ran while one was open for 5% -> 2% of each run, Pallas kernels for 10% -> 8%
where the time goes in v9:
time: 163 us; the launch traced here: 162 us
  blocking collectives  85.6 us (53%)
  starting transfers between devices  42.9 us (26%)
  Pallas kernels  18.9 us (12%)
  waiting for transfers between devices  8.8 us (5%)
  matrix products  3.45 us (2%)
    all_to_all x1, blocking collectives, on_device(): received = lax.all_to_all(tiles, BITS[::-1], 0, 0).reshape(2, 256, 8, 128)  53.8 us
    all_to_all x1, blocking collectives, on_device(): lax.all_to_all(jnp.broadcast_to(fragment[None], (32, 2, 8, 128)), ('c', '...  14.2 us
    all_to_all x1, blocking collectives, on_device(): squares = lax.all_to_all(squares, ('y2', 'y1', 'y0', 'xh'), 0, 0)  13.9 us
    ppermute x3, starting transfers between devices, on_device(): same_core = lax.ppermute(same_core, (*YBITS, 'c'), ROUND)  11.3 us
    pallas_call x1, Pallas kernels, on_device(): kernel_call(pair_sums_kernel, jax.ShapeDtypeStruct((8, 1, 512), jnp.float...  6.28 us
    ppermute x1, starting transfers between devices, on_device(): side_here = lax.ppermute(side, BITS, TO_HOST)  5.9 us
    ppermute x1, starting transfers between devices, on_device(): own = lax.ppermute(unit, BITS, TO_HOST)  5.39 us
    ppermute x2, starting transfers between devices, on_device(): other_core = lax.ppermute(other_core, (*YBITS, 'c'), ROUND)  5.27 us
  transfers between devices with their start and end apart: 13, of which 6 were waited for; matrix products, arithmetic and copies ran while one was open for 2% of the time, Pallas kernels for 8%

profile of v9, /device:TPU:8, one launch (start us, length us, event | category | flops | bytes accessed | tf_op | source)
XLA Modules:
  0.0 161.8 jit_solution(6550160966381276910)
XLA Ops:
  0.0 4.3 %units.1 = (bf16[256,512]{1,0:T(8,128)(2,1)}, f32[1,256]{1,0:T(1,128)}) custom-call(bf16[256,2048]{1,0:T(8,128)(2,1)} %features_ref.1, bf16[2048,512]{1,0:T(8,128)(2,1)} %weight_ref.1), custom_call_target="tpu_custom_call" | custom-call | flops 536870912 | bytes 3000000 | tf_op jit(solution)/shard_map/units/pallas_call | solution.py:235
  4.3 4.4 %collective-permute-start = (bf16[256,512]{1,0:T(8,128)(2,1)}, bf16[256,512]{1,0:T(8,128)(2,1)S(1)}, u32[]{:S(2)}, u32[]{:S(2)}) collective-permute-start(bf16[256,512]{1,0:T(8,128)(2,1)} %get-tuple-element.13), channel_id=1, source_target_pairs={{0,80},{1,112},{2,82},{3,114},{4,84},{5,116},{6,86},{7,118},{8,88}... | collective-permute-start | bytes 786440 | tf_op jit(solution)/shard_map/ppermute | solution.py:307
  8.7 2.0 %collective-permute-start.7 = (bf16[256,512]{1,0:T(8,128)(2,1)}, bf16[256,512]{1,0:T(8,128)(2,1)S(1)}, u32[]{:S(2)}, u32[]{:S(2)}) collective-permute-start(bf16[256,512]{1,0:T(8,128)(2,1)} %get-tuple-element.13), channel_id=1, source_target_pairs={{0,465},{1,497},{2,467},{3,499},{4,469},{5,501},{6,471},{7,503},{8... | collective-permute-start | bytes 786440 | tf_op jit(solution)/shard_map/ppermute | solution.py:308
  10.8 5.4 %collective-permute-start.6 = (bf16[256,512]{1,0:T(8,128)(2,1)}, bf16[256,512]{1,0:T(8,128)(2,1)S(1)}, u32[]{:S(2)}, u32[]{:S(2)}) collective-permute-start(bf16[256,512]{1,0:T(8,128)(2,1)} %get-tuple-element.13), channel_id=1, source_target_pairs={{0,16},{1,48},{2,18},{3,50},{4,20},{5,52},{6,22},{7,54},{8,24},{9,... | collective-permute-start | bytes 786440 | tf_op jit(solution)/shard_map/ppermute | solution.py:309
  16.2 2.3 %collective-permute-start.1 = (bf16[256,512]{1,0:T(8,128)(2,1)S(1)}, bf16[256,512]{1,0:T(8,128)(2,1)S(1)}, u32[]{:S(2)}, u32[]{:S(2)}) collective-permute-start(bf16[256,512]{1,0:T(8,128)(2,1)S(1)} %collective-permute-done.refs_1_), channel_id=1, source_target_pairs={{0,64},{1,449},{64,128},{65,1},{128,192},{129,65},{192,256},{193,1... | collective-permute-start | bytes 786440 | tf_op jit(solution)/shard_map/ppermute | solution.py:315
  18.6 0.6 pad_maximum_fusion
  19.3 5.9 %collective-permute-start.5 = (f32[2,256]{0,1:T(8,128)S(1)}, f32[2,256]{0,1:T(8,128)S(1)}, u32[]{:S(2)}, u32[]{:S(2)}) collective-permute-start(f32[2,256]{0,1:T(8,128)S(1)} %copy.8), channel_id=1, source_target_pairs={{0,16},{1,48},{2,18},{3,50},{4,20},{5,52},{6,22},{7,54},{8,24},{9,... | collective-permute-start | bytes 6152 | tf_op jit(solution)/shard_map/ppermute | solution.py:310
  25.3 1.9 %collective-permute-start.8 = (bf16[256,512]{1,0:T(8,128)(2,1)S(1)}, bf16[256,512]{1,0:T(8,128)(2,1)S(1)}, u32[]{:S(2)}, u32[]{:S(2)}) collective-permute-start(bf16[256,512]{1,0:T(8,128)(2,1)S(1)} %collective-permute-done.7.refs_2_), channel_id=1, source_target_pairs={{0,64},{1,449},{64,128},{65,1},{128,192},{129,65},{192,256},{193,1... | collective-permute-start | bytes 786440 | tf_op jit(solution)/shard_map/ppermute | solution.py:335
  27.3 0.8 collective-permute-done.1.refs_3_
  28.0 5.1 %collective-permute-start.2 = (bf16[256,512]{1,0:T(8,128)(2,1)S(1)}, bf16[256,512]{1,0:T(8,128)(2,1)S(1)}, u32[]{:S(2)}, u32[]{:S(2)}) collective-permute-start(bf16[256,512]{1,0:T(8,128)(2,1)S(1)} %collective-permute-done.1.refs_3_), channel_id=1, source_target_pairs={{0,64},{1,449},{64,128},{65,1},{128,192},{129,65},{192,256},{193,1... | collective-permute-start | bytes 786440 | tf_op jit(solution)/shard_map/ppermute | solution.py:315
  33.1 0.4 collective-permute-done.8.refs_4_
  33.5 3.4 %collective-permute-start.9 = (bf16[256,512]{1,0:T(8,128)(2,1)S(1)}, bf16[256,512]{1,0:T(8,128)(2,1)S(1)}, u32[]{:S(2)}, u32[]{:S(2)}) collective-permute-start(bf16[256,512]{1,0:T(8,128)(2,1)S(1)} %collective-permute-done.8.refs_4_), channel_id=1, source_target_pairs={{0,64},{1,449},{64,128},{65,1},{128,192},{129,65},{192,256},{193,1... | collective-permute-start | bytes 786440 | tf_op jit(solution)/shard_map/ppermute | solution.py:335
  37.0 0.5 collective-permute-done.2.refs_5_
  37.5 3.9 %collective-permute-start.4 = (bf16[256,512]{1,0:T(8,128)(2,1)S(1)}, bf16[256,512]{1,0:T(8,128)(2,1)S(1)}, u32[]{:S(2)}, u32[]{:S(2)}) collective-permute-start(bf16[256,512]{1,0:T(8,128)(2,1)S(1)} %collective-permute-done.2.refs_5_), channel_id=1, source_target_pairs={{0,64},{1,449},{64,128},{65,1},{128,192},{129,65},{192,256},{193,1... | collective-permute-start | bytes 786440 | tf_op jit(solution)/shard_map/ppermute | solution.py:315
  41.4 2.1 %early_sums.1.early_ref = f32[3,1,512]{2,1,0:T(1,128)S(1)} custom-call(bf16[256,512]{1,0:T(8,128)(2,1)S(1)} %collective-permute-done.6.refs_0_, bf16[256,512]{1,0:T(8,128)(2,1)S(1)} %collective-permute-done.refs_1_, bf16[256,512]{1,0:T(8,128)(2,1)S(1)} %collective-permute-done.7.refs_2_, bf16[256,512]{1,0:T(8,128)(2,1)S(1)} %collective-permute-done.1.refs_3_, ...), custom_call_target="tpu_custom_call" | custom-call | flops 2000000000 | bytes 2000000 | tf_op jit(solution)/shard_map/early_sums/pallas_call | solution.py:317
  43.6 3.4 %collective-permute-done.4 = bf16[256,512]{1,0:T(8,128)(2,1)S(1)} collective-permute-done((bf16[256,512]{1,0:T(8,128)(2,1)S(1)}, bf16[256,512]{1,0:T(8,128)(2,1)S(1)}, u32[]{:S(2)}, u32[]{:S(2)}) %collective-permute-start.4) | collective-permute-done | bytes 262176 | tf_op jit(solution)/shard_map/ppermute | solution.py:315
  47.0 1.9 %collective-permute-start.10 = (bf16[2048,512]{1,0:T(8,128)(2,1)S(1)}, bf16[2048,512]{1,0:T(8,128)(2,1)}, u32[]{:S(2)}, u32[]{:S(2)}) collective-permute-start(bf16[2048,512]{1,0:T(8,128)(2,1)S(1)} %constant_dynamic-update-slice_fusion.mine_hbm.mine_ref), channel_id=1, source_target_pairs={{0,1},{1,0},{2,3},{3,2},{4,5},{5,4},{6,7},{7,6},{8,9},{9,8},{10,11... | collective-permute-start | bytes 6291464 | tf_op jit(solution)/shard_map/ppermute | solution.py:347
  48.9 2.1 %collective-permute-start.11 = (bf16[256,2048]{1,0:T(8,128)(2,1)}, bf16[256,2048]{1,0:T(8,128)(2,1)}, u32[]{:S(2)}, u32[]{:S(2)}) collective-permute-start(bf16[256,2048]{1,0:T(8,128)(2,1)} %features_ref.1), channel_id=1, source_target_pairs={{0,17},{1,49},{2,19},{3,51},{4,21},{5,53},{6,23},{7,55},{8,25},{9,... | collective-permute-start | bytes 3145736 | tf_op jit(solution)/shard_map/ppermute | solution.py:333
  51.3 2.5 %collective-permute-start.3 = (bf16[256,2048]{1,0:T(8,128)(2,1)}, bf16[256,2048]{1,0:T(8,128)(2,1)}, u32[]{:S(2)}, u32[]{:S(2)}) collective-permute-start(bf16[256,2048]{1,0:T(8,128)(2,1)} %features_ref.1), channel_id=1, source_target_pairs={{0,16},{1,48},{2,18},{3,50},{4,20},{5,52},{6,22},{7,54},{8,24},{9,... | collective-permute-start | bytes 3145736 | tf_op jit(solution)/shard_map/ppermute | solution.py:332
  53.8 6.3 %pair_sums.1 = f32[8,1,512]{2,1,0:T(1,128)S(1)} custom-call(s32[1]{0:T(128)} %bitcast.core_ref, bf16[2048,512]{1,0:T(8,128)(2,1)S(1)} %constant_dynamic-update-slice_fusion.mine_hbm.mine_ref, bf16[2048,512]{1,0:T(8,128)(2,1)} %collective-permute-done.10.sibling_hbm.sibling_ref, f32[3,1,512]{2,1,0:T(1,128)S(1)} %early_sums.1.early_ref), custom_call_target="tpu_custom_call" | custom-call | flops 3000000000 | bytes 2000000 | tf_op jit(solution)/shard_map/pair_sums/pallas_call | solution.py:350
  60.1 3.8 %psum.7.sums_ref = f32[8,1,512]{2,1,0:T(1,128)S(1)} all-reduce(f32[8,1,512]{2,1,0:T(1,128)S(1)} %pair_sums.1), channel_id=1, replica_groups=mesh['y2'=2,'y1'=2,'y0'=2,'xh'=2,'xl'=2,'z2'=2,'z1'=2,'z0'=2,'c'=2] {'c'}, use_global_device_ids=true, to_apply=%region_0.1 | all-reduce | flops 4096 | bytes 32768 | tf_op jit(solution)/shard_map/psum | solution.py:363
  63.9 5.2 %weights.1 = (bf16[256,256]{1,0:T(8,128)(2,1)S(1)}, bf16[256,256]{1,0:T(8,128)(2,1)S(1)}) custom-call(s32[1]{0:T(128)} %bitcast.core_ref, s32[16]{0:T(128)S(1)} %broadcast_multiply_fusion.start_ref, f32[256,2]{1,0:T(8,128)S(1)} %bitcast.35, f32[8,1,512]{2,1,0:T(1,128)S(1)} %psum.7.sums_ref, ...), custom_call_target="tpu_custom_call" | custom-call | flops 2000000000 | bytes 2000000 | tf_op jit(solution)/shard_map/weights/pallas_call | solution.py:365
  69.1 2.1 %collective-permute-start.12 = (bf16[256,256]{1,0:T(8,128)(2,1)S(1)}, bf16[256,256]{1,0:T(8,128)(2,1)S(1)}, u32[]{:S(2)}, u32[]{:S(2)}) collective-permute-start(bf16[256,256]{1,0:T(8,128)(2,1)S(1)} %get-tuple-element.20), channel_id=1, source_target_pairs={{0,1},{1,0},{2,3},{3,2},{4,5},{5,4},{6,7},{7,6},{8,9},{9,8},{10,11... | collective-permute-start | bytes 393224 | tf_op jit(solution)/shard_map/ppermute | solution.py:373
  71.2 1.2 collective-permute-done.12
  72.4 1.7 %fusion.1 = f32[2048,256]{1,0:T(8,128)S(1)} fusion(bf16[256,2048]{1,0:T(8,128)(2,1)} %collective-permute-done.11, bf16[256,256]{1,0:T(8,128)(2,1)S(1)} %collective-permute-done.12), kind=kOutput, calls=%fused_computation.13 | convolution fusion | flops 268435456 | bytes 3276800 | tf_op jit(solution)/shard_map/dot_general | solution.py:376
  74.1 2.6 %collective-permute-done.3 = bf16[256,2048]{1,0:T(8,128)(2,1)} collective-permute-done((bf16[256,2048]{1,0:T(8,128)(2,1)}, bf16[256,2048]{1,0:T(8,128)(2,1)}, u32[]{:S(2)}, u32[]{:S(2)}) %collective-permute-start.3) | collective-permute-done | bytes 1048608 | tf_op jit(solution)/shard_map/ppermute | solution.py:332
  76.7 1.7 %fusion = bf16[2048,256]{1,0:T(8,128)(2,1)S(1)} fusion(f32[2048,256]{1,0:T(8,128)S(1)} %fusion.1, bf16[256,2048]{1,0:T(8,128)(2,1)} %collective-permute-done.3, bf16[256,256]{1,0:T(8,128)(2,1)S(1)} %get-tuple-element.19), kind=kOutput, calls=%fused_computation.1 | convolution fusion | flops 269484032 | bytes 4325376 | tf_op jit(solution)/shard_map/dot_general | solution.py:376
  78.4 0.3 copy.9
  78.7 53.8 %all_to_all.21 = bf16[512,8,128]{2,1,0:T(8,128)(2,1)S(1)} all-to-all(bf16[512,8,128]{2,1,0:T(8,128)(2,1)S(1)} %bitcast.36), channel_id=1, replica_groups=mesh['y2'=2,'y1'=2,'y0'=2,'xh'=2,'xl'=2,'z2'=2,'z1'=2,'z0'=2,'c'=2] {'c'..., dimensions={0} | all-to-all | bytes 2097152 | tf_op jit(solution)/shard_map/all_to_all | solution.py:383
  132.8 14.2 %all_to_all.22.spread_ref = bf16[32,2,8,128]{3,2,1,0:T(8,128)(2,1)S(1)} all-to-all(bf16[32,2,8,128]{3,2,1,0:T(8,128)(2,1)S(1)} %broadcast_in_dim.10), channel_id=1, replica_groups=mesh['y2'=2,'y1'=2,'y0'=2,'xh'=2,'xl'=2,'z2'=2,'z1'=2,'z0'=2,'c'=2] {'c'..., dimensions={0} | all-to-all | bytes 262144 | tf_op jit(solution)/shard_map/all_to_all | solution.py:385
  147.2 13.9 %all_to_all.23 = f32[16,1,128]{2,1,0:T(1,128)S(1)} all-to-all(f32[16,1,128]{2,1,0:T(1,128)S(1)} %bitcast.34), channel_id=1, replica_groups=mesh['y2'=2,'y1'=2,'y0'=2,'xh'=2,'xl'=2,'z2'=2,'z1'=2,'z0'=2,'c'=2] {'y2..., dimensions={0} | all-to-all | bytes 16384 | tf_op jit(solution)/shard_map/all_to_all | solution.py:391
  161.0 0.7 scale.1
  (24 shorter events, 0.9 us)
Async XLA Ops:
  0.0 16.2 %copy-start = (s32[256]{0:T(256)S(1)}, s32[256]{0:T(256)}, u32[]{:S(2)}) copy-start(s32[256]{0:T(256)} %param.5) | copy-start | bytes 3076
  4.3 11.9 %collective-permute-start = (bf16[256,512]{1,0:T(8,128)(2,1)}, bf16[256,512]{1,0:T(8,128)(2,1)S(1)}, u32[]{:S(2)}, u32[]{:S(2)}) collective-permute-start(bf16[256,512]{1,0:T(8,128)(2,1)} %get-tuple-element.13), channel_id=1, source_target_pairs={{0,80},{1,112},{2,82},{3,114},{4,84},{5,116},{6,86},{7,118},{8,88}... | collective-permute-start | bytes 786440 | tf_op jit(solution)/shard_map/ppermute | solution.py:307
  8.7 16.5 %collective-permute-start.7 = (bf16[256,512]{1,0:T(8,128)(2,1)}, bf16[256,512]{1,0:T(8,128)(2,1)S(1)}, u32[]{:S(2)}, u32[]{:S(2)}) collective-permute-start(bf16[256,512]{1,0:T(8,128)(2,1)} %get-tuple-element.13), channel_id=1, source_target_pairs={{0,465},{1,497},{2,467},{3,499},{4,469},{5,501},{6,471},{7,503},{8... | collective-permute-start | bytes 786440 | tf_op jit(solution)/shard_map/ppermute | solution.py:308
  10.8 16.4 %collective-permute-start.6 = (bf16[256,512]{1,0:T(8,128)(2,1)}, bf16[256,512]{1,0:T(8,128)(2,1)S(1)}, u32[]{:S(2)}, u32[]{:S(2)}) collective-permute-start(bf16[256,512]{1,0:T(8,128)(2,1)} %get-tuple-element.13), channel_id=1, source_target_pairs={{0,16},{1,48},{2,18},{3,50},{4,20},{5,52},{6,22},{7,54},{8,24},{9,... | collective-permute-start | bytes 786440 | tf_op jit(solution)/shard_map/ppermute | solution.py:309
  16.2 11.8 %collective-permute-start.1 = (bf16[256,512]{1,0:T(8,128)(2,1)S(1)}, bf16[256,512]{1,0:T(8,128)(2,1)S(1)}, u32[]{:S(2)}, u32[]{:S(2)}) collective-permute-start(bf16[256,512]{1,0:T(8,128)(2,1)S(1)} %collective-permute-done.refs_1_), channel_id=1, source_target_pairs={{0,64},{1,449},{64,128},{65,1},{128,192},{129,65},{192,256},{193,1... | collective-permute-start | bytes 786440 | tf_op jit(solution)/shard_map/ppermute | solution.py:315
  19.3 24.2 %collective-permute-start.5 = (f32[2,256]{0,1:T(8,128)S(1)}, f32[2,256]{0,1:T(8,128)S(1)}, u32[]{:S(2)}, u32[]{:S(2)}) collective-permute-start(f32[2,256]{0,1:T(8,128)S(1)} %copy.8), channel_id=1, source_target_pairs={{0,16},{1,48},{2,18},{3,50},{4,20},{5,52},{6,22},{7,54},{8,24},{9,... | collective-permute-start | bytes 6152 | tf_op jit(solution)/shard_map/ppermute | solution.py:310
  25.3 8.3 %collective-permute-start.8 = (bf16[256,512]{1,0:T(8,128)(2,1)S(1)}, bf16[256,512]{1,0:T(8,128)(2,1)S(1)}, u32[]{:S(2)}, u32[]{:S(2)}) collective-permute-start(bf16[256,512]{1,0:T(8,128)(2,1)S(1)} %collective-permute-done.7.refs_2_), channel_id=1, source_target_pairs={{0,64},{1,449},{64,128},{65,1},{128,192},{129,65},{192,256},{193,1... | collective-permute-start | bytes 786440 | tf_op jit(solution)/shard_map/ppermute | solution.py:335
  28.0 9.5 %collective-permute-start.2 = (bf16[256,512]{1,0:T(8,128)(2,1)S(1)}, bf16[256,512]{1,0:T(8,128)(2,1)S(1)}, u32[]{:S(2)}, u32[]{:S(2)}) collective-permute-start(bf16[256,512]{1,0:T(8,128)(2,1)S(1)} %collective-permute-done.1.refs_3_), channel_id=1, source_target_pairs={{0,64},{1,449},{64,128},{65,1},{128,192},{129,65},{192,256},{193,1... | collective-permute-start | bytes 786440 | tf_op jit(solution)/shard_map/ppermute | solution.py:315
  33.5 10.0 %collective-permute-start.9 = (bf16[256,512]{1,0:T(8,128)(2,1)S(1)}, bf16[256,512]{1,0:T(8,128)(2,1)S(1)}, u32[]{:S(2)}, u32[]{:S(2)}) collective-permute-start(bf16[256,512]{1,0:T(8,128)(2,1)S(1)} %collective-permute-done.8.refs_4_), channel_id=1, source_target_pairs={{0,64},{1,449},{64,128},{65,1},{128,192},{129,65},{192,256},{193,1... | collective-permute-start | bytes 786440 | tf_op jit(solution)/shard_map/ppermute | solution.py:335
  37.5 9.5 %collective-permute-start.4 = (bf16[256,512]{1,0:T(8,128)(2,1)S(1)}, bf16[256,512]{1,0:T(8,128)(2,1)S(1)}, u32[]{:S(2)}, u32[]{:S(2)}) collective-permute-start(bf16[256,512]{1,0:T(8,128)(2,1)S(1)} %collective-permute-done.2.refs_5_), channel_id=1, source_target_pairs={{0,64},{1,449},{64,128},{65,1},{128,192},{129,65},{192,256},{193,1... | collective-permute-start | bytes 786440 | tf_op jit(solution)/shard_map/ppermute | solution.py:315
  47.0 6.8 %collective-permute-start.10 = (bf16[2048,512]{1,0:T(8,128)(2,1)S(1)}, bf16[2048,512]{1,0:T(8,128)(2,1)}, u32[]{:S(2)}, u32[]{:S(2)}) collective-permute-start(bf16[2048,512]{1,0:T(8,128)(2,1)S(1)} %constant_dynamic-update-slice_fusion.mine_hbm.mine_ref), channel_id=1, source_target_pairs={{0,1},{1,0},{2,3},{3,2},{4,5},{5,4},{6,7},{7,6},{8,9},{9,8},{10,11... | collective-permute-start | bytes 6291464 | tf_op jit(solution)/shard_map/ppermute | solution.py:347
  48.9 22.3 %collective-permute-start.11 = (bf16[256,2048]{1,0:T(8,128)(2,1)}, bf16[256,2048]{1,0:T(8,128)(2,1)}, u32[]{:S(2)}, u32[]{:S(2)}) collective-permute-start(bf16[256,2048]{1,0:T(8,128)(2,1)} %features_ref.1), channel_id=1, source_target_pairs={{0,17},{1,49},{2,19},{3,51},{4,21},{5,53},{6,23},{7,55},{8,25},{9,... | collective-permute-start | bytes 3145736 | tf_op jit(solution)/shard_map/ppermute | solution.py:333
  51.3 25.4 %collective-permute-start.3 = (bf16[256,2048]{1,0:T(8,128)(2,1)}, bf16[256,2048]{1,0:T(8,128)(2,1)}, u32[]{:S(2)}, u32[]{:S(2)}) collective-permute-start(bf16[256,2048]{1,0:T(8,128)(2,1)} %features_ref.1), channel_id=1, source_target_pairs={{0,16},{1,48},{2,18},{3,50},{4,20},{5,52},{6,22},{7,54},{8,24},{9,... | collective-permute-start | bytes 3145736 | tf_op jit(solution)/shard_map/ppermute | solution.py:332
  69.1 3.2 %collective-permute-start.12 = (bf16[256,256]{1,0:T(8,128)(2,1)S(1)}, bf16[256,256]{1,0:T(8,128)(2,1)S(1)}, u32[]{:S(2)}, u32[]{:S(2)}) collective-permute-start(bf16[256,256]{1,0:T(8,128)(2,1)S(1)} %get-tuple-element.20), channel_id=1, source_target_pairs={{0,1},{1,0},{2,3},{3,2},{4,5},{5,4},{6,7},{7,6},{8,9},{9,8},{10,11... | collective-permute-start | bytes 393224 | tf_op jit(solution)/shard_map/ppermute | solution.py:373

commit v10 on v8

--- a/solution.py
+++ b/solution.py
@@ -166,24 +166,16 @@
     start_ref,
     side_ref,
     sums_ref,
-    mine_hbm,
-    sibling_hbm,
+    mine_ref,
+    sibling_ref,
     keep_ref,
     send_ref,
-    mine_ref,
-    sibling_ref,
     weights,
-    semaphores,
 ):
     core = core_ref[0]
     wide = sums_ref.shape[2]
     blocks = sums_ref.shape[0] // 2
     rows = side_ref.shape[0]
-    copies = (
-        block_copies(mine_hbm, mine_ref, semaphores, range(blocks), 0),
-        block_copies(sibling_hbm, sibling_ref, semaphores, range(blocks), blocks),
-    )
-    copies[0][0].wait()
     own = mine_ref[:rows, :]
     mine_sums = sums_ref[blocks * core][:, :rows]
     inverse_own = 1.0 / jnp.broadcast_to(mine_sums, (128, rows)).T[:, :1]
@@ -192,8 +184,6 @@
     for part, ref in enumerate((mine_ref, sibling_ref)):
         for k in range(blocks):
             which = core if part == 0 else 1 - core
-            if part > 0 or k > 0:
-                copies[part][k].wait()
             right = ref[k * wide : (k + 1) * wide, :]
             inverse = 1.0 / sums_ref[blocks * which + k]
             values = exponentials(own, right)
@@ -216,6 +206,22 @@
     first, second = grad_hidden[:, :middle], grad_hidden[:, middle:]
     keep_ref[...] = jnp.where(core == 0, first, second)
     send_ref[...] = jnp.where(core == 0, second, first)
+
+
+def squares_kernel(spread_ref, squares_ref):
+    values = spread_ref[...].astype(jnp.float32)
+    squares_ref[...] = jnp.full(squares_ref.shape, jnp.sum(values * values), jnp.float32)
+
+
+def scale_kernel(spread_ref, squares_ref, update_ref):
+    total = jnp.sum(squares_ref[...], axis=0, keepdims=True)
+    entries = 16 * update_ref.shape[0] * update_ref.shape[1]
+    scale = 1.0 / jnp.sqrt(total * (1.0 / entries) + 1e-06)
+    scale = jnp.concatenate([scale, scale], axis=1)
+    for core in range(2):
+        for row in range(16):
+            tile = spread_ref[16 * core + row].astype(jnp.float32)
+            update_ref[8 * row : 8 * row + 8, 256 * core : 256 * core + 256] = tile * scale
 
 
 VMEM = pl.BlockSpec(memory_space=pltpu.VMEM)
@@ -312,8 +318,8 @@
     kept, sent = kernel_call(
         weight_kernel,
         (piece, piece),
-        [SMEM, SMEM, VMEM, VMEM, ANYWHERE, ANYWHERE],
-        held + [pltpu.VMEM((2, 2 * rows, 8 * rows), jnp.bfloat16), semaphores],
+        [SMEM, SMEM, VMEM, VMEM, VMEM, VMEM],
+        [pltpu.VMEM((2, 2 * rows, 8 * rows), jnp.bfloat16)],
         2_000_000_000,
         "weights",
     )(core_scalar, starts, side_here.T, sums, mine, sibling)
@@ -334,14 +340,18 @@
     spread = lax.all_to_all(
         jnp.broadcast_to(fragment[None], (32, 8, 256)), ("c", "xl", "z2", "z1", "z0"), 0, 0
     )
-    gradient = spread.reshape(2, 16, 8, 256).transpose(1, 2, 0, 3).reshape(128, width)
-    gradient = gradient.astype(jnp.float32)
-    squares = jnp.sum(gradient * gradient)
-    squares = lax.all_to_all(
-        jnp.broadcast_to(squares, (16, 128)), ("y2", "y1", "y0", "xh"), 0, 0
-    )
-    total = jnp.sum(squares[:, 0])
-    return gradient * lax.rsqrt(total / (channels * width) + 1e-06)
+    squares = kernel_call(
+        squares_kernel, jax.ShapeDtypeStruct((16, 128), jnp.float32), [VMEM], [], 100_000, "squares"
+    )(spread)
+    squares = lax.all_to_all(squares, ("y2", "y1", "y0", "xh"), 0, 0)
+    return kernel_call(
+        scale_kernel,
+        jax.ShapeDtypeStruct((channels // 16, width), jnp.float32),
+        [VMEM, VMEM],
+        [],
+        100_000,
+        "scale",
+    )(spread, squares)
 
 
 def solution(mesh):

time: 160 us -> 156 us (0.975)
  local copies, waits for them, and re-layouts: 10.1 us -> 8.39 us
    unnamed x12 -> x11, local copies, waits for them, and re-layouts: 7.45 us -> 6.64 us
    pallas_call x1 -> x3, Pallas kernels: 7.11 us -> 6.79 us  [the longest x1 5.86 us: on_device(): kernel_call(weight_kernel, (piece, piece), [SMEM, SMEM, VMEM, VMEM, VMEM,...]
where the time goes in v10:
time: 156 us; the launch traced here: 155 us
  blocking collectives  78.9 us (51%)
  starting transfers between devices  43.8 us (28%)
  Pallas kernels  16.1 us (10%)
  local copies, waits for them, and re-layouts  8.39 us (5%)
  matrix products  5.46 us (4%)
  waiting for transfers between devices  1.78 us (1%)
    all_to_all x1, blocking collectives, on_device(): received = lax.all_to_all(near_sum, ('z2', 'z1', 'y2', 'y1'), 0, 0)  24.4 us
    all_to_all x1, blocking collectives, on_device(): received = lax.all_to_all(tiles, ('z0', 'xl', 'y0', 'xh'), 0, 0)  24.3 us
    all_to_all x1, blocking collectives, on_device(): squares = lax.all_to_all(squares, ('y2', 'y1', 'y0', 'xh'), 0, 0)  13.3 us
    all_to_all x1, blocking collectives, on_device(): lax.all_to_all(jnp.broadcast_to(fragment[None], (32, 8, 256)), ('c', 'xl'...  13.1 us
    ppermute x3, starting transfers between devices, on_device(): same_core = lax.ppermute(same_core, (*YBITS, 'c'), ROUND)  11.8 us
    pallas_call x1, Pallas kernels, on_device(): kernel_call(pair_sums_kernel, jax.ShapeDtypeStruct((8, 1, 512), jnp.float...  7.15 us
    unnamed x11, local copies, waits for them, and re-layouts  6.64 us
    ppermute x1, starting transfers between devices, on_device(): side_here = lax.ppermute(side, BITS, TO_HOST)  6 us
  transfers between devices with their start and end apart: 13, of which 2 were waited for; matrix products, arithmetic and copies ran while one was open for 5% of the time, Pallas kernels for 10%

profile of v10, /device:TPU:8, one launch (start us, length us, event | category | flops | bytes accessed | tf_op | source)
XLA Modules:
  0.0 155.2 jit_solution(938803781247196119)
XLA Ops:
  0.0 1.6 %copy-done = bf16[2048,512]{1,0:T(8,128)(2,1)S(1)} copy-done((bf16[2048,512]{1,0:T(8,128)(2,1)S(1)}, bf16[2048,512]{1,0:T(8,128)(2,1)}, u32[]{:S(2)}) %copy-start) | copy-done | bytes 2097176
  1.6 2.0 %multiply_reduce_fusion = (f32[256]{0:T(256)S(1)}, f32[256,512]{1,0:T(8,128)S(1)}) fusion(bf16[256,2048]{1,0:T(8,128)(2,1)} %param.3, bf16[2048,512]{1,0:T(8,128)(2,1)S(1)} %copy-done), kind=kOutput, calls=%fused_computation.3 | convolution fusion | flops 537132800 | bytes 3671040 | tf_op jit(solution)/shard_map/dot_general | solution.py:254
  3.8 4.4 %collective-permute-start = (bf16[256,512]{1,0:T(8,128)(2,1)S(1)}, bf16[256,512]{1,0:T(8,128)(2,1)S(1)}, u32[]{:S(2)}, u32[]{:S(2)}) collective-permute-start(bf16[256,512]{1,0:T(8,128)(2,1)S(1)} %divide_convert_fusion), channel_id=1, source_target_pairs={{0,80},{1,112},{2,82},{3,114},{4,84},{5,116},{6,86},{7,118},{8,88}... | collective-permute-start | bytes 786440 | tf_op jit(solution)/shard_map/ppermute | solution.py:260
  8.2 2.0 %collective-permute-start.7 = (bf16[256,512]{1,0:T(8,128)(2,1)S(1)}, bf16[256,512]{1,0:T(8,128)(2,1)S(1)}, u32[]{:S(2)}, u32[]{:S(2)}) collective-permute-start(bf16[256,512]{1,0:T(8,128)(2,1)S(1)} %divide_convert_fusion), channel_id=1, source_target_pairs={{0,465},{1,497},{2,467},{3,499},{4,469},{5,501},{6,471},{7,503},{8... | collective-permute-start | bytes 786440 | tf_op jit(solution)/shard_map/ppermute | solution.py:261
  10.2 5.4 %collective-permute-start.6 = (bf16[256,512]{1,0:T(8,128)(2,1)S(1)}, bf16[256,512]{1,0:T(8,128)(2,1)S(1)}, u32[]{:S(2)}, u32[]{:S(2)}) collective-permute-start(bf16[256,512]{1,0:T(8,128)(2,1)S(1)} %divide_convert_fusion), channel_id=1, source_target_pairs={{0,16},{1,48},{2,18},{3,50},{4,20},{5,52},{6,22},{7,54},{8,24},{9,... | collective-permute-start | bytes 786440 | tf_op jit(solution)/shard_map/ppermute | solution.py:262
  15.7 2.0 %collective-permute-start.1 = (bf16[256,512]{1,0:T(8,128)(2,1)S(1)}, bf16[256,512]{1,0:T(8,128)(2,1)S(1)}, u32[]{:S(2)}, u32[]{:S(2)}) collective-permute-start(bf16[256,512]{1,0:T(8,128)(2,1)S(1)} %collective-permute-done.refs_1_), channel_id=1, source_target_pairs={{0,64},{1,449},{64,128},{65,1},{128,192},{129,65},{192,256},{193,1... | collective-permute-start | bytes 786440 | tf_op jit(solution)/shard_map/ppermute | solution.py:268
  17.7 0.8 copy.10
  18.5 6.0 %collective-permute-start.5 = (f32[2,256]{0,1:T(8,128)}, f32[2,256]{0,1:T(8,128)S(1)}, u32[]{:S(2)}, u32[]{:S(2)}) collective-permute-start(f32[2,256]{0,1:T(8,128)} %copy.10), channel_id=1, source_target_pairs={{0,16},{1,48},{2,18},{3,50},{4,20},{5,52},{6,22},{7,54},{8,24},{9,... | collective-permute-start | bytes 6152 | tf_op jit(solution)/shard_map/ppermute | solution.py:263
  24.5 2.1 %collective-permute-start.8 = (bf16[256,512]{1,0:T(8,128)(2,1)S(1)}, bf16[256,512]{1,0:T(8,128)(2,1)S(1)}, u32[]{:S(2)}, u32[]{:S(2)}) collective-permute-start(bf16[256,512]{1,0:T(8,128)(2,1)S(1)} %collective-permute-done.7.refs_2_), channel_id=1, source_target_pairs={{0,64},{1,449},{64,128},{65,1},{128,192},{129,65},{192,256},{193,1... | collective-permute-start | bytes 786440 | tf_op jit(solution)/shard_map/ppermute | solution.py:288
  27.3 0.7 constant_dynamic-update-slice_fusion.6
  28.1 5.7 %collective-permute-start.2 = (bf16[256,512]{1,0:T(8,128)(2,1)S(1)}, bf16[256,512]{1,0:T(8,128)(2,1)S(1)}, u32[]{:S(2)}, u32[]{:S(2)}) collective-permute-start(bf16[256,512]{1,0:T(8,128)(2,1)S(1)} %collective-permute-done.1.refs_3_), channel_id=1, source_target_pairs={{0,64},{1,449},{64,128},{65,1},{128,192},{129,65},{192,256},{193,1... | collective-permute-start | bytes 786440 | tf_op jit(solution)/shard_map/ppermute | solution.py:268
  33.7 0.7 constant_dynamic-update-slice_fusion.5
  34.4 1.9 %collective-permute-start.9 = (bf16[256,512]{1,0:T(8,128)(2,1)S(1)}, bf16[256,512]{1,0:T(8,128)(2,1)S(1)}, u32[]{:S(2)}, u32[]{:S(2)}) collective-permute-start(bf16[256,512]{1,0:T(8,128)(2,1)S(1)} %collective-permute-done.8.refs_4_), channel_id=1, source_target_pairs={{0,64},{1,449},{64,128},{65,1},{128,192},{129,65},{192,256},{193,1... | collective-permute-start | bytes 786440 | tf_op jit(solution)/shard_map/ppermute | solution.py:288
  36.4 0.7 constant_dynamic-update-slice_fusion.4
  37.8 4.2 %collective-permute-start.4 = (bf16[256,512]{1,0:T(8,128)(2,1)S(1)}, bf16[256,512]{1,0:T(8,128)(2,1)S(1)}, u32[]{:S(2)}, u32[]{:S(2)}) collective-permute-start(bf16[256,512]{1,0:T(8,128)(2,1)S(1)} %collective-permute-done.2.refs_5_), channel_id=1, source_target_pairs={{0,64},{1,449},{64,128},{65,1},{128,192},{129,65},{192,256},{193,1... | collective-permute-start | bytes 786440 | tf_op jit(solution)/shard_map/ppermute | solution.py:268
  42.0 2.1 %early_sums.1.early_ref = f32[3,1,512]{2,1,0:T(1,128)S(1)} custom-call(bf16[256,512]{1,0:T(8,128)(2,1)S(1)} %collective-permute-done.6.refs_0_, bf16[256,512]{1,0:T(8,128)(2,1)S(1)} %collective-permute-done.refs_1_, bf16[256,512]{1,0:T(8,128)(2,1)S(1)} %collective-permute-done.7.refs_2_, bf16[256,512]{1,0:T(8,128)(2,1)S(1)} %collective-permute-done.1.refs_3_, ...), custom_call_target="tpu_custom_call" | custom-call | flops 2000000000 | bytes 2000000 | tf_op jit(solution)/shard_map/early_sums/pallas_call | solution.py:270
  44.9 0.7 constant_dynamic-update-slice_fusion.1
  46.9 1.9 %collective-permute-start.10 = (bf16[2048,512]{1,0:T(8,128)(2,1)}, bf16[2048,512]{1,0:T(8,128)(2,1)}, u32[]{:S(2)}, u32[]{:S(2)}) collective-permute-start(bf16[2048,512]{1,0:T(8,128)(2,1)} %constant_dynamic-update-slice_fusion.mine_hbm.mine_ref), channel_id=1, source_target_pairs={{0,1},{1,0},{2,3},{3,2},{4,5},{5,4},{6,7},{7,6},{8,9},{9,8},{10,11... | collective-permute-start | bytes 6291464 | tf_op jit(solution)/shard_map/ppermute | solution.py:300
  48.8 3.7 %collective-permute-start.11 = (bf16[256,2048]{1,0:T(8,128)(2,1)}, bf16[256,2048]{1,0:T(8,128)(2,1)}, u32[]{:S(2)}, u32[]{:S(2)}) collective-permute-start(bf16[256,2048]{1,0:T(8,128)(2,1)} %param.3), channel_id=1, source_target_pairs={{0,17},{1,49},{2,19},{3,51},{4,21},{5,53},{6,23},{7,55},{8,25},{9,... | collective-permute-start | bytes 3145736 | tf_op jit(solution)/shard_map/ppermute | solution.py:286
  52.8 2.5 %collective-permute-start.3 = (bf16[256,2048]{1,0:T(8,128)(2,1)}, bf16[256,2048]{1,0:T(8,128)(2,1)}, u32[]{:S(2)}, u32[]{:S(2)}) collective-permute-start(bf16[256,2048]{1,0:T(8,128)(2,1)} %param.3), channel_id=1, source_target_pairs={{0,16},{1,48},{2,18},{3,50},{4,20},{5,52},{6,22},{7,54},{8,24},{9,... | collective-permute-start | bytes 3145736 | tf_op jit(solution)/shard_map/ppermute | solution.py:285
  55.3 7.1 %pair_sums.1 = f32[8,1,512]{2,1,0:T(1,128)S(1)} custom-call(s32[1]{0:T(128)} %bitcast.core_ref, bf16[2048,512]{1,0:T(8,128)(2,1)} %constant_dynamic-update-slice_fusion.mine_hbm.mine_ref, bf16[2048,512]{1,0:T(8,128)(2,1)} %collective-permute-done.10.sibling_hbm.sibling_ref, f32[3,1,512]{2,1,0:T(1,128)S(1)} %early_sums.1.early_ref), custom_call_target="tpu_custom_call" | custom-call | flops 3000000000 | bytes 2000000 | tf_op jit(solution)/shard_map/pair_sums/pallas_call | solution.py:303
  62.5 3.8 %psum.7.sums_ref = f32[8,1,512]{2,1,0:T(1,128)S(1)} all-reduce(f32[8,1,512]{2,1,0:T(1,128)S(1)} %pair_sums.1), channel_id=1, replica_groups=mesh['y2'=2,'y1'=2,'y0'=2,'xh'=2,'xl'=2,'z2'=2,'z1'=2,'z0'=2,'c'=2] {'c'}, use_global_device_ids=true, to_apply=%region_1.2 | all-reduce | flops 4096 | bytes 32768 | tf_op jit(solution)/shard_map/psum | solution.py:316
  66.3 5.9 %weights.1 = (bf16[256,256]{1,0:T(8,128)(2,1)S(1)}, bf16[256,256]{1,0:T(8,128)(2,1)S(1)}) custom-call(s32[1]{0:T(128)} %bitcast.core_ref, s32[16]{0:T(128)S(1)} %broadcast_multiply_fusion.start_ref, f32[256,2]{1,0:T(8,128)S(1)} %bitcast.37, f32[8,1,512]{2,1,0:T(1,128)S(1)} %psum.7.sums_ref, ...), custom_call_target="tpu_custom_call" | custom-call | flops 2000000000 | bytes 2000000 | tf_op jit(solution)/shard_map/weights/pallas_call | solution.py:318
  72.1 2.1 %collective-permute-start.12 = (bf16[256,256]{1,0:T(8,128)(2,1)S(1)}, bf16[256,256]{1,0:T(8,128)(2,1)S(1)}, u32[]{:S(2)}, u32[]{:S(2)}) collective-permute-start(bf16[256,256]{1,0:T(8,128)(2,1)S(1)} %get-tuple-element.16), channel_id=1, source_target_pairs={{0,1},{1,0},{2,3},{3,2},{4,5},{5,4},{6,7},{7,6},{8,9},{9,8},{10,11... | collective-permute-start | bytes 393224 | tf_op jit(solution)/shard_map/ppermute | solution.py:326
  74.2 1.1 collective-permute-done.12
  75.4 1.7 %fusion.1 = f32[2048,256]{1,0:T(8,128)S(1)} fusion(bf16[256,2048]{1,0:T(8,128)(2,1)} %collective-permute-done.11, bf16[256,256]{1,0:T(8,128)(2,1)S(1)} %collective-permute-done.12), kind=kOutput, calls=%fused_computation.16 | convolution fusion | flops 268435456 | bytes 3276800 | tf_op jit(solution)/shard_map/dot_general | solution.py:329
  77.1 1.7 %fusion = bf16[2048,256]{1,0:T(8,128)(2,1)S(1)} fusion(f32[2048,256]{1,0:T(8,128)S(1)} %fusion.1, bf16[256,2048]{1,0:T(8,128)(2,1)} %collective-permute-done.3, bf16[256,256]{1,0:T(8,128)(2,1)S(1)} %get-tuple-element.15), kind=kOutput, calls=%fused_computation.1 | convolution fusion | flops 269484032 | bytes 4325376 | tf_op jit(solution)/shard_map/dot_general | solution.py:329
  79.0 24.3 %all_to_all.26 = bf16[16,128,256]{2,1,0:T(8,128)(2,1)S(1)} all-to-all(bf16[16,128,256]{2,1,0:T(8,128)(2,1)S(1)} %bitcast.38), channel_id=1, replica_groups=mesh['y2'=2,'y1'=2,'y0'=2,'xh'=2,'xl'=2,'z2'=2,'z1'=2,'z0'=2,'c'=2] {'z0..., dimensions={0} | all-to-all | bytes 2097152 | tf_op jit(solution)/shard_map/all_to_all | solution.py:336
  103.4 24.4 %all_to_all.27 = bf16[16,8,256]{2,1,0:T(8,128)(2,1)S(1)} all-to-all(bf16[16,8,256]{2,1,0:T(8,128)(2,1)S(1)} %bitcast.40), channel_id=1, replica_groups=mesh['y2'=2,'y1'=2,'y0'=2,'xh'=2,'xl'=2,'z2'=2,'z1'=2,'z0'=2,'c'=2] {'z2..., dimensions={0} | all-to-all | bytes 131072 | tf_op jit(solution)/shard_map/all_to_all | solution.py:338
  127.9 13.1 %all_to_all.28.spread_ref = bf16[32,8,256]{2,1,0:T(8,128)(2,1)S(1)} all-to-all(bf16[32,8,256]{2,1,0:T(8,128)(2,1)S(1)} %broadcast_in_dim.2), channel_id=1, replica_groups=mesh['y2'=2,'y1'=2,'y0'=2,'xh'=2,'xl'=2,'z2'=2,'z1'=2,'z0'=2,'c'=2] {'c'..., dimensions={0} | all-to-all | bytes 262144 | tf_op jit(solution)/shard_map/all_to_all | solution.py:340
  141.2 13.3 %all_to_all.29 = f32[16,1,128]{2,1,0:T(1,128)S(1)} all-to-all(f32[16,1,128]{2,1,0:T(1,128)S(1)} %bitcast.36), channel_id=1, replica_groups=mesh['y2'=2,'y1'=2,'y0'=2,'xh'=2,'xl'=2,'z2'=2,'z1'=2,'z0'=2,'c'=2] {'y2..., dimensions={0} | all-to-all | bytes 16384 | tf_op jit(solution)/shard_map/all_to_all | solution.py:346
  154.4 0.7 scale.1
  (30 shorter events, 4.2 us)
Async XLA Ops:
  0.0 1.6 %copy-start = (bf16[2048,512]{1,0:T(8,128)(2,1)S(1)}, bf16[2048,512]{1,0:T(8,128)(2,1)}, u32[]{:S(2)}) copy-start(bf16[2048,512]{1,0:T(8,128)(2,1)} %param.4) | copy-start | bytes 6291460
  1.6 14.0 %copy-start.1 = (s32[256]{0:T(256)S(1)}, s32[256]{0:T(256)}, u32[]{:S(2)}) copy-start(s32[256]{0:T(256)} %param.5) | copy-start | bytes 3076
  3.8 11.9 %collective-permute-start = (bf16[256,512]{1,0:T(8,128)(2,1)S(1)}, bf16[256,512]{1,0:T(8,128)(2,1)S(1)}, u32[]{:S(2)}, u32[]{:S(2)}) collective-permute-start(bf16[256,512]{1,0:T(8,128)(2,1)S(1)} %divide_convert_fusion), channel_id=1, source_target_pairs={{0,80},{1,112},{2,82},{3,114},{4,84},{5,116},{6,86},{7,118},{8,88}... | collective-permute-start | bytes 786440 | tf_op jit(solution)/shard_map/ppermute | solution.py:260
  8.2 16.3 %collective-permute-start.7 = (bf16[256,512]{1,0:T(8,128)(2,1)S(1)}, bf16[256,512]{1,0:T(8,128)(2,1)S(1)}, u32[]{:S(2)}, u32[]{:S(2)}) collective-permute-start(bf16[256,512]{1,0:T(8,128)(2,1)S(1)} %divide_convert_fusion), channel_id=1, source_target_pairs={{0,465},{1,497},{2,467},{3,499},{4,469},{5,501},{6,471},{7,503},{8... | collective-permute-start | bytes 786440 | tf_op jit(solution)/shard_map/ppermute | solution.py:261
  10.2 16.4 %collective-permute-start.6 = (bf16[256,512]{1,0:T(8,128)(2,1)S(1)}, bf16[256,512]{1,0:T(8,128)(2,1)S(1)}, u32[]{:S(2)}, u32[]{:S(2)}) collective-permute-start(bf16[256,512]{1,0:T(8,128)(2,1)S(1)} %divide_convert_fusion), channel_id=1, source_target_pairs={{0,16},{1,48},{2,18},{3,50},{4,20},{5,52},{6,22},{7,54},{8,24},{9,... | collective-permute-start | bytes 786440 | tf_op jit(solution)/shard_map/ppermute | solution.py:262
  15.7 12.4 %collective-permute-start.1 = (bf16[256,512]{1,0:T(8,128)(2,1)S(1)}, bf16[256,512]{1,0:T(8,128)(2,1)S(1)}, u32[]{:S(2)}, u32[]{:S(2)}) collective-permute-start(bf16[256,512]{1,0:T(8,128)(2,1)S(1)} %collective-permute-done.refs_1_), channel_id=1, source_target_pairs={{0,64},{1,449},{64,128},{65,1},{128,192},{129,65},{192,256},{193,1... | collective-permute-start | bytes 786440 | tf_op jit(solution)/shard_map/ppermute | solution.py:268
  18.5 27.1 %collective-permute-start.5 = (f32[2,256]{0,1:T(8,128)}, f32[2,256]{0,1:T(8,128)S(1)}, u32[]{:S(2)}, u32[]{:S(2)}) collective-permute-start(f32[2,256]{0,1:T(8,128)} %copy.10), channel_id=1, source_target_pairs={{0,16},{1,48},{2,18},{3,50},{4,20},{5,52},{6,22},{7,54},{8,24},{9,... | collective-permute-start | bytes 6152 | tf_op jit(solution)/shard_map/ppermute | solution.py:263
  24.5 9.9 %collective-permute-start.8 = (bf16[256,512]{1,0:T(8,128)(2,1)S(1)}, bf16[256,512]{1,0:T(8,128)(2,1)S(1)}, u32[]{:S(2)}, u32[]{:S(2)}) collective-permute-start(bf16[256,512]{1,0:T(8,128)(2,1)S(1)} %collective-permute-done.7.refs_2_), channel_id=1, source_target_pairs={{0,64},{1,449},{64,128},{65,1},{128,192},{129,65},{192,256},{193,1... | collective-permute-start | bytes 786440 | tf_op jit(solution)/shard_map/ppermute | solution.py:288
  28.1 9.8 %collective-permute-start.2 = (bf16[256,512]{1,0:T(8,128)(2,1)S(1)}, bf16[256,512]{1,0:T(8,128)(2,1)S(1)}, u32[]{:S(2)}, u32[]{:S(2)}) collective-permute-start(bf16[256,512]{1,0:T(8,128)(2,1)S(1)} %collective-permute-done.1.refs_3_), channel_id=1, source_target_pairs={{0,64},{1,449},{64,128},{65,1},{128,192},{129,65},{192,256},{193,1... | collective-permute-start | bytes 786440 | tf_op jit(solution)/shard_map/ppermute | solution.py:268
  34.4 10.4 %collective-permute-start.9 = (bf16[256,512]{1,0:T(8,128)(2,1)S(1)}, bf16[256,512]{1,0:T(8,128)(2,1)S(1)}, u32[]{:S(2)}, u32[]{:S(2)}) collective-permute-start(bf16[256,512]{1,0:T(8,128)(2,1)S(1)} %collective-permute-done.8.refs_4_), channel_id=1, source_target_pairs={{0,64},{1,449},{64,128},{65,1},{128,192},{129,65},{192,256},{193,1... | collective-permute-start | bytes 786440 | tf_op jit(solution)/shard_map/ppermute | solution.py:288
  37.8 8.4 %collective-permute-start.4 = (bf16[256,512]{1,0:T(8,128)(2,1)S(1)}, bf16[256,512]{1,0:T(8,128)(2,1)S(1)}, u32[]{:S(2)}, u32[]{:S(2)}) collective-permute-start(bf16[256,512]{1,0:T(8,128)(2,1)S(1)} %collective-permute-done.2.refs_5_), channel_id=1, source_target_pairs={{0,64},{1,449},{64,128},{65,1},{128,192},{129,65},{192,256},{193,1... | collective-permute-start | bytes 786440 | tf_op jit(solution)/shard_map/ppermute | solution.py:268
  46.9 8.4 %collective-permute-start.10 = (bf16[2048,512]{1,0:T(8,128)(2,1)}, bf16[2048,512]{1,0:T(8,128)(2,1)}, u32[]{:S(2)}, u32[]{:S(2)}) collective-permute-start(bf16[2048,512]{1,0:T(8,128)(2,1)} %constant_dynamic-update-slice_fusion.mine_hbm.mine_ref), channel_id=1, source_target_pairs={{0,1},{1,0},{2,3},{3,2},{4,5},{5,4},{6,7},{7,6},{8,9},{9,8},{10,11... | collective-permute-start | bytes 6291464 | tf_op jit(solution)/shard_map/ppermute | solution.py:300
  48.8 25.4 %collective-permute-start.11 = (bf16[256,2048]{1,0:T(8,128)(2,1)}, bf16[256,2048]{1,0:T(8,128)(2,1)}, u32[]{:S(2)}, u32[]{:S(2)}) collective-permute-start(bf16[256,2048]{1,0:T(8,128)(2,1)} %param.3), channel_id=1, source_target_pairs={{0,17},{1,49},{2,19},{3,51},{4,21},{5,53},{6,23},{7,55},{8,25},{9,... | collective-permute-start | bytes 3145736 | tf_op jit(solution)/shard_map/ppermute | solution.py:286
  52.8 24.3 %collective-permute-start.3 = (bf16[256,2048]{1,0:T(8,128)(2,1)}, bf16[256,2048]{1,0:T(8,128)(2,1)}, u32[]{:S(2)}, u32[]{:S(2)}) collective-permute-start(bf16[256,2048]{1,0:T(8,128)(2,1)} %param.3), channel_id=1, source_target_pairs={{0,16},{1,48},{2,18},{3,50},{4,20},{5,52},{6,22},{7,54},{8,24},{9,... | collective-permute-start | bytes 3145736 | tf_op jit(solution)/shard_map/ppermute | solution.py:285
  72.1 3.2 %collective-permute-start.12 = (bf16[256,256]{1,0:T(8,128)(2,1)S(1)}, bf16[256,256]{1,0:T(8,128)(2,1)S(1)}, u32[]{:S(2)}, u32[]{:S(2)}) collective-permute-start(bf16[256,256]{1,0:T(8,128)(2,1)S(1)} %get-tuple-element.16), channel_id=1, source_target_pairs={{0,1},{1,0},{2,3},{3,2},{4,5},{5,4},{6,7},{7,6},{8,9},{9,8},{10,11... | collective-permute-start | bytes 393224 | tf_op jit(solution)/shard_map/ppermute | solution.py:326

commit v11 on v10

--- a/solution.py
+++ b/solution.py
@@ -332,10 +332,10 @@
 
     partial = (contract(rows_here, kept) + contract(rows_beside, beside)).astype(jnp.bfloat16)
     tiles = partial.reshape(4, 2, 2, 2, 4, 2, 8, 256)
-    tiles = tiles.transpose(5, 3, 1, 2, 4, 0, 6, 7).reshape(16, 16 * 8, 256)
+    tiles = tiles.transpose(5, 3, 1, 2, 0, 4, 6, 7).reshape(16, 16 * 8, 256)
     received = lax.all_to_all(tiles, ("z0", "xl", "y0", "xh"), 0, 0)
     near_sum = received.astype(jnp.float32).sum(0).astype(jnp.bfloat16).reshape(16, 8, 256)
-    received = lax.all_to_all(near_sum, ("z2", "z1", "y2", "y1"), 0, 0)
+    received = lax.all_to_all(near_sum, ("y2", "y1", "z2", "z1"), 0, 0)
     fragment = received.astype(jnp.float32).sum(0).astype(jnp.bfloat16)
     spread = lax.all_to_all(
         jnp.broadcast_to(fragment[None], (32, 8, 256)), ("c", "xl", "z2", "z1", "z0"), 0, 0

time: 156 us -> 156 us (level)
  no operation moved by 1% of the time
where the time goes in v11:
time: 156 us; the launch traced here: 155 us
  blocking collectives  79 us (51%)
  starting transfers between devices  43.8 us (28%)
  Pallas kernels  16.1 us (10%)
  local copies, waits for them, and re-layouts  8.38 us (5%)
  matrix products  5.46 us (4%)
  waiting for transfers between devices  1.78 us (1%)
    all_to_all x1, blocking collectives, on_device(): received = lax.all_to_all(near_sum, ('y2', 'y1', 'z2', 'z1'), 0, 0)  24.4 us
    all_to_all x1, blocking collectives, on_device(): received = lax.all_to_all(tiles, ('z0', 'xl', 'y0', 'xh'), 0, 0)  24.3 us
    all_to_all x1, blocking collectives, on_device(): squares = lax.all_to_all(squares, ('y2', 'y1', 'y0', 'xh'), 0, 0)  13.3 us
    all_to_all x1, blocking collectives, on_device(): lax.all_to_all(jnp.broadcast_to(fragment[None], (32, 8, 256)), ('c', 'xl'...  13.2 us
    ppermute x3, starting transfers between devices, on_device(): same_core = lax.ppermute(same_core, (*YBITS, 'c'), ROUND)  11.8 us
    pallas_call x1, Pallas kernels, on_device(): kernel_call(pair_sums_kernel, jax.ShapeDtypeStruct((8, 1, 512), jnp.float...  7.15 us
    unnamed x11, local copies, waits for them, and re-layouts  6.64 us
    ppermute x1, starting transfers between devices, on_device(): side_here = lax.ppermute(side, BITS, TO_HOST)  6 us
  transfers between devices with their start and end apart: 13, of which 2 were waited for; matrix products, arithmetic and copies ran while one was open for 5% of the time, Pallas kernels for 10%

profile of v11, /device:TPU:8, one launch (start us, length us, event | category | flops | bytes accessed | tf_op | source)
XLA Modules:
  0.0 155.2 jit_solution(11915002833148841741)
XLA Ops:
  0.0 1.6 %copy-done = bf16[2048,512]{1,0:T(8,128)(2,1)S(1)} copy-done((bf16[2048,512]{1,0:T(8,128)(2,1)S(1)}, bf16[2048,512]{1,0:T(8,128)(2,1)}, u32[]{:S(2)}) %copy-start) | copy-done | bytes 2097176
  1.6 2.0 %multiply_reduce_fusion = (f32[256]{0:T(256)S(1)}, f32[256,512]{1,0:T(8,128)S(1)}) fusion(bf16[256,2048]{1,0:T(8,128)(2,1)} %param.3, bf16[2048,512]{1,0:T(8,128)(2,1)S(1)} %copy-done), kind=kOutput, calls=%fused_computation.3 | convolution fusion | flops 537132800 | bytes 3671040 | tf_op jit(solution)/shard_map/dot_general | solution.py:254
  3.8 4.4 %collective-permute-start = (bf16[256,512]{1,0:T(8,128)(2,1)S(1)}, bf16[256,512]{1,0:T(8,128)(2,1)S(1)}, u32[]{:S(2)}, u32[]{:S(2)}) collective-permute-start(bf16[256,512]{1,0:T(8,128)(2,1)S(1)} %divide_convert_fusion), channel_id=1, source_target_pairs={{0,80},{1,112},{2,82},{3,114},{4,84},{5,116},{6,86},{7,118},{8,88}... | collective-permute-start | bytes 786440 | tf_op jit(solution)/shard_map/ppermute | solution.py:260
  8.2 2.0 %collective-permute-start.7 = (bf16[256,512]{1,0:T(8,128)(2,1)S(1)}, bf16[256,512]{1,0:T(8,128)(2,1)S(1)}, u32[]{:S(2)}, u32[]{:S(2)}) collective-permute-start(bf16[256,512]{1,0:T(8,128)(2,1)S(1)} %divide_convert_fusion), channel_id=1, source_target_pairs={{0,465},{1,497},{2,467},{3,499},{4,469},{5,501},{6,471},{7,503},{8... | collective-permute-start | bytes 786440 | tf_op jit(solution)/shard_map/ppermute | solution.py:261
  10.2 5.4 %collective-permute-start.6 = (bf16[256,512]{1,0:T(8,128)(2,1)S(1)}, bf16[256,512]{1,0:T(8,128)(2,1)S(1)}, u32[]{:S(2)}, u32[]{:S(2)}) collective-permute-start(bf16[256,512]{1,0:T(8,128)(2,1)S(1)} %divide_convert_fusion), channel_id=1, source_target_pairs={{0,16},{1,48},{2,18},{3,50},{4,20},{5,52},{6,22},{7,54},{8,24},{9,... | collective-permute-start | bytes 786440 | tf_op jit(solution)/shard_map/ppermute | solution.py:262
  15.7 2.0 %collective-permute-start.1 = (bf16[256,512]{1,0:T(8,128)(2,1)S(1)}, bf16[256,512]{1,0:T(8,128)(2,1)S(1)}, u32[]{:S(2)}, u32[]{:S(2)}) collective-permute-start(bf16[256,512]{1,0:T(8,128)(2,1)S(1)} %collective-permute-done.refs_1_), channel_id=1, source_target_pairs={{0,64},{1,449},{64,128},{65,1},{128,192},{129,65},{192,256},{193,1... | collective-permute-start | bytes 786440 | tf_op jit(solution)/shard_map/ppermute | solution.py:268
  17.7 0.8 copy.10
  18.5 6.0 %collective-permute-start.5 = (f32[2,256]{0,1:T(8,128)}, f32[2,256]{0,1:T(8,128)S(1)}, u32[]{:S(2)}, u32[]{:S(2)}) collective-permute-start(f32[2,256]{0,1:T(8,128)} %copy.10), channel_id=1, source_target_pairs={{0,16},{1,48},{2,18},{3,50},{4,20},{5,52},{6,22},{7,54},{8,24},{9,... | collective-permute-start | bytes 6152 | tf_op jit(solution)/shard_map/ppermute | solution.py:263
  24.5 2.1 %collective-permute-start.8 = (bf16[256,512]{1,0:T(8,128)(2,1)S(1)}, bf16[256,512]{1,0:T(8,128)(2,1)S(1)}, u32[]{:S(2)}, u32[]{:S(2)}) collective-permute-start(bf16[256,512]{1,0:T(8,128)(2,1)S(1)} %collective-permute-done.7.refs_2_), channel_id=1, source_target_pairs={{0,64},{1,449},{64,128},{65,1},{128,192},{129,65},{192,256},{193,1... | collective-permute-start | bytes 786440 | tf_op jit(solution)/shard_map/ppermute | solution.py:288
  27.3 0.7 constant_dynamic-update-slice_fusion.6
  28.1 5.7 %collective-permute-start.2 = (bf16[256,512]{1,0:T(8,128)(2,1)S(1)}, bf16[256,512]{1,0:T(8,128)(2,1)S(1)}, u32[]{:S(2)}, u32[]{:S(2)}) collective-permute-start(bf16[256,512]{1,0:T(8,128)(2,1)S(1)} %collective-permute-done.1.refs_3_), channel_id=1, source_target_pairs={{0,64},{1,449},{64,128},{65,1},{128,192},{129,65},{192,256},{193,1... | collective-permute-start | bytes 786440 | tf_op jit(solution)/shard_map/ppermute | solution.py:268
  33.7 0.7 constant_dynamic-update-slice_fusion.5
  34.4 1.9 %collective-permute-start.9 = (bf16[256,512]{1,0:T(8,128)(2,1)S(1)}, bf16[256,512]{1,0:T(8,128)(2,1)S(1)}, u32[]{:S(2)}, u32[]{:S(2)}) collective-permute-start(bf16[256,512]{1,0:T(8,128)(2,1)S(1)} %collective-permute-done.8.refs_4_), channel_id=1, source_target_pairs={{0,64},{1,449},{64,128},{65,1},{128,192},{129,65},{192,256},{193,1... | collective-permute-start | bytes 786440 | tf_op jit(solution)/shard_map/ppermute | solution.py:288
  36.4 0.7 constant_dynamic-update-slice_fusion.4
  37.8 4.2 %collective-permute-start.4 = (bf16[256,512]{1,0:T(8,128)(2,1)S(1)}, bf16[256,512]{1,0:T(8,128)(2,1)S(1)}, u32[]{:S(2)}, u32[]{:S(2)}) collective-permute-start(bf16[256,512]{1,0:T(8,128)(2,1)S(1)} %collective-permute-done.2.refs_5_), channel_id=1, source_target_pairs={{0,64},{1,449},{64,128},{65,1},{128,192},{129,65},{192,256},{193,1... | collective-permute-start | bytes 786440 | tf_op jit(solution)/shard_map/ppermute | solution.py:268
  42.0 2.1 %early_sums.1.early_ref = f32[3,1,512]{2,1,0:T(1,128)S(1)} custom-call(bf16[256,512]{1,0:T(8,128)(2,1)S(1)} %collective-permute-done.6.refs_0_, bf16[256,512]{1,0:T(8,128)(2,1)S(1)} %collective-permute-done.refs_1_, bf16[256,512]{1,0:T(8,128)(2,1)S(1)} %collective-permute-done.7.refs_2_, bf16[256,512]{1,0:T(8,128)(2,1)S(1)} %collective-permute-done.1.refs_3_, ...), custom_call_target="tpu_custom_call" | custom-call | flops 2000000000 | bytes 2000000 | tf_op jit(solution)/shard_map/early_sums/pallas_call | solution.py:270
  44.9 0.7 constant_dynamic-update-slice_fusion.1
  46.9 1.9 %collective-permute-start.10 = (bf16[2048,512]{1,0:T(8,128)(2,1)}, bf16[2048,512]{1,0:T(8,128)(2,1)}, u32[]{:S(2)}, u32[]{:S(2)}) collective-permute-start(bf16[2048,512]{1,0:T(8,128)(2,1)} %constant_dynamic-update-slice_fusion.mine_hbm.mine_ref), channel_id=1, source_target_pairs={{0,1},{1,0},{2,3},{3,2},{4,5},{5,4},{6,7},{7,6},{8,9},{9,8},{10,11... | collective-permute-start | bytes 6291464 | tf_op jit(solution)/shard_map/ppermute | solution.py:300
  48.8 3.7 %collective-permute-start.11 = (bf16[256,2048]{1,0:T(8,128)(2,1)}, bf16[256,2048]{1,0:T(8,128)(2,1)}, u32[]{:S(2)}, u32[]{:S(2)}) collective-permute-start(bf16[256,2048]{1,0:T(8,128)(2,1)} %param.3), channel_id=1, source_target_pairs={{0,17},{1,49},{2,19},{3,51},{4,21},{5,53},{6,23},{7,55},{8,25},{9,... | collective-permute-start | bytes 3145736 | tf_op jit(solution)/shard_map/ppermute | solution.py:286
  52.8 2.5 %collective-permute-start.3 = (bf16[256,2048]{1,0:T(8,128)(2,1)}, bf16[256,2048]{1,0:T(8,128)(2,1)}, u32[]{:S(2)}, u32[]{:S(2)}) collective-permute-start(bf16[256,2048]{1,0:T(8,128)(2,1)} %param.3), channel_id=1, source_target_pairs={{0,16},{1,48},{2,18},{3,50},{4,20},{5,52},{6,22},{7,54},{8,24},{9,... | collective-permute-start | bytes 3145736 | tf_op jit(solution)/shard_map/ppermute | solution.py:285
  55.3 7.1 %pair_sums.1 = f32[8,1,512]{2,1,0:T(1,128)S(1)} custom-call(s32[1]{0:T(128)} %bitcast.core_ref, bf16[2048,512]{1,0:T(8,128)(2,1)} %constant_dynamic-update-slice_fusion.mine_hbm.mine_ref, bf16[2048,512]{1,0:T(8,128)(2,1)} %collective-permute-done.10.sibling_hbm.sibling_ref, f32[3,1,512]{2,1,0:T(1,128)S(1)} %early_sums.1.early_ref), custom_call_target="tpu_custom_call" | custom-call | flops 3000000000 | bytes 2000000 | tf_op jit(solution)/shard_map/pair_sums/pallas_call | solution.py:303
  62.5 3.8 %psum.7.sums_ref = f32[8,1,512]{2,1,0:T(1,128)S(1)} all-reduce(f32[8,1,512]{2,1,0:T(1,128)S(1)} %pair_sums.1), channel_id=1, replica_groups=mesh['y2'=2,'y1'=2,'y0'=2,'xh'=2,'xl'=2,'z2'=2,'z1'=2,'z0'=2,'c'=2] {'c'}, use_global_device_ids=true, to_apply=%region_1.2 | all-reduce | flops 4096 | bytes 32768 | tf_op jit(solution)/shard_map/psum | solution.py:316
  66.3 5.9 %weights.1 = (bf16[256,256]{1,0:T(8,128)(2,1)S(1)}, bf16[256,256]{1,0:T(8,128)(2,1)S(1)}) custom-call(s32[1]{0:T(128)} %bitcast.core_ref, s32[16]{0:T(128)S(1)} %broadcast_multiply_fusion.start_ref, f32[256,2]{1,0:T(8,128)S(1)} %bitcast.37, f32[8,1,512]{2,1,0:T(1,128)S(1)} %psum.7.sums_ref, ...), custom_call_target="tpu_custom_call" | custom-call | flops 2000000000 | bytes 2000000 | tf_op jit(solution)/shard_map/weights/pallas_call | solution.py:318
  72.1 2.1 %collective-permute-start.12 = (bf16[256,256]{1,0:T(8,128)(2,1)S(1)}, bf16[256,256]{1,0:T(8,128)(2,1)S(1)}, u32[]{:S(2)}, u32[]{:S(2)}) collective-permute-start(bf16[256,256]{1,0:T(8,128)(2,1)S(1)} %get-tuple-element.16), channel_id=1, source_target_pairs={{0,1},{1,0},{2,3},{3,2},{4,5},{5,4},{6,7},{7,6},{8,9},{9,8},{10,11... | collective-permute-start | bytes 393224 | tf_op jit(solution)/shard_map/ppermute | solution.py:326
  74.2 1.1 collective-permute-done.12
  75.4 1.7 %fusion.1 = f32[2048,256]{1,0:T(8,128)S(1)} fusion(bf16[256,2048]{1,0:T(8,128)(2,1)} %collective-permute-done.11, bf16[256,256]{1,0:T(8,128)(2,1)S(1)} %collective-permute-done.12), kind=kOutput, calls=%fused_computation.16 | convolution fusion | flops 268435456 | bytes 3276800 | tf_op jit(solution)/shard_map/dot_general | solution.py:329
  77.1 1.7 %fusion = bf16[2048,256]{1,0:T(8,128)(2,1)S(1)} fusion(f32[2048,256]{1,0:T(8,128)S(1)} %fusion.1, bf16[256,2048]{1,0:T(8,128)(2,1)} %collective-permute-done.3, bf16[256,256]{1,0:T(8,128)(2,1)S(1)} %get-tuple-element.15), kind=kOutput, calls=%fused_computation.1 | convolution fusion | flops 269484032 | bytes 4325376 | tf_op jit(solution)/shard_map/dot_general | solution.py:329
  79.0 24.3 %all_to_all.26 = bf16[16,128,256]{2,1,0:T(8,128)(2,1)S(1)} all-to-all(bf16[16,128,256]{2,1,0:T(8,128)(2,1)S(1)} %bitcast.38), channel_id=1, replica_groups=mesh['y2'=2,'y1'=2,'y0'=2,'xh'=2,'xl'=2,'z2'=2,'z1'=2,'z0'=2,'c'=2] {'z0..., dimensions={0} | all-to-all | bytes 2097152 | tf_op jit(solution)/shard_map/all_to_all | solution.py:336
  103.4 24.4 %all_to_all.27 = bf16[16,8,256]{2,1,0:T(8,128)(2,1)S(1)} all-to-all(bf16[16,8,256]{2,1,0:T(8,128)(2,1)S(1)} %bitcast.40), channel_id=1, replica_groups=mesh['y2'=2,'y1'=2,'y0'=2,'xh'=2,'xl'=2,'z2'=2,'z1'=2,'z0'=2,'c'=2] {'y2..., dimensions={0} | all-to-all | bytes 131072 | tf_op jit(solution)/shard_map/all_to_all | solution.py:338
  127.8 13.2 %all_to_all.28.spread_ref = bf16[32,8,256]{2,1,0:T(8,128)(2,1)S(1)} all-to-all(bf16[32,8,256]{2,1,0:T(8,128)(2,1)S(1)} %broadcast_in_dim.2), channel_id=1, replica_groups=mesh['y2'=2,'y1'=2,'y0'=2,'xh'=2,'xl'=2,'z2'=2,'z1'=2,'z0'=2,'c'=2] {'c'..., dimensions={0} | all-to-all | bytes 262144 | tf_op jit(solution)/shard_map/all_to_all | solution.py:340
  141.2 13.3 %all_to_all.29 = f32[16,1,128]{2,1,0:T(1,128)S(1)} all-to-all(f32[16,1,128]{2,1,0:T(1,128)S(1)} %bitcast.36), channel_id=1, replica_groups=mesh['y2'=2,'y1'=2,'y0'=2,'xh'=2,'xl'=2,'z2'=2,'z1'=2,'z0'=2,'c'=2] {'y2..., dimensions={0} | all-to-all | bytes 16384 | tf_op jit(solution)/shard_map/all_to_all | solution.py:346
  154.5 0.7 scale.1
  (30 shorter events, 4.2 us)
Async XLA Ops:
  0.0 1.6 %copy-start = (bf16[2048,512]{1,0:T(8,128)(2,1)S(1)}, bf16[2048,512]{1,0:T(8,128)(2,1)}, u32[]{:S(2)}) copy-start(bf16[2048,512]{1,0:T(8,128)(2,1)} %param.4) | copy-start | bytes 6291460
  1.6 14.0 %copy-start.1 = (s32[256]{0:T(256)S(1)}, s32[256]{0:T(256)}, u32[]{:S(2)}) copy-start(s32[256]{0:T(256)} %param.5) | copy-start | bytes 3076
  3.8 11.9 %collective-permute-start = (bf16[256,512]{1,0:T(8,128)(2,1)S(1)}, bf16[256,512]{1,0:T(8,128)(2,1)S(1)}, u32[]{:S(2)}, u32[]{:S(2)}) collective-permute-start(bf16[256,512]{1,0:T(8,128)(2,1)S(1)} %divide_convert_fusion), channel_id=1, source_target_pairs={{0,80},{1,112},{2,82},{3,114},{4,84},{5,116},{6,86},{7,118},{8,88}... | collective-permute-start | bytes 786440 | tf_op jit(solution)/shard_map/ppermute | solution.py:260
  8.2 16.3 %collective-permute-start.7 = (bf16[256,512]{1,0:T(8,128)(2,1)S(1)}, bf16[256,512]{1,0:T(8,128)(2,1)S(1)}, u32[]{:S(2)}, u32[]{:S(2)}) collective-permute-start(bf16[256,512]{1,0:T(8,128)(2,1)S(1)} %divide_convert_fusion), channel_id=1, source_target_pairs={{0,465},{1,497},{2,467},{3,499},{4,469},{5,501},{6,471},{7,503},{8... | collective-permute-start | bytes 786440 | tf_op jit(solution)/shard_map/ppermute | solution.py:261
  10.2 16.4 %collective-permute-start.6 = (bf16[256,512]{1,0:T(8,128)(2,1)S(1)}, bf16[256,512]{1,0:T(8,128)(2,1)S(1)}, u32[]{:S(2)}, u32[]{:S(2)}) collective-permute-start(bf16[256,512]{1,0:T(8,128)(2,1)S(1)} %divide_convert_fusion), channel_id=1, source_target_pairs={{0,16},{1,48},{2,18},{3,50},{4,20},{5,52},{6,22},{7,54},{8,24},{9,... | collective-permute-start | bytes 786440 | tf_op jit(solution)/shard_map/ppermute | solution.py:262
  15.7 12.4 %collective-permute-start.1 = (bf16[256,512]{1,0:T(8,128)(2,1)S(1)}, bf16[256,512]{1,0:T(8,128)(2,1)S(1)}, u32[]{:S(2)}, u32[]{:S(2)}) collective-permute-start(bf16[256,512]{1,0:T(8,128)(2,1)S(1)} %collective-permute-done.refs_1_), channel_id=1, source_target_pairs={{0,64},{1,449},{64,128},{65,1},{128,192},{129,65},{192,256},{193,1... | collective-permute-start | bytes 786440 | tf_op jit(solution)/shard_map/ppermute | solution.py:268
  18.5 27.1 %collective-permute-start.5 = (f32[2,256]{0,1:T(8,128)}, f32[2,256]{0,1:T(8,128)S(1)}, u32[]{:S(2)}, u32[]{:S(2)}) collective-permute-start(f32[2,256]{0,1:T(8,128)} %copy.10), channel_id=1, source_target_pairs={{0,16},{1,48},{2,18},{3,50},{4,20},{5,52},{6,22},{7,54},{8,24},{9,... | collective-permute-start | bytes 6152 | tf_op jit(solution)/shard_map/ppermute | solution.py:263
  24.5 9.9 %collective-permute-start.8 = (bf16[256,512]{1,0:T(8,128)(2,1)S(1)}, bf16[256,512]{1,0:T(8,128)(2,1)S(1)}, u32[]{:S(2)}, u32[]{:S(2)}) collective-permute-start(bf16[256,512]{1,0:T(8,128)(2,1)S(1)} %collective-permute-done.7.refs_2_), channel_id=1, source_target_pairs={{0,64},{1,449},{64,128},{65,1},{128,192},{129,65},{192,256},{193,1... | collective-permute-start | bytes 786440 | tf_op jit(solution)/shard_map/ppermute | solution.py:288
  28.1 9.8 %collective-permute-start.2 = (bf16[256,512]{1,0:T(8,128)(2,1)S(1)}, bf16[256,512]{1,0:T(8,128)(2,1)S(1)}, u32[]{:S(2)}, u32[]{:S(2)}) collective-permute-start(bf16[256,512]{1,0:T(8,128)(2,1)S(1)} %collective-permute-done.1.refs_3_), channel_id=1, source_target_pairs={{0,64},{1,449},{64,128},{65,1},{128,192},{129,65},{192,256},{193,1... | collective-permute-start | bytes 786440 | tf_op jit(solution)/shard_map/ppermute | solution.py:268
  34.4 10.4 %collective-permute-start.9 = (bf16[256,512]{1,0:T(8,128)(2,1)S(1)}, bf16[256,512]{1,0:T(8,128)(2,1)S(1)}, u32[]{:S(2)}, u32[]{:S(2)}) collective-permute-start(bf16[256,512]{1,0:T(8,128)(2,1)S(1)} %collective-permute-done.8.refs_4_), channel_id=1, source_target_pairs={{0,64},{1,449},{64,128},{65,1},{128,192},{129,65},{192,256},{193,1... | collective-permute-start | bytes 786440 | tf_op jit(solution)/shard_map/ppermute | solution.py:288
  37.8 8.4 %collective-permute-start.4 = (bf16[256,512]{1,0:T(8,128)(2,1)S(1)}, bf16[256,512]{1,0:T(8,128)(2,1)S(1)}, u32[]{:S(2)}, u32[]{:S(2)}) collective-permute-start(bf16[256,512]{1,0:T(8,128)(2,1)S(1)} %collective-permute-done.2.refs_5_), channel_id=1, source_target_pairs={{0,64},{1,449},{64,128},{65,1},{128,192},{129,65},{192,256},{193,1... | collective-permute-start | bytes 786440 | tf_op jit(solution)/shard_map/ppermute | solution.py:268
  46.9 8.4 %collective-permute-start.10 = (bf16[2048,512]{1,0:T(8,128)(2,1)}, bf16[2048,512]{1,0:T(8,128)(2,1)}, u32[]{:S(2)}, u32[]{:S(2)}) collective-permute-start(bf16[2048,512]{1,0:T(8,128)(2,1)} %constant_dynamic-update-slice_fusion.mine_hbm.mine_ref), channel_id=1, source_target_pairs={{0,1},{1,0},{2,3},{3,2},{4,5},{5,4},{6,7},{7,6},{8,9},{9,8},{10,11... | collective-permute-start | bytes 6291464 | tf_op jit(solution)/shard_map/ppermute | solution.py:300
  48.8 25.4 %collective-permute-start.11 = (bf16[256,2048]{1,0:T(8,128)(2,1)}, bf16[256,2048]{1,0:T(8,128)(2,1)}, u32[]{:S(2)}, u32[]{:S(2)}) collective-permute-start(bf16[256,2048]{1,0:T(8,128)(2,1)} %param.3), channel_id=1, source_target_pairs={{0,17},{1,49},{2,19},{3,51},{4,21},{5,53},{6,23},{7,55},{8,25},{9,... | collective-permute-start | bytes 3145736 | tf_op jit(solution)/shard_map/ppermute | solution.py:286
  52.8 24.3 %collective-permute-start.3 = (bf16[256,2048]{1,0:T(8,128)(2,1)}, bf16[256,2048]{1,0:T(8,128)(2,1)}, u32[]{:S(2)}, u32[]{:S(2)}) collective-permute-start(bf16[256,2048]{1,0:T(8,128)(2,1)} %param.3), channel_id=1, source_target_pairs={{0,16},{1,48},{2,18},{3,50},{4,20},{5,52},{6,22},{7,54},{8,24},{9,... | collective-permute-start | bytes 3145736 | tf_op jit(solution)/shard_map/ppermute | solution.py:285
  72.1 3.2 %collective-permute-start.12 = (bf16[256,256]{1,0:T(8,128)(2,1)S(1)}, bf16[256,256]{1,0:T(8,128)(2,1)S(1)}, u32[]{:S(2)}, u32[]{:S(2)}) collective-permute-start(bf16[256,256]{1,0:T(8,128)(2,1)S(1)} %get-tuple-element.16), channel_id=1, source_target_pairs={{0,1},{1,0},{2,3},{3,2},{4,5},{5,4},{6,7},{7,6},{8,9},{9,8},{10,11... | collective-permute-start | bytes 393224 | tf_op jit(solution)/shard_map/ppermute | solution.py:326

commit v12 on v11

--- a/solution.py
+++ b/solution.py
@@ -166,22 +166,32 @@
     start_ref,
     side_ref,
     sums_ref,
+    mine_hbm,
+    sibling_hbm,
+    keep_ref,
+    send_ref,
     mine_ref,
     sibling_ref,
-    keep_ref,
-    send_ref,
     weights,
+    semaphores,
 ):
     core = core_ref[0]
     wide = sums_ref.shape[2]
     blocks = sums_ref.shape[0] // 2
     rows = side_ref.shape[0]
+    copies = (
+        block_copies(mine_hbm, mine_ref, semaphores, (0,), 0)[0],
+        block_copies(sibling_hbm, sibling_ref, semaphores, (0,), 1)[0],
+    )
+    copies[0].wait()
     own = mine_ref[:rows, :]
     mine_sums = sums_ref[blocks * core][:, :rows]
     inverse_own = 1.0 / jnp.broadcast_to(mine_sums, (128, rows)).T[:, :1]
     partner = side_ref[:, 0:1].astype(jnp.int32)
     lanes = lax.broadcasted_iota(jnp.int32, (1, wide), 1)
     for part, ref in enumerate((mine_ref, sibling_ref)):
+        if part > 0:
+            copies[part].wait()
         for k in range(blocks):
             which = core if part == 0 else 1 - core
             right = ref[k * wide : (k + 1) * wide, :]
@@ -318,8 +328,8 @@
     kept, sent = kernel_call(
         weight_kernel,
         (piece, piece),
-        [SMEM, SMEM, VMEM, VMEM, VMEM, VMEM],
-        [pltpu.VMEM((2, 2 * rows, 8 * rows), jnp.bfloat16)],
+        [SMEM, SMEM, VMEM, VMEM, ANYWHERE, ANYWHERE],
+        held + [pltpu.VMEM((2, 2 * rows, 8 * rows), jnp.bfloat16), pltpu.SemaphoreType.DMA((2,))],
         2_000_000_000,
         "weights",
     )(core_scalar, starts, side_here.T, sums, mine, sibling)

time: 156 us -> 156 us (level)
  no operation moved by 1% of the time
where the time goes in v12:
time: 156 us
  blocking collectives  79 us (51%)
  starting transfers between devices  43.9 us (28%)
  Pallas kernels  16.3 us (10%)
  local copies, waits for them, and re-layouts  8.38 us (5%)
  matrix products  5.47 us (4%)
  waiting for transfers between devices  1.77 us (1%)
    all_to_all x1, blocking collectives, on_device(): received = lax.all_to_all(near_sum, ('y2', 'y1', 'z2', 'z1'), 0, 0)  24.4 us
    all_to_all x1, blocking collectives, on_device(): received = lax.all_to_all(tiles, ('z0', 'xl', 'y0', 'xh'), 0, 0)  24.2 us
    all_to_all x1, blocking collectives, on_device(): lax.all_to_all(jnp.broadcast_to(fragment[None], (32, 8, 256)), ('c', 'xl'...  13.4 us
    all_to_all x1, blocking collectives, on_device(): squares = lax.all_to_all(squares, ('y2', 'y1', 'y0', 'xh'), 0, 0)  13.3 us
    ppermute x3, starting transfers between devices, on_device(): same_core = lax.ppermute(same_core, (*YBITS, 'c'), ROUND)  11.8 us
    pallas_call x1, Pallas kernels, on_device(): kernel_call(pair_sums_kernel, jax.ShapeDtypeStruct((8, 1, 512), jnp.float...  7.15 us
    unnamed x11, local copies, waits for them, and re-layouts  6.64 us
    pallas_call x1, Pallas kernels, on_device(): kernel_call(weight_kernel, (piece, piece), [SMEM, SMEM, VMEM, VMEM, ANYWH...  6.03 us
  transfers between devices with their start and end apart: 13, of which 2 were waited for; matrix products, arithmetic and copies ran while one was open for 5% of the time, Pallas kernels for 10%

profile of v12, /device:TPU:8, one launch (start us, length us, event | category | flops | bytes accessed | tf_op | source)
XLA Modules:
  0.0 155.5 jit_solution(14139557446783113171)
XLA Ops:
  0.0 1.6 %copy-done = bf16[2048,512]{1,0:T(8,128)(2,1)S(1)} copy-done((bf16[2048,512]{1,0:T(8,128)(2,1)S(1)}, bf16[2048,512]{1,0:T(8,128)(2,1)}, u32[]{:S(2)}) %copy-start) | copy-done | bytes 2097176
  1.6 2.0 %multiply_reduce_fusion = (f32[256]{0:T(256)S(1)}, f32[256,512]{1,0:T(8,128)S(1)}) fusion(bf16[256,2048]{1,0:T(8,128)(2,1)} %param.3, bf16[2048,512]{1,0:T(8,128)(2,1)S(1)} %copy-done), kind=kOutput, calls=%fused_computation.3 | convolution fusion | flops 537132800 | bytes 3671040 | tf_op jit(solution)/shard_map/dot_general | solution.py:264
  3.8 4.4 %collective-permute-start = (bf16[256,512]{1,0:T(8,128)(2,1)S(1)}, bf16[256,512]{1,0:T(8,128)(2,1)S(1)}, u32[]{:S(2)}, u32[]{:S(2)}) collective-permute-start(bf16[256,512]{1,0:T(8,128)(2,1)S(1)} %divide_convert_fusion), channel_id=1, source_target_pairs={{0,80},{1,112},{2,82},{3,114},{4,84},{5,116},{6,86},{7,118},{8,88}... | collective-permute-start | bytes 786440 | tf_op jit(solution)/shard_map/ppermute | solution.py:270
  8.2 2.0 %collective-permute-start.7 = (bf16[256,512]{1,0:T(8,128)(2,1)S(1)}, bf16[256,512]{1,0:T(8,128)(2,1)S(1)}, u32[]{:S(2)}, u32[]{:S(2)}) collective-permute-start(bf16[256,512]{1,0:T(8,128)(2,1)S(1)} %divide_convert_fusion), channel_id=1, source_target_pairs={{0,465},{1,497},{2,467},{3,499},{4,469},{5,501},{6,471},{7,503},{8... | collective-permute-start | bytes 786440 | tf_op jit(solution)/shard_map/ppermute | solution.py:271
  10.2 5.4 %collective-permute-start.6 = (bf16[256,512]{1,0:T(8,128)(2,1)S(1)}, bf16[256,512]{1,0:T(8,128)(2,1)S(1)}, u32[]{:S(2)}, u32[]{:S(2)}) collective-permute-start(bf16[256,512]{1,0:T(8,128)(2,1)S(1)} %divide_convert_fusion), channel_id=1, source_target_pairs={{0,16},{1,48},{2,18},{3,50},{4,20},{5,52},{6,22},{7,54},{8,24},{9,... | collective-permute-start | bytes 786440 | tf_op jit(solution)/shard_map/ppermute | solution.py:272
  15.7 2.0 %collective-permute-start.1 = (bf16[256,512]{1,0:T(8,128)(2,1)S(1)}, bf16[256,512]{1,0:T(8,128)(2,1)S(1)}, u32[]{:S(2)}, u32[]{:S(2)}) collective-permute-start(bf16[256,512]{1,0:T(8,128)(2,1)S(1)} %collective-permute-done.refs_1_), channel_id=1, source_target_pairs={{0,64},{1,449},{64,128},{65,1},{128,192},{129,65},{192,256},{193,1... | collective-permute-start | bytes 786440 | tf_op jit(solution)/shard_map/ppermute | solution.py:278
  17.7 0.8 copy.10
  18.5 6.0 %collective-permute-start.5 = (f32[2,256]{0,1:T(8,128)}, f32[2,256]{0,1:T(8,128)S(1)}, u32[]{:S(2)}, u32[]{:S(2)}) collective-permute-start(f32[2,256]{0,1:T(8,128)} %copy.10), channel_id=1, source_target_pairs={{0,16},{1,48},{2,18},{3,50},{4,20},{5,52},{6,22},{7,54},{8,24},{9,... | collective-permute-start | bytes 6152 | tf_op jit(solution)/shard_map/ppermute | solution.py:273
  24.5 2.1 %collective-permute-start.8 = (bf16[256,512]{1,0:T(8,128)(2,1)S(1)}, bf16[256,512]{1,0:T(8,128)(2,1)S(1)}, u32[]{:S(2)}, u32[]{:S(2)}) collective-permute-start(bf16[256,512]{1,0:T(8,128)(2,1)S(1)} %collective-permute-done.7.refs_2_), channel_id=1, source_target_pairs={{0,64},{1,449},{64,128},{65,1},{128,192},{129,65},{192,256},{193,1... | collective-permute-start | bytes 786440 | tf_op jit(solution)/shard_map/ppermute | solution.py:298
  27.3 0.7 constant_dynamic-update-slice_fusion.6
  28.1 5.7 %collective-permute-start.2 = (bf16[256,512]{1,0:T(8,128)(2,1)S(1)}, bf16[256,512]{1,0:T(8,128)(2,1)S(1)}, u32[]{:S(2)}, u32[]{:S(2)}) collective-permute-start(bf16[256,512]{1,0:T(8,128)(2,1)S(1)} %collective-permute-done.1.refs_3_), channel_id=1, source_target_pairs={{0,64},{1,449},{64,128},{65,1},{128,192},{129,65},{192,256},{193,1... | collective-permute-start | bytes 786440 | tf_op jit(solution)/shard_map/ppermute | solution.py:278
  33.7 0.7 constant_dynamic-update-slice_fusion.5
  34.4 1.9 %collective-permute-start.9 = (bf16[256,512]{1,0:T(8,128)(2,1)S(1)}, bf16[256,512]{1,0:T(8,128)(2,1)S(1)}, u32[]{:S(2)}, u32[]{:S(2)}) collective-permute-start(bf16[256,512]{1,0:T(8,128)(2,1)S(1)} %collective-permute-done.8.refs_4_), channel_id=1, source_target_pairs={{0,64},{1,449},{64,128},{65,1},{128,192},{129,65},{192,256},{193,1... | collective-permute-start | bytes 786440 | tf_op jit(solution)/shard_map/ppermute | solution.py:298
  36.4 0.7 constant_dynamic-update-slice_fusion.4
  37.8 4.2 %collective-permute-start.4 = (bf16[256,512]{1,0:T(8,128)(2,1)S(1)}, bf16[256,512]{1,0:T(8,128)(2,1)S(1)}, u32[]{:S(2)}, u32[]{:S(2)}) collective-permute-start(bf16[256,512]{1,0:T(8,128)(2,1)S(1)} %collective-permute-done.2.refs_5_), channel_id=1, source_target_pairs={{0,64},{1,449},{64,128},{65,1},{128,192},{129,65},{192,256},{193,1... | collective-permute-start | bytes 786440 | tf_op jit(solution)/shard_map/ppermute | solution.py:278
  42.0 2.1 %early_sums.1.early_ref = f32[3,1,512]{2,1,0:T(1,128)S(1)} custom-call(bf16[256,512]{1,0:T(8,128)(2,1)S(1)} %collective-permute-done.6.refs_0_, bf16[256,512]{1,0:T(8,128)(2,1)S(1)} %collective-permute-done.refs_1_, bf16[256,512]{1,0:T(8,128)(2,1)S(1)} %collective-permute-done.7.refs_2_, bf16[256,512]{1,0:T(8,128)(2,1)S(1)} %collective-permute-done.1.refs_3_, ...), custom_call_target="tpu_custom_call" | custom-call | flops 2000000000 | bytes 2000000 | tf_op jit(solution)/shard_map/early_sums/pallas_call | solution.py:280
  44.9 0.7 constant_dynamic-update-slice_fusion.1
  46.9 1.9 %collective-permute-start.10 = (bf16[2048,512]{1,0:T(8,128)(2,1)}, bf16[2048,512]{1,0:T(8,128)(2,1)}, u32[]{:S(2)}, u32[]{:S(2)}) collective-permute-start(bf16[2048,512]{1,0:T(8,128)(2,1)} %constant_dynamic-update-slice_fusion.mine_hbm), channel_id=1, source_target_pairs={{0,1},{1,0},{2,3},{3,2},{4,5},{5,4},{6,7},{7,6},{8,9},{9,8},{10,11... | collective-permute-start | bytes 6291464 | tf_op jit(solution)/shard_map/ppermute | solution.py:310
  48.8 3.7 %collective-permute-start.11 = (bf16[256,2048]{1,0:T(8,128)(2,1)}, bf16[256,2048]{1,0:T(8,128)(2,1)}, u32[]{:S(2)}, u32[]{:S(2)}) collective-permute-start(bf16[256,2048]{1,0:T(8,128)(2,1)} %param.3), channel_id=1, source_target_pairs={{0,17},{1,49},{2,19},{3,51},{4,21},{5,53},{6,23},{7,55},{8,25},{9,... | collective-permute-start | bytes 3145736 | tf_op jit(solution)/shard_map/ppermute | solution.py:296
  52.8 2.5 %collective-permute-start.3 = (bf16[256,2048]{1,0:T(8,128)(2,1)}, bf16[256,2048]{1,0:T(8,128)(2,1)}, u32[]{:S(2)}, u32[]{:S(2)}) collective-permute-start(bf16[256,2048]{1,0:T(8,128)(2,1)} %param.3), channel_id=1, source_target_pairs={{0,16},{1,48},{2,18},{3,50},{4,20},{5,52},{6,22},{7,54},{8,24},{9,... | collective-permute-start | bytes 3145736 | tf_op jit(solution)/shard_map/ppermute | solution.py:295
  55.3 7.1 %pair_sums.1 = f32[8,1,512]{2,1,0:T(1,128)S(1)} custom-call(s32[1]{0:T(128)} %bitcast.core_ref, bf16[2048,512]{1,0:T(8,128)(2,1)} %constant_dynamic-update-slice_fusion.mine_hbm, bf16[2048,512]{1,0:T(8,128)(2,1)} %collective-permute-done.10.sibling_hbm, f32[3,1,512]{2,1,0:T(1,128)S(1)} %early_sums.1.early_ref), custom_call_target="tpu_custom_call" | custom-call | flops 3000000000 | bytes 2000000 | tf_op jit(solution)/shard_map/pair_sums/pallas_call | solution.py:313
  62.5 3.8 %psum.7.sums_ref = f32[8,1,512]{2,1,0:T(1,128)S(1)} all-reduce(f32[8,1,512]{2,1,0:T(1,128)S(1)} %pair_sums.1), channel_id=1, replica_groups=mesh['y2'=2,'y1'=2,'y0'=2,'xh'=2,'xl'=2,'z2'=2,'z1'=2,'z0'=2,'c'=2] {'c'}, use_global_device_ids=true, to_apply=%region_1.2 | all-reduce | flops 4096 | bytes 32768 | tf_op jit(solution)/shard_map/psum | solution.py:326
  66.3 6.0 %weights.1 = (bf16[256,256]{1,0:T(8,128)(2,1)S(1)}, bf16[256,256]{1,0:T(8,128)(2,1)S(1)}) custom-call(s32[1]{0:T(128)} %bitcast.core_ref, s32[16]{0:T(128)S(1)} %broadcast_multiply_fusion.start_ref, f32[256,2]{1,0:T(8,128)S(1)} %bitcast.37, f32[8,1,512]{2,1,0:T(1,128)S(1)} %psum.7.sums_ref, bf16[2048,512]{1,0:T(8,128)(2,1)} %constant_dynamic-update-slice_fusion.mine_hbm, ...), custom_call_target="tpu_custom_call" | custom-call | flops 2000000000 | bytes 2000000 | tf_op jit(solution)/shard_map/weights/pallas_call | solution.py:328
  72.3 2.1 %collective-permute-start.12 = (bf16[256,256]{1,0:T(8,128)(2,1)S(1)}, bf16[256,256]{1,0:T(8,128)(2,1)S(1)}, u32[]{:S(2)}, u32[]{:S(2)}) collective-permute-start(bf16[256,256]{1,0:T(8,128)(2,1)S(1)} %get-tuple-element.16), channel_id=1, source_target_pairs={{0,1},{1,0},{2,3},{3,2},{4,5},{5,4},{6,7},{7,6},{8,9},{9,8},{10,11... | collective-permute-start | bytes 393224 | tf_op jit(solution)/shard_map/ppermute | solution.py:336
  74.4 1.1 collective-permute-done.12
  75.5 1.7 %fusion.1 = f32[2048,256]{1,0:T(8,128)S(1)} fusion(bf16[256,2048]{1,0:T(8,128)(2,1)} %collective-permute-done.11, bf16[256,256]{1,0:T(8,128)(2,1)S(1)} %collective-permute-done.12), kind=kOutput, calls=%fused_computation.16 | convolution fusion | flops 268435456 | bytes 3276800 | tf_op jit(solution)/shard_map/dot_general | solution.py:339
  77.3 1.7 %fusion = bf16[2048,256]{1,0:T(8,128)(2,1)S(1)} fusion(f32[2048,256]{1,0:T(8,128)S(1)} %fusion.1, bf16[256,2048]{1,0:T(8,128)(2,1)} %collective-permute-done.3, bf16[256,256]{1,0:T(8,128)(2,1)S(1)} %get-tuple-element.15), kind=kOutput, calls=%fused_computation.1 | convolution fusion | flops 269484032 | bytes 4325376 | tf_op jit(solution)/shard_map/dot_general | solution.py:339
  79.1 24.2 %all_to_all.26 = bf16[16,128,256]{2,1,0:T(8,128)(2,1)S(1)} all-to-all(bf16[16,128,256]{2,1,0:T(8,128)(2,1)S(1)} %bitcast.38), channel_id=1, replica_groups=mesh['y2'=2,'y1'=2,'y0'=2,'xh'=2,'xl'=2,'z2'=2,'z1'=2,'z0'=2,'c'=2] {'z0..., dimensions={0} | all-to-all | bytes 2097152 | tf_op jit(solution)/shard_map/all_to_all | solution.py:346
  103.5 24.4 %all_to_all.27 = bf16[16,8,256]{2,1,0:T(8,128)(2,1)S(1)} all-to-all(bf16[16,8,256]{2,1,0:T(8,128)(2,1)S(1)} %bitcast.40), channel_id=1, replica_groups=mesh['y2'=2,'y1'=2,'y0'=2,'xh'=2,'xl'=2,'z2'=2,'z1'=2,'z0'=2,'c'=2] {'y2..., dimensions={0} | all-to-all | bytes 131072 | tf_op jit(solution)/shard_map/all_to_all | solution.py:348
  128.0 13.4 %all_to_all.28.spread_ref = bf16[32,8,256]{2,1,0:T(8,128)(2,1)S(1)} all-to-all(bf16[32,8,256]{2,1,0:T(8,128)(2,1)S(1)} %broadcast_in_dim.2), channel_id=1, replica_groups=mesh['y2'=2,'y1'=2,'y0'=2,'xh'=2,'xl'=2,'z2'=2,'z1'=2,'z0'=2,'c'=2] {'c'..., dimensions={0} | all-to-all | bytes 262144 | tf_op jit(solution)/shard_map/all_to_all | solution.py:350
  141.5 13.3 %all_to_all.29 = f32[16,1,128]{2,1,0:T(1,128)S(1)} all-to-all(f32[16,1,128]{2,1,0:T(1,128)S(1)} %bitcast.36), channel_id=1, replica_groups=mesh['y2'=2,'y1'=2,'y0'=2,'xh'=2,'xl'=2,'z2'=2,'z1'=2,'z0'=2,'c'=2] {'y2..., dimensions={0} | all-to-all | bytes 16384 | tf_op jit(solution)/shard_map/all_to_all | solution.py:356
  154.8 0.7 scale.1
  (30 shorter events, 4.2 us)
Async XLA Ops:
  0.0 1.6 %copy-start = (bf16[2048,512]{1,0:T(8,128)(2,1)S(1)}, bf16[2048,512]{1,0:T(8,128)(2,1)}, u32[]{:S(2)}) copy-start(bf16[2048,512]{1,0:T(8,128)(2,1)} %param.4) | copy-start | bytes 6291460
  1.6 14.0 %copy-start.1 = (s32[256]{0:T(256)S(1)}, s32[256]{0:T(256)}, u32[]{:S(2)}) copy-start(s32[256]{0:T(256)} %param.5) | copy-start | bytes 3076
  3.8 11.9 %collective-permute-start = (bf16[256,512]{1,0:T(8,128)(2,1)S(1)}, bf16[256,512]{1,0:T(8,128)(2,1)S(1)}, u32[]{:S(2)}, u32[]{:S(2)}) collective-permute-start(bf16[256,512]{1,0:T(8,128)(2,1)S(1)} %divide_convert_fusion), channel_id=1, source_target_pairs={{0,80},{1,112},{2,82},{3,114},{4,84},{5,116},{6,86},{7,118},{8,88}... | collective-permute-start | bytes 786440 | tf_op jit(solution)/shard_map/ppermute | solution.py:270
  8.2 16.3 %collective-permute-start.7 = (bf16[256,512]{1,0:T(8,128)(2,1)S(1)}, bf16[256,512]{1,0:T(8,128)(2,1)S(1)}, u32[]{:S(2)}, u32[]{:S(2)}) collective-permute-start(bf16[256,512]{1,0:T(8,128)(2,1)S(1)} %divide_convert_fusion), channel_id=1, source_target_pairs={{0,465},{1,497},{2,467},{3,499},{4,469},{5,501},{6,471},{7,503},{8... | collective-permute-start | bytes 786440 | tf_op jit(solution)/shard_map/ppermute | solution.py:271
  10.2 16.4 %collective-permute-start.6 = (bf16[256,512]{1,0:T(8,128)(2,1)S(1)}, bf16[256,512]{1,0:T(8,128)(2,1)S(1)}, u32[]{:S(2)}, u32[]{:S(2)}) collective-permute-start(bf16[256,512]{1,0:T(8,128)(2,1)S(1)} %divide_convert_fusion), channel_id=1, source_target_pairs={{0,16},{1,48},{2,18},{3,50},{4,20},{5,52},{6,22},{7,54},{8,24},{9,... | collective-permute-start | bytes 786440 | tf_op jit(solution)/shard_map/ppermute | solution.py:272
  15.7 12.4 %collective-permute-start.1 = (bf16[256,512]{1,0:T(8,128)(2,1)S(1)}, bf16[256,512]{1,0:T(8,128)(2,1)S(1)}, u32[]{:S(2)}, u32[]{:S(2)}) collective-permute-start(bf16[256,512]{1,0:T(8,128)(2,1)S(1)} %collective-permute-done.refs_1_), channel_id=1, source_target_pairs={{0,64},{1,449},{64,128},{65,1},{128,192},{129,65},{192,256},{193,1... | collective-permute-start | bytes 786440 | tf_op jit(solution)/shard_map/ppermute | solution.py:278
  18.5 27.1 %collective-permute-start.5 = (f32[2,256]{0,1:T(8,128)}, f32[2,256]{0,1:T(8,128)S(1)}, u32[]{:S(2)}, u32[]{:S(2)}) collective-permute-start(f32[2,256]{0,1:T(8,128)} %copy.10), channel_id=1, source_target_pairs={{0,16},{1,48},{2,18},{3,50},{4,20},{5,52},{6,22},{7,54},{8,24},{9,... | collective-permute-start | bytes 6152 | tf_op jit(solution)/shard_map/ppermute | solution.py:273
  24.5 9.9 %collective-permute-start.8 = (bf16[256,512]{1,0:T(8,128)(2,1)S(1)}, bf16[256,512]{1,0:T(8,128)(2,1)S(1)}, u32[]{:S(2)}, u32[]{:S(2)}) collective-permute-start(bf16[256,512]{1,0:T(8,128)(2,1)S(1)} %collective-permute-done.7.refs_2_), channel_id=1, source_target_pairs={{0,64},{1,449},{64,128},{65,1},{128,192},{129,65},{192,256},{193,1... | collective-permute-start | bytes 786440 | tf_op jit(solution)/shard_map/ppermute | solution.py:298
  28.1 9.8 %collective-permute-start.2 = (bf16[256,512]{1,0:T(8,128)(2,1)S(1)}, bf16[256,512]{1,0:T(8,128)(2,1)S(1)}, u32[]{:S(2)}, u32[]{:S(2)}) collective-permute-start(bf16[256,512]{1,0:T(8,128)(2,1)S(1)} %collective-permute-done.1.refs_3_), channel_id=1, source_target_pairs={{0,64},{1,449},{64,128},{65,1},{128,192},{129,65},{192,256},{193,1... | collective-permute-start | bytes 786440 | tf_op jit(solution)/shard_map/ppermute | solution.py:278
  34.4 10.4 %collective-permute-start.9 = (bf16[256,512]{1,0:T(8,128)(2,1)S(1)}, bf16[256,512]{1,0:T(8,128)(2,1)S(1)}, u32[]{:S(2)}, u32[]{:S(2)}) collective-permute-start(bf16[256,512]{1,0:T(8,128)(2,1)S(1)} %collective-permute-done.8.refs_4_), channel_id=1, source_target_pairs={{0,64},{1,449},{64,128},{65,1},{128,192},{129,65},{192,256},{193,1... | collective-permute-start | bytes 786440 | tf_op jit(solution)/shard_map/ppermute | solution.py:298
  37.8 8.4 %collective-permute-start.4 = (bf16[256,512]{1,0:T(8,128)(2,1)S(1)}, bf16[256,512]{1,0:T(8,128)(2,1)S(1)}, u32[]{:S(2)}, u32[]{:S(2)}) collective-permute-start(bf16[256,512]{1,0:T(8,128)(2,1)S(1)} %collective-permute-done.2.refs_5_), channel_id=1, source_target_pairs={{0,64},{1,449},{64,128},{65,1},{128,192},{129,65},{192,256},{193,1... | collective-permute-start | bytes 786440 | tf_op jit(solution)/shard_map/ppermute | solution.py:278
  46.9 8.4 %collective-permute-start.10 = (bf16[2048,512]{1,0:T(8,128)(2,1)}, bf16[2048,512]{1,0:T(8,128)(2,1)}, u32[]{:S(2)}, u32[]{:S(2)}) collective-permute-start(bf16[2048,512]{1,0:T(8,128)(2,1)} %constant_dynamic-update-slice_fusion.mine_hbm), channel_id=1, source_target_pairs={{0,1},{1,0},{2,3},{3,2},{4,5},{5,4},{6,7},{7,6},{8,9},{9,8},{10,11... | collective-permute-start | bytes 6291464 | tf_op jit(solution)/shard_map/ppermute | solution.py:310
  48.8 25.6 %collective-permute-start.11 = (bf16[256,2048]{1,0:T(8,128)(2,1)}, bf16[256,2048]{1,0:T(8,128)(2,1)}, u32[]{:S(2)}, u32[]{:S(2)}) collective-permute-start(bf16[256,2048]{1,0:T(8,128)(2,1)} %param.3), channel_id=1, source_target_pairs={{0,17},{1,49},{2,19},{3,51},{4,21},{5,53},{6,23},{7,55},{8,25},{9,... | collective-permute-start | bytes 3145736 | tf_op jit(solution)/shard_map/ppermute | solution.py:296
  52.8 24.5 %collective-permute-start.3 = (bf16[256,2048]{1,0:T(8,128)(2,1)}, bf16[256,2048]{1,0:T(8,128)(2,1)}, u32[]{:S(2)}, u32[]{:S(2)}) collective-permute-start(bf16[256,2048]{1,0:T(8,128)(2,1)} %param.3), channel_id=1, source_target_pairs={{0,16},{1,48},{2,18},{3,50},{4,20},{5,52},{6,22},{7,54},{8,24},{9,... | collective-permute-start | bytes 3145736 | tf_op jit(solution)/shard_map/ppermute | solution.py:295
  72.3 3.2 %collective-permute-start.12 = (bf16[256,256]{1,0:T(8,128)(2,1)S(1)}, bf16[256,256]{1,0:T(8,128)(2,1)S(1)}, u32[]{:S(2)}, u32[]{:S(2)}) collective-permute-start(bf16[256,256]{1,0:T(8,128)(2,1)S(1)} %get-tuple-element.16), channel_id=1, source_target_pairs={{0,1},{1,0},{2,3},{3,2},{4,5},{5,4},{6,7},{7,6},{8,9},{9,8},{10,11... | collective-permute-start | bytes 393224 | tf_op jit(solution)/shard_map/ppermute | solution.py:336

commit v13 on v11

--- a/solution.py
+++ b/solution.py
@@ -29,7 +29,7 @@
     return (((y * 2 + xh) * 2 + xl) * 8 + z) * 2 + core
 
 
-TO_HOST, TO_SIBLING = moves(0, 0), moves(1, 0)
+TO_HOST = moves(0, 0)
 TO_NEXT_SAME, TO_NEXT_OTHER = moves(0, 1), moves(1, 1)
 ROUND = [(2 * y + c, 2 * ((y + (1, -1)[c]) % Y) + c) for y in range(Y) for c in range(2)]
 
@@ -283,7 +283,6 @@
         if distance == 3:
             later, unused = lax.optimization_barrier((features, same_core))
             rows_here = lax.ppermute(later, BITS, TO_HOST)
-            rows_beside = lax.ppermute(later, BITS, TO_SIBLING)
         if distance > 1:
             other_core = lax.ppermute(other_core, (*YBITS, "c"), ROUND)
         pieces.append(other_core)
@@ -323,14 +322,14 @@
         2_000_000_000,
         "weights",
     )(core_scalar, starts, side_here.T, sums, mine, sibling)
-    beside = lax.ppermute(sent, "c", OTHER_CORE)
-
     def contract(left, right):
         return lax.dot_general(
             left, right, (((0,), (0,)), ((), ())), preferred_element_type=jnp.float32
         )
 
-    partial = (contract(rows_here, kept) + contract(rows_beside, beside)).astype(jnp.bfloat16)
+    theirs = contract(rows_here, sent).astype(jnp.bfloat16)
+    arrived = lax.ppermute(theirs, "c", OTHER_CORE)
+    partial = (contract(rows_here, kept) + arrived.astype(jnp.float32)).astype(jnp.bfloat16)
     tiles = partial.reshape(4, 2, 2, 2, 4, 2, 8, 256)
     tiles = tiles.transpose(5, 3, 1, 2, 0, 4, 6, 7).reshape(16, 16 * 8, 256)
     received = lax.all_to_all(tiles, ("z0", "xl", "y0", "xh"), 0, 0)

time: 156 us -> 155 us (level)
  starting transfers between devices: 43.8 us -> 41.4 us
  waiting for transfers between devices: 1.78 us -> 3.52 us
    ppermute x2 -> x1, starting transfers between devices: 5.8 us -> 2.25 us  [on_device(): arrived = lax.ppermute(theirs, 'c', OTHER_CORE)]
  transfers between devices with their start and end apart: 13 -> 12, of which waited for: 2 -> 3; matrix products, arithmetic and copies ran while one was open for 5% -> 4% of each run, Pallas kernels for 10% -> 10%
where the time goes in v13:
time: 155 us
  blocking collectives  79 us (51%)
  starting transfers between devices  41.4 us (27%)
  Pallas kernels  16.1 us (10%)
  local copies, waits for them, and re-layouts  8.36 us (5%)
  matrix products  5.45 us (4%)
  waiting for transfers between devices  3.52 us (2%)
    all_to_all x1, blocking collectives, on_device(): received = lax.all_to_all(tiles, ('z0', 'xl', 'y0', 'xh'), 0, 0)  24.6 us
    all_to_all x1, blocking collectives, on_device(): received = lax.all_to_all(near_sum, ('y2', 'y1', 'z2', 'z1'), 0, 0)  24.4 us
    all_to_all x1, blocking collectives, on_device(): lax.all_to_all(jnp.broadcast_to(fragment[None], (32, 8, 256)), ('c', 'xl'...  13.4 us
    all_to_all x1, blocking collectives, on_device(): squares = lax.all_to_all(squares, ('y2', 'y1', 'y0', 'xh'), 0, 0)  13.3 us
    ppermute x3, starting transfers between devices, on_device(): same_core = lax.ppermute(same_core, (*YBITS, 'c'), ROUND)  11.8 us
    pallas_call x1, Pallas kernels, on_device(): kernel_call(pair_sums_kernel, jax.ShapeDtypeStruct((8, 1, 512), jnp.float...  7.14 us
    unnamed x11, local copies, waits for them, and re-layouts  6.61 us
    ppermute x1, starting transfers between devices, on_device(): side_here = lax.ppermute(side, BITS, TO_HOST)  6 us
  transfers between devices with their start and end apart: 12, of which 3 were waited for; matrix products, arithmetic and copies ran while one was open for 4% of the time, Pallas kernels for 10%

profile of v13, /device:TPU:8, one launch (start us, length us, event | category | flops | bytes accessed | tf_op | source)
XLA Modules:
  0.0 154.6 jit_solution(2843320207832655680)
XLA Ops:
  0.0 1.6 %copy-done = bf16[2048,512]{1,0:T(8,128)(2,1)S(1)} copy-done((bf16[2048,512]{1,0:T(8,128)(2,1)S(1)}, bf16[2048,512]{1,0:T(8,128)(2,1)}, u32[]{:S(2)}) %copy-start) | copy-done | bytes 2097176
  1.6 2.0 %multiply_reduce_fusion = (f32[256]{0:T(256)S(1)}, f32[256,512]{1,0:T(8,128)S(1)}) fusion(bf16[256,2048]{1,0:T(8,128)(2,1)} %param.3, bf16[2048,512]{1,0:T(8,128)(2,1)S(1)} %copy-done), kind=kOutput, calls=%fused_computation.4 | convolution fusion | flops 537132800 | bytes 3671040 | tf_op jit(solution)/shard_map/dot_general | solution.py:254
  3.8 4.4 %collective-permute-start = (bf16[256,512]{1,0:T(8,128)(2,1)S(1)}, bf16[256,512]{1,0:T(8,128)(2,1)S(1)}, u32[]{:S(2)}, u32[]{:S(2)}) collective-permute-start(bf16[256,512]{1,0:T(8,128)(2,1)S(1)} %divide_convert_fusion), channel_id=1, source_target_pairs={{0,80},{1,112},{2,82},{3,114},{4,84},{5,116},{6,86},{7,118},{8,88}... | collective-permute-start | bytes 786440 | tf_op jit(solution)/shard_map/ppermute | solution.py:260
  8.2 2.0 %collective-permute-start.7 = (bf16[256,512]{1,0:T(8,128)(2,1)S(1)}, bf16[256,512]{1,0:T(8,128)(2,1)S(1)}, u32[]{:S(2)}, u32[]{:S(2)}) collective-permute-start(bf16[256,512]{1,0:T(8,128)(2,1)S(1)} %divide_convert_fusion), channel_id=1, source_target_pairs={{0,465},{1,497},{2,467},{3,499},{4,469},{5,501},{6,471},{7,503},{8... | collective-permute-start | bytes 786440 | tf_op jit(solution)/shard_map/ppermute | solution.py:261
  10.2 5.4 %collective-permute-start.6 = (bf16[256,512]{1,0:T(8,128)(2,1)S(1)}, bf16[256,512]{1,0:T(8,128)(2,1)S(1)}, u32[]{:S(2)}, u32[]{:S(2)}) collective-permute-start(bf16[256,512]{1,0:T(8,128)(2,1)S(1)} %divide_convert_fusion), channel_id=1, source_target_pairs={{0,16},{1,48},{2,18},{3,50},{4,20},{5,52},{6,22},{7,54},{8,24},{9,... | collective-permute-start | bytes 786440 | tf_op jit(solution)/shard_map/ppermute | solution.py:262
  15.7 2.0 %collective-permute-start.1 = (bf16[256,512]{1,0:T(8,128)(2,1)S(1)}, bf16[256,512]{1,0:T(8,128)(2,1)S(1)}, u32[]{:S(2)}, u32[]{:S(2)}) collective-permute-start(bf16[256,512]{1,0:T(8,128)(2,1)S(1)} %collective-permute-done.refs_1_), channel_id=1, source_target_pairs={{0,64},{1,449},{64,128},{65,1},{128,192},{129,65},{192,256},{193,1... | collective-permute-start | bytes 786440 | tf_op jit(solution)/shard_map/ppermute | solution.py:268
  17.7 0.8 copy.10
  18.5 6.0 %collective-permute-start.5 = (f32[2,256]{0,1:T(8,128)}, f32[2,256]{0,1:T(8,128)S(1)}, u32[]{:S(2)}, u32[]{:S(2)}) collective-permute-start(f32[2,256]{0,1:T(8,128)} %copy.10), channel_id=1, source_target_pairs={{0,16},{1,48},{2,18},{3,50},{4,20},{5,52},{6,22},{7,54},{8,24},{9,... | collective-permute-start | bytes 6152 | tf_op jit(solution)/shard_map/ppermute | solution.py:263
  24.5 2.1 %collective-permute-start.8 = (bf16[256,512]{1,0:T(8,128)(2,1)S(1)}, bf16[256,512]{1,0:T(8,128)(2,1)S(1)}, u32[]{:S(2)}, u32[]{:S(2)}) collective-permute-start(bf16[256,512]{1,0:T(8,128)(2,1)S(1)} %collective-permute-done.7.refs_2_), channel_id=1, source_target_pairs={{0,64},{1,449},{64,128},{65,1},{128,192},{129,65},{192,256},{193,1... | collective-permute-start | bytes 786440 | tf_op jit(solution)/shard_map/ppermute | solution.py:287
  26.6 0.7 constant_dynamic-update-slice_fusion.7
  27.3 0.7 constant_dynamic-update-slice_fusion.6
  28.1 5.7 %collective-permute-start.2 = (bf16[256,512]{1,0:T(8,128)(2,1)S(1)}, bf16[256,512]{1,0:T(8,128)(2,1)S(1)}, u32[]{:S(2)}, u32[]{:S(2)}) collective-permute-start(bf16[256,512]{1,0:T(8,128)(2,1)S(1)} %collective-permute-done.1.refs_3_), channel_id=1, source_target_pairs={{0,64},{1,449},{64,128},{65,1},{128,192},{129,65},{192,256},{193,1... | collective-permute-start | bytes 786440 | tf_op jit(solution)/shard_map/ppermute | solution.py:268
  33.7 0.7 constant_dynamic-update-slice_fusion.5
  34.5 1.9 %collective-permute-start.9 = (bf16[256,512]{1,0:T(8,128)(2,1)S(1)}, bf16[256,512]{1,0:T(8,128)(2,1)S(1)}, u32[]{:S(2)}, u32[]{:S(2)}) collective-permute-start(bf16[256,512]{1,0:T(8,128)(2,1)S(1)} %collective-permute-done.8.refs_4_), channel_id=1, source_target_pairs={{0,64},{1,449},{64,128},{65,1},{128,192},{129,65},{192,256},{193,1... | collective-permute-start | bytes 786440 | tf_op jit(solution)/shard_map/ppermute | solution.py:287
  36.4 0.7 constant_dynamic-update-slice_fusion.4
  37.8 4.2 %collective-permute-start.4 = (bf16[256,512]{1,0:T(8,128)(2,1)S(1)}, bf16[256,512]{1,0:T(8,128)(2,1)S(1)}, u32[]{:S(2)}, u32[]{:S(2)}) collective-permute-start(bf16[256,512]{1,0:T(8,128)(2,1)S(1)} %collective-permute-done.2.refs_5_), channel_id=1, source_target_pairs={{0,64},{1,449},{64,128},{65,1},{128,192},{129,65},{192,256},{193,1... | collective-permute-start | bytes 786440 | tf_op jit(solution)/shard_map/ppermute | solution.py:268
  42.0 2.1 %early_sums.1.early_ref = f32[3,1,512]{2,1,0:T(1,128)S(1)} custom-call(bf16[256,512]{1,0:T(8,128)(2,1)S(1)} %collective-permute-done.6.refs_0_, bf16[256,512]{1,0:T(8,128)(2,1)S(1)} %collective-permute-done.refs_1_, bf16[256,512]{1,0:T(8,128)(2,1)S(1)} %collective-permute-done.7.refs_2_, bf16[256,512]{1,0:T(8,128)(2,1)S(1)} %collective-permute-done.1.refs_3_, ...), custom_call_target="tpu_custom_call" | custom-call | flops 2000000000 | bytes 2000000 | tf_op jit(solution)/shard_map/early_sums/pallas_call | solution.py:270
  46.2 0.7 constant_dynamic-update-slice_fusion.mine_hbm.mine_ref
  46.9 1.9 %collective-permute-start.10 = (bf16[2048,512]{1,0:T(8,128)(2,1)}, bf16[2048,512]{1,0:T(8,128)(2,1)}, u32[]{:S(2)}, u32[]{:S(2)}) collective-permute-start(bf16[2048,512]{1,0:T(8,128)(2,1)} %constant_dynamic-update-slice_fusion.mine_hbm.mine_ref), channel_id=1, source_target_pairs={{0,1},{1,0},{2,3},{3,2},{4,5},{5,4},{6,7},{7,6},{8,9},{9,8},{10,11... | collective-permute-start | bytes 6291464 | tf_op jit(solution)/shard_map/ppermute | solution.py:299
  48.8 3.6 %collective-permute-start.3 = (bf16[256,2048]{1,0:T(8,128)(2,1)}, bf16[256,2048]{1,0:T(8,128)(2,1)}, u32[]{:S(2)}, u32[]{:S(2)}) collective-permute-start(bf16[256,2048]{1,0:T(8,128)(2,1)} %param.3), channel_id=1, source_target_pairs={{0,16},{1,48},{2,18},{3,50},{4,20},{5,52},{6,22},{7,54},{8,24},{9,... | collective-permute-start | bytes 3145736 | tf_op jit(solution)/shard_map/ppermute | solution.py:285
  53.3 7.1 %pair_sums.1 = f32[8,1,512]{2,1,0:T(1,128)S(1)} custom-call(s32[1]{0:T(128)} %bitcast.core_ref, bf16[2048,512]{1,0:T(8,128)(2,1)} %constant_dynamic-update-slice_fusion.mine_hbm.mine_ref, bf16[2048,512]{1,0:T(8,128)(2,1)} %collective-permute-done.10.sibling_hbm.sibling_ref, f32[3,1,512]{2,1,0:T(1,128)S(1)} %early_sums.1.early_ref), custom_call_target="tpu_custom_call" | custom-call | flops 3000000000 | bytes 2000000 | tf_op jit(solution)/shard_map/pair_sums/pallas_call | solution.py:302
  60.4 3.4 %psum.7.sums_ref = f32[8,1,512]{2,1,0:T(1,128)S(1)} all-reduce(f32[8,1,512]{2,1,0:T(1,128)S(1)} %pair_sums.1), channel_id=1, replica_groups=mesh['y2'=2,'y1'=2,'y0'=2,'xh'=2,'xl'=2,'z2'=2,'z1'=2,'z0'=2,'c'=2] {'c'}, use_global_device_ids=true, to_apply=%region_1.2 | all-reduce | flops 4096 | bytes 32768 | tf_op jit(solution)/shard_map/psum | solution.py:315
  63.8 5.9 %weights.1 = (bf16[256,256]{1,0:T(8,128)(2,1)S(1)}, bf16[256,256]{1,0:T(8,128)(2,1)S(1)}) custom-call(s32[1]{0:T(128)} %bitcast.core_ref, s32[16]{0:T(128)S(1)} %broadcast_multiply_fusion.start_ref, f32[256,2]{1,0:T(8,128)S(1)} %bitcast.37, f32[8,1,512]{2,1,0:T(1,128)S(1)} %psum.7.sums_ref, ...), custom_call_target="tpu_custom_call" | custom-call | flops 2000000000 | bytes 2000000 | tf_op jit(solution)/shard_map/weights/pallas_call | solution.py:317
  69.7 1.7 %convolution_convert_fusion = bf16[2048,256]{1,0:T(8,128)(2,1)S(1)} fusion(bf16[256,2048]{1,0:T(8,128)(2,1)} %collective-permute-done.3, bf16[256,256]{1,0:T(8,128)(2,1)S(1)} %get-tuple-element.16), kind=kOutput, calls=%fused_computation.2 | convolution fusion | flops 268959744 | bytes 2228224 | tf_op jit(solution)/shard_map/dot_general | solution.py:326
  71.4 2.2 %collective-permute-start.11 = (bf16[2048,256]{1,0:T(8,128)(2,1)S(1)}, bf16[2048,256]{1,0:T(8,128)(2,1)S(1)}, u32[]{:S(2)}, u32[]{:S(2)}) collective-permute-start(bf16[2048,256]{1,0:T(8,128)(2,1)S(1)} %convolution_convert_fusion), channel_id=1, source_target_pairs={{0,1},{1,0},{2,3},{3,2},{4,5},{5,4},{6,7},{7,6},{8,9},{9,8},{10,11... | collective-permute-start | bytes 3145736 | tf_op jit(solution)/shard_map/ppermute | solution.py:331
  73.6 2.3 %collective-permute-done.11 = bf16[2048,256]{1,0:T(8,128)(2,1)S(1)} collective-permute-done((bf16[2048,256]{1,0:T(8,128)(2,1)S(1)}, bf16[2048,256]{1,0:T(8,128)(2,1)S(1)}, u32[]{:S(2)}, u32[]{:S(2)}) %collective-permute-start.11) | collective-permute-done | bytes 1048608 | tf_op jit(solution)/shard_map/ppermute | solution.py:331
  75.9 1.7 %fusion = bf16[2048,256]{1,0:T(8,128)(2,1)S(1)} fusion(bf16[256,2048]{1,0:T(8,128)(2,1)} %collective-permute-done.3, bf16[256,256]{1,0:T(8,128)(2,1)S(1)} %get-tuple-element.15, bf16[2048,256]{1,0:T(8,128)(2,1)S(1)} %collective-permute-done.11), kind=kOutput, calls=%fused_computation.1 | convolution fusion | flops 270008320 | bytes 3276800 | tf_op jit(solution)/shard_map/dot_general | solution.py:326
  77.8 24.6 %all_to_all.26 = bf16[16,128,256]{2,1,0:T(8,128)(2,1)S(1)} all-to-all(bf16[16,128,256]{2,1,0:T(8,128)(2,1)S(1)} %bitcast.39), channel_id=1, replica_groups=mesh['y2'=2,'y1'=2,'y0'=2,'xh'=2,'xl'=2,'z2'=2,'z1'=2,'z0'=2,'c'=2] {'z0..., dimensions={0} | all-to-all | bytes 2097152 | tf_op jit(solution)/shard_map/all_to_all | solution.py:335
  102.5 24.4 %all_to_all.27 = bf16[16,8,256]{2,1,0:T(8,128)(2,1)S(1)} all-to-all(bf16[16,8,256]{2,1,0:T(8,128)(2,1)S(1)} %bitcast.40), channel_id=1, replica_groups=mesh['y2'=2,'y1'=2,'y0'=2,'xh'=2,'xl'=2,'z2'=2,'z1'=2,'z0'=2,'c'=2] {'y2..., dimensions={0} | all-to-all | bytes 131072 | tf_op jit(solution)/shard_map/all_to_all | solution.py:337
  127.0 13.4 %all_to_all.28.spread_ref = bf16[32,8,256]{2,1,0:T(8,128)(2,1)S(1)} all-to-all(bf16[32,8,256]{2,1,0:T(8,128)(2,1)S(1)} %broadcast_in_dim.2), channel_id=1, replica_groups=mesh['y2'=2,'y1'=2,'y0'=2,'xh'=2,'xl'=2,'z2'=2,'z1'=2,'z0'=2,'c'=2] {'c'..., dimensions={0} | all-to-all | bytes 262144 | tf_op jit(solution)/shard_map/all_to_all | solution.py:339
  140.6 13.3 %all_to_all.29 = f32[16,1,128]{2,1,0:T(1,128)S(1)} all-to-all(f32[16,1,128]{2,1,0:T(1,128)S(1)} %bitcast.36), channel_id=1, replica_groups=mesh['y2'=2,'y1'=2,'y0'=2,'xh'=2,'xl'=2,'z2'=2,'z1'=2,'z0'=2,'c'=2] {'y2..., dimensions={0} | all-to-all | bytes 16384 | tf_op jit(solution)/shard_map/all_to_all | solution.py:345
  153.9 0.7 scale.1
  (28 shorter events, 4.1 us)
Async XLA Ops:
  0.0 1.6 %copy-start = (bf16[2048,512]{1,0:T(8,128)(2,1)S(1)}, bf16[2048,512]{1,0:T(8,128)(2,1)}, u32[]{:S(2)}) copy-start(bf16[2048,512]{1,0:T(8,128)(2,1)} %param.4) | copy-start | bytes 6291460
  1.6 14.0 %copy-start.1 = (s32[256]{0:T(256)S(1)}, s32[256]{0:T(256)}, u32[]{:S(2)}) copy-start(s32[256]{0:T(256)} %param.5) | copy-start | bytes 3076
  3.8 11.9 %collective-permute-start = (bf16[256,512]{1,0:T(8,128)(2,1)S(1)}, bf16[256,512]{1,0:T(8,128)(2,1)S(1)}, u32[]{:S(2)}, u32[]{:S(2)}) collective-permute-start(bf16[256,512]{1,0:T(8,128)(2,1)S(1)} %divide_convert_fusion), channel_id=1, source_target_pairs={{0,80},{1,112},{2,82},{3,114},{4,84},{5,116},{6,86},{7,118},{8,88}... | collective-permute-start | bytes 786440 | tf_op jit(solution)/shard_map/ppermute | solution.py:260
  8.2 16.3 %collective-permute-start.7 = (bf16[256,512]{1,0:T(8,128)(2,1)S(1)}, bf16[256,512]{1,0:T(8,128)(2,1)S(1)}, u32[]{:S(2)}, u32[]{:S(2)}) collective-permute-start(bf16[256,512]{1,0:T(8,128)(2,1)S(1)} %divide_convert_fusion), channel_id=1, source_target_pairs={{0,465},{1,497},{2,467},{3,499},{4,469},{5,501},{6,471},{7,503},{8... | collective-permute-start | bytes 786440 | tf_op jit(solution)/shard_map/ppermute | solution.py:261
  10.2 16.4 %collective-permute-start.6 = (bf16[256,512]{1,0:T(8,128)(2,1)S(1)}, bf16[256,512]{1,0:T(8,128)(2,1)S(1)}, u32[]{:S(2)}, u32[]{:S(2)}) collective-permute-start(bf16[256,512]{1,0:T(8,128)(2,1)S(1)} %divide_convert_fusion), channel_id=1, source_target_pairs={{0,16},{1,48},{2,18},{3,50},{4,20},{5,52},{6,22},{7,54},{8,24},{9,... | collective-permute-start | bytes 786440 | tf_op jit(solution)/shard_map/ppermute | solution.py:262
  15.7 12.4 %collective-permute-start.1 = (bf16[256,512]{1,0:T(8,128)(2,1)S(1)}, bf16[256,512]{1,0:T(8,128)(2,1)S(1)}, u32[]{:S(2)}, u32[]{:S(2)}) collective-permute-start(bf16[256,512]{1,0:T(8,128)(2,1)S(1)} %collective-permute-done.refs_1_), channel_id=1, source_target_pairs={{0,64},{1,449},{64,128},{65,1},{128,192},{129,65},{192,256},{193,1... | collective-permute-start | bytes 786440 | tf_op jit(solution)/shard_map/ppermute | solution.py:268
  18.5 27.1 %collective-permute-start.5 = (f32[2,256]{0,1:T(8,128)}, f32[2,256]{0,1:T(8,128)S(1)}, u32[]{:S(2)}, u32[]{:S(2)}) collective-permute-start(f32[2,256]{0,1:T(8,128)} %copy.10), channel_id=1, source_target_pairs={{0,16},{1,48},{2,18},{3,50},{4,20},{5,52},{6,22},{7,54},{8,24},{9,... | collective-permute-start | bytes 6152 | tf_op jit(solution)/shard_map/ppermute | solution.py:263
  24.5 9.9 %collective-permute-start.8 = (bf16[256,512]{1,0:T(8,128)(2,1)S(1)}, bf16[256,512]{1,0:T(8,128)(2,1)S(1)}, u32[]{:S(2)}, u32[]{:S(2)}) collective-permute-start(bf16[256,512]{1,0:T(8,128)(2,1)S(1)} %collective-permute-done.7.refs_2_), channel_id=1, source_target_pairs={{0,64},{1,449},{64,128},{65,1},{128,192},{129,65},{192,256},{193,1... | collective-permute-start | bytes 786440 | tf_op jit(solution)/shard_map/ppermute | solution.py:287
  28.1 9.8 %collective-permute-start.2 = (bf16[256,512]{1,0:T(8,128)(2,1)S(1)}, bf16[256,512]{1,0:T(8,128)(2,1)S(1)}, u32[]{:S(2)}, u32[]{:S(2)}) collective-permute-start(bf16[256,512]{1,0:T(8,128)(2,1)S(1)} %collective-permute-done.1.refs_3_), channel_id=1, source_target_pairs={{0,64},{1,449},{64,128},{65,1},{128,192},{129,65},{192,256},{193,1... | collective-permute-start | bytes 786440 | tf_op jit(solution)/shard_map/ppermute | solution.py:268
  34.5 10.4 %collective-permute-start.9 = (bf16[256,512]{1,0:T(8,128)(2,1)S(1)}, bf16[256,512]{1,0:T(8,128)(2,1)S(1)}, u32[]{:S(2)}, u32[]{:S(2)}) collective-permute-start(bf16[256,512]{1,0:T(8,128)(2,1)S(1)} %collective-permute-done.8.refs_4_), channel_id=1, source_target_pairs={{0,64},{1,449},{64,128},{65,1},{128,192},{129,65},{192,256},{193,1... | collective-permute-start | bytes 786440 | tf_op jit(solution)/shard_map/ppermute | solution.py:287
  37.8 8.4 %collective-permute-start.4 = (bf16[256,512]{1,0:T(8,128)(2,1)S(1)}, bf16[256,512]{1,0:T(8,128)(2,1)S(1)}, u32[]{:S(2)}, u32[]{:S(2)}) collective-permute-start(bf16[256,512]{1,0:T(8,128)(2,1)S(1)} %collective-permute-done.2.refs_5_), channel_id=1, source_target_pairs={{0,64},{1,449},{64,128},{65,1},{128,192},{129,65},{192,256},{193,1... | collective-permute-start | bytes 786440 | tf_op jit(solution)/shard_map/ppermute | solution.py:268
  46.9 6.4 %collective-permute-start.10 = (bf16[2048,512]{1,0:T(8,128)(2,1)}, bf16[2048,512]{1,0:T(8,128)(2,1)}, u32[]{:S(2)}, u32[]{:S(2)}) collective-permute-start(bf16[2048,512]{1,0:T(8,128)(2,1)} %constant_dynamic-update-slice_fusion.mine_hbm.mine_ref), channel_id=1, source_target_pairs={{0,1},{1,0},{2,3},{3,2},{4,5},{5,4},{6,7},{7,6},{8,9},{9,8},{10,11... | collective-permute-start | bytes 6291464 | tf_op jit(solution)/shard_map/ppermute | solution.py:299
  48.8 20.8 %collective-permute-start.3 = (bf16[256,2048]{1,0:T(8,128)(2,1)}, bf16[256,2048]{1,0:T(8,128)(2,1)}, u32[]{:S(2)}, u32[]{:S(2)}) collective-permute-start(bf16[256,2048]{1,0:T(8,128)(2,1)} %param.3), channel_id=1, source_target_pairs={{0,16},{1,48},{2,18},{3,50},{4,20},{5,52},{6,22},{7,54},{8,24},{9,... | collective-permute-start | bytes 3145736 | tf_op jit(solution)/shard_map/ppermute | solution.py:285
  71.4 4.6 %collective-permute-start.11 = (bf16[2048,256]{1,0:T(8,128)(2,1)S(1)}, bf16[2048,256]{1,0:T(8,128)(2,1)S(1)}, u32[]{:S(2)}, u32[]{:S(2)}) collective-permute-start(bf16[2048,256]{1,0:T(8,128)(2,1)S(1)} %convolution_convert_fusion), channel_id=1, source_target_pairs={{0,1},{1,0},{2,3},{3,2},{4,5},{5,4},{6,7},{7,6},{8,9},{9,8},{10,11... | collective-permute-start | bytes 3145736 | tf_op jit(solution)/shard_map/ppermute | solution.py:331

commit v14 on v9

--- a/solution.py
+++ b/solution.py
@@ -29,7 +29,7 @@
     return (((y * 2 + xh) * 2 + xl) * 8 + z) * 2 + core
 
 
-TO_HOST, TO_SIBLING = moves(0, 0), moves(1, 0)
+TO_HOST = moves(0, 0)
 TO_NEXT_SAME, TO_NEXT_OTHER = moves(0, 1), moves(1, 1)
 ROUND = [(2 * y + c, 2 * ((y + (1, -1)[c]) % Y) + c) for y in range(Y) for c in range(2)]
 
@@ -225,7 +225,7 @@
         squares = hidden[...] * hidden[...]
         inverse = 1.0 / jnp.sqrt(jnp.sum(squares, axis=1, keepdims=True) + 1e-05)
         unit_ref[...] = (hidden[...] * inverse).astype(jnp.bfloat16)
-        inverse_ref[...] = 1.0 / jnp.sqrt(row_totals(over_lane_groups(squares)) + 1e-05)
+        inverse_ref[...] = jnp.broadcast_to(inverse, (inverse.shape[0], 128)).T[0:1, :]
 
 
 def units(features, head_weight):
@@ -265,12 +265,11 @@
     total = jnp.sum(squares_ref[...], axis=0, keepdims=True)
     entries = 16 * update_ref.shape[0] * update_ref.shape[1]
     scale = 1.0 / jnp.sqrt(total * (1.0 / entries) + 1e-06)
+    scale = jnp.concatenate([scale, scale], axis=1)
     for core in range(2):
         for row in range(16):
-            for half in range(2):
-                column = 256 * half + 128 * core
-                tile = spread_ref[16 * core + row, half].astype(jnp.float32)
-                update_ref[8 * row : 8 * row + 8, column : column + 128] = tile * scale
+            tile = spread_ref[16 * core + row].astype(jnp.float32)
+            update_ref[8 * row : 8 * row + 8, 256 * core : 256 * core + 256] = tile * scale
 
 
 VMEM = pl.BlockSpec(memory_space=pltpu.VMEM)
@@ -330,7 +329,6 @@
         if distance == 3:
             later, unused = lax.optimization_barrier((features, same_core))
             rows_here = lax.ppermute(later, BITS, TO_HOST)
-            rows_beside = lax.ppermute(later, BITS, TO_SIBLING)
         if distance > 1:
             other_core = lax.ppermute(other_core, (*YBITS, "c"), ROUND)
         pieces.append(other_core)
@@ -370,20 +368,23 @@
         2_000_000_000,
         "weights",
     )(core_scalar, starts, side_here.T, sums, mine, sibling)
-    beside = lax.ppermute(sent, "c", OTHER_CORE)
-
     def contract(left, right):
         return lax.dot_general(
             left, right, (((0,), (0,)), ((), ())), preferred_element_type=jnp.float32
         )
 
-    partial = (contract(rows_here, kept) + contract(rows_beside, beside)).astype(jnp.bfloat16)
-    tiles = partial.reshape(*(2,) * 8, 8, 2, 128)
-    tiles = tiles.transpose(9, 7, 6, 5, 4, 3, 2, 1, 0, 8, 10).reshape(512, 8, 128)
-    received = lax.all_to_all(tiles, BITS[::-1], 0, 0).reshape(2, 256, 8, 128)
-    fragment = received.astype(jnp.float32).sum(1).astype(jnp.bfloat16)
+    theirs = contract(rows_here, sent).astype(jnp.bfloat16)
+    arrived = lax.ppermute(theirs, "c", OTHER_CORE)
+    ours, arrived = lax.optimization_barrier((contract(rows_here, kept), arrived))
+    partial = (ours + arrived.astype(jnp.float32)).astype(jnp.bfloat16)
+    tiles = partial.reshape(4, 2, 2, 2, 4, 2, 8, 256)
+    tiles = tiles.transpose(5, 3, 1, 2, 0, 4, 6, 7).reshape(16, 16 * 8, 256)
+    received = lax.all_to_all(tiles, ("z0", "xl", "y0", "xh"), 0, 0)
+    near_sum = received.astype(jnp.float32).sum(0).astype(jnp.bfloat16).reshape(16, 8, 256)
+    received = lax.all_to_all(near_sum, ("y2", "y1", "z2", "z1"), 0, 0)
+    fragment = received.astype(jnp.float32).sum(0).astype(jnp.bfloat16)
     spread = lax.all_to_all(
-        jnp.broadcast_to(fragment[None], (32, 2, 8, 128)), ("c", "xl", "z2", "z1", "z0"), 0, 0
+        jnp.broadcast_to(fragment[None], (32, 8, 256)), ("c", "xl", "z2", "z1", "z0"), 0, 0
     )
     squares = kernel_call(
         squares_kernel, jax.ShapeDtypeStruct((16, 128), jnp.float32), [VMEM], [], 100_000, "squares"

time: 163 us -> 152 us (0.933)
  blocking collectives: 85.6 us -> 79.1 us
  starting transfers between devices: 42.9 us -> 40.6 us
    all_to_all x2 -> x3, blocking collectives: 67.9 us -> 62.4 us  [the longest x1 26.5 us: on_device(): received = lax.all_to_all(near_sum, ('y2', 'y1', 'z2', 'z1'), 0, 0)]
    ppermute x1, waiting for transfers between devices: 2.59 us -> 0.01 us  [on_device(): rows_here = lax.ppermute(later, BITS, TO_HOST)]
    ppermute x2 -> x1, starting transfers between devices: 4.18 us -> 2.25 us  [on_device(): arrived = lax.ppermute(theirs, 'c', OTHER_CORE)]
    ppermute x1, waiting for transfers between devices: 0.01 us -> 1.93 us  [on_device(): sibling = lax.ppermute(mine, 'c', OTHER_CORE)]
  transfers between devices with their start and end apart: 13 -> 12, of which waited for: 6 -> 6; matrix products, arithmetic and copies ran while one was open for 2% -> 2% of each run, Pallas kernels for 8% -> 9%
where the time goes in v14:
time: 152 us
  blocking collectives  79.1 us (52%)
  starting transfers between devices  40.6 us (27%)
  Pallas kernels  18.9 us (12%)
  waiting for transfers between devices  7.42 us (5%)
  matrix products  3.43 us (2%)
    all_to_all x1, blocking collectives, on_device(): received = lax.all_to_all(near_sum, ('y2', 'y1', 'z2', 'z1'), 0, 0)  26.5 us
    all_to_all x1, blocking collectives, on_device(): received = lax.all_to_all(tiles, ('z0', 'xl', 'y0', 'xh'), 0, 0)  22.5 us
    all_to_all x1, blocking collectives, on_device(): lax.all_to_all(jnp.broadcast_to(fragment[None], (32, 8, 256)), ('c', 'xl'...  13.4 us
    all_to_all x1, blocking collectives, on_device(): squares = lax.all_to_all(squares, ('y2', 'y1', 'y0', 'xh'), 0, 0)  13.3 us
    ppermute x3, starting transfers between devices, on_device(): same_core = lax.ppermute(same_core, (*YBITS, 'c'), ROUND)  11.4 us
    pallas_call x1, Pallas kernels, on_device(): kernel_call(pair_sums_kernel, jax.ShapeDtypeStruct((8, 1, 512), jnp.float...  6.28 us
    ppermute x1, starting transfers between devices, on_device(): side_here = lax.ppermute(side, BITS, TO_HOST)  5.9 us
    ppermute x1, starting transfers between devices, on_device(): own = lax.ppermute(unit, BITS, TO_HOST)  5.39 us
  transfers between devices with their start and end apart: 12, of which 6 were waited for; matrix products, arithmetic and copies ran while one was open for 2% of the time, Pallas kernels for 9%

profile of v14, /device:TPU:8, one launch (start us, length us, event | category | flops | bytes accessed | tf_op | source)
XLA Modules:
  0.0 151.5 jit_solution(3189736520896296305)
XLA Ops:
  0.0 4.3 %units.1 = (bf16[256,512]{1,0:T(8,128)(2,1)}, f32[1,256]{1,0:T(1,128)}) custom-call(bf16[256,2048]{1,0:T(8,128)(2,1)} %features_ref.1, bf16[2048,512]{1,0:T(8,128)(2,1)} %weight_ref.1), custom_call_target="tpu_custom_call" | custom-call | flops 536870912 | bytes 3000000 | tf_op jit(solution)/shard_map/units/pallas_call | solution.py:235
  4.3 4.4 %collective-permute-start = (bf16[256,512]{1,0:T(8,128)(2,1)}, bf16[256,512]{1,0:T(8,128)(2,1)S(1)}, u32[]{:S(2)}, u32[]{:S(2)}) collective-permute-start(bf16[256,512]{1,0:T(8,128)(2,1)} %get-tuple-element.15), channel_id=1, source_target_pairs={{0,80},{1,112},{2,82},{3,114},{4,84},{5,116},{6,86},{7,118},{8,88}... | collective-permute-start | bytes 786440 | tf_op jit(solution)/shard_map/ppermute | solution.py:306
  8.7 2.0 %collective-permute-start.7 = (bf16[256,512]{1,0:T(8,128)(2,1)}, bf16[256,512]{1,0:T(8,128)(2,1)S(1)}, u32[]{:S(2)}, u32[]{:S(2)}) collective-permute-start(bf16[256,512]{1,0:T(8,128)(2,1)} %get-tuple-element.15), channel_id=1, source_target_pairs={{0,465},{1,497},{2,467},{3,499},{4,469},{5,501},{6,471},{7,503},{8... | collective-permute-start | bytes 786440 | tf_op jit(solution)/shard_map/ppermute | solution.py:307
  10.7 5.4 %collective-permute-start.6 = (bf16[256,512]{1,0:T(8,128)(2,1)}, bf16[256,512]{1,0:T(8,128)(2,1)S(1)}, u32[]{:S(2)}, u32[]{:S(2)}) collective-permute-start(bf16[256,512]{1,0:T(8,128)(2,1)} %get-tuple-element.15), channel_id=1, source_target_pairs={{0,16},{1,48},{2,18},{3,50},{4,20},{5,52},{6,22},{7,54},{8,24},{9,... | collective-permute-start | bytes 786440 | tf_op jit(solution)/shard_map/ppermute | solution.py:308
  16.2 2.3 %collective-permute-start.1 = (bf16[256,512]{1,0:T(8,128)(2,1)S(1)}, bf16[256,512]{1,0:T(8,128)(2,1)S(1)}, u32[]{:S(2)}, u32[]{:S(2)}) collective-permute-start(bf16[256,512]{1,0:T(8,128)(2,1)S(1)} %collective-permute-done.refs_1_), channel_id=1, source_target_pairs={{0,64},{1,449},{64,128},{65,1},{128,192},{129,65},{192,256},{193,1... | collective-permute-start | bytes 786440 | tf_op jit(solution)/shard_map/ppermute | solution.py:314
  18.5 0.7 pad_maximum_fusion
  19.3 5.9 %collective-permute-start.5 = (f32[2,256]{0,1:T(8,128)S(1)}, f32[2,256]{0,1:T(8,128)S(1)}, u32[]{:S(2)}, u32[]{:S(2)}) collective-permute-start(f32[2,256]{0,1:T(8,128)S(1)} %copy.11), channel_id=1, source_target_pairs={{0,16},{1,48},{2,18},{3,50},{4,20},{5,52},{6,22},{7,54},{8,24},{9,... | collective-permute-start | bytes 6152 | tf_op jit(solution)/shard_map/ppermute | solution.py:309
  25.3 1.9 %collective-permute-start.8 = (bf16[256,512]{1,0:T(8,128)(2,1)S(1)}, bf16[256,512]{1,0:T(8,128)(2,1)S(1)}, u32[]{:S(2)}, u32[]{:S(2)}) collective-permute-start(bf16[256,512]{1,0:T(8,128)(2,1)S(1)} %collective-permute-done.7.refs_2_), channel_id=1, source_target_pairs={{0,64},{1,449},{64,128},{65,1},{128,192},{129,65},{192,256},{193,1... | collective-permute-start | bytes 786440 | tf_op jit(solution)/shard_map/ppermute | solution.py:333
  27.3 0.7 collective-permute-done.1.refs_3_
  28.0 5.1 %collective-permute-start.2 = (bf16[256,512]{1,0:T(8,128)(2,1)S(1)}, bf16[256,512]{1,0:T(8,128)(2,1)S(1)}, u32[]{:S(2)}, u32[]{:S(2)}) collective-permute-start(bf16[256,512]{1,0:T(8,128)(2,1)S(1)} %collective-permute-done.1.refs_3_), channel_id=1, source_target_pairs={{0,64},{1,449},{64,128},{65,1},{128,192},{129,65},{192,256},{193,1... | collective-permute-start | bytes 786440 | tf_op jit(solution)/shard_map/ppermute | solution.py:314
  33.1 0.4 collective-permute-done.8.refs_4_
  33.5 3.4 %collective-permute-start.9 = (bf16[256,512]{1,0:T(8,128)(2,1)S(1)}, bf16[256,512]{1,0:T(8,128)(2,1)S(1)}, u32[]{:S(2)}, u32[]{:S(2)}) collective-permute-start(bf16[256,512]{1,0:T(8,128)(2,1)S(1)} %collective-permute-done.8.refs_4_), channel_id=1, source_target_pairs={{0,64},{1,449},{64,128},{65,1},{128,192},{129,65},{192,256},{193,1... | collective-permute-start | bytes 786440 | tf_op jit(solution)/shard_map/ppermute | solution.py:333
  36.9 0.5 collective-permute-done.2.refs_5_
  37.4 3.9 %collective-permute-start.4 = (bf16[256,512]{1,0:T(8,128)(2,1)S(1)}, bf16[256,512]{1,0:T(8,128)(2,1)S(1)}, u32[]{:S(2)}, u32[]{:S(2)}) collective-permute-start(bf16[256,512]{1,0:T(8,128)(2,1)S(1)} %collective-permute-done.2.refs_5_), channel_id=1, source_target_pairs={{0,64},{1,449},{64,128},{65,1},{128,192},{129,65},{192,256},{193,1... | collective-permute-start | bytes 786440 | tf_op jit(solution)/shard_map/ppermute | solution.py:314
  41.4 2.2 %early_sums.1.early_ref = f32[3,1,512]{2,1,0:T(1,128)S(1)} custom-call(bf16[256,512]{1,0:T(8,128)(2,1)S(1)} %collective-permute-done.6.refs_0_, bf16[256,512]{1,0:T(8,128)(2,1)S(1)} %collective-permute-done.refs_1_, bf16[256,512]{1,0:T(8,128)(2,1)S(1)} %collective-permute-done.7.refs_2_, bf16[256,512]{1,0:T(8,128)(2,1)S(1)} %collective-permute-done.1.refs_3_, ...), custom_call_target="tpu_custom_call" | custom-call | flops 2000000000 | bytes 2000000 | tf_op jit(solution)/shard_map/early_sums/pallas_call | solution.py:316
  43.6 3.3 %collective-permute-done.4 = bf16[256,512]{1,0:T(8,128)(2,1)S(1)} collective-permute-done((bf16[256,512]{1,0:T(8,128)(2,1)S(1)}, bf16[256,512]{1,0:T(8,128)(2,1)S(1)}, u32[]{:S(2)}, u32[]{:S(2)}) %collective-permute-start.4) | collective-permute-done | bytes 262176 | tf_op jit(solution)/shard_map/ppermute | solution.py:314
  46.9 1.9 %collective-permute-start.10 = (bf16[2048,512]{1,0:T(8,128)(2,1)S(1)}, bf16[2048,512]{1,0:T(8,128)(2,1)}, u32[]{:S(2)}, u32[]{:S(2)}) collective-permute-start(bf16[2048,512]{1,0:T(8,128)(2,1)S(1)} %constant_dynamic-update-slice_fusion.mine_hbm.mine_ref), channel_id=1, source_target_pairs={{0,1},{1,0},{2,3},{3,2},{4,5},{5,4},{6,7},{7,6},{8,9},{9,8},{10,11... | collective-permute-start | bytes 6291464 | tf_op jit(solution)/shard_map/ppermute | solution.py:345
  48.9 2.0 %collective-permute-start.3 = (bf16[256,2048]{1,0:T(8,128)(2,1)}, bf16[256,2048]{1,0:T(8,128)(2,1)}, u32[]{:S(2)}, u32[]{:S(2)}) collective-permute-start(bf16[256,2048]{1,0:T(8,128)(2,1)} %features_ref.1), channel_id=1, source_target_pairs={{0,16},{1,48},{2,18},{3,50},{4,20},{5,52},{6,22},{7,54},{8,24},{9,... | collective-permute-start | bytes 3145736 | tf_op jit(solution)/shard_map/ppermute | solution.py:331
  51.2 1.9 %collective-permute-done.10.sibling_hbm.sibling_ref = bf16[2048,512]{1,0:T(8,128)(2,1)} collective-permute-done((bf16[2048,512]{1,0:T(8,128)(2,1)S(1)}, bf16[2048,512]{1,0:T(8,128)(2,1)}, u32[]{:S(2)}, u32[]{:S(2)}) %collective-permute-start.10) | collective-permute-done | bytes 2097184 | tf_op jit(solution)/shard_map/ppermute | solution.py:345
  53.1 6.3 %pair_sums.1 = f32[8,1,512]{2,1,0:T(1,128)S(1)} custom-call(s32[1]{0:T(128)} %bitcast.core_ref, bf16[2048,512]{1,0:T(8,128)(2,1)S(1)} %constant_dynamic-update-slice_fusion.mine_hbm.mine_ref, bf16[2048,512]{1,0:T(8,128)(2,1)} %collective-permute-done.10.sibling_hbm.sibling_ref, f32[3,1,512]{2,1,0:T(1,128)S(1)} %early_sums.1.early_ref), custom_call_target="tpu_custom_call" | custom-call | flops 3000000000 | bytes 2000000 | tf_op jit(solution)/shard_map/pair_sums/pallas_call | solution.py:348
  59.4 3.4 %psum.7.sums_ref = f32[8,1,512]{2,1,0:T(1,128)S(1)} all-reduce(f32[8,1,512]{2,1,0:T(1,128)S(1)} %pair_sums.1), channel_id=1, replica_groups=mesh['y2'=2,'y1'=2,'y0'=2,'xh'=2,'xl'=2,'z2'=2,'z1'=2,'z0'=2,'c'=2] {'c'}, use_global_device_ids=true, to_apply=%region_0.1 | all-reduce | flops 4096 | bytes 32768 | tf_op jit(solution)/shard_map/psum | solution.py:361
  62.8 5.2 %weights.1 = (bf16[256,256]{1,0:T(8,128)(2,1)S(1)}, bf16[256,256]{1,0:T(8,128)(2,1)S(1)}) custom-call(s32[1]{0:T(128)} %bitcast.core_ref, s32[16]{0:T(128)S(1)} %broadcast_multiply_fusion.start_ref, f32[256,2]{1,0:T(8,128)S(1)} %bitcast.34, f32[8,1,512]{2,1,0:T(1,128)S(1)} %psum.7.sums_ref, ...), custom_call_target="tpu_custom_call" | custom-call | flops 2000000000 | bytes 2000000 | tf_op jit(solution)/shard_map/weights/pallas_call | solution.py:363
  68.0 1.7 %convolution_convert_fusion = bf16[2048,256]{1,0:T(8,128)(2,1)S(1)} fusion(bf16[256,2048]{1,0:T(8,128)(2,1)} %collective-permute-done.3, bf16[256,256]{1,0:T(8,128)(2,1)S(1)} %get-tuple-element.22), kind=kOutput, calls=%fused_computation | convolution fusion | flops 268959744 | bytes 2228224 | tf_op jit(solution)/shard_map/dot_general | solution.py:372
  69.7 2.3 %collective-permute-start.11 = (bf16[2048,256]{1,0:T(8,128)(2,1)S(1)}, bf16[2048,256]{1,0:T(8,128)(2,1)S(1)}, u32[]{:S(2)}, u32[]{:S(2)}) collective-permute-start(bf16[2048,256]{1,0:T(8,128)(2,1)S(1)} %convolution_convert_fusion), channel_id=1, source_target_pairs={{0,1},{1,0},{2,3},{3,2},{4,5},{5,4},{6,7},{7,6},{8,9},{9,8},{10,11... | collective-permute-start | bytes 3145736 | tf_op jit(solution)/shard_map/ppermute | solution.py:377
  72.0 1.7 %fusion = f32[2048,256]{1,0:T(8,128)S(1)} fusion(bf16[256,2048]{1,0:T(8,128)(2,1)} %collective-permute-done.3, bf16[256,256]{1,0:T(8,128)(2,1)S(1)} %get-tuple-element.21), kind=kOutput, calls=%fused_computation.12 | convolution fusion | flops 268435456 | bytes 3276800 | tf_op jit(solution)/shard_map/dot_general | solution.py:372
  73.7 0.6 collective-permute-done.11
  74.3 0.3 add_convert_fusion
  74.7 22.5 %all_to_all.26 = bf16[16,128,256]{2,1,0:T(8,128)(2,1)S(1)} all-to-all(bf16[16,128,256]{2,1,0:T(8,128)(2,1)S(1)} %bitcast.35), channel_id=1, replica_groups=mesh['y2'=2,'y1'=2,'y0'=2,'xh'=2,'xl'=2,'z2'=2,'z1'=2,'z0'=2,'c'=2] {'z0..., dimensions={0} | all-to-all | bytes 2097152 | tf_op jit(solution)/shard_map/all_to_all | solution.py:382
  97.4 26.5 %all_to_all.27 = bf16[16,8,256]{2,1,0:T(8,128)(2,1)S(1)} all-to-all(bf16[16,8,256]{2,1,0:T(8,128)(2,1)S(1)} %bitcast.37), channel_id=1, replica_groups=mesh['y2'=2,'y1'=2,'y0'=2,'xh'=2,'xl'=2,'z2'=2,'z1'=2,'z0'=2,'c'=2] {'y2..., dimensions={0} | all-to-all | bytes 131072 | tf_op jit(solution)/shard_map/all_to_all | solution.py:384
  123.9 13.4 %all_to_all.28.spread_ref = bf16[32,8,256]{2,1,0:T(8,128)(2,1)S(1)} all-to-all(bf16[32,8,256]{2,1,0:T(8,128)(2,1)S(1)} %broadcast_in_dim.10), channel_id=1, replica_groups=mesh['y2'=2,'y1'=2,'y0'=2,'xh'=2,'xl'=2,'z2'=2,'z1'=2,'z0'=2,'c'=2] {'c'..., dimensions={0} | all-to-all | bytes 262144 | tf_op jit(solution)/shard_map/all_to_all | solution.py:386
  137.5 13.3 %all_to_all.29 = f32[16,1,128]{2,1,0:T(1,128)S(1)} all-to-all(f32[16,1,128]{2,1,0:T(1,128)S(1)} %bitcast.33), channel_id=1, replica_groups=mesh['y2'=2,'y1'=2,'y0'=2,'xh'=2,'xl'=2,'z2'=2,'z1'=2,'z0'=2,'c'=2] {'y2..., dimensions={0} | all-to-all | bytes 16384 | tf_op jit(solution)/shard_map/all_to_all | solution.py:392
  150.8 0.7 scale.1
  (25 shorter events, 0.9 us)
Async XLA Ops:
  0.0 16.1 %copy-start = (s32[256]{0:T(256)S(1)}, s32[256]{0:T(256)}, u32[]{:S(2)}) copy-start(s32[256]{0:T(256)} %param.5) | copy-start | bytes 3076
  4.3 11.9 %collective-permute-start = (bf16[256,512]{1,0:T(8,128)(2,1)}, bf16[256,512]{1,0:T(8,128)(2,1)S(1)}, u32[]{:S(2)}, u32[]{:S(2)}) collective-permute-start(bf16[256,512]{1,0:T(8,128)(2,1)} %get-tuple-element.15), channel_id=1, source_target_pairs={{0,80},{1,112},{2,82},{3,114},{4,84},{5,116},{6,86},{7,118},{8,88}... | collective-permute-start | bytes 786440 | tf_op jit(solution)/shard_map/ppermute | solution.py:306
  8.7 16.6 %collective-permute-start.7 = (bf16[256,512]{1,0:T(8,128)(2,1)}, bf16[256,512]{1,0:T(8,128)(2,1)S(1)}, u32[]{:S(2)}, u32[]{:S(2)}) collective-permute-start(bf16[256,512]{1,0:T(8,128)(2,1)} %get-tuple-element.15), channel_id=1, source_target_pairs={{0,465},{1,497},{2,467},{3,499},{4,469},{5,501},{6,471},{7,503},{8... | collective-permute-start | bytes 786440 | tf_op jit(solution)/shard_map/ppermute | solution.py:307
  10.7 16.5 %collective-permute-start.6 = (bf16[256,512]{1,0:T(8,128)(2,1)}, bf16[256,512]{1,0:T(8,128)(2,1)S(1)}, u32[]{:S(2)}, u32[]{:S(2)}) collective-permute-start(bf16[256,512]{1,0:T(8,128)(2,1)} %get-tuple-element.15), channel_id=1, source_target_pairs={{0,16},{1,48},{2,18},{3,50},{4,20},{5,52},{6,22},{7,54},{8,24},{9,... | collective-permute-start | bytes 786440 | tf_op jit(solution)/shard_map/ppermute | solution.py:308
  16.2 11.8 %collective-permute-start.1 = (bf16[256,512]{1,0:T(8,128)(2,1)S(1)}, bf16[256,512]{1,0:T(8,128)(2,1)S(1)}, u32[]{:S(2)}, u32[]{:S(2)}) collective-permute-start(bf16[256,512]{1,0:T(8,128)(2,1)S(1)} %collective-permute-done.refs_1_), channel_id=1, source_target_pairs={{0,64},{1,449},{64,128},{65,1},{128,192},{129,65},{192,256},{193,1... | collective-permute-start | bytes 786440 | tf_op jit(solution)/shard_map/ppermute | solution.py:314
  19.3 24.3 %collective-permute-start.5 = (f32[2,256]{0,1:T(8,128)S(1)}, f32[2,256]{0,1:T(8,128)S(1)}, u32[]{:S(2)}, u32[]{:S(2)}) collective-permute-start(f32[2,256]{0,1:T(8,128)S(1)} %copy.11), channel_id=1, source_target_pairs={{0,16},{1,48},{2,18},{3,50},{4,20},{5,52},{6,22},{7,54},{8,24},{9,... | collective-permute-start | bytes 6152 | tf_op jit(solution)/shard_map/ppermute | solution.py:309
  25.3 8.3 %collective-permute-start.8 = (bf16[256,512]{1,0:T(8,128)(2,1)S(1)}, bf16[256,512]{1,0:T(8,128)(2,1)S(1)}, u32[]{:S(2)}, u32[]{:S(2)}) collective-permute-start(bf16[256,512]{1,0:T(8,128)(2,1)S(1)} %collective-permute-done.7.refs_2_), channel_id=1, source_target_pairs={{0,64},{1,449},{64,128},{65,1},{128,192},{129,65},{192,256},{193,1... | collective-permute-start | bytes 786440 | tf_op jit(solution)/shard_map/ppermute | solution.py:333
  28.0 9.5 %collective-permute-start.2 = (bf16[256,512]{1,0:T(8,128)(2,1)S(1)}, bf16[256,512]{1,0:T(8,128)(2,1)S(1)}, u32[]{:S(2)}, u32[]{:S(2)}) collective-permute-start(bf16[256,512]{1,0:T(8,128)(2,1)S(1)} %collective-permute-done.1.refs_3_), channel_id=1, source_target_pairs={{0,64},{1,449},{64,128},{65,1},{128,192},{129,65},{192,256},{193,1... | collective-permute-start | bytes 786440 | tf_op jit(solution)/shard_map/ppermute | solution.py:314
  33.5 10.0 %collective-permute-start.9 = (bf16[256,512]{1,0:T(8,128)(2,1)S(1)}, bf16[256,512]{1,0:T(8,128)(2,1)S(1)}, u32[]{:S(2)}, u32[]{:S(2)}) collective-permute-start(bf16[256,512]{1,0:T(8,128)(2,1)S(1)} %collective-permute-done.8.refs_4_), channel_id=1, source_target_pairs={{0,64},{1,449},{64,128},{65,1},{128,192},{129,65},{192,256},{193,1... | collective-permute-start | bytes 786440 | tf_op jit(solution)/shard_map/ppermute | solution.py:333
  37.4 9.5 %collective-permute-start.4 = (bf16[256,512]{1,0:T(8,128)(2,1)S(1)}, bf16[256,512]{1,0:T(8,128)(2,1)S(1)}, u32[]{:S(2)}, u32[]{:S(2)}) collective-permute-start(bf16[256,512]{1,0:T(8,128)(2,1)S(1)} %collective-permute-done.2.refs_5_), channel_id=1, source_target_pairs={{0,64},{1,449},{64,128},{65,1},{128,192},{129,65},{192,256},{193,1... | collective-permute-start | bytes 786440 | tf_op jit(solution)/shard_map/ppermute | solution.py:314
  46.9 6.2 %collective-permute-start.10 = (bf16[2048,512]{1,0:T(8,128)(2,1)S(1)}, bf16[2048,512]{1,0:T(8,128)(2,1)}, u32[]{:S(2)}, u32[]{:S(2)}) collective-permute-start(bf16[2048,512]{1,0:T(8,128)(2,1)S(1)} %constant_dynamic-update-slice_fusion.mine_hbm.mine_ref), channel_id=1, source_target_pairs={{0,1},{1,0},{2,3},{3,2},{4,5},{5,4},{6,7},{7,6},{8,9},{9,8},{10,11... | collective-permute-start | bytes 6291464 | tf_op jit(solution)/shard_map/ppermute | solution.py:345
  48.9 19.1 %collective-permute-start.3 = (bf16[256,2048]{1,0:T(8,128)(2,1)}, bf16[256,2048]{1,0:T(8,128)(2,1)}, u32[]{:S(2)}, u32[]{:S(2)}) collective-permute-start(bf16[256,2048]{1,0:T(8,128)(2,1)} %features_ref.1), channel_id=1, source_target_pairs={{0,16},{1,48},{2,18},{3,50},{4,20},{5,52},{6,22},{7,54},{8,24},{9,... | collective-permute-start | bytes 3145736 | tf_op jit(solution)/shard_map/ppermute | solution.py:331
  69.7 4.6 %collective-permute-start.11 = (bf16[2048,256]{1,0:T(8,128)(2,1)S(1)}, bf16[2048,256]{1,0:T(8,128)(2,1)S(1)}, u32[]{:S(2)}, u32[]{:S(2)}) collective-permute-start(bf16[2048,256]{1,0:T(8,128)(2,1)S(1)} %convolution_convert_fusion), channel_id=1, source_target_pairs={{0,1},{1,0},{2,3},{3,2},{4,5},{5,4},{6,7},{7,6},{8,9},{9,8},{10,11... | collective-permute-start | bytes 3145736 | tf_op jit(solution)/shard_map/ppermute | solution.py:377

commit v15 on v14

--- a/solution.py
+++ b/solution.py
@@ -284,7 +284,7 @@
         in_specs=in_specs,
         out_specs=jax.tree.map(lambda unused: VMEM, outputs),
         scratch_shapes=scratch,
-        compiler_params=pltpu.CompilerParams(vmem_limit_bytes=24 * 1024 * 1024),
+        compiler_params=pltpu.CompilerParams(vmem_limit_bytes=16 * 1024 * 1024),
         cost_estimate=pl.CostEstimate(
             flops=flops, bytes_accessed=2_000_000, transcendentals=100_000
         ),

time: 152 us -> 152 us (level)
  no operation moved by 1% of the time
where the time goes in v15:
time: 152 us
  blocking collectives  79.1 us (52%)
  starting transfers between devices  40.6 us (27%)
  Pallas kernels  18.9 us (12%)
  waiting for transfers between devices  7.42 us (5%)
  matrix products  3.43 us (2%)
    all_to_all x1, blocking collectives, on_device(): received = lax.all_to_all(near_sum, ('y2', 'y1', 'z2', 'z1'), 0, 0)  26.5 us
    all_to_all x1, blocking collectives, on_device(): received = lax.all_to_all(tiles, ('z0', 'xl', 'y0', 'xh'), 0, 0)  22.5 us
    all_to_all x1, blocking collectives, on_device(): lax.all_to_all(jnp.broadcast_to(fragment[None], (32, 8, 256)), ('c', 'xl'...  13.4 us
    all_to_all x1, blocking collectives, on_device(): squares = lax.all_to_all(squares, ('y2', 'y1', 'y0', 'xh'), 0, 0)  13.3 us
    ppermute x3, starting transfers between devices, on_device(): same_core = lax.ppermute(same_core, (*YBITS, 'c'), ROUND)  11.4 us
    pallas_call x1, Pallas kernels, on_device(): kernel_call(pair_sums_kernel, jax.ShapeDtypeStruct((8, 1, 512), jnp.float...  6.28 us
    ppermute x1, starting transfers between devices, on_device(): side_here = lax.ppermute(side, BITS, TO_HOST)  5.9 us
    ppermute x1, starting transfers between devices, on_device(): own = lax.ppermute(unit, BITS, TO_HOST)  5.39 us
  transfers between devices with their start and end apart: 12, of which 6 were waited for; matrix products, arithmetic and copies ran while one was open for 2% of the time, Pallas kernels for 9%

profile of v15, /device:TPU:8, one launch (start us, length us, event | category | flops | bytes accessed | tf_op | source)
XLA Modules:
  0.0 151.5 jit_solution(257831648953817297)
XLA Ops:
  0.0 4.3 %units.1 = (bf16[256,512]{1,0:T(8,128)(2,1)}, f32[1,256]{1,0:T(1,128)}) custom-call(bf16[256,2048]{1,0:T(8,128)(2,1)} %features_ref.1, bf16[2048,512]{1,0:T(8,128)(2,1)} %weight_ref.1), custom_call_target="tpu_custom_call" | custom-call | flops 536870912 | bytes 3000000 | tf_op jit(solution)/shard_map/units/pallas_call | solution.py:235
  4.3 4.4 %collective-permute-start = (bf16[256,512]{1,0:T(8,128)(2,1)}, bf16[256,512]{1,0:T(8,128)(2,1)S(1)}, u32[]{:S(2)}, u32[]{:S(2)}) collective-permute-start(bf16[256,512]{1,0:T(8,128)(2,1)} %get-tuple-element.15), channel_id=1, source_target_pairs={{0,80},{1,112},{2,82},{3,114},{4,84},{5,116},{6,86},{7,118},{8,88}... | collective-permute-start | bytes 786440 | tf_op jit(solution)/shard_map/ppermute | solution.py:306
  8.7 2.0 %collective-permute-start.7 = (bf16[256,512]{1,0:T(8,128)(2,1)}, bf16[256,512]{1,0:T(8,128)(2,1)S(1)}, u32[]{:S(2)}, u32[]{:S(2)}) collective-permute-start(bf16[256,512]{1,0:T(8,128)(2,1)} %get-tuple-element.15), channel_id=1, source_target_pairs={{0,465},{1,497},{2,467},{3,499},{4,469},{5,501},{6,471},{7,503},{8... | collective-permute-start | bytes 786440 | tf_op jit(solution)/shard_map/ppermute | solution.py:307
  10.7 5.4 %collective-permute-start.6 = (bf16[256,512]{1,0:T(8,128)(2,1)}, bf16[256,512]{1,0:T(8,128)(2,1)S(1)}, u32[]{:S(2)}, u32[]{:S(2)}) collective-permute-start(bf16[256,512]{1,0:T(8,128)(2,1)} %get-tuple-element.15), channel_id=1, source_target_pairs={{0,16},{1,48},{2,18},{3,50},{4,20},{5,52},{6,22},{7,54},{8,24},{9,... | collective-permute-start | bytes 786440 | tf_op jit(solution)/shard_map/ppermute | solution.py:308
  16.2 2.3 %collective-permute-start.1 = (bf16[256,512]{1,0:T(8,128)(2,1)S(1)}, bf16[256,512]{1,0:T(8,128)(2,1)S(1)}, u32[]{:S(2)}, u32[]{:S(2)}) collective-permute-start(bf16[256,512]{1,0:T(8,128)(2,1)S(1)} %collective-permute-done.refs_1_), channel_id=1, source_target_pairs={{0,64},{1,449},{64,128},{65,1},{128,192},{129,65},{192,256},{193,1... | collective-permute-start | bytes 786440 | tf_op jit(solution)/shard_map/ppermute | solution.py:314
  18.5 0.7 pad_maximum_fusion
  19.3 5.9 %collective-permute-start.5 = (f32[2,256]{0,1:T(8,128)S(1)}, f32[2,256]{0,1:T(8,128)S(1)}, u32[]{:S(2)}, u32[]{:S(2)}) collective-permute-start(f32[2,256]{0,1:T(8,128)S(1)} %copy.11), channel_id=1, source_target_pairs={{0,16},{1,48},{2,18},{3,50},{4,20},{5,52},{6,22},{7,54},{8,24},{9,... | collective-permute-start | bytes 6152 | tf_op jit(solution)/shard_map/ppermute | solution.py:309
  25.3 1.9 %collective-permute-start.8 = (bf16[256,512]{1,0:T(8,128)(2,1)S(1)}, bf16[256,512]{1,0:T(8,128)(2,1)S(1)}, u32[]{:S(2)}, u32[]{:S(2)}) collective-permute-start(bf16[256,512]{1,0:T(8,128)(2,1)S(1)} %collective-permute-done.7.refs_2_), channel_id=1, source_target_pairs={{0,64},{1,449},{64,128},{65,1},{128,192},{129,65},{192,256},{193,1... | collective-permute-start | bytes 786440 | tf_op jit(solution)/shard_map/ppermute | solution.py:333
  27.3 0.7 collective-permute-done.1.refs_3_
  28.0 5.1 %collective-permute-start.2 = (bf16[256,512]{1,0:T(8,128)(2,1)S(1)}, bf16[256,512]{1,0:T(8,128)(2,1)S(1)}, u32[]{:S(2)}, u32[]{:S(2)}) collective-permute-start(bf16[256,512]{1,0:T(8,128)(2,1)S(1)} %collective-permute-done.1.refs_3_), channel_id=1, source_target_pairs={{0,64},{1,449},{64,128},{65,1},{128,192},{129,65},{192,256},{193,1... | collective-permute-start | bytes 786440 | tf_op jit(solution)/shard_map/ppermute | solution.py:314
  33.1 0.4 collective-permute-done.8.refs_4_
  33.5 3.4 %collective-permute-start.9 = (bf16[256,512]{1,0:T(8,128)(2,1)S(1)}, bf16[256,512]{1,0:T(8,128)(2,1)S(1)}, u32[]{:S(2)}, u32[]{:S(2)}) collective-permute-start(bf16[256,512]{1,0:T(8,128)(2,1)S(1)} %collective-permute-done.8.refs_4_), channel_id=1, source_target_pairs={{0,64},{1,449},{64,128},{65,1},{128,192},{129,65},{192,256},{193,1... | collective-permute-start | bytes 786440 | tf_op jit(solution)/shard_map/ppermute | solution.py:333
  36.9 0.5 collective-permute-done.2.refs_5_
  37.4 3.9 %collective-permute-start.4 = (bf16[256,512]{1,0:T(8,128)(2,1)S(1)}, bf16[256,512]{1,0:T(8,128)(2,1)S(1)}, u32[]{:S(2)}, u32[]{:S(2)}) collective-permute-start(bf16[256,512]{1,0:T(8,128)(2,1)S(1)} %collective-permute-done.2.refs_5_), channel_id=1, source_target_pairs={{0,64},{1,449},{64,128},{65,1},{128,192},{129,65},{192,256},{193,1... | collective-permute-start | bytes 786440 | tf_op jit(solution)/shard_map/ppermute | solution.py:314
  41.4 2.2 %early_sums.1.early_ref = f32[3,1,512]{2,1,0:T(1,128)S(1)} custom-call(bf16[256,512]{1,0:T(8,128)(2,1)S(1)} %collective-permute-done.6.refs_0_, bf16[256,512]{1,0:T(8,128)(2,1)S(1)} %collective-permute-done.refs_1_, bf16[256,512]{1,0:T(8,128)(2,1)S(1)} %collective-permute-done.7.refs_2_, bf16[256,512]{1,0:T(8,128)(2,1)S(1)} %collective-permute-done.1.refs_3_, ...), custom_call_target="tpu_custom_call" | custom-call | flops 2000000000 | bytes 2000000 | tf_op jit(solution)/shard_map/early_sums/pallas_call | solution.py:316
  43.6 3.3 %collective-permute-done.4 = bf16[256,512]{1,0:T(8,128)(2,1)S(1)} collective-permute-done((bf16[256,512]{1,0:T(8,128)(2,1)S(1)}, bf16[256,512]{1,0:T(8,128)(2,1)S(1)}, u32[]{:S(2)}, u32[]{:S(2)}) %collective-permute-start.4) | collective-permute-done | bytes 262176 | tf_op jit(solution)/shard_map/ppermute | solution.py:314
  46.9 1.9 %collective-permute-start.10 = (bf16[2048,512]{1,0:T(8,128)(2,1)S(1)}, bf16[2048,512]{1,0:T(8,128)(2,1)}, u32[]{:S(2)}, u32[]{:S(2)}) collective-permute-start(bf16[2048,512]{1,0:T(8,128)(2,1)S(1)} %constant_dynamic-update-slice_fusion.mine_hbm.mine_ref), channel_id=1, source_target_pairs={{0,1},{1,0},{2,3},{3,2},{4,5},{5,4},{6,7},{7,6},{8,9},{9,8},{10,11... | collective-permute-start | bytes 6291464 | tf_op jit(solution)/shard_map/ppermute | solution.py:345
  48.9 2.0 %collective-permute-start.3 = (bf16[256,2048]{1,0:T(8,128)(2,1)}, bf16[256,2048]{1,0:T(8,128)(2,1)}, u32[]{:S(2)}, u32[]{:S(2)}) collective-permute-start(bf16[256,2048]{1,0:T(8,128)(2,1)} %features_ref.1), channel_id=1, source_target_pairs={{0,16},{1,48},{2,18},{3,50},{4,20},{5,52},{6,22},{7,54},{8,24},{9,... | collective-permute-start | bytes 3145736 | tf_op jit(solution)/shard_map/ppermute | solution.py:331
  51.2 1.9 %collective-permute-done.10.sibling_hbm.sibling_ref = bf16[2048,512]{1,0:T(8,128)(2,1)} collective-permute-done((bf16[2048,512]{1,0:T(8,128)(2,1)S(1)}, bf16[2048,512]{1,0:T(8,128)(2,1)}, u32[]{:S(2)}, u32[]{:S(2)}) %collective-permute-start.10) | collective-permute-done | bytes 2097184 | tf_op jit(solution)/shard_map/ppermute | solution.py:345
  53.1 6.3 %pair_sums.1 = f32[8,1,512]{2,1,0:T(1,128)S(1)} custom-call(s32[1]{0:T(128)} %bitcast.core_ref, bf16[2048,512]{1,0:T(8,128)(2,1)S(1)} %constant_dynamic-update-slice_fusion.mine_hbm.mine_ref, bf16[2048,512]{1,0:T(8,128)(2,1)} %collective-permute-done.10.sibling_hbm.sibling_ref, f32[3,1,512]{2,1,0:T(1,128)S(1)} %early_sums.1.early_ref), custom_call_target="tpu_custom_call" | custom-call | flops 3000000000 | bytes 2000000 | tf_op jit(solution)/shard_map/pair_sums/pallas_call | solution.py:348
  59.4 3.4 %psum.7.sums_ref = f32[8,1,512]{2,1,0:T(1,128)S(1)} all-reduce(f32[8,1,512]{2,1,0:T(1,128)S(1)} %pair_sums.1), channel_id=1, replica_groups=mesh['y2'=2,'y1'=2,'y0'=2,'xh'=2,'xl'=2,'z2'=2,'z1'=2,'z0'=2,'c'=2] {'c'}, use_global_device_ids=true, to_apply=%region_0.1 | all-reduce | flops 4096 | bytes 32768 | tf_op jit(solution)/shard_map/psum | solution.py:361
  62.8 5.2 %weights.1 = (bf16[256,256]{1,0:T(8,128)(2,1)S(1)}, bf16[256,256]{1,0:T(8,128)(2,1)S(1)}) custom-call(s32[1]{0:T(128)} %bitcast.core_ref, s32[16]{0:T(128)S(1)} %broadcast_multiply_fusion.start_ref, f32[256,2]{1,0:T(8,128)S(1)} %bitcast.34, f32[8,1,512]{2,1,0:T(1,128)S(1)} %psum.7.sums_ref, ...), custom_call_target="tpu_custom_call" | custom-call | flops 2000000000 | bytes 2000000 | tf_op jit(solution)/shard_map/weights/pallas_call | solution.py:363
  68.0 1.7 %convolution_convert_fusion = bf16[2048,256]{1,0:T(8,128)(2,1)S(1)} fusion(bf16[256,2048]{1,0:T(8,128)(2,1)} %collective-permute-done.3, bf16[256,256]{1,0:T(8,128)(2,1)S(1)} %get-tuple-element.22), kind=kOutput, calls=%fused_computation | convolution fusion | flops 268959744 | bytes 2228224 | tf_op jit(solution)/shard_map/dot_general | solution.py:372
  69.7 2.3 %collective-permute-start.11 = (bf16[2048,256]{1,0:T(8,128)(2,1)S(1)}, bf16[2048,256]{1,0:T(8,128)(2,1)S(1)}, u32[]{:S(2)}, u32[]{:S(2)}) collective-permute-start(bf16[2048,256]{1,0:T(8,128)(2,1)S(1)} %convolution_convert_fusion), channel_id=1, source_target_pairs={{0,1},{1,0},{2,3},{3,2},{4,5},{5,4},{6,7},{7,6},{8,9},{9,8},{10,11... | collective-permute-start | bytes 3145736 | tf_op jit(solution)/shard_map/ppermute | solution.py:377
  72.0 1.7 %fusion = f32[2048,256]{1,0:T(8,128)S(1)} fusion(bf16[256,2048]{1,0:T(8,128)(2,1)} %collective-permute-done.3, bf16[256,256]{1,0:T(8,128)(2,1)S(1)} %get-tuple-element.21), kind=kOutput, calls=%fused_computation.12 | convolution fusion | flops 268435456 | bytes 3276800 | tf_op jit(solution)/shard_map/dot_general | solution.py:372
  73.7 0.6 collective-permute-done.11
  74.3 0.3 add_convert_fusion
  74.7 22.5 %all_to_all.26 = bf16[16,128,256]{2,1,0:T(8,128)(2,1)S(1)} all-to-all(bf16[16,128,256]{2,1,0:T(8,128)(2,1)S(1)} %bitcast.35), channel_id=1, replica_groups=mesh['y2'=2,'y1'=2,'y0'=2,'xh'=2,'xl'=2,'z2'=2,'z1'=2,'z0'=2,'c'=2] {'z0..., dimensions={0} | all-to-all | bytes 2097152 | tf_op jit(solution)/shard_map/all_to_all | solution.py:382
  97.4 26.5 %all_to_all.27 = bf16[16,8,256]{2,1,0:T(8,128)(2,1)S(1)} all-to-all(bf16[16,8,256]{2,1,0:T(8,128)(2,1)S(1)} %bitcast.37), channel_id=1, replica_groups=mesh['y2'=2,'y1'=2,'y0'=2,'xh'=2,'xl'=2,'z2'=2,'z1'=2,'z0'=2,'c'=2] {'y2..., dimensions={0} | all-to-all | bytes 131072 | tf_op jit(solution)/shard_map/all_to_all | solution.py:384
  123.9 13.4 %all_to_all.28.spread_ref = bf16[32,8,256]{2,1,0:T(8,128)(2,1)S(1)} all-to-all(bf16[32,8,256]{2,1,0:T(8,128)(2,1)S(1)} %broadcast_in_dim.10), channel_id=1, replica_groups=mesh['y2'=2,'y1'=2,'y0'=2,'xh'=2,'xl'=2,'z2'=2,'z1'=2,'z0'=2,'c'=2] {'c'..., dimensions={0} | all-to-all | bytes 262144 | tf_op jit(solution)/shard_map/all_to_all | solution.py:386
  137.5 13.3 %all_to_all.29 = f32[16,1,128]{2,1,0:T(1,128)S(1)} all-to-all(f32[16,1,128]{2,1,0:T(1,128)S(1)} %bitcast.33), channel_id=1, replica_groups=mesh['y2'=2,'y1'=2,'y0'=2,'xh'=2,'xl'=2,'z2'=2,'z1'=2,'z0'=2,'c'=2] {'y2..., dimensions={0} | all-to-all | bytes 16384 | tf_op jit(solution)/shard_map/all_to_all | solution.py:392
  150.8 0.7 scale.1
  (25 shorter events, 0.9 us)
Async XLA Ops:
  0.0 16.1 %copy-start = (s32[256]{0:T(256)S(1)}, s32[256]{0:T(256)}, u32[]{:S(2)}) copy-start(s32[256]{0:T(256)} %param.5) | copy-start | bytes 3076
  4.3 11.9 %collective-permute-start = (bf16[256,512]{1,0:T(8,128)(2,1)}, bf16[256,512]{1,0:T(8,128)(2,1)S(1)}, u32[]{:S(2)}, u32[]{:S(2)}) collective-permute-start(bf16[256,512]{1,0:T(8,128)(2,1)} %get-tuple-element.15), channel_id=1, source_target_pairs={{0,80},{1,112},{2,82},{3,114},{4,84},{5,116},{6,86},{7,118},{8,88}... | collective-permute-start | bytes 786440 | tf_op jit(solution)/shard_map/ppermute | solution.py:306
  8.7 16.6 %collective-permute-start.7 = (bf16[256,512]{1,0:T(8,128)(2,1)}, bf16[256,512]{1,0:T(8,128)(2,1)S(1)}, u32[]{:S(2)}, u32[]{:S(2)}) collective-permute-start(bf16[256,512]{1,0:T(8,128)(2,1)} %get-tuple-element.15), channel_id=1, source_target_pairs={{0,465},{1,497},{2,467},{3,499},{4,469},{5,501},{6,471},{7,503},{8... | collective-permute-start | bytes 786440 | tf_op jit(solution)/shard_map/ppermute | solution.py:307
  10.7 16.5 %collective-permute-start.6 = (bf16[256,512]{1,0:T(8,128)(2,1)}, bf16[256,512]{1,0:T(8,128)(2,1)S(1)}, u32[]{:S(2)}, u32[]{:S(2)}) collective-permute-start(bf16[256,512]{1,0:T(8,128)(2,1)} %get-tuple-element.15), channel_id=1, source_target_pairs={{0,16},{1,48},{2,18},{3,50},{4,20},{5,52},{6,22},{7,54},{8,24},{9,... | collective-permute-start | bytes 786440 | tf_op jit(solution)/shard_map/ppermute | solution.py:308
  16.2 11.8 %collective-permute-start.1 = (bf16[256,512]{1,0:T(8,128)(2,1)S(1)}, bf16[256,512]{1,0:T(8,128)(2,1)S(1)}, u32[]{:S(2)}, u32[]{:S(2)}) collective-permute-start(bf16[256,512]{1,0:T(8,128)(2,1)S(1)} %collective-permute-done.refs_1_), channel_id=1, source_target_pairs={{0,64},{1,449},{64,128},{65,1},{128,192},{129,65},{192,256},{193,1... | collective-permute-start | bytes 786440 | tf_op jit(solution)/shard_map/ppermute | solution.py:314
  19.3 24.3 %collective-permute-start.5 = (f32[2,256]{0,1:T(8,128)S(1)}, f32[2,256]{0,1:T(8,128)S(1)}, u32[]{:S(2)}, u32[]{:S(2)}) collective-permute-start(f32[2,256]{0,1:T(8,128)S(1)} %copy.11), channel_id=1, source_target_pairs={{0,16},{1,48},{2,18},{3,50},{4,20},{5,52},{6,22},{7,54},{8,24},{9,... | collective-permute-start | bytes 6152 | tf_op jit(solution)/shard_map/ppermute | solution.py:309
  25.3 8.3 %collective-permute-start.8 = (bf16[256,512]{1,0:T(8,128)(2,1)S(1)}, bf16[256,512]{1,0:T(8,128)(2,1)S(1)}, u32[]{:S(2)}, u32[]{:S(2)}) collective-permute-start(bf16[256,512]{1,0:T(8,128)(2,1)S(1)} %collective-permute-done.7.refs_2_), channel_id=1, source_target_pairs={{0,64},{1,449},{64,128},{65,1},{128,192},{129,65},{192,256},{193,1... | collective-permute-start | bytes 786440 | tf_op jit(solution)/shard_map/ppermute | solution.py:333
  28.0 9.5 %collective-permute-start.2 = (bf16[256,512]{1,0:T(8,128)(2,1)S(1)}, bf16[256,512]{1,0:T(8,128)(2,1)S(1)}, u32[]{:S(2)}, u32[]{:S(2)}) collective-permute-start(bf16[256,512]{1,0:T(8,128)(2,1)S(1)} %collective-permute-done.1.refs_3_), channel_id=1, source_target_pairs={{0,64},{1,449},{64,128},{65,1},{128,192},{129,65},{192,256},{193,1... | collective-permute-start | bytes 786440 | tf_op jit(solution)/shard_map/ppermute | solution.py:314
  33.5 10.0 %collective-permute-start.9 = (bf16[256,512]{1,0:T(8,128)(2,1)S(1)}, bf16[256,512]{1,0:T(8,128)(2,1)S(1)}, u32[]{:S(2)}, u32[]{:S(2)}) collective-permute-start(bf16[256,512]{1,0:T(8,128)(2,1)S(1)} %collective-permute-done.8.refs_4_), channel_id=1, source_target_pairs={{0,64},{1,449},{64,128},{65,1},{128,192},{129,65},{192,256},{193,1... | collective-permute-start | bytes 786440 | tf_op jit(solution)/shard_map/ppermute | solution.py:333
  37.4 9.5 %collective-permute-start.4 = (bf16[256,512]{1,0:T(8,128)(2,1)S(1)}, bf16[256,512]{1,0:T(8,128)(2,1)S(1)}, u32[]{:S(2)}, u32[]{:S(2)}) collective-permute-start(bf16[256,512]{1,0:T(8,128)(2,1)S(1)} %collective-permute-done.2.refs_5_), channel_id=1, source_target_pairs={{0,64},{1,449},{64,128},{65,1},{128,192},{129,65},{192,256},{193,1... | collective-permute-start | bytes 786440 | tf_op jit(solution)/shard_map/ppermute | solution.py:314
  46.9 6.2 %collective-permute-start.10 = (bf16[2048,512]{1,0:T(8,128)(2,1)S(1)}, bf16[2048,512]{1,0:T(8,128)(2,1)}, u32[]{:S(2)}, u32[]{:S(2)}) collective-permute-start(bf16[2048,512]{1,0:T(8,128)(2,1)S(1)} %constant_dynamic-update-slice_fusion.mine_hbm.mine_ref), channel_id=1, source_target_pairs={{0,1},{1,0},{2,3},{3,2},{4,5},{5,4},{6,7},{7,6},{8,9},{9,8},{10,11... | collective-permute-start | bytes 6291464 | tf_op jit(solution)/shard_map/ppermute | solution.py:345
  48.9 19.1 %collective-permute-start.3 = (bf16[256,2048]{1,0:T(8,128)(2,1)}, bf16[256,2048]{1,0:T(8,128)(2,1)}, u32[]{:S(2)}, u32[]{:S(2)}) collective-permute-start(bf16[256,2048]{1,0:T(8,128)(2,1)} %features_ref.1), channel_id=1, source_target_pairs={{0,16},{1,48},{2,18},{3,50},{4,20},{5,52},{6,22},{7,54},{8,24},{9,... | collective-permute-start | bytes 3145736 | tf_op jit(solution)/shard_map/ppermute | solution.py:331
  69.7 4.6 %collective-permute-start.11 = (bf16[2048,256]{1,0:T(8,128)(2,1)S(1)}, bf16[2048,256]{1,0:T(8,128)(2,1)S(1)}, u32[]{:S(2)}, u32[]{:S(2)}) collective-permute-start(bf16[2048,256]{1,0:T(8,128)(2,1)S(1)} %convolution_convert_fusion), channel_id=1, source_target_pairs={{0,1},{1,0},{2,3},{3,2},{4,5},{5,4},{6,7},{7,6},{8,9},{9,8},{10,11... | collective-permute-start | bytes 3145736 | tf_op jit(solution)/shard_map/ppermute | solution.py:377
